TPU v7x, 32 devices: a whole 2x2x4 slice. The times are simulated.
32 devices in a mesh: rep: 4 (over y, x), shard: 8 (over z, core).
Axes of the slice: x: 2, y: 2, z: 4, core: 2. Of those that a mesh axis runs over, the one named last changes fastest.
Arguments:
- grad_wide: float32 [4, 1, 384, 5376], P('rep', None, 'shard')
- grad_down: float32 [4, 1, 1536, 384], P('rep', None, None, 'shard')
- grad_embed: float32 [4, 1001, 384], P('rep', None, 'shard')
- mom_wide: float32 [1, 384, 5376], P(None, 'shard'), may hold values from -6 to 6
- mom_down: float32 [1, 1536, 384], P(None, None, 'shard'), may hold values from -6 to 6
- mom_embed: float32 [1001, 384], P(None, 'shard'), may hold values from -6 to 6
Outputs:
- new_mom_wide: float32 [1, 384, 5376], P(None, 'shard')
- new_mom_down: float32 [1, 1536, 384], P(None, None, 'shard')
- new_mom_embed: float32 [1001, 384], P(None, 'shard')
- upd_wide: bfloat16 [1, 384, 5376], P(None, 'shard')
- upd_down: bfloat16 [1, 1536, 384], P(None, None, 'shard')
- upd_embed: bfloat16 [1001, 384], P(None, 'shard')
All inputs are finite; a program needn't handle non-finite values.
Results may differ from a plain program's by a relative error of at most 0.03.
Values may be sent and summed in bfloat16 or wider, within the bound.
No kernel may reach another device: no remote copies, remote signals or barrier semaphores. Data moves between devices by JAX's collectives and lax.ppermute only.
A program may use at most 64 MiB of HBM per device.

v0:
```python
import math

import jax
import jax.numpy as jnp
from jax import lax
from jax.sharding import PartitionSpec as P

D = 384
MLP = 1536
ADA = 2304
NS_ITERS = 5
QKV = 1152


COEF_A = 3.4445
COEF_B = -4.775
COEF_C = 2.0315
MOMENTUM = 0.95
EPSILON = 1e-07


def broadcast_2(block, axis, source):
    block = jnp.where(lax.axis_index(axis) == source, block, jnp.zeros_like(block))
    return lax.psum(block, axis)


def newton_step(iterate, gram):
    polynomial = (
        COEF_B * gram.astype(jnp.float32)
        + COEF_C * jnp.dot(gram, gram, preferred_element_type=jnp.float32)
    ).astype(jnp.bfloat16)
    return (
        COEF_A * iterate.astype(jnp.float32)
        + jnp.dot(polynomial, iterate, preferred_element_type=jnp.float32)
    ).astype(jnp.bfloat16)


def newton_schulz(iterate):
    for sweep in range(NS_ITERS):
        gram = jnp.dot(iterate, iterate.T, preferred_element_type=jnp.float32).astype(jnp.bfloat16)
        iterate = newton_step(iterate, gram)
    return iterate


def finish(iterate, column_total):
    factor = math.sqrt(max(D, column_total))
    return (iterate.astype(jnp.float32) * factor).astype(jnp.bfloat16)


def normalize(matrix, squares):
    return (matrix / (jnp.sqrt(squares) + EPSILON)).astype(jnp.bfloat16)


def settle(matrices, identities, matrix_total, shard_total, my_index):
    row_count = matrices[0].shape[0]
    widths = [matrix.shape[1] for matrix in matrices]
    offsets = [sum(widths[:number]) for number in range(len(widths))]
    widest = max(widths)
    squares = lax.psum(jnp.stack([jnp.sum(matrix * matrix) for matrix in matrices]), "shard")
    normed = jnp.concatenate(
        [normalize(matrix, squares[number]) for number, matrix in enumerate(matrices)], axis=1
    )
    whole = lax.all_gather(normed, "shard", axis=0, tiled=True)
    starts = [
        whole[:, offsets[number] : offsets[number] + widths[number]]
        for number in range(len(widths))
    ]
    owners = [matrix_id * shard_total // matrix_total for matrix_id in identities]
    padded = jnp.stack([jnp.pad(start, ((0, 0), (0, widest - start.shape[1]))) for start in starts])
    picked = jnp.int32(0)
    for number in range(len(owners)):
        picked = picked + jnp.where(my_index == owners[number], number, 0).astype(jnp.int32)
    chosen = lax.dynamic_index_in_dim(padded, picked, 0, keepdims=False)
    final_iterate = newton_schulz(chosen)
    own_updates = [
        finish(final_iterate[:, : widths[number]], widths[number]) for number in range(len(widths))
    ]
    results = []
    for number in range(len(own_updates)):
        broadcast = broadcast_2(own_updates[number], "shard", owners[number])
        results.append(lax.dynamic_slice_in_dim(broadcast, my_index * row_count, row_count, 0))
    return results


def per_device(grad_wide, grad_down, grad_embed, mom_wide, mom_down, mom_embed):
    g_wide, g_down, g_embed = lax.psum((grad_wide[0], grad_down[0], grad_embed[0]), "rep")
    new_wide = MOMENTUM * mom_wide + g_wide
    new_down = MOMENTUM * mom_down + g_down
    new_embed = MOMENTUM * mom_embed + g_embed
    nest_wide = g_wide + MOMENTUM * new_wide
    nest_down = g_down + MOMENTUM * new_down
    nest_embed = g_embed + MOMENTUM * new_embed
    segments = [(0, QKV), (QKV, D), (QKV + D, MLP), (QKV + D + MLP, ADA)]
    matrices = []
    for offset, width in segments:
        matrices.append(nest_wide[0][:, offset : offset + width])
    matrices.append(nest_down[0].T)
    matrices.append(nest_embed.T)
    matrix_total = len(matrices)
    shard_total = lax.axis_size("shard")
    my_index = lax.axis_index("shard")
    finals = settle(matrices, list(range(matrix_total)), matrix_total, shard_total, my_index)
    position = 0
    wide_list = [jnp.concatenate(finals[position : position + 4], axis=1)]
    down_list = [finals[position + 4].T]
    position = position + 5
    upd_wide = jnp.stack(wide_list)
    upd_down = jnp.stack(down_list)
    upd_embed = finals[position].T
    return (new_wide, new_down, new_embed, upd_wide, upd_down, upd_embed)


def solution(mesh):
    placed = (
        P("rep", None, "shard", None),
        P("rep", None, None, "shard"),
        P("rep", None, "shard"),
        P(None, "shard", None),
        P(None, None, "shard"),
        P(None, "shard"),
    )
    return jax.shard_map(
        per_device,
        mesh=mesh,
        in_specs=placed,
        out_specs=(
            P(None, "shard", None),
            P(None, None, "shard"),
            P(None, "shard"),
            P(None, "shard", None),
            P(None, None, "shard"),
            P(None, "shard"),
        ),
        check_vma=False,
    )
```

profile of v0, /device:TPU:0, one launch (start us, length us, event | category | flops | bytes accessed | tf_op | source)
XLA Modules:
  0.0 353.9 jit_solution(18440939966519413700)
XLA Ops:
  8.0 66.9 %all-reduce.9.cloned.1.call-done = (f32[1,48,5376]{2,1,0:T(8,128)}, f32[1,1536,48]{1,2,0:T(8,128)}, f32[1001,48]{0,1:T(8,128)}) async-done(((f32[1,48,5376]{2,1,0:T(8,128)}, f32[1,1536,48]{1,2,0:T(8,128)}, f32[1001,48]{0,1:T(8,128)}), (f32[1,48,5376]{2,1,0:T(8,128)}, f32[1,1536,48]{1,2,0:T(8,128)}, f32[1001,48]{0,1:T(8,128)})) %all-reduce.9.cloned.1.call-update) | async-done | bytes 1519312 | tf_op jit(solution)/shard_map/psum | solution.py:86
  74.9 2.4 add_bitcast_fusion
  81.4 3.8 %stack.54 = f32[6]{0:T(128)S(1)} concatenate(f32[1]{0:T(128)} %bitcast.4, f32[1]{0:T(128)} %bitcast.5, f32[1]{0:T(128)} %bitcast.6, f32[1]{0:T(128)} %bitcast.7, f32[1]{0:T(128)} %bitcast.8, f32[1]{0:T(128)} %bitcast.9), dimensions={0} | concatenate | bytes 48 | tf_op jit(solution)/shard_map/stack | solution.py:59
  85.2 16.3 %psum.73 = f32[6]{0:T(128)S(1)} all-reduce(f32[6]{0:T(128)S(1)} %stack.54), channel_id=1, replica_groups=mesh['rep'=4,'shard'=8] {'shard'}, use_global_device_ids=true, to_apply=%region_9.0 | all-reduce | flops 6 | bytes 48 | tf_op jit(solution)/shard_map/psum | solution.py:59
  106.5 0.9 copy-done.3
  107.5 60.6 %all-gather.2.cloned.1.call-done = bf16[384,7913]{1,0:T(8,128)(2,1)} async-done(((bf16[48,7913]{1,0:T(8,128)(2,1)}), bf16[384,7913]{1,0:T(8,128)(2,1)}) %all-gather.2.cloned.1.call-update) | async-done | bytes 6077200 | tf_op jit(solution)/shard_map/all_gather | solution.py:63
  168.1 1.9 fusion.8
  170.2 1.9 fusion.66
  172.2 0.8 slice-done.1
  173.3 1.0 slice-done.3
  174.5 4.0 %copy-done.6 = bf16[6,384,2304]{2,1,0:T(8,128)(2,1)} copy-done((bf16[6,384,2304]{2,1,0:T(8,128)(2,1)}, bf16[6,384,2304]{2,1,0:T(8,128)(2,1)S(1)}, u32[]{:S(2)}) %copy-start.6) | copy-done | bytes 10616856
  178.5 1.1 fusion.24
  179.6 3.5 fusion
  183.1 1.8 convolution_convert_fusion.3
  184.9 2.6 fusion.1
  187.5 1.8 convolution_convert_fusion.2
  189.4 2.6 fusion.2
  192.0 1.8 convolution_convert_fusion.1
  193.8 2.6 fusion.3
  196.4 1.8 convolution_convert_fusion
  198.2 3.8 %fusion.5 = (bf16[384,2304]{1,0:T(8,128)(2,1)}, bf16[384,2304]{1,0:T(8,128)(2,1)S(1)}) fusion(pred[]{:T(512)S(6)} %eq.27, bf16[384,2304]{1,0:T(8,128)(2,1)S(1)} %fusion.3, bf16[384,384]{1,0:T(8,128)(2,1)} %convolution_convert_fusion), kind=kOutput, calls=%fused_computation.12 | convolution fusion | flops 800538624 | bytes 5603329 | tf_op jit(solution)/shard_map/dot_general | solution.py:34
  202.1 1.8 broadcast_select_fusion
  203.9 1.1 fusion.28
  205.0 0.8 fusion.39
  205.8 1.1 fusion.27
  207.0 132.9 %all-reduce.11.cloned.1.call-done = (bf16[384,2304]{1,0:T(8,128)(2,1)}, bf16[384,1536]{1,0:T(8,128)(2,1)}, bf16[384,384]{1,0:T(8,128)(2,1)}, bf16[384,1152]{1,0:...) async-done(((bf16[384,2304]{1,0:T(8,128)(2,1)}, bf16[384,1536]{1,0:T(8,128)(2,1)}, bf16[384,384]{1,0:T(8,128)(2,1)}, bf16[384,1152]{1,0:T(8,128)(2,1)}, ...) | async-done | bytes 6077200 | tf_op jit(solution)/shard_map/psum | solution.py:24
  339.9 0.9 constant_dynamic-slice_fusion
  340.8 0.9 constant_dynamic-slice_fusion.1
  341.8 0.9 constant_dynamic-slice_fusion.3
  343.5 1.6 dynamic-slice_bitcast_fusion
  345.0 1.5 dynamic-slice_bitcast_fusion.1
  346.6 0.8 maximum_bitcast_fusion
  (50 shorter events, 7.2 us)
Async XLA Ops:
  7.2 67.7 %copy-start.2 = (f32[1,48,5376]{2,1,0:T(8,128)S(1)}, f32[1,48,5376]{2,1,0:T(8,128)}, u32[]{:S(2)}) copy-start(f32[1,48,5376]{2,1,0:T(8,128)} %param.9) | copy-start | bytes 3096580
  7.2 67.7 %all-reduce.9.cloned.1.call-start = ((), (), s32[]{:S(2)}) async-start(), calls=%async_computation.1 | async-start | bytes 3047424 | tf_op jit(solution)/shard_map/psum | solution.py:86
  7.9 160.2 %all-gather.2.cloned.1.call-start = ((), (), s32[]{:S(2)}) async-start(), calls=%async_computation | async-start | bytes 6856704 | tf_op jit(solution)/shard_map/all_gather | solution.py:63
  74.9 5.2 %copy-start.1 = (f32[1,1536,48]{1,2,0:T(8,128)S(1)}, f32[1,1536,48]{1,2,0:T(8,128)}, u32[]{:S(2)}) copy-start(f32[1,1536,48]{1,2,0:T(8,128)} %get-tuple-element.7) | copy-start | bytes 884740
  74.9 5.2 %copy-start.7 = (f32[1,1536,48]{1,2,0:T(8,128)S(1)}, f32[1,1536,48]{1,2,0:T(8,128)}, u32[]{:S(2)}) copy-start(f32[1,1536,48]{1,2,0:T(8,128)} %param.10) | copy-start | bytes 884740
  77.3 3.4 copy-start.5
  77.3 3.4 copy-start.8
  80.7 26.6 %copy-start = (f32[1,1536,48]{1,2,0:T(8,128)}, f32[1,1536,48]{1,2,0:T(8,128)S(1)}, u32[]{:S(2)}) copy-start(f32[1,1536,48]{1,2,0:T(8,128)S(1)} %get-tuple-element.18) | copy-start | bytes 884740
  81.4 26.0 %copy-start.4 = (f32[1001,48]{0,1:T(8,128)}, f32[1001,48]{0,1:T(8,128)S(1)}, u32[]{:S(2)}) copy-start(f32[1001,48]{0,1:T(8,128)S(1)} %get-tuple-element.16) | copy-start | bytes 576580
  106.3 61.8 %copy-start.9 = (pred[2304]{0:T(1024)(128)(4,1)S(1)}, pred[2304]{0:T(1024)(128)(4,1)}, u32[]{:S(2)}) copy-start(pred[2304]{0:T(1024)(128)(4,1)} %constant.26.clone.1) | copy-start | bytes 6916
  106.5 0.9 copy-start.3
  107.4 232.5 %all-reduce.11.cloned.1.call-start = ((), (), s32[]{:S(2)}) async-start(), calls=%async_computation.2 | async-start | bytes 12189696 | tf_op jit(solution)/shard_map/psum | solution.py:24
  168.1 1.9 slice-start.2
  168.1 4.2 %slice-start = ((s8[6094848]{0:T(1024)(128)(4,1)}), s8[1900544]{0:T(1024)(128)(4,1)S(1)}, s32[]{:S(2)}) async-start(s8[6094848]{0:T(1024)(128)(4,1)} %bitcast.76), calls=%async_computation.3 | async-start | bytes 3801088
  170.2 2.9 slice-start.1
  173.2 1.1 slice-start.3
  174.5 4.0 %copy-start.6 = (bf16[6,384,2304]{2,1,0:T(8,128)(2,1)}, bf16[6,384,2304]{2,1,0:T(8,128)(2,1)S(1)}, u32[]{:S(2)}) copy-start(bf16[6,384,2304]{2,1,0:T(8,128)(2,1)S(1)} %bitcast_dynamic-update-slice_fusion) | copy-start | bytes 31850500
Sparse Core Ops, SparseCore 0:
  11.5 63.3 all-reduce.8
  107.5 60.5 all-gather.1
  207.1 132.7 all-reduce.10
where the time goes:
time: 355 us; the launch traced here: 354 us
  waiting for transfers between devices  261 us (74%)
  matrix products  23.6 us (7%)
  local copies, waits for them, and re-layouts  20.5 us (6%)
  between operations  18 us (5%)
  blocking collectives  16.3 us (5%)
  other arithmetic  14.3 us (4%)
    psum x1, waiting for transfers between devices, broadcast_2(): return lax.psum(block, axis)  133 us
    psum x1, waiting for transfers between devices, per_device(): lax.psum((grad_wide[0], grad_down[0], grad_embed[0]), 'rep')  66.9 us
    all_gather x1, waiting for transfers between devices, settle(): whole = lax.all_gather(normed, 'shard', axis=0, tiled=True)  60.6 us
    psum x1, blocking collectives, settle(): lax.psum(jnp.stack([jnp.sum(matrix * matrix) for matrix in matrices]), 's...  16.3 us
    dot_general x5, matrix products, newton_step(): jnp.dot(polynomial, iterate, preferred_element_type=jnp.float32)  15.2 us
    dot_general x5, matrix products, newton_schulz(): jnp.dot(iterate, iterate.T, preferred_element_type=jnp.float32)  8.35 us
  transfers between devices with their start and end apart: 3, of which 3 were waited for; matrix products, arithmetic and copies ran while one was open for 0% of the time, Pallas kernels for 0%

commit v1 on v0

v1 whole, which is shorter than its diff:
```python
import functools
import math

import jax
import jax.numpy as jnp
from jax import lax
from jax.experimental import pallas as pl
from jax.experimental.pallas import tpu as pltpu
from jax.sharding import PartitionSpec as P

D = 384
MLP = 1536
ADA = 2304
CLASSES = 1001
NS_ITERS = 5
QKV = 1152

COEF_A = 3.4445
COEF_B = -4.775
COEF_C = 2.0315
MOMENTUM = 0.95
EPSILON = 1e-07

VMEM_LIMIT = 48 * 1024 * 1024

WIDTHS = [QKV, D, MLP, ADA, MLP, CLASSES]
OFFSETS = [0, QKV, QKV + D, QKV + D + MLP]
PADDED = [-(-width // 128) * 128 for width in WIDTHS]
DOWN, EMBED = 4, 5


def plan(n_rep):
    bins = [[] for _ in range(n_rep)]
    loads = [0] * n_rep
    for matrix in sorted(range(6), key=lambda m: -PADDED[m]):
        owner = loads.index(min(loads))
        bins[owner].append(matrix)
        loads[owner] += PADDED[matrix]
    return bins, max(loads)


def placed(bins):
    where = {}
    for owner, group in enumerate(bins):
        offset = 0
        for matrix in group:
            where[matrix] = (owner, offset)
            offset += PADDED[matrix]
    return where


def turned(ref, scratch, total):
    value = ref[...].T
    if total > value.shape[1]:
        value = jnp.concatenate(
            [value, jnp.zeros((value.shape[0], total - value.shape[1]), value.dtype)], axis=1
        )
    scratch[...] = value


def part(matrix, wide, down_t, embed_t):
    if matrix == DOWN:
        return down_t[...]
    if matrix == EMBED:
        return embed_t[...]
    return wide[:, OFFSETS[matrix] : OFFSETS[matrix] + WIDTHS[matrix]]


def put_chunk(dst, group, wide, down_t, embed_t):
    offset = 0
    for matrix in group:
        dst[:, offset : offset + PADDED[matrix]] = part(matrix, wide, down_t, embed_t).astype(dst.dtype)
        offset += PADDED[matrix]
    if offset < dst.shape[1]:
        dst[:, offset:] = jnp.zeros((dst.shape[0], dst.shape[1] - offset), dst.dtype)


def split_kernel(bins, index, wide, down, embed, own, *rest):
    sends, (down_t, embed_t) = rest[:-2], rest[-2:]
    turned(down, down_t, PADDED[DOWN])
    turned(embed, embed_t, PADDED[EMBED])
    for k, dst in enumerate((own,) + sends):
        for target, group in enumerate(bins):

            @pl.when((index[0] ^ k) == target)
            def _():
                put_chunk(dst, group, wide, down_t, embed_t)


def sum_kernel(count, own, *rest):
    received, mom, g_out, y_out = rest[:count], rest[count], rest[count + 1], rest[count + 2]
    g = own[...]
    for piece in received:
        g = g + piece[...].astype(jnp.float32)
    g_out[...] = g.astype(jnp.bfloat16)
    y_out[...] = (g + MOMENTUM * (MOMENTUM * mom[...] + g)).astype(jnp.bfloat16)


def newton_kernel(bins, count, rows, index, *rest):
    pieces, out, x_ref = rest[:count], rest[count], rest[count + 1]
    piece_rows = pieces[0].shape[0]
    for number, piece in enumerate(pieces):
        x_ref[number * piece_rows : (number + 1) * piece_rows, :] = piece[...]

    def polynomial(x, scale):
        gram = lax.dot_general(x, x, (((1,), (1,)), ((), ())), preferred_element_type=jnp.float32)
        gram = (gram * scale * scale).astype(jnp.bfloat16)
        square = jnp.dot(gram, gram, preferred_element_type=jnp.float32)
        return (COEF_B * gram.astype(jnp.float32) + COEF_C * square).astype(jnp.bfloat16)

    def branch(group):
        spans = []
        offset = 0
        for matrix in group:
            spans.append((offset, PADDED[matrix], WIDTHS[matrix]))
            offset += PADDED[matrix]
        scales = []
        for offset, width, _ in spans:
            x = x_ref[:, offset : offset + width].astype(jnp.float32)
            scales.append(1.0 / (jnp.sqrt(jnp.sum(x * x)) + EPSILON))

        def step(number, scales):
            for (offset, width, _), scale in zip(spans, scales):
                x = x_ref[:, offset : offset + width]
                poly = polynomial(x, scale)
                x_ref[:, offset : offset + width] = (
                    scale
                    * (COEF_A * x.astype(jnp.float32) + jnp.dot(poly, x, preferred_element_type=jnp.float32))
                ).astype(jnp.bfloat16)
            return tuple(jnp.float32(1.0) for _ in scales)

        scales = lax.fori_loop(0, NS_ITERS - 1, step, tuple(scales))
        for (offset, width, true_width), scale in zip(spans, scales):
            x = x_ref[:, offset : offset + width]
            poly = polynomial(x, scale)
            factor = math.sqrt(max(D, true_width))
            out[:, offset : offset + width] = (
                (scale * factor)
                * (
                    COEF_A * x[:rows].astype(jnp.float32)
                    + jnp.dot(poly[:rows], x, preferred_element_type=jnp.float32)
                )
            ).astype(jnp.bfloat16)

    for target, group in enumerate(bins):
        if group:

            @pl.when(index[0] == target)
            def _():
                branch(group)


def per_index(bins, index, body):
    for mine in range(len(bins)):

        @pl.when(index[0] == mine)
        def _():
            body(mine)


def momentum_kernel(bins, index, wide, down, embed, *rest):
    n = len(bins)
    pieces, (new_wide, new_down, new_embed) = rest[:n], rest[n:]
    where = placed(bins)

    def body(mine):
        for matrix in range(6):
            owner, offset = where[matrix]
            g = pieces[mine ^ owner][:, offset : offset + PADDED[matrix]].astype(jnp.float32)
            if matrix == DOWN:
                new_down[...] = MOMENTUM * down[...] + g.T
            elif matrix == EMBED:
                new_embed[...] = MOMENTUM * embed[...] + g.T[:CLASSES]
            else:
                span = slice(OFFSETS[matrix], OFFSETS[matrix] + WIDTHS[matrix])
                new_wide[:, span] = MOMENTUM * wide[:, span] + g

    per_index(bins, index, body)


def update_kernel(bins, index, *rest):
    n = len(bins)
    pieces, (upd_wide, upd_down, upd_embed) = rest[:n], rest[n:]
    where = placed(bins)

    def body(mine):
        for matrix in range(6):
            owner, offset = where[matrix]
            value = pieces[mine ^ owner][:, offset : offset + PADDED[matrix]]
            if matrix == DOWN:
                upd_down[...] = value.astype(jnp.float32).T.astype(jnp.bfloat16)
            elif matrix == EMBED:
                upd_embed[...] = value.astype(jnp.float32).T[:CLASSES].astype(jnp.bfloat16)
            else:
                upd_wide[:, OFFSETS[matrix] : OFFSETS[matrix] + WIDTHS[matrix]] = value

    per_index(bins, index, body)


def call(kernel, outs, args, scratch=(), indexed=True, flops=0):
    vmem = pl.BlockSpec(memory_space=pltpu.VMEM)
    specs = [vmem] * len(args)
    if indexed:
        specs[0] = pl.BlockSpec(memory_space=pltpu.SMEM)
    size = sum(a.size * a.dtype.itemsize for a in args) + sum(
        math.prod(o.shape) * o.dtype.itemsize for o in outs
    )
    return pl.pallas_call(
        kernel,
        out_shape=tuple(outs),
        in_specs=specs,
        out_specs=tuple([vmem] * len(outs)),
        scratch_shapes=list(scratch),
        compiler_params=pltpu.CompilerParams(vmem_limit_bytes=VMEM_LIMIT),
        cost_estimate=pl.CostEstimate(flops=flops, bytes_accessed=size, transcendentals=0),
    )(*args)


def swap(value, axis, k, n):
    return lax.ppermute(value, axis, [(i, i ^ k) for i in range(n)])


def spread(value, axis, n):
    return [value] + [swap(value, axis, k, n) for k in range(1, n)]


def gather_rows(value, n):
    pieces = [value] + [swap(value, "shard", 2 * k, n) for k in range(1, n // 2)]
    return pieces + [swap(piece, "shard", 1, n) for piece in pieces]


def per_device(grad_wide, grad_down, grad_embed, mom_wide, mom_down, mom_embed):
    n_rep, n_shard = lax.axis_size("rep"), lax.axis_size("shard")
    bins, width = plan(n_rep)
    index = lax.axis_index("rep").astype(jnp.int32).reshape(1)
    grads = (grad_wide[0, 0], grad_down[0, 0], grad_embed[0])
    moms = (mom_wide[0], mom_down[0], mom_embed)
    rows = grads[0].shape[0]
    chunk32 = jax.ShapeDtypeStruct((rows, width), jnp.float32)
    chunk16 = jax.ShapeDtypeStruct((rows, width), jnp.bfloat16)
    turn = (pltpu.VMEM((rows, PADDED[DOWN]), jnp.float32), pltpu.VMEM((rows, PADDED[EMBED]), jnp.float32))

    own, *sends = call(
        functools.partial(split_kernel, bins), [chunk32] + [chunk16] * (n_rep - 1), (index,) + grads, turn
    )
    received = [swap(piece, "rep", k + 1, n_rep) for k, piece in enumerate(sends)]
    (mom_own,) = call(functools.partial(split_kernel, bins), [chunk32], (index,) + moms, turn)
    g, y = call(
        functools.partial(sum_kernel, n_rep - 1),
        [chunk16, chunk16],
        (own, *received, mom_own),
        indexed=False,
    )

    pieces = gather_rows(y, n_shard)
    g_all = spread(g, "rep", n_rep)
    news = call(
        functools.partial(momentum_kernel, bins),
        [jax.ShapeDtypeStruct(m.shape, jnp.float32) for m in moms],
        (index,) + moms + tuple(g_all),
    )
    if rows % 16:
        pieces = [jnp.concatenate(pieces, axis=0)]
    (upd,) = call(
        functools.partial(newton_kernel, bins, len(pieces), rows),
        [chunk16],
        (index,) + tuple(pieces),
        (pltpu.VMEM((D, width), jnp.bfloat16),),
        flops=NS_ITERS * (4 * D * D * width + 2 * D * D * D),
    )
    updates = call(
        functools.partial(update_kernel, bins),
        [jax.ShapeDtypeStruct(m.shape, jnp.bfloat16) for m in moms],
        (index,) + tuple(spread(upd, "rep", n_rep)),
    )
    return (news[0][None], news[1][None], news[2], updates[0][None], updates[1][None], updates[2])


def solution(mesh):
    placed_in = (
        P("rep", None, "shard", None),
        P("rep", None, None, "shard"),
        P("rep", None, "shard"),
        P(None, "shard", None),
        P(None, None, "shard"),
        P(None, "shard"),
    )
    return jax.shard_map(
        per_device,
        mesh=mesh,
        in_specs=placed_in,
        out_specs=placed_in[3:] + placed_in[3:],
        check_vma=False,
    )
```

time: 355 us -> 74.2 us (0.21)
  waiting for transfers between devices: 261 us -> 29.3 us
  matrix products: 23.6 us -> 0 us
  Pallas kernels: 0 us -> 18.3 us
  between operations: 18 us -> 0.73 us
  starting transfers between devices: 0.12 us -> 16.5 us
  blocking collectives: 16.3 us -> 0 us
  other arithmetic: 14.3 us -> 0 us
  local copies, waits for them, and re-layouts: 20.5 us -> 9.06 us
    psum x2 -> x0, waiting for transfers between devices: 200 us -> none  [the longest x1 133 us: broadcast_2(): return lax.psum(block, axis)]
    all_gather x1 -> x0, waiting for transfers between devices: 60.6 us -> none  [settle(): whole = lax.all_gather(normed, 'shard', axis=0, tiled=True)]
    ppermute x0 -> x16, waiting for transfers between devices: none -> 29.3 us  [swap(): return lax.ppermute(value, axis, [(i, i ^ k) for i in range(n)])]
    dot_general x10 -> x0, matrix products: 23.6 us -> none  [the longest x5 15.2 us: newton_step(): jnp.dot(polynomial, iterate, preferred_element_type=jnp.float32)]
    pallas_call x0 -> x6, Pallas kernels: none -> 18.3 us  [call(): pl.pallas_call(kernel, out_shape=tuple(outs), in_specs=specs, out_specs=t...]
    ppermute x0 -> x16, starting transfers between devices: none -> 16.5 us  [swap(): return lax.ppermute(value, axis, [(i, i ^ k) for i in range(n)])]
    psum x1 -> x0, blocking collectives: 16.3 us -> none  [settle(): lax.psum(jnp.stack([jnp.sum(matrix * matrix) for matrix in matrices]), 's...]
    another operation x3 -> x0, local copies, waits for them, and re-layouts: 5.54 us -> none  [the longest x1 3.83 us: settle(): jnp.stack([jnp.sum(matrix * matrix) for matrix in matrices])]
  transfers between devices with their start and end apart: 3 -> 16, of which waited for: 3 -> 6; matrix products, arithmetic and copies ran while one was open for 0% -> 6% of each run, Pallas kernels for 0% -> 20%
where the time goes in v1:
time: 74.2 us; the launch traced here: 73.9 us
  waiting for transfers between devices  29.3 us (39%)
  Pallas kernels  18.3 us (25%)
  starting transfers between devices  16.5 us (22%)
  local copies, waits for them, and re-layouts  9.06 us (12%)
    ppermute x16, waiting for transfers between devices, swap(): return lax.ppermute(value, axis, [(i, i ^ k) for i in range(n)])  29.3 us
    pallas_call x6, Pallas kernels, call(): pl.pallas_call(kernel, out_shape=tuple(outs), in_specs=specs, out_specs=t...  18.3 us
    ppermute x16, starting transfers between devices, swap(): return lax.ppermute(value, axis, [(i, i ^ k) for i in range(n)])  16.5 us
    unnamed x16, local copies, waits for them, and re-layouts  9.06 us
  transfers between devices with their start and end apart: 16, of which 6 were waited for; matrix products, arithmetic and copies ran while one was open for 6% of the time, Pallas kernels for 20%

profile of v1, /device:TPU:0, one launch (start us, length us, event | category | flops | bytes accessed | tf_op | source)
XLA Modules:
  0.0 73.9 jit_solution(1959889973642558645)
XLA Ops:
  0.6 1.2 %copy.14 = f32[1,1001,48]{2,1,0:T(8,128)S(1)} copy(f32[1,1001,48]{1,2,0:T(8,128)} %param.8) | data formatting | bytes 384384 | tf_op args[2]
  1.9 1.2 %copy.13 = f32[1,1,1536,48]{3,2,1,0:T(8,128)S(1)} copy(f32[1,1,1536,48]{2,3,1,0:T(8,128)} %param.7) | data formatting | bytes 589824 | tf_op args[1]
  3.1 1.4 %shard_map.109 = (f32[48,2304]{1,0:T(8,128)S(1)}, bf16[48,2304]{1,0:T(8,128)(2,1)}, bf16[48,2304]{1,0:T(8,128)(2,1)}, bf16[48,2304]{1,0:T(8,128)(2,1)}) custom-call(s32[1]{0:T(128)} %bitcast.index, f32[48,5376]{1,0:T(8,128)S(1)} %bitcast.16, f32[1536,48]{1,0:T(8,128)S(1)} %bitcast.14, f32[1001,48]{1,0:T(8,128)S(1)} %bitcast.15), custom_call_target="tpu_custom_call" | custom-call | bytes 2625220 | tf_op jit(solution)/shard_map/pallas_call | solution.py:208
  4.5 3.0 %collective-permute-start = (bf16[48,2304]{1,0:T(8,128)(2,1)}, bf16[48,2304]{1,0:T(8,128)(2,1)S(1)}, u32[]{:S(2)}, u32[]{:S(2)}) collective-permute-start(bf16[48,2304]{1,0:T(8,128)(2,1)} %get-tuple-element.19), channel_id=1, source_target_pairs={{0,8},{8,0},{16,24},{24,16},{1,9},{9,1},{17,25},{25,17},{2,10},{10... | collective-permute-start | bytes 663560 | tf_op jit(solution)/shard_map/ppermute | solution.py:220
  7.5 1.5 %collective-permute-start.1 = (bf16[48,2304]{1,0:T(8,128)(2,1)}, bf16[48,2304]{1,0:T(8,128)(2,1)S(1)}, u32[]{:S(2)}, u32[]{:S(2)}) collective-permute-start(bf16[48,2304]{1,0:T(8,128)(2,1)} %get-tuple-element.20), channel_id=1, source_target_pairs={{0,16},{8,24},{16,0},{24,8},{1,17},{9,25},{17,1},{25,9},{2,18},{10... | collective-permute-start | bytes 663560 | tf_op jit(solution)/shard_map/ppermute | solution.py:220
  9.0 1.1 %copy.16.embed = f32[1001,48]{1,0:T(8,128)S(1)} copy(f32[1001,48]{0,1:T(8,128)} %param.11) | data formatting | bytes 384384 | tf_op args[5]
  10.1 1.2 %copy.12 = f32[1,1536,48]{2,1,0:T(8,128)S(1)} copy(f32[1,1536,48]{1,2,0:T(8,128)} %param.10) | data formatting | bytes 589824 | tf_op args[4]
  11.3 0.4 shard_map.110.rest_3_
  11.8 2.2 %collective-permute-done.rest_0_ = bf16[48,2304]{1,0:T(8,128)(2,1)S(1)} collective-permute-done((bf16[48,2304]{1,0:T(8,128)(2,1)}, bf16[48,2304]{1,0:T(8,128)(2,1)S(1)}, u32[]{:S(2)}, u32[]{:S(2)}) %collective-permute-start) | collective-permute-done | bytes 221216 | tf_op jit(solution)/shard_map/ppermute | solution.py:220
  13.9 5.4 %collective-permute-done.1.rest_1_ = bf16[48,2304]{1,0:T(8,128)(2,1)S(1)} collective-permute-done((bf16[48,2304]{1,0:T(8,128)(2,1)}, bf16[48,2304]{1,0:T(8,128)(2,1)S(1)}, u32[]{:S(2)}, u32[]{:S(2)}) %collective-permute-start.1) | collective-permute-done | bytes 221216 | tf_op jit(solution)/shard_map/ppermute | solution.py:220
  19.3 0.2 shard_map.111
  19.5 3.7 %collective-permute-start.8 = (bf16[48,2304]{1,0:T(8,128)(2,1)S(1)}, bf16[48,2304]{1,0:T(8,128)(2,1)S(1)}, u32[]{:S(2)}, u32[]{:S(2)}) collective-permute-start(bf16[48,2304]{1,0:T(8,128)(2,1)S(1)} %get-tuple-element.26.rest_0_), channel_id=1, source_target_pairs={{0,6},{1,7},{2,4},{3,5},{4,2},{5,3},{6,0},{7,1},{8,14},{9,15},{10,... | collective-permute-start | bytes 663560 | tf_op jit(solution)/shard_map/ppermute | solution.py:220
  23.2 0.8 %collective-permute-start.6 = (bf16[48,2304]{1,0:T(8,128)(2,1)S(1)}, bf16[48,2304]{1,0:T(8,128)(2,1)S(1)}, u32[]{:S(2)}, u32[]{:S(2)}) collective-permute-start(bf16[48,2304]{1,0:T(8,128)(2,1)S(1)} %get-tuple-element.26.rest_0_), channel_id=1, source_target_pairs={{0,2},{1,3},{2,0},{3,1},{4,6},{5,7},{6,4},{7,5},{8,10},{9,11},{10,... | collective-permute-start | bytes 663560 | tf_op jit(solution)/shard_map/ppermute | solution.py:220
  23.9 5.8 %collective-permute-done.8.rest_3_ = bf16[48,2304]{1,0:T(8,128)(2,1)S(1)} collective-permute-done((bf16[48,2304]{1,0:T(8,128)(2,1)S(1)}, bf16[48,2304]{1,0:T(8,128)(2,1)S(1)}, u32[]{:S(2)}, u32[]{:S(2)}) %collective-permute-start.8) | collective-permute-done | bytes 221216 | tf_op jit(solution)/shard_map/ppermute | solution.py:220
  29.8 11.1 %collective-permute-done.7.rest_2_ = bf16[48,2304]{1,0:T(8,128)(2,1)S(1)} collective-permute-done((bf16[48,2304]{1,0:T(8,128)(2,1)S(1)}, bf16[48,2304]{1,0:T(8,128)(2,1)S(1)}, u32[]{:S(2)}, u32[]{:S(2)}) %collective-permute-start.7) | collective-permute-done | bytes 221216 | tf_op jit(solution)/shard_map/ppermute | solution.py:220
  40.9 0.5 collective-permute-start.10
  41.4 1.4 %collective-permute-start.5 = (bf16[48,2304]{1,0:T(8,128)(2,1)S(1)}, bf16[48,2304]{1,0:T(8,128)(2,1)S(1)}, u32[]{:S(2)}, u32[]{:S(2)}) collective-permute-start(bf16[48,2304]{1,0:T(8,128)(2,1)S(1)} %get-tuple-element.22.rest_0_), channel_id=1, source_target_pairs={{0,24},{8,16},{16,8},{24,0},{1,25},{9,17},{17,9},{25,1},{2,26},{10... | collective-permute-start | bytes 663560 | tf_op jit(solution)/shard_map/ppermute | solution.py:220
  42.8 1.5 %collective-permute-start.4 = (bf16[48,2304]{1,0:T(8,128)(2,1)S(1)}, bf16[48,2304]{1,0:T(8,128)(2,1)S(1)}, u32[]{:S(2)}, u32[]{:S(2)}) collective-permute-start(bf16[48,2304]{1,0:T(8,128)(2,1)S(1)} %get-tuple-element.22.rest_0_), channel_id=1, source_target_pairs={{0,16},{8,24},{16,0},{24,8},{1,17},{9,25},{17,1},{25,9},{2,18},{10... | collective-permute-start | bytes 663560 | tf_op jit(solution)/shard_map/ppermute | solution.py:220
  44.3 0.6 collective-permute-start.3
  44.9 12.7 %shard_map.113.rest_0_ = bf16[48,2304]{1,0:T(8,128)(2,1)S(1)} custom-call(s32[1]{0:T(128)} %bitcast.index, bf16[48,2304]{1,0:T(8,128)(2,1)S(1)} %get-tuple-element.26.rest_0_, bf16[48,2304]{1,0:T(8,128)(2,1)S(1)} %collective-permute-done.6.rest_1_, bf16[48,2304]{1,0:T(8,128)(2,1)S(1)} %collective-permute-done.7.rest_2_, ...), custom_call_target="tpu_custom_call" | custom-call | flops 7361003520 | bytes 1990660 | tf_op jit(solution)/shard_map/pallas_call | solution.py:208
  57.6 2.9 %collective-permute-start.15 = (bf16[48,2304]{1,0:T(8,128)(2,1)S(1)}, bf16[48,2304]{1,0:T(8,128)(2,1)}, u32[]{:S(2)}, u32[]{:S(2)}) collective-permute-start(bf16[48,2304]{1,0:T(8,128)(2,1)S(1)} %shard_map.113.rest_0_), channel_id=1, source_target_pairs={{0,24},{8,16},{16,8},{24,0},{1,25},{9,17},{17,9},{25,1},{2,26},{10... | collective-permute-start | bytes 663560 | tf_op jit(solution)/shard_map/ppermute | solution.py:220
  60.5 0.6 collective-permute-start.14
  61.1 1.4 %shard_map.112 = (f32[48,5376]{1,0:T(8,128)}, f32[1536,48]{1,0:T(8,128)S(1)}, f32[1001,48]{1,0:T(8,128)S(1)}) custom-call(s32[1]{0:T(128)} %bitcast.index, f32[48,5376]{1,0:T(8,128)S(1)} %bitcast.13, f32[1536,48]{1,0:T(8,128)S(1)} %bitcast.11, f32[1001,48]{1,0:T(8,128)S(1)} %copy.16.embed, bf16[48,2304]{1,0:T(8,128)(2,1)S(1)} %get-tuple-element.22.rest_0_, ...), custom_call_target="tpu_custom_call" | custom-call | bytes 3923332 | tf_op jit(solution)/shard_map/pallas_call | solution.py:208
  62.5 0.8 %copy-done.2 = f32[1001,48]{1,0:T(8,128)} copy-done((f32[1001,48]{1,0:T(8,128)}, f32[1001,48]{1,0:T(8,128)S(1)}, u32[]{:S(2)}) %copy-start.2) | copy-done | bytes 192216
  63.3 1.0 %copy.17 = f32[1,1536,48]{1,2,0:T(8,128)} copy(f32[1,1536,48]{2,1,0:T(8,128)S(1)} %bitcast.17) | data formatting | bytes 589824
  64.3 0.1 copy-done.3
  64.3 0.9 %copy.18 = f32[1001,48]{0,1:T(8,128)} copy(f32[1001,48]{1,0:T(8,128)S(1)} %copy-done.3) | data formatting | bytes 384384
  65.2 1.8 %collective-permute-done.15.rest_3_ = bf16[48,2304]{1,0:T(8,128)(2,1)} collective-permute-done((bf16[48,2304]{1,0:T(8,128)(2,1)S(1)}, bf16[48,2304]{1,0:T(8,128)(2,1)}, u32[]{:S(2)}, u32[]{:S(2)}) %collective-permute-start.15) | collective-permute-done | bytes 221216 | tf_op jit(solution)/shard_map/ppermute | solution.py:220
  67.0 3.1 %collective-permute-done.14.rest_2_ = bf16[48,2304]{1,0:T(8,128)(2,1)} collective-permute-done((bf16[48,2304]{1,0:T(8,128)(2,1)S(1)}, bf16[48,2304]{1,0:T(8,128)(2,1)}, u32[]{:S(2)}, u32[]{:S(2)}) %collective-permute-start.14) | collective-permute-done | bytes 221216 | tf_op jit(solution)/shard_map/ppermute | solution.py:220
  70.1 2.2 %shard_map.114 = (bf16[48,5376]{1,0:T(8,128)(2,1)}, bf16[1536,48]{1,0:T(8,128)(2,1)S(1)}, bf16[1001,48]{1,0:T(8,128)(2,1)S(1)}) custom-call(s32[1]{0:T(128)} %bitcast.index, bf16[48,2304]{1,0:T(8,128)(2,1)S(1)} %shard_map.113.rest_0_, bf16[48,2304]{1,0:T(8,128)(2,1)} %collective-permute-done.13.rest_1_, bf16[48,2304]{1,0:T(8,128)(2,1)} %collective-permute-done.14.rest_2_, ...), custom_call_target="tpu_custom_call" | custom-call | bytes 1644388 | tf_op jit(solution)/shard_map/pallas_call | solution.py:208
  72.3 0.8 %copy.19 = bf16[1,1536,48]{1,2,0:T(8,128)(2,1)} copy(bf16[1,1536,48]{2,1,0:T(8,128)(2,1)S(1)} %bitcast.18) | data formatting | bytes 294912
  73.1 0.8 %copy.20 = bf16[1001,48]{0,1:T(8,128)(2,1)} copy(bf16[1001,48]{1,0:T(8,128)(2,1)S(1)} %get-tuple-element.35) | data formatting | bytes 192192
  (22 shorter events, 0.1 us)
Async XLA Ops:
  0.6 2.5 %copy-start.1 = (f32[1,1,48,5376]{3,2,1,0:T(8,128)S(1)}, f32[1,1,48,5376]{3,2,1,0:T(8,128)}, u32[]{:S(2)}) copy-start(f32[1,1,48,5376]{3,2,1,0:T(8,128)} %param.6) | copy-start | bytes 3096580
  4.5 6.8 %copy-start = (f32[1,48,5376]{2,1,0:T(8,128)S(1)}, f32[1,48,5376]{2,1,0:T(8,128)}, u32[]{:S(2)}) copy-start(f32[1,48,5376]{2,1,0:T(8,128)} %param.9) | copy-start | bytes 3096580
  4.5 9.4 %collective-permute-start = (bf16[48,2304]{1,0:T(8,128)(2,1)}, bf16[48,2304]{1,0:T(8,128)(2,1)S(1)}, u32[]{:S(2)}, u32[]{:S(2)}) collective-permute-start(bf16[48,2304]{1,0:T(8,128)(2,1)} %get-tuple-element.19), channel_id=1, source_target_pairs={{0,8},{8,0},{16,24},{24,16},{1,9},{9,1},{17,25},{25,17},{2,10},{10... | collective-permute-start | bytes 663560 | tf_op jit(solution)/shard_map/ppermute | solution.py:220
  7.5 11.8 %collective-permute-start.1 = (bf16[48,2304]{1,0:T(8,128)(2,1)}, bf16[48,2304]{1,0:T(8,128)(2,1)S(1)}, u32[]{:S(2)}, u32[]{:S(2)}) collective-permute-start(bf16[48,2304]{1,0:T(8,128)(2,1)} %get-tuple-element.20), channel_id=1, source_target_pairs={{0,16},{8,24},{16,0},{24,8},{1,17},{9,25},{17,1},{25,9},{2,18},{10... | collective-permute-start | bytes 663560 | tf_op jit(solution)/shard_map/ppermute | solution.py:220
  9.0 10.3 %collective-permute-start.2 = (bf16[48,2304]{1,0:T(8,128)(2,1)}, bf16[48,2304]{1,0:T(8,128)(2,1)S(1)}, u32[]{:S(2)}, u32[]{:S(2)}) collective-permute-start(bf16[48,2304]{1,0:T(8,128)(2,1)} %get-tuple-element.21), channel_id=1, source_target_pairs={{0,24},{8,16},{16,8},{24,0},{1,25},{9,17},{17,9},{25,1},{2,26},{10... | collective-permute-start | bytes 663560 | tf_op jit(solution)/shard_map/ppermute | solution.py:220
  19.5 10.3 %collective-permute-start.8 = (bf16[48,2304]{1,0:T(8,128)(2,1)S(1)}, bf16[48,2304]{1,0:T(8,128)(2,1)S(1)}, u32[]{:S(2)}, u32[]{:S(2)}) collective-permute-start(bf16[48,2304]{1,0:T(8,128)(2,1)S(1)} %get-tuple-element.26.rest_0_), channel_id=1, source_target_pairs={{0,6},{1,7},{2,4},{3,5},{4,2},{5,3},{6,0},{7,1},{8,14},{9,15},{10,... | collective-permute-start | bytes 663560 | tf_op jit(solution)/shard_map/ppermute | solution.py:220
  23.1 17.7 %collective-permute-start.7 = (bf16[48,2304]{1,0:T(8,128)(2,1)S(1)}, bf16[48,2304]{1,0:T(8,128)(2,1)S(1)}, u32[]{:S(2)}, u32[]{:S(2)}) collective-permute-start(bf16[48,2304]{1,0:T(8,128)(2,1)S(1)} %get-tuple-element.26.rest_0_), channel_id=1, source_target_pairs={{0,4},{1,5},{2,6},{3,7},{4,0},{5,1},{6,2},{7,3},{8,12},{9,13},{10,... | collective-permute-start | bytes 663560 | tf_op jit(solution)/shard_map/ppermute | solution.py:220
  23.2 17.7 %collective-permute-start.6 = (bf16[48,2304]{1,0:T(8,128)(2,1)S(1)}, bf16[48,2304]{1,0:T(8,128)(2,1)S(1)}, u32[]{:S(2)}, u32[]{:S(2)}) collective-permute-start(bf16[48,2304]{1,0:T(8,128)(2,1)S(1)} %get-tuple-element.26.rest_0_), channel_id=1, source_target_pairs={{0,2},{1,3},{2,0},{3,1},{4,6},{5,7},{6,4},{7,5},{8,10},{9,11},{10,... | collective-permute-start | bytes 663560 | tf_op jit(solution)/shard_map/ppermute | solution.py:220
  23.9 18.9 %collective-permute-start.9 = (bf16[48,2304]{1,0:T(8,128)(2,1)S(1)}, bf16[48,2304]{1,0:T(8,128)(2,1)S(1)}, u32[]{:S(2)}, u32[]{:S(2)}) collective-permute-start(bf16[48,2304]{1,0:T(8,128)(2,1)S(1)} %get-tuple-element.26.rest_0_), channel_id=1, source_target_pairs={{0,1},{1,0},{2,3},{3,2},{4,5},{5,4},{6,7},{7,6},{8,9},{9,8},{10,11... | collective-permute-start | bytes 663560 | tf_op jit(solution)/shard_map/ppermute | solution.py:220
  29.8 14.5 %collective-permute-start.12 = (bf16[48,2304]{1,0:T(8,128)(2,1)S(1)}, bf16[48,2304]{1,0:T(8,128)(2,1)S(1)}, u32[]{:S(2)}, u32[]{:S(2)}) collective-permute-start(bf16[48,2304]{1,0:T(8,128)(2,1)S(1)} %collective-permute-done.8.rest_3_), channel_id=1, source_target_pairs={{0,1},{1,0},{2,3},{3,2},{4,5},{5,4},{6,7},{7,6},{8,9},{9,8},{10,11... | collective-permute-start | bytes 663560 | tf_op jit(solution)/shard_map/ppermute | solution.py:220
  40.9 4.0 %collective-permute-start.11 = (bf16[48,2304]{1,0:T(8,128)(2,1)S(1)}, bf16[48,2304]{1,0:T(8,128)(2,1)S(1)}, u32[]{:S(2)}, u32[]{:S(2)}) collective-permute-start(bf16[48,2304]{1,0:T(8,128)(2,1)S(1)} %collective-permute-done.7.rest_2_), channel_id=1, source_target_pairs={{0,1},{1,0},{2,3},{3,2},{4,5},{5,4},{6,7},{7,6},{8,9},{9,8},{10,11... | collective-permute-start | bytes 663560 | tf_op jit(solution)/shard_map/ppermute | solution.py:220
  40.9 4.0 %collective-permute-start.10 = (bf16[48,2304]{1,0:T(8,128)(2,1)S(1)}, bf16[48,2304]{1,0:T(8,128)(2,1)S(1)}, u32[]{:S(2)}, u32[]{:S(2)}) collective-permute-start(bf16[48,2304]{1,0:T(8,128)(2,1)S(1)} %collective-permute-done.6.rest_1_), channel_id=1, source_target_pairs={{0,1},{1,0},{2,3},{3,2},{4,5},{5,4},{6,7},{7,6},{8,9},{9,8},{10,11... | collective-permute-start | bytes 663560 | tf_op jit(solution)/shard_map/ppermute | solution.py:220
  41.4 19.7 %collective-permute-start.5 = (bf16[48,2304]{1,0:T(8,128)(2,1)S(1)}, bf16[48,2304]{1,0:T(8,128)(2,1)S(1)}, u32[]{:S(2)}, u32[]{:S(2)}) collective-permute-start(bf16[48,2304]{1,0:T(8,128)(2,1)S(1)} %get-tuple-element.22.rest_0_), channel_id=1, source_target_pairs={{0,24},{8,16},{16,8},{24,0},{1,25},{9,17},{17,9},{25,1},{2,26},{10... | collective-permute-start | bytes 663560 | tf_op jit(solution)/shard_map/ppermute | solution.py:220
  42.8 18.3 %collective-permute-start.4 = (bf16[48,2304]{1,0:T(8,128)(2,1)S(1)}, bf16[48,2304]{1,0:T(8,128)(2,1)S(1)}, u32[]{:S(2)}, u32[]{:S(2)}) collective-permute-start(bf16[48,2304]{1,0:T(8,128)(2,1)S(1)} %get-tuple-element.22.rest_0_), channel_id=1, source_target_pairs={{0,16},{8,24},{16,0},{24,8},{1,17},{9,25},{17,1},{25,9},{2,18},{10... | collective-permute-start | bytes 663560 | tf_op jit(solution)/shard_map/ppermute | solution.py:220
  44.3 16.9 %collective-permute-start.3 = (bf16[48,2304]{1,0:T(8,128)(2,1)S(1)}, bf16[48,2304]{1,0:T(8,128)(2,1)S(1)}, u32[]{:S(2)}, u32[]{:S(2)}) collective-permute-start(bf16[48,2304]{1,0:T(8,128)(2,1)S(1)} %get-tuple-element.22.rest_0_), channel_id=1, source_target_pairs={{0,8},{8,0},{16,24},{24,16},{1,9},{9,1},{17,25},{25,17},{2,10},{10... | collective-permute-start | bytes 663560 | tf_op jit(solution)/shard_map/ppermute | solution.py:220
  57.6 9.4 %collective-permute-start.15 = (bf16[48,2304]{1,0:T(8,128)(2,1)S(1)}, bf16[48,2304]{1,0:T(8,128)(2,1)}, u32[]{:S(2)}, u32[]{:S(2)}) collective-permute-start(bf16[48,2304]{1,0:T(8,128)(2,1)S(1)} %shard_map.113.rest_0_), channel_id=1, source_target_pairs={{0,24},{8,16},{16,8},{24,0},{1,25},{9,17},{17,9},{25,1},{2,26},{10... | collective-permute-start | bytes 663560 | tf_op jit(solution)/shard_map/ppermute | solution.py:220
  60.5 9.6 %collective-permute-start.14 = (bf16[48,2304]{1,0:T(8,128)(2,1)S(1)}, bf16[48,2304]{1,0:T(8,128)(2,1)}, u32[]{:S(2)}, u32[]{:S(2)}) collective-permute-start(bf16[48,2304]{1,0:T(8,128)(2,1)S(1)} %shard_map.113.rest_0_), channel_id=1, source_target_pairs={{0,16},{8,24},{16,0},{24,8},{1,17},{9,25},{17,1},{25,9},{2,18},{10... | collective-permute-start | bytes 663560 | tf_op jit(solution)/shard_map/ppermute | solution.py:220
  61.1 9.0 %collective-permute-start.13 = (bf16[48,2304]{1,0:T(8,128)(2,1)S(1)}, bf16[48,2304]{1,0:T(8,128)(2,1)}, u32[]{:S(2)}, u32[]{:S(2)}) collective-permute-start(bf16[48,2304]{1,0:T(8,128)(2,1)S(1)} %shard_map.113.rest_0_), channel_id=1, source_target_pairs={{0,8},{8,0},{16,24},{24,16},{1,9},{9,1},{17,25},{25,17},{2,10},{10... | collective-permute-start | bytes 663560 | tf_op jit(solution)/shard_map/ppermute | solution.py:220
  62.5 0.8 %copy-start.2 = (f32[1001,48]{1,0:T(8,128)}, f32[1001,48]{1,0:T(8,128)S(1)}, u32[]{:S(2)}) copy-start(f32[1001,48]{1,0:T(8,128)S(1)} %get-tuple-element.32) | copy-start | bytes 576580
  63.3 1.0 %copy-start.3 = (f32[1001,48]{1,0:T(8,128)S(1)}, f32[1001,48]{1,0:T(8,128)}, u32[]{:S(2)}) copy-start(f32[1001,48]{1,0:T(8,128)} %copy-done.2) | copy-start | bytes 576580

commit v2 on v1

v2 whole, which is shorter than its diff:
```python
import functools
import math

import jax
import jax.numpy as jnp
from jax import lax
from jax.experimental import pallas as pl
from jax.experimental.pallas import tpu as pltpu
from jax.sharding import PartitionSpec as P

D = 384
MLP = 1536
ADA = 2304
CLASSES = 1001
NS_ITERS = 5
QKV = 1152

COEF_A = 3.4445
COEF_B = -4.775
COEF_C = 2.0315
MOMENTUM = 0.95
EPSILON = 1e-07

VMEM_LIMIT = 48 * 1024 * 1024

WIDTHS = [QKV, D, MLP, ADA, MLP, CLASSES]
OFFSETS = [0, QKV, QKV + D, QKV + D + MLP]
PADDED = [-(-width // 128) * 128 for width in WIDTHS]
DOWN, EMBED = 4, 5
TILE = 256


def plan(n_rep):
    bins = [[] for _ in range(n_rep)]
    loads = [0] * n_rep
    for matrix in sorted(range(6), key=lambda m: -PADDED[m]):
        owner = loads.index(min(loads))
        bins[owner].append(matrix)
        loads[owner] += PADDED[matrix]
    return bins, max(loads)


def placed(bins):
    where = {}
    for owner, group in enumerate(bins):
        offset = 0
        for matrix in group:
            where[matrix] = (owner, offset)
            offset += PADDED[matrix]
    return where


def part(matrix, wide, down, embed):
    if matrix == DOWN:
        return down[...]
    if matrix == EMBED:
        value = embed[...]
        tail = jnp.zeros((value.shape[0], PADDED[EMBED] - CLASSES), value.dtype)
        return jnp.concatenate([value, tail], axis=1)
    return wide[:, OFFSETS[matrix] : OFFSETS[matrix] + WIDTHS[matrix]]


def put_chunk(dst, group, wide, down, embed):
    offset = 0
    for matrix in group:
        dst[:, offset : offset + PADDED[matrix]] = part(matrix, wide, down, embed).astype(dst.dtype)
        offset += PADDED[matrix]
    if offset < dst.shape[1]:
        dst[:, offset:] = jnp.zeros((dst.shape[0], dst.shape[1] - offset), dst.dtype)


def split_kernel(bins, index, wide, down, embed, *outs):
    for k, dst in enumerate(outs):
        for target, group in enumerate(bins):

            @pl.when((index[0] ^ k) == target)
            def _():
                put_chunk(dst, group, wide, down, embed)


def sum_kernel(count, own, *rest):
    received, mom, g_out, y_out = rest[:count], rest[count], rest[count + 1], rest[count + 2]
    g = own[...]
    for piece in received:
        g = g + piece[...].astype(jnp.float32)
    g_out[...] = g.astype(jnp.bfloat16)
    y_out[...] = (g + MOMENTUM * (MOMENTUM * mom[...] + g)).astype(jnp.bfloat16)


def newton_kernel(bins, blocks, rows, index, *rest):
    count = sum(len(block) for block in blocks)
    pieces, out, x_ref, gram_ref = rest[:count], rest[-3], rest[-2], rest[-1]
    piece_rows = D // len(blocks)
    for number, block in enumerate(blocks):
        value = pieces[block[0]][...]
        for extra in block[1:]:
            value = value + pieces[extra][...]
        x_ref[number * piece_rows : (number + 1) * piece_rows, :] = value

    def outer(x):
        return lax.dot_general(x, x, (((1,), (1,)), ((), ())), preferred_element_type=jnp.float32)

    def branch(group):
        spans = []
        offset = 0
        for matrix in group:
            end = offset + PADDED[matrix]
            tiles = [slice(low, min(low + TILE, end)) for low in range(offset, end, TILE)]
            spans.append((tiles, math.sqrt(max(D, WIDTHS[matrix]))))
            offset = end

        diagonal = lax.broadcasted_iota(jnp.int32, (D, D), 0) == lax.broadcasted_iota(jnp.int32, (D, D), 1)
        scales = []
        for number, (tiles, _) in enumerate(spans):
            gram = jnp.zeros((D, D), jnp.float32)
            for tile in tiles:
                gram = gram + outer(x_ref[:, tile])
            gram_ref[number] = gram
            squares = jnp.sum(jnp.where(diagonal, gram, 0.0))
            scales.append(1.0 / (jnp.sqrt(squares) + EPSILON))

        def polynomial(number, scale):
            gram = (gram_ref[number] * scale * scale).astype(jnp.bfloat16)
            square = jnp.dot(gram, gram, preferred_element_type=jnp.float32)
            return COEF_B * gram.astype(jnp.float32) + COEF_C * square

        def step(_, scales):
            for number, ((tiles, _), scale) in enumerate(zip(spans, scales)):
                poly = (scale * polynomial(number, scale)).astype(jnp.bfloat16)
                gram = jnp.zeros((D, D), jnp.float32)
                for tile in tiles:
                    x = x_ref[:, tile]
                    x = (
                        (COEF_A * scale) * x.astype(jnp.float32)
                        + jnp.dot(poly, x, preferred_element_type=jnp.float32)
                    ).astype(jnp.bfloat16)
                    x_ref[:, tile] = x
                    gram = gram + outer(x)
                gram_ref[number] = gram
            return tuple(jnp.float32(1.0) for _ in scales)

        scales = lax.fori_loop(0, NS_ITERS - 1, step, tuple(scales))
        for number, ((tiles, factor), scale) in enumerate(zip(spans, scales)):
            factor = factor * scale
            poly = polynomial(number, scale)[:rows].astype(jnp.bfloat16)
            for tile in tiles:
                x = x_ref[:, tile]
                out[:, tile] = (
                    factor
                    * (COEF_A * x[:rows].astype(jnp.float32) + jnp.dot(poly, x, preferred_element_type=jnp.float32))
                ).astype(jnp.bfloat16)

    for target, group in enumerate(bins):
        if group:

            @pl.when(index[0] == target)
            def _():
                branch(group)


def per_index(bins, index, body):
    for mine in range(len(bins)):

        @pl.when(index[0] == mine)
        def _():
            body(mine)


def momentum_kernel(bins, index, wide, down, embed, *rest):
    n = len(bins)
    pieces, (new_wide, new_down, new_embed) = rest[:n], rest[n:]
    where = placed(bins)

    def body(mine):
        for matrix in range(6):
            owner, offset = where[matrix]
            g = pieces[mine ^ owner][:, offset : offset + PADDED[matrix]].astype(jnp.float32)
            if matrix == DOWN:
                new_down[...] = MOMENTUM * down[...] + g
            elif matrix == EMBED:
                new_embed[...] = MOMENTUM * embed[...] + g[:, :CLASSES]
            else:
                span = slice(OFFSETS[matrix], OFFSETS[matrix] + WIDTHS[matrix])
                new_wide[:, span] = MOMENTUM * wide[:, span] + g

    per_index(bins, index, body)


def update_kernel(bins, index, *rest):
    n = len(bins)
    pieces, (upd_wide, upd_down, upd_embed) = rest[:n], rest[n:]
    where = placed(bins)

    def body(mine):
        for matrix in range(6):
            owner, offset = where[matrix]
            value = pieces[mine ^ owner][:, offset : offset + PADDED[matrix]]
            if matrix == DOWN:
                upd_down[...] = value
            elif matrix == EMBED:
                upd_embed[...] = value[:, :CLASSES]
            else:
                upd_wide[:, OFFSETS[matrix] : OFFSETS[matrix] + WIDTHS[matrix]] = value

    per_index(bins, index, body)


def call(kernel, outs, args, scratch=(), indexed=True, flops=0, tied=0):
    vmem = pl.BlockSpec(memory_space=pltpu.VMEM)
    specs = [vmem] * (len(args) - tied) + [pl.BlockSpec(memory_space=pl.ANY)] * tied
    if indexed:
        specs[0] = pl.BlockSpec(memory_space=pltpu.SMEM)
    size = sum(a.size * a.dtype.itemsize for a in args) + sum(
        math.prod(o.shape) * o.dtype.itemsize for o in outs
    )
    return pl.pallas_call(
        kernel,
        out_shape=tuple(outs),
        in_specs=specs,
        out_specs=tuple([vmem] * len(outs)),
        scratch_shapes=list(scratch),
        compiler_params=pltpu.CompilerParams(vmem_limit_bytes=VMEM_LIMIT),
        cost_estimate=pl.CostEstimate(flops=flops, bytes_accessed=size, transcendentals=0),
    )(*args)


def swap(value, axis, k, n):
    return lax.ppermute(value, axis, [(i, i ^ k) for i in range(n)])


def spread(value, axis, n):
    return [swap(value, axis, k, n) for k in range(1, n)]


def along(value, hops):
    return lax.ppermute(value, "shard", [(2 * a + c, 2 * b + c) for a, b in hops for c in range(2)])


def gather_rows(value, n):
    if n == 8:
        far = along(value, [(0, 2), (2, 0), (1, 3), (3, 1)])
        near = along(value, [(0, 1), (1, 0), (2, 3), (3, 2)])
        middle = along(value, [(1, 2), (2, 1)])
        ends = along(far, [(2, 3), (1, 0)])
        pieces = [value, near, far, middle, ends]
        blocks = [[0], [1], [2], [3, 4]]
    else:
        pieces = [value] + [swap(value, "shard", 2 * k, n) for k in range(1, n // 2)]
        blocks = [[number] for number in range(n // 2)]
    count = len(pieces)
    pieces = pieces + [swap(piece, "shard", 1, n) for piece in pieces]
    return pieces, blocks + [[number + count for number in block] for block in blocks]


def per_device(grad_wide, grad_down, grad_embed, mom_wide, mom_down, mom_embed):
    n_rep, n_shard = lax.axis_size("rep"), lax.axis_size("shard")
    bins, width = plan(n_rep)
    index = lax.axis_index("rep").astype(jnp.int32).reshape(1)
    grads = (grad_wide[0, 0], grad_down[0, 0].T, grad_embed[0].T)
    moms = (mom_wide[0], mom_down[0].T, mom_embed.T)
    rows = grads[0].shape[0]
    chunk32 = jax.ShapeDtypeStruct((rows, width), jnp.float32)
    chunk16 = jax.ShapeDtypeStruct((rows, width), jnp.bfloat16)
    split = functools.partial(split_kernel, bins)

    own, *sends = call(split, [chunk32] + [chunk16] * (n_rep - 1), (index,) + grads)
    received = [swap(piece, "rep", k + 1, n_rep) for k, piece in enumerate(sends)]
    (mom_own,) = call(split, [chunk32], (index,) + moms)
    g, y = call(
        functools.partial(sum_kernel, n_rep - 1),
        [chunk16, chunk16],
        (own, *received, mom_own),
        indexed=False,
    )

    pieces, blocks = gather_rows(y, n_shard)
    g_others = spread(g, "rep", n_rep)
    if rows % 16:
        pieces = [jnp.concatenate(pieces, axis=0)]
        blocks = [[0]]
    (upd,) = call(
        functools.partial(newton_kernel, bins, blocks, rows),
        [chunk16],
        (index, *pieces, *g_others),
        (pltpu.VMEM((D, width), jnp.bfloat16), pltpu.VMEM((2, D, D), jnp.float32)),
        flops=NS_ITERS * (4 * D * D * width + 2 * D * D * D),
        tied=len(g_others),
    )
    upd_others = spread(upd, "rep", n_rep)
    news = call(
        functools.partial(momentum_kernel, bins),
        [jax.ShapeDtypeStruct(m.shape, jnp.float32) for m in moms],
        (index, *moms, g, *g_others),
    )
    updates = call(
        functools.partial(update_kernel, bins),
        [jax.ShapeDtypeStruct(m.shape, jnp.bfloat16) for m in moms],
        (index, upd, *upd_others),
    )
    return (
        news[0][None],
        news[1].T[None],
        news[2].T,
        updates[0][None],
        updates[1].T[None],
        updates[2].T,
    )


def solution(mesh):
    placed_in = (
        P("rep", None, "shard", None),
        P("rep", None, None, "shard"),
        P("rep", None, "shard"),
        P(None, "shard", None),
        P(None, None, "shard"),
        P(None, "shard"),
    )
    return jax.shard_map(
        per_device,
        mesh=mesh,
        in_specs=placed_in,
        out_specs=placed_in[3:] + placed_in[3:],
        check_vma=False,
    )
```

time: 74.2 us -> 74.1 us (level)
  local copies, waits for them, and re-layouts: 9.06 us -> 3.2 us
  Pallas kernels: 18.3 us -> 20.5 us
  starting transfers between devices: 16.5 us -> 18.7 us
  waiting for transfers between devices: 29.3 us -> 30.8 us
    ppermute x0 -> x4, waiting for transfers between devices: none -> 10.2 us  [along(): lax.ppermute(value, 'shard', [(2 * a + c, 2 * b + c) for a, b in hops for...]
    ppermute x16 -> x14, waiting for transfers between devices: 29.3 us -> 20.6 us  [swap(): return lax.ppermute(value, axis, [(i, i ^ k) for i in range(n)])]
    ppermute x0 -> x4, starting transfers between devices: none -> 6.28 us  [along(): lax.ppermute(value, 'shard', [(2 * a + c, 2 * b + c) for a, b in hops for...]
    unnamed x16 -> x12, local copies, waits for them, and re-layouts: 9.06 us -> 3.2 us
    ppermute x16 -> x14, starting transfers between devices: 16.5 us -> 12.4 us  [swap(): return lax.ppermute(value, axis, [(i, i ^ k) for i in range(n)])]
    pallas_call x6, Pallas kernels: 18.3 us -> 20.5 us  [call(): pl.pallas_call(kernel, out_shape=tuple(outs), in_specs=specs, out_specs=t...]
  transfers between devices with their start and end apart: 16 -> 18, of which waited for: 6 -> 9; matrix products, arithmetic and copies ran while one was open for 6% -> 0% of each run, Pallas kernels for 20% -> 2%
where the time goes in v2:
time: 74.1 us; the launch traced here: 73.9 us
  waiting for transfers between devices  30.8 us (42%)
  Pallas kernels  20.5 us (28%)
  starting transfers between devices  18.7 us (25%)
  local copies, waits for them, and re-layouts  3.2 us (4%)
  between operations  0.76 us (1%)
    ppermute x14, waiting for transfers between devices, swap(): return lax.ppermute(value, axis, [(i, i ^ k) for i in range(n)])  20.6 us
    pallas_call x6, Pallas kernels, call(): pl.pallas_call(kernel, out_shape=tuple(outs), in_specs=specs, out_specs=t...  20.5 us
    ppermute x14, starting transfers between devices, swap(): return lax.ppermute(value, axis, [(i, i ^ k) for i in range(n)])  12.4 us
    ppermute x4, waiting for transfers between devices, along(): lax.ppermute(value, 'shard', [(2 * a + c, 2 * b + c) for a, b in hops for...  10.2 us
    ppermute x4, starting transfers between devices, along(): lax.ppermute(value, 'shard', [(2 * a + c, 2 * b + c) for a, b in hops for...  6.28 us
    unnamed x12, local copies, waits for them, and re-layouts  3.2 us
  transfers between devices with their start and end apart: 18, of which 9 were waited for; matrix products, arithmetic and copies ran while one was open for 0% of the time, Pallas kernels for 2%

profile of v2, /device:TPU:0, one launch (start us, length us, event | category | flops | bytes accessed | tf_op | source)
XLA Modules:
  0.0 73.9 jit_solution(13067706487727941253)
XLA Ops:
  0.7 1.3 %copy-done.2 = f32[1,1,48,5376]{3,2,1,0:T(8,128)S(1)} copy-done((f32[1,1,48,5376]{3,2,1,0:T(8,128)S(1)}, f32[1,1,48,5376]{3,2,1,0:T(8,128)}, u32[]{:S(2)}) %copy-start.2) | copy-done | bytes 1032216
  2.0 1.0 %copy-done.4 = f32[1,1,1536,48]{2,3,1,0:T(8,128)S(1)} copy-done((f32[1,1,1536,48]{2,3,1,0:T(8,128)S(1)}, f32[1,1,1536,48]{2,3,1,0:T(8,128)}, u32[]{:S(2)}) %copy-start.4) | copy-done | bytes 294936
  2.9 0.9 %copy-done.5 = f32[1,1001,48]{1,2,0:T(8,128)S(1)} copy-done((f32[1,1001,48]{1,2,0:T(8,128)S(1)}, f32[1,1001,48]{1,2,0:T(8,128)}, u32[]{:S(2)}) %copy-start.5) | copy-done | bytes 192216
  3.8 0.2 shard_map.109
  4.1 3.0 %collective-permute-start = (bf16[48,2304]{1,0:T(8,128)(2,1)S(1)}, bf16[48,2304]{1,0:T(8,128)(2,1)S(1)}, u32[]{:S(2)}, u32[]{:S(2)}) collective-permute-start(bf16[48,2304]{1,0:T(8,128)(2,1)S(1)} %get-tuple-element.19), channel_id=1, source_target_pairs={{0,8},{8,0},{16,24},{24,16},{1,9},{9,1},{17,25},{25,17},{2,10},{10... | collective-permute-start | bytes 663560 | tf_op jit(solution)/shard_map/ppermute | solution.py:228
  7.1 1.5 %collective-permute-start.1 = (bf16[48,2304]{1,0:T(8,128)(2,1)S(1)}, bf16[48,2304]{1,0:T(8,128)(2,1)S(1)}, u32[]{:S(2)}, u32[]{:S(2)}) collective-permute-start(bf16[48,2304]{1,0:T(8,128)(2,1)S(1)} %get-tuple-element.20), channel_id=1, source_target_pairs={{0,16},{8,24},{16,0},{24,8},{1,17},{9,25},{17,1},{25,9},{2,18},{10... | collective-permute-start | bytes 663560 | tf_op jit(solution)/shard_map/ppermute | solution.py:228
  8.7 4.6 %collective-permute-done.rest_0_ = bf16[48,2304]{1,0:T(8,128)(2,1)S(1)} collective-permute-done((bf16[48,2304]{1,0:T(8,128)(2,1)S(1)}, bf16[48,2304]{1,0:T(8,128)(2,1)S(1)}, u32[]{:S(2)}, u32[]{:S(2)}) %collective-permute-start) | collective-permute-done | bytes 221216 | tf_op jit(solution)/shard_map/ppermute | solution.py:228
  13.3 5.4 %collective-permute-done.1.rest_1_ = bf16[48,2304]{1,0:T(8,128)(2,1)S(1)} collective-permute-done((bf16[48,2304]{1,0:T(8,128)(2,1)S(1)}, bf16[48,2304]{1,0:T(8,128)(2,1)S(1)}, u32[]{:S(2)}, u32[]{:S(2)}) %collective-permute-start.1) | collective-permute-done | bytes 221216 | tf_op jit(solution)/shard_map/ppermute | solution.py:228
  18.7 0.2 shard_map.111
  18.9 1.6 %collective-permute-start.5 = (bf16[48,2304]{1,0:T(8,128)(2,1)S(1)}, bf16[48,2304]{1,0:T(8,128)(2,1)S(1)}, u32[]{:S(2)}, u32[]{:S(2)}) collective-permute-start(bf16[48,2304]{1,0:T(8,128)(2,1)S(1)} %get-tuple-element.22.rest_0_), channel_id=1, source_target_pairs={{0,24},{8,16},{16,8},{24,0},{1,25},{9,17},{17,9},{25,1},{2,26},{10... | collective-permute-start | bytes 663560 | tf_op jit(solution)/shard_map/ppermute | solution.py:228
  20.4 2.6 %collective-permute-start.7 = (bf16[48,2304]{1,0:T(8,128)(2,1)S(1)}, bf16[48,2304]{1,0:T(8,128)(2,1)S(1)}, u32[]{:S(2)}, u32[]{:S(2)}) collective-permute-start(bf16[48,2304]{1,0:T(8,128)(2,1)S(1)} %get-tuple-element.26.rest_0_), channel_id=1, source_target_pairs={{0,4},{1,5},{4,0},{5,1},{2,6},{3,7},{6,2},{7,3},{8,12},{9,13},{12,... | collective-permute-start | bytes 663560 | tf_op jit(solution)/shard_map/ppermute | solution.py:236
  23.0 1.2 %collective-permute-start.4 = (bf16[48,2304]{1,0:T(8,128)(2,1)S(1)}, bf16[48,2304]{1,0:T(8,128)(2,1)S(1)}, u32[]{:S(2)}, u32[]{:S(2)}) collective-permute-start(bf16[48,2304]{1,0:T(8,128)(2,1)S(1)} %get-tuple-element.22.rest_0_), channel_id=1, source_target_pairs={{0,16},{8,24},{16,0},{24,8},{1,17},{9,25},{17,1},{25,9},{2,18},{10... | collective-permute-start | bytes 663560 | tf_op jit(solution)/shard_map/ppermute | solution.py:228
  24.2 0.8 %collective-permute-start.3 = (bf16[48,2304]{1,0:T(8,128)(2,1)S(1)}, bf16[48,2304]{1,0:T(8,128)(2,1)S(1)}, u32[]{:S(2)}, u32[]{:S(2)}) collective-permute-start(bf16[48,2304]{1,0:T(8,128)(2,1)S(1)} %get-tuple-element.22.rest_0_), channel_id=1, source_target_pairs={{0,8},{8,0},{16,24},{24,16},{1,9},{9,1},{17,25},{25,17},{2,10},{10... | collective-permute-start | bytes 663560 | tf_op jit(solution)/shard_map/ppermute | solution.py:228
  25.0 0.7 collective-permute-start.8
  25.7 1.1 %collective-permute-done.5.rest_3_.rest_12_ = bf16[48,2304]{1,0:T(8,128)(2,1)S(1)} collective-permute-done((bf16[48,2304]{1,0:T(8,128)(2,1)S(1)}, bf16[48,2304]{1,0:T(8,128)(2,1)S(1)}, u32[]{:S(2)}, u32[]{:S(2)}) %collective-permute-start.5) | collective-permute-done | bytes 221216 | tf_op jit(solution)/shard_map/ppermute | solution.py:228
  26.8 1.7 %collective-permute-start.6 = (bf16[48,2304]{1,0:T(8,128)(2,1)S(1)}, bf16[48,2304]{1,0:T(8,128)(2,1)S(1)}, u32[]{:S(2)}, u32[]{:S(2)}) collective-permute-start(bf16[48,2304]{1,0:T(8,128)(2,1)S(1)} %get-tuple-element.26.rest_0_), channel_id=1, source_target_pairs={{0,2},{1,3},{2,0},{3,1},{4,6},{5,7},{6,4},{7,5},{8,10},{9,11},{10,... | collective-permute-start | bytes 663560 | tf_op jit(solution)/shard_map/ppermute | solution.py:236
  28.6 4.4 %collective-permute-done.7.rest_2_ = bf16[48,2304]{1,0:T(8,128)(2,1)S(1)} collective-permute-done((bf16[48,2304]{1,0:T(8,128)(2,1)S(1)}, bf16[48,2304]{1,0:T(8,128)(2,1)S(1)}, u32[]{:S(2)}, u32[]{:S(2)}) %collective-permute-start.7) | collective-permute-done | bytes 221216 | tf_op jit(solution)/shard_map/ppermute | solution.py:236
  33.0 1.3 %collective-permute-start.9 = (bf16[48,2304]{1,0:T(8,128)(2,1)S(1)}, bf16[48,2304]{1,0:T(8,128)(2,1)S(1)}, u32[]{:S(2)}, u32[]{:S(2)}) collective-permute-start(bf16[48,2304]{1,0:T(8,128)(2,1)S(1)} %collective-permute-done.7.rest_2_), channel_id=1, source_target_pairs={{4,6},{5,7},{2,0},{3,1},{12,14},{13,15},{10,8},{11,9},{20,22},{21,... | collective-permute-start | bytes 663560 | tf_op jit(solution)/shard_map/ppermute | solution.py:236
  34.3 0.1 collective-permute-start.10
  34.4 0.5 collective-permute-start.12
  34.9 0.1 collective-permute-start.13
  35.0 0.3 collective-permute-done.6.rest_1_
  35.3 0.1 collective-permute-start.11
  35.4 5.4 %collective-permute-done.9.rest_4_ = bf16[48,2304]{1,0:T(8,128)(2,1)S(1)} collective-permute-done((bf16[48,2304]{1,0:T(8,128)(2,1)S(1)}, bf16[48,2304]{1,0:T(8,128)(2,1)S(1)}, u32[]{:S(2)}, u32[]{:S(2)}) %collective-permute-start.9) | collective-permute-done | bytes 221216 | tf_op jit(solution)/shard_map/ppermute | solution.py:236
  40.9 1.4 %collective-permute-done.14.rest_9_ = bf16[48,2304]{1,0:T(8,128)(2,1)S(1)} collective-permute-done((bf16[48,2304]{1,0:T(8,128)(2,1)S(1)}, bf16[48,2304]{1,0:T(8,128)(2,1)S(1)}, u32[]{:S(2)}, u32[]{:S(2)}) %collective-permute-start.14) | collective-permute-done | bytes 221216 | tf_op jit(solution)/shard_map/ppermute | solution.py:228
  42.3 17.8 %shard_map.113.rest_0_ = bf16[48,2304]{1,0:T(8,128)(2,1)S(1)} custom-call(s32[1]{0:T(128)} %bitcast.index, bf16[48,2304]{1,0:T(8,128)(2,1)S(1)} %get-tuple-element.26.rest_0_, bf16[48,2304]{1,0:T(8,128)(2,1)S(1)} %collective-permute-done.6.rest_1_, bf16[48,2304]{1,0:T(8,128)(2,1)S(1)} %collective-permute-done.7.rest_2_, ...), custom_call_target="tpu_custom_call" | custom-call | flops 7361003520 | bytes 3096580 | tf_op jit(solution)/shard_map/pallas_call | solution.py:216
  60.1 0.9 %collective-permute-start.17 = (bf16[48,2304]{1,0:T(8,128)(2,1)S(1)}, bf16[48,2304]{1,0:T(8,128)(2,1)S(1)}, u32[]{:S(2)}, u32[]{:S(2)}) collective-permute-start(bf16[48,2304]{1,0:T(8,128)(2,1)S(1)} %shard_map.113.rest_0_), channel_id=1, source_target_pairs={{0,24},{8,16},{16,8},{24,0},{1,25},{9,17},{17,9},{25,1},{2,26},{10... | collective-permute-start | bytes 663560 | tf_op jit(solution)/shard_map/ppermute | solution.py:228
  61.0 2.6 %collective-permute-start.15 = (bf16[48,2304]{1,0:T(8,128)(2,1)S(1)}, bf16[48,2304]{1,0:T(8,128)(2,1)S(1)}, u32[]{:S(2)}, u32[]{:S(2)}) collective-permute-start(bf16[48,2304]{1,0:T(8,128)(2,1)S(1)} %shard_map.113.rest_0_), channel_id=1, source_target_pairs={{0,8},{8,0},{16,24},{24,16},{1,9},{9,1},{17,25},{25,17},{2,10},{10... | collective-permute-start | bytes 663560 | tf_op jit(solution)/shard_map/ppermute | solution.py:228
  63.7 1.3 %shard_map.112 = (f32[48,5376]{1,0:T(8,128)}, f32[48,1536]{1,0:T(8,128)}, f32[48,1001]{1,0:T(8,128)}) custom-call(s32[1]{0:T(128)} %bitcast.index, f32[48,5376]{1,0:T(8,128)S(1)} %bitcast.24, f32[48,1536]{1,0:T(8,128)S(1)} %bitcast.26, f32[48,1001]{1,0:T(8,128)S(1)} %bitcast.29, bf16[48,2304]{1,0:T(8,128)(2,1)S(1)} %get-tuple-element.22.rest_0_, ...), custom_call_target="tpu_custom_call" | custom-call | bytes 3923332 | tf_op jit(solution)/shard_map/pallas_call | solution.py:216
  65.0 4.4 %collective-permute-done.17.rest_3_ = bf16[48,2304]{1,0:T(8,128)(2,1)S(1)} collective-permute-done((bf16[48,2304]{1,0:T(8,128)(2,1)S(1)}, bf16[48,2304]{1,0:T(8,128)(2,1)S(1)}, u32[]{:S(2)}, u32[]{:S(2)}) %collective-permute-start.17) | collective-permute-done | bytes 221216 | tf_op jit(solution)/shard_map/ppermute | solution.py:228
  69.4 3.6 %collective-permute-done.16.rest_2_ = bf16[48,2304]{1,0:T(8,128)(2,1)S(1)} collective-permute-done((bf16[48,2304]{1,0:T(8,128)(2,1)S(1)}, bf16[48,2304]{1,0:T(8,128)(2,1)S(1)}, u32[]{:S(2)}, u32[]{:S(2)}) %collective-permute-start.16) | collective-permute-done | bytes 221216 | tf_op jit(solution)/shard_map/ppermute | solution.py:228
  73.0 0.9 %shard_map.114 = (bf16[48,5376]{1,0:T(8,128)(2,1)}, bf16[48,1536]{1,0:T(8,128)(2,1)}, bf16[48,1001]{1,0:T(8,128)(2,1)}) custom-call(s32[1]{0:T(128)} %bitcast.index, bf16[48,2304]{1,0:T(8,128)(2,1)S(1)} %shard_map.113.rest_0_, bf16[48,2304]{1,0:T(8,128)(2,1)S(1)} %collective-permute-done.15.rest_1_, bf16[48,2304]{1,0:T(8,128)(2,1)S(1)} %collective-permute-done.16.rest_2_, ...), custom_call_target="tpu_custom_call" | custom-call | bytes 1644388 | tf_op jit(solution)/shard_map/pallas_call | solution.py:216
  (22 shorter events, 0.1 us)
Async XLA Ops:
  0.6 8.0 %copy-start = (f32[1,48,5376]{2,1,0:T(8,128)S(1)}, f32[1,48,5376]{2,1,0:T(8,128)}, u32[]{:S(2)}) copy-start(f32[1,48,5376]{2,1,0:T(8,128)} %param.9) | copy-start | bytes 3096580
  0.6 1.3 %copy-start.2 = (f32[1,1,48,5376]{3,2,1,0:T(8,128)S(1)}, f32[1,1,48,5376]{3,2,1,0:T(8,128)}, u32[]{:S(2)}) copy-start(f32[1,1,48,5376]{3,2,1,0:T(8,128)} %param.6) | copy-start | bytes 3096580
  2.0 1.0 %copy-start.4 = (f32[1,1,1536,48]{2,3,1,0:T(8,128)S(1)}, f32[1,1,1536,48]{2,3,1,0:T(8,128)}, u32[]{:S(2)}) copy-start(f32[1,1,1536,48]{2,3,1,0:T(8,128)} %param.7) | copy-start | bytes 884740
  2.9 0.9 %copy-start.5 = (f32[1,1001,48]{1,2,0:T(8,128)S(1)}, f32[1,1001,48]{1,2,0:T(8,128)}, u32[]{:S(2)}) copy-start(f32[1,1001,48]{1,2,0:T(8,128)} %param.8) | copy-start | bytes 576580
  3.8 4.8 %copy-start.1 = (f32[1,1536,48]{1,2,0:T(8,128)S(1)}, f32[1,1536,48]{1,2,0:T(8,128)}, u32[]{:S(2)}) copy-start(f32[1,1536,48]{1,2,0:T(8,128)} %param.10) | copy-start | bytes 884740
  3.8 4.8 %copy-start.3 = (f32[1001,48]{0,1:T(8,128)S(1)}, f32[1001,48]{0,1:T(8,128)}, u32[]{:S(2)}) copy-start(f32[1001,48]{0,1:T(8,128)} %param.11) | copy-start | bytes 576580
  4.1 9.3 %collective-permute-start = (bf16[48,2304]{1,0:T(8,128)(2,1)S(1)}, bf16[48,2304]{1,0:T(8,128)(2,1)S(1)}, u32[]{:S(2)}, u32[]{:S(2)}) collective-permute-start(bf16[48,2304]{1,0:T(8,128)(2,1)S(1)} %get-tuple-element.19), channel_id=1, source_target_pairs={{0,8},{8,0},{16,24},{24,16},{1,9},{9,1},{17,25},{25,17},{2,10},{10... | collective-permute-start | bytes 663560 | tf_op jit(solution)/shard_map/ppermute | solution.py:228
  7.1 11.6 %collective-permute-start.1 = (bf16[48,2304]{1,0:T(8,128)(2,1)S(1)}, bf16[48,2304]{1,0:T(8,128)(2,1)S(1)}, u32[]{:S(2)}, u32[]{:S(2)}) collective-permute-start(bf16[48,2304]{1,0:T(8,128)(2,1)S(1)} %get-tuple-element.20), channel_id=1, source_target_pairs={{0,16},{8,24},{16,0},{24,8},{1,17},{9,25},{17,1},{25,9},{2,18},{10... | collective-permute-start | bytes 663560 | tf_op jit(solution)/shard_map/ppermute | solution.py:228
  8.6 10.1 %collective-permute-start.2 = (bf16[48,2304]{1,0:T(8,128)(2,1)S(1)}, bf16[48,2304]{1,0:T(8,128)(2,1)S(1)}, u32[]{:S(2)}, u32[]{:S(2)}) collective-permute-start(bf16[48,2304]{1,0:T(8,128)(2,1)S(1)} %get-tuple-element.21), channel_id=1, source_target_pairs={{0,24},{8,16},{16,8},{24,0},{1,25},{9,17},{17,9},{25,1},{2,26},{10... | collective-permute-start | bytes 663560 | tf_op jit(solution)/shard_map/ppermute | solution.py:228
  18.9 8.0 %collective-permute-start.5 = (bf16[48,2304]{1,0:T(8,128)(2,1)S(1)}, bf16[48,2304]{1,0:T(8,128)(2,1)S(1)}, u32[]{:S(2)}, u32[]{:S(2)}) collective-permute-start(bf16[48,2304]{1,0:T(8,128)(2,1)S(1)} %get-tuple-element.22.rest_0_), channel_id=1, source_target_pairs={{0,24},{8,16},{16,8},{24,0},{1,25},{9,17},{17,9},{25,1},{2,26},{10... | collective-permute-start | bytes 663560 | tf_op jit(solution)/shard_map/ppermute | solution.py:228
  20.4 12.6 %collective-permute-start.7 = (bf16[48,2304]{1,0:T(8,128)(2,1)S(1)}, bf16[48,2304]{1,0:T(8,128)(2,1)S(1)}, u32[]{:S(2)}, u32[]{:S(2)}) collective-permute-start(bf16[48,2304]{1,0:T(8,128)(2,1)S(1)} %get-tuple-element.26.rest_0_), channel_id=1, source_target_pairs={{0,4},{1,5},{4,0},{5,1},{2,6},{3,7},{6,2},{7,3},{8,12},{9,13},{12,... | collective-permute-start | bytes 663560 | tf_op jit(solution)/shard_map/ppermute | solution.py:236
  23.0 11.3 %collective-permute-start.4 = (bf16[48,2304]{1,0:T(8,128)(2,1)S(1)}, bf16[48,2304]{1,0:T(8,128)(2,1)S(1)}, u32[]{:S(2)}, u32[]{:S(2)}) collective-permute-start(bf16[48,2304]{1,0:T(8,128)(2,1)S(1)} %get-tuple-element.22.rest_0_), channel_id=1, source_target_pairs={{0,16},{8,24},{16,0},{24,8},{1,17},{9,25},{17,1},{25,9},{2,18},{10... | collective-permute-start | bytes 663560 | tf_op jit(solution)/shard_map/ppermute | solution.py:228
  24.2 10.2 %collective-permute-start.3 = (bf16[48,2304]{1,0:T(8,128)(2,1)S(1)}, bf16[48,2304]{1,0:T(8,128)(2,1)S(1)}, u32[]{:S(2)}, u32[]{:S(2)}) collective-permute-start(bf16[48,2304]{1,0:T(8,128)(2,1)S(1)} %get-tuple-element.22.rest_0_), channel_id=1, source_target_pairs={{0,8},{8,0},{16,24},{24,16},{1,9},{9,1},{17,25},{25,17},{2,10},{10... | collective-permute-start | bytes 663560 | tf_op jit(solution)/shard_map/ppermute | solution.py:228
  25.0 9.9 %collective-permute-start.8 = (bf16[48,2304]{1,0:T(8,128)(2,1)S(1)}, bf16[48,2304]{1,0:T(8,128)(2,1)S(1)}, u32[]{:S(2)}, u32[]{:S(2)}) collective-permute-start(bf16[48,2304]{1,0:T(8,128)(2,1)S(1)} %get-tuple-element.26.rest_0_), channel_id=1, source_target_pairs={{2,4},{3,5},{4,2},{5,3},{10,12},{11,13},{12,10},{13,11},{18,20},{1... | collective-permute-start | bytes 663560 | tf_op jit(solution)/shard_map/ppermute | solution.py:236
  26.8 8.5 %collective-permute-start.6 = (bf16[48,2304]{1,0:T(8,128)(2,1)S(1)}, bf16[48,2304]{1,0:T(8,128)(2,1)S(1)}, u32[]{:S(2)}, u32[]{:S(2)}) collective-permute-start(bf16[48,2304]{1,0:T(8,128)(2,1)S(1)} %get-tuple-element.26.rest_0_), channel_id=1, source_target_pairs={{0,2},{1,3},{2,0},{3,1},{4,6},{5,7},{6,4},{7,5},{8,10},{9,11},{10,... | collective-permute-start | bytes 663560 | tf_op jit(solution)/shard_map/ppermute | solution.py:236
  33.0 7.8 %collective-permute-start.9 = (bf16[48,2304]{1,0:T(8,128)(2,1)S(1)}, bf16[48,2304]{1,0:T(8,128)(2,1)S(1)}, u32[]{:S(2)}, u32[]{:S(2)}) collective-permute-start(bf16[48,2304]{1,0:T(8,128)(2,1)S(1)} %collective-permute-done.7.rest_2_), channel_id=1, source_target_pairs={{4,6},{5,7},{2,0},{3,1},{12,14},{13,15},{10,8},{11,9},{20,22},{21,... | collective-permute-start | bytes 663560 | tf_op jit(solution)/shard_map/ppermute | solution.py:236
  34.3 6.5 %collective-permute-start.10 = (bf16[48,2304]{1,0:T(8,128)(2,1)S(1)}, bf16[48,2304]{1,0:T(8,128)(2,1)S(1)}, u32[]{:S(2)}, u32[]{:S(2)}) collective-permute-start(bf16[48,2304]{1,0:T(8,128)(2,1)S(1)} %get-tuple-element.26.rest_0_), channel_id=1, source_target_pairs={{0,1},{1,0},{2,3},{3,2},{4,5},{5,4},{6,7},{7,6},{8,9},{9,8},{10,11... | collective-permute-start | bytes 663560 | tf_op jit(solution)/shard_map/ppermute | solution.py:228
  34.4 6.4 %collective-permute-start.12 = (bf16[48,2304]{1,0:T(8,128)(2,1)S(1)}, bf16[48,2304]{1,0:T(8,128)(2,1)S(1)}, u32[]{:S(2)}, u32[]{:S(2)}) collective-permute-start(bf16[48,2304]{1,0:T(8,128)(2,1)S(1)} %collective-permute-done.7.rest_2_), channel_id=1, source_target_pairs={{0,1},{1,0},{2,3},{3,2},{4,5},{5,4},{6,7},{7,6},{8,9},{9,8},{10,11... | collective-permute-start | bytes 663560 | tf_op jit(solution)/shard_map/ppermute | solution.py:228
  34.9 5.9 %collective-permute-start.13 = (bf16[48,2304]{1,0:T(8,128)(2,1)S(1)}, bf16[48,2304]{1,0:T(8,128)(2,1)S(1)}, u32[]{:S(2)}, u32[]{:S(2)}) collective-permute-start(bf16[48,2304]{1,0:T(8,128)(2,1)S(1)} %collective-permute-done.8.rest_3_), channel_id=1, source_target_pairs={{0,1},{1,0},{2,3},{3,2},{4,5},{5,4},{6,7},{7,6},{8,9},{9,8},{10,11... | collective-permute-start | bytes 663560 | tf_op jit(solution)/shard_map/ppermute | solution.py:228
  35.3 5.5 %collective-permute-start.11 = (bf16[48,2304]{1,0:T(8,128)(2,1)S(1)}, bf16[48,2304]{1,0:T(8,128)(2,1)S(1)}, u32[]{:S(2)}, u32[]{:S(2)}) collective-permute-start(bf16[48,2304]{1,0:T(8,128)(2,1)S(1)} %collective-permute-done.6.rest_1_), channel_id=1, source_target_pairs={{0,1},{1,0},{2,3},{3,2},{4,5},{5,4},{6,7},{7,6},{8,9},{9,8},{10,11... | collective-permute-start | bytes 663560 | tf_op jit(solution)/shard_map/ppermute | solution.py:228
  40.8 1.5 %collective-permute-start.14 = (bf16[48,2304]{1,0:T(8,128)(2,1)S(1)}, bf16[48,2304]{1,0:T(8,128)(2,1)S(1)}, u32[]{:S(2)}, u32[]{:S(2)}) collective-permute-start(bf16[48,2304]{1,0:T(8,128)(2,1)S(1)} %collective-permute-done.9.rest_4_), channel_id=1, source_target_pairs={{0,1},{1,0},{2,3},{3,2},{4,5},{5,4},{6,7},{7,6},{8,9},{9,8},{10,11... | collective-permute-start | bytes 663560 | tf_op jit(solution)/shard_map/ppermute | solution.py:228
  60.1 9.3 %collective-permute-start.17 = (bf16[48,2304]{1,0:T(8,128)(2,1)S(1)}, bf16[48,2304]{1,0:T(8,128)(2,1)S(1)}, u32[]{:S(2)}, u32[]{:S(2)}) collective-permute-start(bf16[48,2304]{1,0:T(8,128)(2,1)S(1)} %shard_map.113.rest_0_), channel_id=1, source_target_pairs={{0,24},{8,16},{16,8},{24,0},{1,25},{9,17},{17,9},{25,1},{2,26},{10... | collective-permute-start | bytes 663560 | tf_op jit(solution)/shard_map/ppermute | solution.py:228
  61.0 11.9 %collective-permute-start.16 = (bf16[48,2304]{1,0:T(8,128)(2,1)S(1)}, bf16[48,2304]{1,0:T(8,128)(2,1)S(1)}, u32[]{:S(2)}, u32[]{:S(2)}) collective-permute-start(bf16[48,2304]{1,0:T(8,128)(2,1)S(1)} %shard_map.113.rest_0_), channel_id=1, source_target_pairs={{0,16},{8,24},{16,0},{24,8},{1,17},{9,25},{17,1},{25,9},{2,18},{10... | collective-permute-start | bytes 663560 | tf_op jit(solution)/shard_map/ppermute | solution.py:228
  61.0 11.9 %collective-permute-start.15 = (bf16[48,2304]{1,0:T(8,128)(2,1)S(1)}, bf16[48,2304]{1,0:T(8,128)(2,1)S(1)}, u32[]{:S(2)}, u32[]{:S(2)}) collective-permute-start(bf16[48,2304]{1,0:T(8,128)(2,1)S(1)} %shard_map.113.rest_0_), channel_id=1, source_target_pairs={{0,8},{8,0},{16,24},{24,16},{1,9},{9,1},{17,25},{25,17},{2,10},{10... | collective-permute-start | bytes 663560 | tf_op jit(solution)/shard_map/ppermute | solution.py:228

commit v3 on v2

v3 whole, which is shorter than its diff:
```python
import functools
import math

import jax
import jax.numpy as jnp
from jax import lax
from jax.experimental import pallas as pl
from jax.experimental.pallas import tpu as pltpu
from jax.sharding import PartitionSpec as P

D = 384
MLP = 1536
ADA = 2304
CLASSES = 1001
NS_ITERS = 5
QKV = 1152

COEF_A = 3.4445
COEF_B = -4.775
COEF_C = 2.0315
MOMENTUM = 0.95
EPSILON = 1e-07

VMEM_LIMIT = 48 * 1024 * 1024
VMEM_ALL = 63 * 1024 * 1024

WIDTHS = [QKV, D, MLP, ADA, MLP, CLASSES]
OFFSETS = [0, QKV, QKV + D, QKV + D + MLP]
PADDED = [-(-width // 128) * 128 for width in WIDTHS]
DOWN, EMBED = 4, 5
TILE = 256


def plan(n_rep):
    bins = [[] for _ in range(n_rep)]
    loads = [0] * n_rep
    for matrix in sorted(range(6), key=lambda m: -PADDED[m]):
        owner = loads.index(min(loads))
        bins[owner].append(matrix)
        loads[owner] += PADDED[matrix]
    return bins, max(loads)


def placed(bins):
    where = {}
    for owner, group in enumerate(bins):
        offset = 0
        for matrix in group:
            where[matrix] = (owner, offset)
            offset += PADDED[matrix]
    return where


def window(group, low, high):
    found = []
    offset = 0
    for matrix in group:
        first, last = max(low - offset, 0), min(high - offset, WIDTHS[matrix])
        if first < last:
            found.append((matrix, first, last, offset + first - low))
        offset += PADDED[matrix]
    return found


def source(matrix, first, last, wide, down, embed):
    if matrix == DOWN:
        return down.at[:, first:last]
    if matrix == EMBED:
        return embed.at[:, first:last]
    return wide.at[:, OFFSETS[matrix] + first : OFFSETS[matrix] + last]


def split_kernel(bins, low, high, index, wide, down, embed, *rest):
    outs, sems = rest[:-3], rest[-1]
    held, held_embed = rest[-3], rest[-2]
    copies = []
    for target, group in enumerate(bins):
        for matrix, first, last, place in window(group, low, high):
            if matrix == EMBED:
                dst = held_embed.at[:, first:last] if last < CLASSES or first > 0 else held_embed
                src = embed if dst is held_embed else source(matrix, first, last, wide, down, embed)
            else:
                dst = held.at[target, :, place : place + last - first]
                src = source(matrix, first, last, wide, down, embed)
            copy = pltpu.make_async_copy(src, dst, sems.at[len(copies)])
            copy.start()
            copies.append(copy)
    for copy in copies:
        copy.wait()
    for target, group in enumerate(bins):
        for matrix, first, last, place in window(group, low, high):
            if matrix == EMBED:
                held[target, :, place : place + last - first] = held_embed[:, first:last]
    for k, dst in enumerate(outs):
        for target, group in enumerate(bins):

            @pl.when((index[0] ^ k) == target)
            def _():
                end = 0
                for _, first, last, place in window(group, low, high):
                    dst[:, place : place + last - first] = held[target, :, place : place + last - first].astype(
                        dst.dtype
                    )
                    end = place + last - first
                if end < high - low:
                    dst[:, end:] = jnp.zeros((dst.shape[0], high - low - end), dst.dtype)


def sum_kernel(count, own, *rest):
    received, mom, g_out, y_out = rest[:count], rest[count], rest[count + 1], rest[count + 2]
    g = own[...]
    for piece in received:
        g = g + piece[...].astype(jnp.float32)
    g_out[...] = g.astype(jnp.bfloat16)
    y_out[...] = (g + MOMENTUM * (MOMENTUM * mom[...] + g)).astype(jnp.bfloat16)


def join_kernel(left, right, *rest):
    out, half = rest[-1], left.shape[1]
    out[:, :half] = left[...]
    out[:, half:] = right[...]


def newton_kernel(bins, count, halves, rows, index, *rest):
    pieces, out, x_ref = rest[: count * halves], rest[-2], rest[-1]
    piece_rows, piece_width = pieces[0].shape
    for half in range(halves):
        for number in range(count):
            x_ref[
                number * piece_rows : (number + 1) * piece_rows,
                half * piece_width : (half + 1) * piece_width,
            ] = pieces[half * count + number][...]

    def branch(group):
        spans = []
        offset = 0
        for matrix in group:
            end = offset + PADDED[matrix]
            tiles = [slice(low, min(low + TILE, end)) for low in range(offset, end, TILE)]
            spans.append((slice(offset, end), tiles, math.sqrt(max(D, WIDTHS[matrix]))))
            offset = end

        def outer(span):
            x = x_ref[:, span]
            return lax.dot_general(x, x, (((1,), (1,)), ((), ())), preferred_element_type=jnp.float32)

        def polynomial(gram):
            gram = gram.astype(jnp.bfloat16)
            square = jnp.dot(gram, gram, preferred_element_type=jnp.float32)
            return COEF_B * gram.astype(jnp.float32) + COEF_C * square

        def advance(tiles, poly, factor):
            for tile in tiles:
                x = x_ref[:, tile]
                x_ref[:, tile] = (
                    factor * x.astype(jnp.float32) + jnp.dot(poly, x, preferred_element_type=jnp.float32)
                ).astype(jnp.bfloat16)

        diagonal = lax.broadcasted_iota(jnp.int32, (D, D), 0) == lax.broadcasted_iota(jnp.int32, (D, D), 1)
        for span, tiles, _ in spans:
            gram = outer(span)
            scale = 1.0 / (jnp.sqrt(jnp.sum(jnp.where(diagonal, gram, 0.0))) + EPSILON)
            poly = (scale * polynomial(gram * scale * scale)).astype(jnp.bfloat16)
            advance(tiles, poly, COEF_A * scale)

        def step(_, carry):
            polys = [polynomial(outer(span)).astype(jnp.bfloat16) for span, _, _ in spans]
            for poly, (_, tiles, _) in zip(polys, spans):
                advance(tiles, poly, COEF_A)
            return carry

        lax.fori_loop(0, NS_ITERS - 2, step, 0)
        for span, tiles, factor in spans:
            poly = polynomial(outer(span))[:rows].astype(jnp.bfloat16)
            for tile in tiles:
                x = x_ref[:, tile]
                out[:, tile] = (
                    factor
                    * (COEF_A * x[:rows].astype(jnp.float32) + jnp.dot(poly, x, preferred_element_type=jnp.float32))
                ).astype(jnp.bfloat16)

    for target, group in enumerate(bins):
        if group:

            @pl.when(index[0] == target)
            def _():
                branch(group)


def per_index(bins, index, body):
    for mine in range(len(bins)):

        @pl.when(index[0] == mine)
        def _():
            body(mine)


def momentum_kernel(bins, index, wide, down, embed, *rest):
    n = len(bins)
    pieces, (new_wide, new_down, new_embed) = rest[:n], rest[n:]
    where = placed(bins)

    def body(mine):
        for matrix in range(6):
            owner, offset = where[matrix]
            g = pieces[mine ^ owner][:, offset : offset + PADDED[matrix]].astype(jnp.float32)
            if matrix == DOWN:
                new_down[...] = MOMENTUM * down[...] + g
            elif matrix == EMBED:
                new_embed[...] = MOMENTUM * embed[...] + g[:, :CLASSES]
            else:
                span = slice(OFFSETS[matrix], OFFSETS[matrix] + WIDTHS[matrix])
                new_wide[:, span] = MOMENTUM * wide[:, span] + g

    per_index(bins, index, body)


def update_kernel(bins, index, *rest):
    n = len(bins)
    pieces, (upd_wide, upd_down, upd_embed) = rest[:n], rest[n:]
    where = placed(bins)

    def body(mine):
        for matrix in range(6):
            owner, offset = where[matrix]
            value = pieces[mine ^ owner][:, offset : offset + PADDED[matrix]]
            if matrix == DOWN:
                upd_down[...] = value
            elif matrix == EMBED:
                upd_embed[...] = value[:, :CLASSES]
            else:
                upd_wide[:, OFFSETS[matrix] : OFFSETS[matrix] + WIDTHS[matrix]] = value

    per_index(bins, index, body)


def call(kernel, outs, args, scratch=(), indexed=True, flops=0, tied=0, held=0):
    specs = [pl.BlockSpec(memory_space=pltpu.SMEM)] if indexed else []
    specs += [pl.BlockSpec(memory_space=pltpu.MemorySpace.HBM)] * held
    specs += [pl.BlockSpec(memory_space=pltpu.VMEM)] * (len(args) - tied - len(specs))
    specs += [pl.BlockSpec(memory_space=pl.ANY)] * tied
    size = sum(a.size * a.dtype.itemsize for a in args) + sum(
        math.prod(o.shape) * o.dtype.itemsize for o in outs
    )
    return pl.pallas_call(
        kernel,
        out_shape=tuple(outs),
        in_specs=specs,
        out_specs=tuple([pl.BlockSpec(memory_space=pltpu.VMEM)] * len(outs)),
        scratch_shapes=list(scratch),
        compiler_params=pltpu.CompilerParams(vmem_limit_bytes=VMEM_ALL if held else VMEM_LIMIT),
        cost_estimate=pl.CostEstimate(flops=flops, bytes_accessed=size, transcendentals=0),
    )(*args)


def split(bins, low, high, index, arrays, dtypes):
    rows = arrays[0].shape[0]
    scratch = (
        pltpu.VMEM((len(bins), rows, high - low), jnp.float32),
        pltpu.VMEM((rows, CLASSES), jnp.float32),
        pltpu.SemaphoreType.DMA((8 + len(bins),)),
    )
    outs = [jax.ShapeDtypeStruct((rows, high - low), dtype) for dtype in dtypes]
    return call(functools.partial(split_kernel, bins, low, high), outs, (index, *arrays), scratch, held=3)


def swap(value, axis, k, n):
    return lax.ppermute(value, axis, [(i, i ^ k) for i in range(n)])


def spread(value, axis, n):
    return [swap(value, axis, k, n) for k in range(1, n)]


def gather_rows(value, n):
    pieces = [value] + [swap(value, "shard", k, n) for k in range(2, n, 2)]
    return pieces + [swap(piece, "shard", 1, n) for piece in pieces]


def per_device(grad_wide, grad_down, grad_embed, mom_wide, mom_down, mom_embed):
    n_rep, n_shard = lax.axis_size("rep"), lax.axis_size("shard")
    bins, width = plan(n_rep)
    index = lax.axis_index("rep").astype(jnp.int32).reshape(1)
    grads = (grad_wide[0, 0], grad_down[0, 0].T, grad_embed[0].T)
    moms = (mom_wide[0], mom_down[0].T, mom_embed.T)
    rows = grads[0].shape[0]
    whole = jax.ShapeDtypeStruct((rows, width), jnp.bfloat16)
    windows = [(0, width // 2), (width // 2, width)]

    split_grads = [
        split(bins, low, high, index, grads, [jnp.float32] + [jnp.bfloat16] * (n_rep - 1)) for low, high in windows
    ]
    received = [[swap(piece, "rep", k + 1, n_rep) for k, piece in enumerate(own[1:])] for own in split_grads]
    gs, pieces = [], []
    for half, (low, high) in enumerate(windows):
        (mom_own,) = split(bins, low, high, index, moms, [jnp.float32])
        g, y = call(
            functools.partial(sum_kernel, n_rep - 1),
            [jax.ShapeDtypeStruct((rows, high - low), jnp.bfloat16)] * 2,
            (split_grads[half][0], *received[half], mom_own),
            indexed=False,
        )
        gs.append(g)
        pieces.append(gather_rows(y, n_shard))
    (g,) = call(join_kernel, [whole], (*gs, pieces[0][1]), indexed=False, tied=1)
    g_others = spread(g, "rep", n_rep)
    if rows % 16:
        pieces = [[jnp.concatenate(half, axis=0)] for half in pieces]
    (upd,) = call(
        functools.partial(newton_kernel, bins, len(pieces[0]), len(pieces), rows),
        [whole],
        (index, *pieces[0], *pieces[1], *g_others),
        (pltpu.VMEM((D, width), jnp.bfloat16),),
        flops=NS_ITERS * (4 * D * D * width + 2 * D * D * D),
        tied=len(g_others),
    )
    upd_others = spread(upd, "rep", n_rep)
    news = call(
        functools.partial(momentum_kernel, bins),
        [jax.ShapeDtypeStruct(m.shape, jnp.float32) for m in moms],
        (index, *moms, g, *g_others),
    )
    updates = call(
        functools.partial(update_kernel, bins),
        [jax.ShapeDtypeStruct(m.shape, jnp.bfloat16) for m in moms],
        (index, upd, *upd_others),
    )
    return (
        news[0][None],
        news[1].T[None],
        news[2].T,
        updates[0][None],
        updates[1].T[None],
        updates[2].T,
    )


def solution(mesh):
    placed_in = (
        P("rep", None, "shard", None),
        P("rep", None, None, "shard"),
        P("rep", None, "shard"),
        P(None, "shard", None),
        P(None, None, "shard"),
        P(None, "shard"),
    )
    return jax.shard_map(
        per_device,
        mesh=mesh,
        in_specs=placed_in,
        out_specs=placed_in[3:] + placed_in[3:],
        check_vma=False,
    )
```

time: 74.1 us -> 77.5 us (1.046)
  starting transfers between devices: 18.7 us -> 28.4 us
  waiting for transfers between devices: 30.8 us -> 23.9 us
  Pallas kernels: 20.5 us -> 24.1 us
  local copies, waits for them, and re-layouts: 3.2 us -> 0.04 us
    ppermute x14 -> x26, starting transfers between devices: 12.4 us -> 28.4 us  [swap(): return lax.ppermute(value, axis, [(i, i ^ k) for i in range(n)])]
    ppermute x4 -> x0, waiting for transfers between devices: 10.2 us -> none  [along(): lax.ppermute(value, 'shard', [(2 * a + c, 2 * b + c) for a, b in hops for...]
    ppermute x4 -> x0, starting transfers between devices: 6.28 us -> none  [along(): lax.ppermute(value, 'shard', [(2 * a + c, 2 * b + c) for a, b in hops for...]
    pallas_call x6 -> x10, Pallas kernels: 20.5 us -> 24.1 us  [call(): pl.pallas_call(kernel, out_shape=tuple(outs), in_specs=specs, out_specs=t...]
    ppermute x14 -> x26, waiting for transfers between devices: 20.6 us -> 23.9 us  [swap(): return lax.ppermute(value, axis, [(i, i ^ k) for i in range(n)])]
    unnamed x12 -> x14, local copies, waits for them, and re-layouts: 3.2 us -> 0.04 us
  transfers between devices with their start and end apart: 18 -> 26, of which waited for: 9 -> 10; matrix products, arithmetic and copies ran while one was open for 0% -> 0% of each run, Pallas kernels for 2% -> 12%
where the time goes in v3:
time: 77.5 us; the launch traced here: 77.3 us
  starting transfers between devices  28.4 us (37%)
  Pallas kernels  24.1 us (31%)
  waiting for transfers between devices  23.9 us (31%)
  between operations  0.83 us (1%)
    ppermute x26, starting transfers between devices, swap(): return lax.ppermute(value, axis, [(i, i ^ k) for i in range(n)])  28.4 us
    pallas_call x10, Pallas kernels, call(): pl.pallas_call(kernel, out_shape=tuple(outs), in_specs=specs, out_specs=t...  24.1 us
    ppermute x26, waiting for transfers between devices, swap(): return lax.ppermute(value, axis, [(i, i ^ k) for i in range(n)])  23.9 us
  transfers between devices with their start and end apart: 26, of which 10 were waited for; matrix products, arithmetic and copies ran while one was open for 0% of the time, Pallas kernels for 12%

profile of v3, /device:TPU:0, one launch (start us, length us, event | category | flops | bytes accessed | tf_op | source)
XLA Modules:
  0.0 77.3 jit_solution(5482157526905182344)
XLA Ops:
  0.6 2.2 %shard_map.112 = (f32[48,1152]{1,0:T(8,128)}, bf16[48,1152]{1,0:T(8,128)(2,1)}, bf16[48,1152]{1,0:T(8,128)(2,1)}, bf16[48,1152]{1,0:T(8,128)(2,1)}) custom-call(s32[1]{0:T(128)} %bitcast.index, f32[48,5376]{1,0:T(8,128)} %bitcast.32, f32[48,1536]{1,0:T(8,128)} %bitcast.34, f32[48,1001]{1,0:T(8,128)} %bitcast.36), custom_call_target="tpu_custom_call" | custom-call | bytes 2072260 | tf_op jit(solution)/shard_map/pallas_call | solution.py:245
  2.9 3.0 %collective-permute-start.3 = (bf16[48,1152]{1,0:T(8,128)(2,1)}, bf16[48,1152]{1,0:T(8,128)(2,1)S(1)}, u32[]{:S(2)}, u32[]{:S(2)}) collective-permute-start(bf16[48,1152]{1,0:T(8,128)(2,1)} %get-tuple-element.30), channel_id=1, source_target_pairs={{0,8},{8,0},{16,24},{24,16},{1,9},{9,1},{17,25},{25,17},{2,10},{10... | collective-permute-start | bytes 331784 | tf_op jit(solution)/shard_map/ppermute | solution.py:268
  5.9 1.5 %collective-permute-start.4 = (bf16[48,1152]{1,0:T(8,128)(2,1)}, bf16[48,1152]{1,0:T(8,128)(2,1)}, u32[]{:S(2)}, u32[]{:S(2)}) collective-permute-start(bf16[48,1152]{1,0:T(8,128)(2,1)} %get-tuple-element.31), channel_id=1, source_target_pairs={{0,16},{8,24},{16,0},{24,8},{1,17},{9,25},{17,1},{25,9},{2,18},{10... | collective-permute-start | bytes 331784 | tf_op jit(solution)/shard_map/ppermute | solution.py:268
  7.4 2.3 %shard_map.109 = (f32[48,1152]{1,0:T(8,128)}, bf16[48,1152]{1,0:T(8,128)(2,1)}, bf16[48,1152]{1,0:T(8,128)(2,1)}, bf16[48,1152]{1,0:T(8,128)(2,1)}) custom-call(s32[1]{0:T(128)} %bitcast.index, f32[48,5376]{1,0:T(8,128)} %bitcast.33, f32[48,1536]{1,0:T(8,128)} %bitcast.35, f32[48,1001]{1,0:T(8,128)} %bitcast.37), custom_call_target="tpu_custom_call" | custom-call | bytes 2072260 | tf_op jit(solution)/shard_map/pallas_call | solution.py:245
  9.7 2.0 %collective-permute-start = (bf16[48,1152]{1,0:T(8,128)(2,1)}, bf16[48,1152]{1,0:T(8,128)(2,1)S(1)}, u32[]{:S(2)}, u32[]{:S(2)}) collective-permute-start(bf16[48,1152]{1,0:T(8,128)(2,1)} %get-tuple-element.25), channel_id=1, source_target_pairs={{0,8},{8,0},{16,24},{24,16},{1,9},{9,1},{17,25},{25,17},{2,10},{10... | collective-permute-start | bytes 331784 | tf_op jit(solution)/shard_map/ppermute | solution.py:268
  11.7 1.5 %collective-permute-start.1 = (bf16[48,1152]{1,0:T(8,128)(2,1)}, bf16[48,1152]{1,0:T(8,128)(2,1)S(1)}, u32[]{:S(2)}, u32[]{:S(2)}) collective-permute-start(bf16[48,1152]{1,0:T(8,128)(2,1)} %get-tuple-element.26), channel_id=1, source_target_pairs={{0,16},{8,24},{16,0},{24,8},{1,17},{9,25},{17,1},{25,9},{2,18},{10... | collective-permute-start | bytes 331784 | tf_op jit(solution)/shard_map/ppermute | solution.py:268
  13.3 2.0 %shard_map.113.rest_3_ = f32[48,1152]{1,0:T(8,128)} custom-call(s32[1]{0:T(128)} %bitcast.index, f32[48,5376]{1,0:T(8,128)} %bitcast.23, f32[48,1536]{1,0:T(8,128)} %bitcast.26, f32[48,1001]{1,0:T(8,128)} %bitcast.29), custom_call_target="tpu_custom_call" | custom-call | bytes 1740484 | tf_op jit(solution)/shard_map/pallas_call | solution.py:245
  15.3 2.1 %shard_map.110.rest_3_ = f32[48,1152]{1,0:T(8,128)} custom-call(s32[1]{0:T(128)} %bitcast.index, f32[48,5376]{1,0:T(8,128)} %bitcast.24, f32[48,1536]{1,0:T(8,128)} %bitcast.27, f32[48,1001]{1,0:T(8,128)} %bitcast.30), custom_call_target="tpu_custom_call" | custom-call | bytes 1740484 | tf_op jit(solution)/shard_map/pallas_call | solution.py:245
  17.5 1.1 %shard_map.114 = (bf16[48,1152]{1,0:T(8,128)(2,1)S(1)}, bf16[48,1152]{1,0:T(8,128)(2,1)S(1)}) custom-call(f32[48,1152]{1,0:T(8,128)S(1)} %copy-done.6, bf16[48,1152]{1,0:T(8,128)(2,1)S(1)} %collective-permute-done.3.rest_0_, bf16[48,1152]{1,0:T(8,128)(2,1)} %collective-permute-done.4.rest_1_, bf16[48,1152]{1,0:T(8,128)(2,1)} %collective-permute-done.5.rest_2_, ...), custom_call_target="tpu_custom_call" | custom-call | bytes 995328 | tf_op jit(solution)/shard_map/pallas_call | solution.py:245
  18.7 4.1 %collective-permute-start.18 = (bf16[48,1152]{1,0:T(8,128)(2,1)S(1)}, bf16[48,1152]{1,0:T(8,128)(2,1)S(1)}, u32[]{:S(2)}, u32[]{:S(2)}) collective-permute-start(bf16[48,1152]{1,0:T(8,128)(2,1)S(1)} %get-tuple-element.38.rest_8_), channel_id=1, source_target_pairs={{0,6},{1,7},{2,4},{3,5},{4,2},{5,3},{6,0},{7,1},{8,14},{9,15},{10,... | collective-permute-start | bytes 331784 | tf_op jit(solution)/shard_map/ppermute | solution.py:268
  22.8 0.6 collective-permute-start.16
  23.6 1.5 %collective-permute-start.6 = (bf16[48,1152]{1,0:T(8,128)(2,1)S(1)}, bf16[48,1152]{1,0:T(8,128)(2,1)S(1)}, u32[]{:S(2)}, u32[]{:S(2)}) collective-permute-start(bf16[48,1152]{1,0:T(8,128)(2,1)S(1)} %get-tuple-element.34.rest_0_), channel_id=1, source_target_pairs={{0,2},{1,3},{2,0},{3,1},{4,6},{5,7},{6,4},{7,5},{8,10},{9,11},{10,... | collective-permute-start | bytes 331784 | tf_op jit(solution)/shard_map/ppermute | solution.py:268
  25.1 1.7 %collective-permute-done.18.rest_11_ = bf16[48,1152]{1,0:T(8,128)(2,1)S(1)} collective-permute-done((bf16[48,1152]{1,0:T(8,128)(2,1)S(1)}, bf16[48,1152]{1,0:T(8,128)(2,1)S(1)}, u32[]{:S(2)}, u32[]{:S(2)}) %collective-permute-start.18) | collective-permute-done | bytes 110624 | tf_op jit(solution)/shard_map/ppermute | solution.py:268
  26.8 3.8 %collective-permute-start.11 = (bf16[48,1152]{1,0:T(8,128)(2,1)S(1)}, bf16[48,1152]{1,0:T(8,128)(2,1)S(1)}, u32[]{:S(2)}, u32[]{:S(2)}) collective-permute-start(bf16[48,1152]{1,0:T(8,128)(2,1)S(1)} %get-tuple-element.34.rest_0_), channel_id=1, source_target_pairs={{0,6},{1,7},{2,4},{3,5},{4,2},{5,3},{6,0},{7,1},{8,14},{9,15},{10,... | collective-permute-start | bytes 331784 | tf_op jit(solution)/shard_map/ppermute | solution.py:268
  30.6 2.3 %collective-permute-done.17.rest_10_ = bf16[48,1152]{1,0:T(8,128)(2,1)S(1)} collective-permute-done((bf16[48,1152]{1,0:T(8,128)(2,1)S(1)}, bf16[48,1152]{1,0:T(8,128)(2,1)S(1)}, u32[]{:S(2)}, u32[]{:S(2)}) %collective-permute-start.17) | collective-permute-done | bytes 110624 | tf_op jit(solution)/shard_map/ppermute | solution.py:268
  32.9 1.0 %collective-permute-done.6.rest_0_.rest_1_ = bf16[48,1152]{1,0:T(8,128)(2,1)S(1)} collective-permute-done((bf16[48,1152]{1,0:T(8,128)(2,1)S(1)}, bf16[48,1152]{1,0:T(8,128)(2,1)S(1)}, u32[]{:S(2)}, u32[]{:S(2)}) %collective-permute-start.6) | collective-permute-done | bytes 110624 | tf_op jit(solution)/shard_map/ppermute | solution.py:268
  34.0 2.6 %collective-permute-start.9 = (bf16[48,2304]{1,0:T(8,128)(2,1)S(1)}, bf16[48,2304]{1,0:T(8,128)(2,1)S(1)}, u32[]{:S(2)}, u32[]{:S(2)}) collective-permute-start(bf16[48,2304]{1,0:T(8,128)(2,1)S(1)} %shard_map.115.rest_0_), channel_id=1, source_target_pairs={{0,24},{8,16},{16,8},{24,0},{1,25},{9,17},{17,9},{25,1},{2,26},{10... | collective-permute-start | bytes 663560 | tf_op jit(solution)/shard_map/ppermute | solution.py:268
  36.8 5.4 %collective-permute-done.10.rest_2_ = bf16[48,1152]{1,0:T(8,128)(2,1)S(1)} collective-permute-done((bf16[48,1152]{1,0:T(8,128)(2,1)S(1)}, bf16[48,1152]{1,0:T(8,128)(2,1)S(1)}, u32[]{:S(2)}, u32[]{:S(2)}) %collective-permute-start.10) | collective-permute-done | bytes 110624 | tf_op jit(solution)/shard_map/ppermute | solution.py:268
  42.3 1.5 %collective-permute-start.8 = (bf16[48,2304]{1,0:T(8,128)(2,1)S(1)}, bf16[48,2304]{1,0:T(8,128)(2,1)S(1)}, u32[]{:S(2)}, u32[]{:S(2)}) collective-permute-start(bf16[48,2304]{1,0:T(8,128)(2,1)S(1)} %shard_map.115.rest_0_), channel_id=1, source_target_pairs={{0,16},{8,24},{16,0},{24,8},{1,17},{9,25},{17,1},{25,9},{2,18},{10... | collective-permute-start | bytes 663560 | tf_op jit(solution)/shard_map/ppermute | solution.py:268
  43.7 1.5 %collective-permute-start.7 = (bf16[48,2304]{1,0:T(8,128)(2,1)S(1)}, bf16[48,2304]{1,0:T(8,128)(2,1)S(1)}, u32[]{:S(2)}, u32[]{:S(2)}) collective-permute-start(bf16[48,2304]{1,0:T(8,128)(2,1)S(1)} %shard_map.115.rest_0_), channel_id=1, source_target_pairs={{0,8},{8,0},{16,24},{24,16},{1,9},{9,1},{17,25},{25,17},{2,10},{10... | collective-permute-start | bytes 663560 | tf_op jit(solution)/shard_map/ppermute | solution.py:268
  45.2 0.5 collective-permute-start.13
  45.7 0.8 %collective-permute-done.14.rest_6_ = bf16[48,1152]{1,0:T(8,128)(2,1)S(1)} collective-permute-done((bf16[48,1152]{1,0:T(8,128)(2,1)S(1)}, bf16[48,1152]{1,0:T(8,128)(2,1)S(1)}, u32[]{:S(2)}, u32[]{:S(2)}) %collective-permute-start.14) | collective-permute-done | bytes 110624 | tf_op jit(solution)/shard_map/ppermute | solution.py:268
  46.7 3.4 %collective-permute-done.8.rest_2_.rest_17_ = bf16[48,2304]{1,0:T(8,128)(2,1)S(1)} collective-permute-done((bf16[48,2304]{1,0:T(8,128)(2,1)S(1)}, bf16[48,2304]{1,0:T(8,128)(2,1)S(1)}, u32[]{:S(2)}, u32[]{:S(2)}) %collective-permute-start.8) | collective-permute-done | bytes 221216 | tf_op jit(solution)/shard_map/ppermute | solution.py:268
  50.1 1.2 %collective-permute-done.7.rest_1_.rest_16_ = bf16[48,2304]{1,0:T(8,128)(2,1)S(1)} collective-permute-done((bf16[48,2304]{1,0:T(8,128)(2,1)S(1)}, bf16[48,2304]{1,0:T(8,128)(2,1)S(1)}, u32[]{:S(2)}, u32[]{:S(2)}) %collective-permute-start.7) | collective-permute-done | bytes 221216 | tf_op jit(solution)/shard_map/ppermute | solution.py:268
  51.3 12.0 %shard_map.117.rest_0_ = bf16[48,2304]{1,0:T(8,128)(2,1)S(1)} custom-call(s32[1]{0:T(128)} %bitcast.index, bf16[48,1152]{1,0:T(8,128)(2,1)S(1)} %get-tuple-element.34.rest_0_, bf16[48,1152]{1,0:T(8,128)(2,1)S(1)} %collective-permute-done.6.rest_0_.rest_1_, bf16[48,1152]{1,0:T(8,128)(2,1)S(1)} %collective-permute-done.10.rest_2_, ...), custom_call_target="tpu_custom_call" | custom-call | flops 7361003520 | bytes 2654212 | tf_op jit(solution)/shard_map/pallas_call | solution.py:245
  63.3 3.2 %collective-permute-start.25 = (bf16[48,2304]{1,0:T(8,128)(2,1)S(1)}, bf16[48,2304]{1,0:T(8,128)(2,1)S(1)}, u32[]{:S(2)}, u32[]{:S(2)}) collective-permute-start(bf16[48,2304]{1,0:T(8,128)(2,1)S(1)} %shard_map.117.rest_0_), channel_id=1, source_target_pairs={{0,24},{8,16},{16,8},{24,0},{1,25},{9,17},{17,9},{25,1},{2,26},{10... | collective-permute-start | bytes 663560 | tf_op jit(solution)/shard_map/ppermute | solution.py:268
  66.5 0.4 collective-permute-start.24
  66.9 0.2 collective-permute-start.23
  67.2 1.3 %shard_map.116 = (f32[48,5376]{1,0:T(8,128)}, f32[48,1536]{1,0:T(8,128)}, f32[48,1001]{1,0:T(8,128)}) custom-call(s32[1]{0:T(128)} %bitcast.index, f32[48,5376]{1,0:T(8,128)S(1)} %bitcast.25, f32[48,1536]{1,0:T(8,128)S(1)} %bitcast.28, f32[48,1001]{1,0:T(8,128)S(1)} %bitcast.31, bf16[48,2304]{1,0:T(8,128)(2,1)S(1)} %shard_map.115.rest_0_, ...), custom_call_target="tpu_custom_call" | custom-call | bytes 3923332 | tf_op jit(solution)/shard_map/pallas_call | solution.py:245
  68.5 4.4 %collective-permute-done.25.rest_3_ = bf16[48,2304]{1,0:T(8,128)(2,1)S(1)} collective-permute-done((bf16[48,2304]{1,0:T(8,128)(2,1)S(1)}, bf16[48,2304]{1,0:T(8,128)(2,1)S(1)}, u32[]{:S(2)}, u32[]{:S(2)}) %collective-permute-start.25) | collective-permute-done | bytes 221216 | tf_op jit(solution)/shard_map/ppermute | solution.py:268
  72.9 3.5 %collective-permute-done.24.rest_2_ = bf16[48,2304]{1,0:T(8,128)(2,1)S(1)} collective-permute-done((bf16[48,2304]{1,0:T(8,128)(2,1)S(1)}, bf16[48,2304]{1,0:T(8,128)(2,1)S(1)}, u32[]{:S(2)}, u32[]{:S(2)}) %collective-permute-start.24) | collective-permute-done | bytes 221216 | tf_op jit(solution)/shard_map/ppermute | solution.py:268
  76.3 0.9 %shard_map.118 = (bf16[48,5376]{1,0:T(8,128)(2,1)}, bf16[48,1536]{1,0:T(8,128)(2,1)}, bf16[48,1001]{1,0:T(8,128)(2,1)}) custom-call(s32[1]{0:T(128)} %bitcast.index, bf16[48,2304]{1,0:T(8,128)(2,1)S(1)} %shard_map.117.rest_0_, bf16[48,2304]{1,0:T(8,128)(2,1)S(1)} %collective-permute-done.23.rest_1_, bf16[48,2304]{1,0:T(8,128)(2,1)S(1)} %collective-permute-done.24.rest_2_, ...), custom_call_target="tpu_custom_call" | custom-call | bytes 1644388 | tf_op jit(solution)/shard_map/pallas_call | solution.py:245
  (44 shorter events, 0.7 us)
Async XLA Ops:
  2.9 10.4 %collective-permute-start.3 = (bf16[48,1152]{1,0:T(8,128)(2,1)}, bf16[48,1152]{1,0:T(8,128)(2,1)S(1)}, u32[]{:S(2)}, u32[]{:S(2)}) collective-permute-start(bf16[48,1152]{1,0:T(8,128)(2,1)} %get-tuple-element.30), channel_id=1, source_target_pairs={{0,8},{8,0},{16,24},{24,16},{1,9},{9,1},{17,25},{25,17},{2,10},{10... | collective-permute-start | bytes 331784 | tf_op jit(solution)/shard_map/ppermute | solution.py:268
  5.9 11.6 %collective-permute-start.4 = (bf16[48,1152]{1,0:T(8,128)(2,1)}, bf16[48,1152]{1,0:T(8,128)(2,1)}, u32[]{:S(2)}, u32[]{:S(2)}) collective-permute-start(bf16[48,1152]{1,0:T(8,128)(2,1)} %get-tuple-element.31), channel_id=1, source_target_pairs={{0,16},{8,24},{16,0},{24,8},{1,17},{9,25},{17,1},{25,9},{2,18},{10... | collective-permute-start | bytes 331784 | tf_op jit(solution)/shard_map/ppermute | solution.py:268
  7.4 10.1 %collective-permute-start.5 = (bf16[48,1152]{1,0:T(8,128)(2,1)}, bf16[48,1152]{1,0:T(8,128)(2,1)}, u32[]{:S(2)}, u32[]{:S(2)}) collective-permute-start(bf16[48,1152]{1,0:T(8,128)(2,1)} %get-tuple-element.32), channel_id=1, source_target_pairs={{0,24},{8,16},{16,8},{24,0},{1,25},{9,17},{17,9},{25,1},{2,26},{10... | collective-permute-start | bytes 331784 | tf_op jit(solution)/shard_map/ppermute | solution.py:268
  9.7 13.1 %collective-permute-start = (bf16[48,1152]{1,0:T(8,128)(2,1)}, bf16[48,1152]{1,0:T(8,128)(2,1)S(1)}, u32[]{:S(2)}, u32[]{:S(2)}) collective-permute-start(bf16[48,1152]{1,0:T(8,128)(2,1)} %get-tuple-element.25), channel_id=1, source_target_pairs={{0,8},{8,0},{16,24},{24,16},{1,9},{9,1},{17,25},{25,17},{2,10},{10... | collective-permute-start | bytes 331784 | tf_op jit(solution)/shard_map/ppermute | solution.py:268
  11.7 11.1 %collective-permute-start.1 = (bf16[48,1152]{1,0:T(8,128)(2,1)}, bf16[48,1152]{1,0:T(8,128)(2,1)S(1)}, u32[]{:S(2)}, u32[]{:S(2)}) collective-permute-start(bf16[48,1152]{1,0:T(8,128)(2,1)} %get-tuple-element.26), channel_id=1, source_target_pairs={{0,16},{8,24},{16,0},{24,8},{1,17},{9,25},{17,1},{25,9},{2,18},{10... | collective-permute-start | bytes 331784 | tf_op jit(solution)/shard_map/ppermute | solution.py:268
  13.2 10.2 %collective-permute-start.2 = (bf16[48,1152]{1,0:T(8,128)(2,1)}, bf16[48,1152]{1,0:T(8,128)(2,1)S(1)}, u32[]{:S(2)}, u32[]{:S(2)}) collective-permute-start(bf16[48,1152]{1,0:T(8,128)(2,1)} %get-tuple-element.27), channel_id=1, source_target_pairs={{0,24},{8,16},{16,8},{24,0},{1,25},{9,17},{17,9},{25,1},{2,26},{10... | collective-permute-start | bytes 331784 | tf_op jit(solution)/shard_map/ppermute | solution.py:268
  15.3 2.2 %copy-start.4 = (f32[48,1152]{1,0:T(8,128)S(1)}, f32[48,1152]{1,0:T(8,128)}, u32[]{:S(2)}) copy-start(f32[48,1152]{1,0:T(8,128)} %shard_map.113.rest_3_) | copy-start | bytes 663556
  17.5 6.0 %copy-start.3 = (f32[48,1152]{1,0:T(8,128)S(1)}, f32[48,1152]{1,0:T(8,128)}, u32[]{:S(2)}) copy-start(f32[48,1152]{1,0:T(8,128)} %shard_map.110.rest_3_) | copy-start | bytes 663556
  17.5 6.0 %copy-start.5 = (f32[48,1152]{1,0:T(8,128)S(1)}, f32[48,1152]{1,0:T(8,128)}, u32[]{:S(2)}) copy-start(f32[48,1152]{1,0:T(8,128)} %get-tuple-element.24.own) | copy-start | bytes 663556
  18.6 6.5 %collective-permute-start.19 = (bf16[48,1152]{1,0:T(8,128)(2,1)S(1)}, bf16[48,1152]{1,0:T(8,128)(2,1)S(1)}, u32[]{:S(2)}, u32[]{:S(2)}) collective-permute-start(bf16[48,1152]{1,0:T(8,128)(2,1)S(1)} %get-tuple-element.38.rest_8_), channel_id=1, source_target_pairs={{0,1},{1,0},{2,3},{3,2},{4,5},{5,4},{6,7},{7,6},{8,9},{9,8},{10,11... | collective-permute-start | bytes 331784 | tf_op jit(solution)/shard_map/ppermute | solution.py:268
  18.7 8.1 %collective-permute-start.18 = (bf16[48,1152]{1,0:T(8,128)(2,1)S(1)}, bf16[48,1152]{1,0:T(8,128)(2,1)S(1)}, u32[]{:S(2)}, u32[]{:S(2)}) collective-permute-start(bf16[48,1152]{1,0:T(8,128)(2,1)S(1)} %get-tuple-element.38.rest_8_), channel_id=1, source_target_pairs={{0,6},{1,7},{2,4},{3,5},{4,2},{5,3},{6,0},{7,1},{8,14},{9,15},{10,... | collective-permute-start | bytes 331784 | tf_op jit(solution)/shard_map/ppermute | solution.py:268
  22.8 10.1 %collective-permute-start.17 = (bf16[48,1152]{1,0:T(8,128)(2,1)S(1)}, bf16[48,1152]{1,0:T(8,128)(2,1)S(1)}, u32[]{:S(2)}, u32[]{:S(2)}) collective-permute-start(bf16[48,1152]{1,0:T(8,128)(2,1)S(1)} %get-tuple-element.38.rest_8_), channel_id=1, source_target_pairs={{0,4},{1,5},{2,6},{3,7},{4,0},{5,1},{6,2},{7,3},{8,12},{9,13},{10,... | collective-permute-start | bytes 331784 | tf_op jit(solution)/shard_map/ppermute | solution.py:268
  22.8 10.1 %collective-permute-start.16 = (bf16[48,1152]{1,0:T(8,128)(2,1)S(1)}, bf16[48,1152]{1,0:T(8,128)(2,1)S(1)}, u32[]{:S(2)}, u32[]{:S(2)}) collective-permute-start(bf16[48,1152]{1,0:T(8,128)(2,1)S(1)} %get-tuple-element.38.rest_8_), channel_id=1, source_target_pairs={{0,2},{1,3},{2,0},{3,1},{4,6},{5,7},{6,4},{7,5},{8,10},{9,11},{10,... | collective-permute-start | bytes 331784 | tf_op jit(solution)/shard_map/ppermute | solution.py:268
  23.6 10.4 %collective-permute-start.6 = (bf16[48,1152]{1,0:T(8,128)(2,1)S(1)}, bf16[48,1152]{1,0:T(8,128)(2,1)S(1)}, u32[]{:S(2)}, u32[]{:S(2)}) collective-permute-start(bf16[48,1152]{1,0:T(8,128)(2,1)S(1)} %get-tuple-element.34.rest_0_), channel_id=1, source_target_pairs={{0,2},{1,3},{2,0},{3,1},{4,6},{5,7},{6,4},{7,5},{8,10},{9,11},{10,... | collective-permute-start | bytes 331784 | tf_op jit(solution)/shard_map/ppermute | solution.py:268
  25.1 8.9 %collective-permute-start.12 = (bf16[48,1152]{1,0:T(8,128)(2,1)S(1)}, bf16[48,1152]{1,0:T(8,128)(2,1)S(1)}, u32[]{:S(2)}, u32[]{:S(2)}) collective-permute-start(bf16[48,1152]{1,0:T(8,128)(2,1)S(1)} %get-tuple-element.34.rest_0_), channel_id=1, source_target_pairs={{0,1},{1,0},{2,3},{3,2},{4,5},{5,4},{6,7},{7,6},{8,9},{9,8},{10,11... | collective-permute-start | bytes 331784 | tf_op jit(solution)/shard_map/ppermute | solution.py:268
  26.8 9.8 %collective-permute-start.11 = (bf16[48,1152]{1,0:T(8,128)(2,1)S(1)}, bf16[48,1152]{1,0:T(8,128)(2,1)S(1)}, u32[]{:S(2)}, u32[]{:S(2)}) collective-permute-start(bf16[48,1152]{1,0:T(8,128)(2,1)S(1)} %get-tuple-element.34.rest_0_), channel_id=1, source_target_pairs={{0,6},{1,7},{2,4},{3,5},{4,2},{5,3},{6,0},{7,1},{8,14},{9,15},{10,... | collective-permute-start | bytes 331784 | tf_op jit(solution)/shard_map/ppermute | solution.py:268
  32.9 9.4 %collective-permute-start.10 = (bf16[48,1152]{1,0:T(8,128)(2,1)S(1)}, bf16[48,1152]{1,0:T(8,128)(2,1)S(1)}, u32[]{:S(2)}, u32[]{:S(2)}) collective-permute-start(bf16[48,1152]{1,0:T(8,128)(2,1)S(1)} %get-tuple-element.34.rest_0_), channel_id=1, source_target_pairs={{0,4},{1,5},{2,6},{3,7},{4,0},{5,1},{6,2},{7,3},{8,12},{9,13},{10,... | collective-permute-start | bytes 331784 | tf_op jit(solution)/shard_map/ppermute | solution.py:268
  32.9 9.4 %collective-permute-start.22 = (bf16[48,1152]{1,0:T(8,128)(2,1)S(1)}, bf16[48,1152]{1,0:T(8,128)(2,1)S(1)}, u32[]{:S(2)}, u32[]{:S(2)}) collective-permute-start(bf16[48,1152]{1,0:T(8,128)(2,1)S(1)} %collective-permute-done.18.rest_11_), channel_id=1, source_target_pairs={{0,1},{1,0},{2,3},{3,2},{4,5},{5,4},{6,7},{7,6},{8,9},{9,8},{10,11... | collective-permute-start | bytes 331784 | tf_op jit(solution)/shard_map/ppermute | solution.py:268
  33.9 9.8 %collective-permute-start.21 = (bf16[48,1152]{1,0:T(8,128)(2,1)S(1)}, bf16[48,1152]{1,0:T(8,128)(2,1)S(1)}, u32[]{:S(2)}, u32[]{:S(2)}) collective-permute-start(bf16[48,1152]{1,0:T(8,128)(2,1)S(1)} %collective-permute-done.17.rest_10_), channel_id=1, source_target_pairs={{0,1},{1,0},{2,3},{3,2},{4,5},{5,4},{6,7},{7,6},{8,9},{9,8},{10,11... | collective-permute-start | bytes 331784 | tf_op jit(solution)/shard_map/ppermute | solution.py:268
  34.0 33.2 %copy-start = (f32[1,48,5376]{2,1,0:T(8,128)S(1)}, f32[1,48,5376]{2,1,0:T(8,128)}, u32[]{:S(2)}) copy-start(f32[1,48,5376]{2,1,0:T(8,128)} %param.9) | copy-start | bytes 3096580
  34.0 33.2 %copy-start.1 = (f32[1,1536,48]{1,2,0:T(8,128)S(1)}, f32[1,1536,48]{1,2,0:T(8,128)}, u32[]{:S(2)}) copy-start(f32[1,1536,48]{1,2,0:T(8,128)} %param.10) | copy-start | bytes 884740
  34.0 33.2 %copy-start.2 = (f32[1001,48]{0,1:T(8,128)S(1)}, f32[1001,48]{0,1:T(8,128)}, u32[]{:S(2)}) copy-start(f32[1001,48]{0,1:T(8,128)} %param.11) | copy-start | bytes 576580
  34.0 12.7 %collective-permute-start.9 = (bf16[48,2304]{1,0:T(8,128)(2,1)S(1)}, bf16[48,2304]{1,0:T(8,128)(2,1)S(1)}, u32[]{:S(2)}, u32[]{:S(2)}) collective-permute-start(bf16[48,2304]{1,0:T(8,128)(2,1)S(1)} %shard_map.115.rest_0_), channel_id=1, source_target_pairs={{0,24},{8,16},{16,8},{24,0},{1,25},{9,17},{17,9},{25,1},{2,26},{10... | collective-permute-start | bytes 663560 | tf_op jit(solution)/shard_map/ppermute | solution.py:268
  36.6 8.6 %collective-permute-start.20 = (bf16[48,1152]{1,0:T(8,128)(2,1)S(1)}, bf16[48,1152]{1,0:T(8,128)(2,1)S(1)}, u32[]{:S(2)}, u32[]{:S(2)}) collective-permute-start(bf16[48,1152]{1,0:T(8,128)(2,1)S(1)} %collective-permute-done.16.rest_9_), channel_id=1, source_target_pairs={{0,1},{1,0},{2,3},{3,2},{4,5},{5,4},{6,7},{7,6},{8,9},{9,8},{10,11... | collective-permute-start | bytes 331784 | tf_op jit(solution)/shard_map/ppermute | solution.py:268
  42.2 3.0 %collective-permute-start.15 = (bf16[48,1152]{1,0:T(8,128)(2,1)S(1)}, bf16[48,1152]{1,0:T(8,128)(2,1)S(1)}, u32[]{:S(2)}, u32[]{:S(2)}) collective-permute-start(bf16[48,1152]{1,0:T(8,128)(2,1)S(1)} %collective-permute-done.11.rest_3_), channel_id=1, source_target_pairs={{0,1},{1,0},{2,3},{3,2},{4,5},{5,4},{6,7},{7,6},{8,9},{9,8},{10,11... | collective-permute-start | bytes 331784 | tf_op jit(solution)/shard_map/ppermute | solution.py:268
  42.3 7.8 %collective-permute-start.8 = (bf16[48,2304]{1,0:T(8,128)(2,1)S(1)}, bf16[48,2304]{1,0:T(8,128)(2,1)S(1)}, u32[]{:S(2)}, u32[]{:S(2)}) collective-permute-start(bf16[48,2304]{1,0:T(8,128)(2,1)S(1)} %shard_map.115.rest_0_), channel_id=1, source_target_pairs={{0,16},{8,24},{16,0},{24,8},{1,17},{9,25},{17,1},{25,9},{2,18},{10... | collective-permute-start | bytes 663560 | tf_op jit(solution)/shard_map/ppermute | solution.py:268
  43.7 7.6 %collective-permute-start.7 = (bf16[48,2304]{1,0:T(8,128)(2,1)S(1)}, bf16[48,2304]{1,0:T(8,128)(2,1)S(1)}, u32[]{:S(2)}, u32[]{:S(2)}) collective-permute-start(bf16[48,2304]{1,0:T(8,128)(2,1)S(1)} %shard_map.115.rest_0_), channel_id=1, source_target_pairs={{0,8},{8,0},{16,24},{24,16},{1,9},{9,1},{17,25},{25,17},{2,10},{10... | collective-permute-start | bytes 663560 | tf_op jit(solution)/shard_map/ppermute | solution.py:268
  45.2 1.3 %collective-permute-start.14 = (bf16[48,1152]{1,0:T(8,128)(2,1)S(1)}, bf16[48,1152]{1,0:T(8,128)(2,1)S(1)}, u32[]{:S(2)}, u32[]{:S(2)}) collective-permute-start(bf16[48,1152]{1,0:T(8,128)(2,1)S(1)} %collective-permute-done.10.rest_2_), channel_id=1, source_target_pairs={{0,1},{1,0},{2,3},{3,2},{4,5},{5,4},{6,7},{7,6},{8,9},{9,8},{10,11... | collective-permute-start | bytes 331784 | tf_op jit(solution)/shard_map/ppermute | solution.py:268
  45.2 1.5 %collective-permute-start.13 = (bf16[48,1152]{1,0:T(8,128)(2,1)S(1)}, bf16[48,1152]{1,0:T(8,128)(2,1)S(1)}, u32[]{:S(2)}, u32[]{:S(2)}) collective-permute-start(bf16[48,1152]{1,0:T(8,128)(2,1)S(1)} %collective-permute-done.6.rest_0_.rest_1_), channel_id=1, source_target_pairs={{0,1},{1,0},{2,3},{3,2},{4,5},{5,4},{6,7},{7,6},{8,9},{9,8},{10,11... | collective-permute-start | bytes 331784 | tf_op jit(solution)/shard_map/ppermute | solution.py:268
  63.3 9.6 %collective-permute-start.25 = (bf16[48,2304]{1,0:T(8,128)(2,1)S(1)}, bf16[48,2304]{1,0:T(8,128)(2,1)S(1)}, u32[]{:S(2)}, u32[]{:S(2)}) collective-permute-start(bf16[48,2304]{1,0:T(8,128)(2,1)S(1)} %shard_map.117.rest_0_), channel_id=1, source_target_pairs={{0,24},{8,16},{16,8},{24,0},{1,25},{9,17},{17,9},{25,1},{2,26},{10... | collective-permute-start | bytes 663560 | tf_op jit(solution)/shard_map/ppermute | solution.py:268
  66.5 9.8 %collective-permute-start.24 = (bf16[48,2304]{1,0:T(8,128)(2,1)S(1)}, bf16[48,2304]{1,0:T(8,128)(2,1)S(1)}, u32[]{:S(2)}, u32[]{:S(2)}) collective-permute-start(bf16[48,2304]{1,0:T(8,128)(2,1)S(1)} %shard_map.117.rest_0_), channel_id=1, source_target_pairs={{0,16},{8,24},{16,0},{24,8},{1,17},{9,25},{17,1},{25,9},{2,18},{10... | collective-permute-start | bytes 663560 | tf_op jit(solution)/shard_map/ppermute | solution.py:268
  66.9 9.4 %collective-permute-start.23 = (bf16[48,2304]{1,0:T(8,128)(2,1)S(1)}, bf16[48,2304]{1,0:T(8,128)(2,1)S(1)}, u32[]{:S(2)}, u32[]{:S(2)}) collective-permute-start(bf16[48,2304]{1,0:T(8,128)(2,1)S(1)} %shard_map.117.rest_0_), channel_id=1, source_target_pairs={{0,8},{8,0},{16,24},{24,16},{1,9},{9,1},{17,25},{25,17},{2,10},{10... | collective-permute-start | bytes 663560 | tf_op jit(solution)/shard_map/ppermute | solution.py:268
  (1 other events, 2.2 us)

commit v4 on v3

v4 whole, which is shorter than its diff:
```python
import functools
import math

import jax
import jax.numpy as jnp
from jax import lax
from jax.experimental import pallas as pl
from jax.experimental.pallas import tpu as pltpu
from jax.sharding import PartitionSpec as P

D = 384
MLP = 1536
ADA = 2304
CLASSES = 1001
NS_ITERS = 5
QKV = 1152

COEF_A = 3.4445
COEF_B = -4.775
COEF_C = 2.0315
MOMENTUM = 0.95
EPSILON = 1e-07

VMEM_LIMIT = 48 * 1024 * 1024
VMEM_ALL = 63 * 1024 * 1024

WIDTHS = [QKV, D, MLP, ADA, MLP, CLASSES]
OFFSETS = [0, QKV, QKV + D, QKV + D + MLP]
PADDED = [-(-width // 128) * 128 for width in WIDTHS]
DOWN, EMBED = 4, 5
TILE = 256


def plan(n_rep):
    bins = [[] for _ in range(n_rep)]
    loads = [0] * n_rep
    for matrix in sorted(range(6), key=lambda m: -PADDED[m]):
        owner = loads.index(min(loads))
        bins[owner].append(matrix)
        loads[owner] += PADDED[matrix]
    return bins, max(loads)


def layout(bins):
    found = []
    for owner, group in enumerate(bins):
        offset = 0
        for matrix in group:
            found.append((matrix, owner, offset))
            offset += PADDED[matrix]
    return found


def source(matrix, wide, down, embed):
    if matrix == DOWN:
        return down
    if matrix == EMBED:
        return embed
    return wide.at[:, OFFSETS[matrix] : OFFSETS[matrix] + WIDTHS[matrix]]


def split_kernel(bins, wide, down, embed, out, held, held_embed, sems):
    parts = sorted(layout(bins), key=lambda p: -WIDTHS[p[0]])
    copies = []
    for number, (matrix, owner, offset) in enumerate(parts):
        span = slice(offset, offset + WIDTHS[matrix])
        dst = held_embed if matrix == EMBED else held.at[owner, :, span]
        copies.append(pltpu.make_async_copy(source(matrix, wide, down, embed), dst, sems.at[number]))
        copies[-1].start()
    for copy, (matrix, owner, offset) in zip(copies, parts):
        copy.wait()
        span = slice(offset, offset + WIDTHS[matrix])
        if matrix == EMBED:
            value = held_embed[...]
            out[owner, :, offset : offset + PADDED[matrix]] = jnp.concatenate(
                [value, jnp.zeros((value.shape[0], PADDED[EMBED] - CLASSES), value.dtype)], axis=1
            ).astype(out.dtype)
        else:
            out[owner, :, span] = held[owner, :, span].astype(out.dtype)
    for owner, group in enumerate(bins):
        end = sum(PADDED[matrix] for matrix in group)
        if end < out.shape[2]:
            out[owner, :, end:] = jnp.zeros((out.shape[1], out.shape[2] - end), out.dtype)


def sum_kernel(bins, copies_z, index, received, wide, down, embed, g_out, y_out):
    n = received.shape[0]

    def body(group):
        offset = 0
        for matrix in group:
            span = slice(offset, offset + PADDED[matrix])
            if matrix == DOWN:
                mom = down[...]
            elif matrix == EMBED:
                mom = embed[...]
                mom = jnp.concatenate(
                    [mom, jnp.zeros((mom.shape[0], PADDED[EMBED] - CLASSES), mom.dtype)], axis=1
                )
            else:
                mom = wide[:, OFFSETS[matrix] : OFFSETS[matrix] + WIDTHS[matrix]]
            g = received[0, :, span].astype(jnp.float32)
            for number in range(1, n):
                g = g + received[number, :, span].astype(jnp.float32)
            y = (g + MOMENTUM * (MOMENTUM * mom + g)).astype(jnp.bfloat16)
            g = g.astype(jnp.bfloat16)
            for number in range(n):
                g_out[number, :, span] = g
            for number in range(copies_z):
                y_out[number, :, span] = y
            offset += PADDED[matrix]
        if offset < g_out.shape[2]:
            zeros = jnp.zeros((g_out.shape[1], g_out.shape[2] - offset), jnp.bfloat16)
            for number in range(n):
                g_out[number, :, offset:] = zeros
            for number in range(copies_z):
                y_out[number, :, offset:] = zeros

    for target, group in enumerate(bins):

        @pl.when(index[0] == target)
        def _():
            body(group)


def newton_kernel(bins, copies, index, same, other, *rest):
    out, x_ref, poly_ref = rest[-3:]
    half, rows = D // 2, out.shape[1]
    x_ref[:half, :] = same[...]
    x_ref[half:, :] = other[...]
    mine = pl.ds(0, D) if rows == D else pl.ds(pl.multiple_of(index[1] * rows, rows), rows)

    def branch(group):
        spans = []
        offset = 0
        for matrix in group:
            end = offset + PADDED[matrix]
            tiles = [slice(low, min(low + TILE, end)) for low in range(offset, end, TILE)]
            spans.append((slice(offset, end), tiles, math.sqrt(max(D, WIDTHS[matrix]))))
            offset = end

        def outer(span):
            x = x_ref[:, span]
            return lax.dot_general(x, x, (((1,), (1,)), ((), ())), preferred_element_type=jnp.float32)

        def polynomial(gram):
            gram = gram.astype(jnp.bfloat16)
            square = jnp.dot(gram, gram, preferred_element_type=jnp.float32)
            return COEF_B * gram.astype(jnp.float32) + COEF_C * square

        def advance(tiles, poly, factor):
            for tile in tiles:
                x = x_ref[:, tile]
                x_ref[:, tile] = (
                    factor * x.astype(jnp.float32) + jnp.dot(poly, x, preferred_element_type=jnp.float32)
                ).astype(jnp.bfloat16)

        diagonal = lax.broadcasted_iota(jnp.int32, (D, D), 0) == lax.broadcasted_iota(jnp.int32, (D, D), 1)
        for span, tiles, _ in spans:
            gram = outer(span)
            scale = 1.0 / (jnp.sqrt(jnp.sum(jnp.where(diagonal, gram, 0.0))) + EPSILON)
            poly = (scale * polynomial(gram * scale * scale)).astype(jnp.bfloat16)
            advance(tiles, poly, COEF_A * scale)

        def step(_, carry):
            polys = [polynomial(outer(span)).astype(jnp.bfloat16) for span, _, _ in spans]
            for poly, (_, tiles, _) in zip(polys, spans):
                advance(tiles, poly, COEF_A)
            return carry

        lax.fori_loop(0, NS_ITERS - 2, step, 0)
        for span, tiles, factor in spans:
            poly_ref[...] = polynomial(outer(span)).astype(jnp.bfloat16)
            poly = poly_ref[mine, :]
            for tile in tiles:
                value = (
                    factor
                    * (
                        COEF_A * x_ref[mine, tile].astype(jnp.float32)
                        + jnp.dot(poly, x_ref[:, tile], preferred_element_type=jnp.float32)
                    )
                ).astype(jnp.bfloat16)
                for number in range(copies):
                    out[number, :, tile] = value

    for target, group in enumerate(bins):
        if group:

            @pl.when(index[0] == target)
            def _():
                branch(group)


def momentum_kernel(bins, gathered, wide, down, embed, new_wide, new_down, new_embed):
    for matrix, owner, offset in layout(bins):
        g = gathered[owner, :, offset : offset + PADDED[matrix]].astype(jnp.float32)
        if matrix == DOWN:
            new_down[...] = MOMENTUM * down[...] + g
        elif matrix == EMBED:
            new_embed[...] = MOMENTUM * embed[...] + g[:, :CLASSES]
        else:
            span = slice(OFFSETS[matrix], OFFSETS[matrix] + WIDTHS[matrix])
            new_wide[:, span] = MOMENTUM * wide[:, span] + g


def update_kernel(bins, gathered, upd_wide, upd_down, upd_embed):
    for matrix, owner, offset in layout(bins):
        value = gathered[owner, :, offset : offset + PADDED[matrix]]
        if matrix == DOWN:
            upd_down[...] = value
        elif matrix == EMBED:
            upd_embed[...] = value[:, :CLASSES]
        else:
            upd_wide[:, OFFSETS[matrix] : OFFSETS[matrix] + WIDTHS[matrix]] = value


VMEM = pl.BlockSpec(memory_space=pltpu.VMEM)
SMEM = pl.BlockSpec(memory_space=pltpu.SMEM)
ANY = pl.BlockSpec(memory_space=pl.ANY)


def call(kernel, outs, args, specs, scratch=(), flops=0, limit=VMEM_LIMIT):
    size = sum(a.size * a.dtype.itemsize for a in args) + sum(
        math.prod(o.shape) * o.dtype.itemsize for o in outs
    )
    return pl.pallas_call(
        kernel,
        out_shape=tuple(outs),
        in_specs=specs,
        out_specs=tuple([VMEM] * len(outs)),
        scratch_shapes=list(scratch),
        compiler_params=pltpu.CompilerParams(vmem_limit_bytes=limit),
        cost_estimate=pl.CostEstimate(flops=flops, bytes_accessed=size, transcendentals=0),
    )(*args)


def exchange(value, axis, groups=None):
    return lax.all_to_all(value, axis, 0, 0, axis_index_groups=groups)


def per_device(grad_wide, grad_down, grad_embed, mom_wide, mom_down, mom_embed):
    n_rep, n_shard = lax.axis_size("rep"), lax.axis_size("shard")
    chips = n_shard // 2
    bins, width = plan(n_rep)
    index = jnp.stack([lax.axis_index("rep"), lax.axis_index("shard") // 2]).astype(jnp.int32)
    grads = (grad_wide[0, 0], grad_down[0, 0].T, grad_embed[0].T)
    moms = (mom_wide[0], mom_down[0].T, mom_embed.T)
    rows = grads[0].shape[0]

    def stacked(count):
        return jax.ShapeDtypeStruct((count, rows, width), jnp.bfloat16)

    (sends,) = call(
        functools.partial(split_kernel, bins),
        [stacked(n_rep)],
        grads,
        [ANY] * 3,
        (
            pltpu.VMEM((n_rep, rows, width), jnp.float32),
            pltpu.VMEM((rows, CLASSES), jnp.float32),
            pltpu.SemaphoreType.DMA((6,)),
        ),
        limit=VMEM_ALL,
    )
    g, y = call(
        functools.partial(sum_kernel, bins, chips),
        [stacked(n_rep), stacked(chips)],
        (index, exchange(sends, "rep"), *moms),
        [SMEM] + [VMEM] * 4,
    )
    groups = [[2 * chip + core for chip in range(chips)] for core in range(2)]
    same = exchange(y, "shard", groups).reshape(chips * rows, width)
    other = lax.ppermute(same, "shard", [(i, i ^ 1) for i in range(n_shard)])
    g_all = exchange(g, "rep")
    aligned = rows % 16 == 0
    (upd,) = call(
        functools.partial(newton_kernel, bins, n_rep if aligned else 1),
        [stacked(n_rep) if aligned else jax.ShapeDtypeStruct((1, D, width), jnp.bfloat16)],
        (index, same, other, g_all),
        [SMEM, VMEM, VMEM, ANY],
        (pltpu.VMEM((D, width), jnp.bfloat16), pltpu.VMEM((D, D), jnp.bfloat16)),
        flops=NS_ITERS * (4 * D * D * width + 2 * D * D * D),
    )
    if not aligned:
        upd = lax.dynamic_slice_in_dim(upd, index[1] * rows, rows, 1)
        upd = jnp.broadcast_to(upd, (n_rep, rows, width))
    upd_all = exchange(upd, "rep")
    news = call(
        functools.partial(momentum_kernel, bins),
        [jax.ShapeDtypeStruct(m.shape, jnp.float32) for m in moms],
        (g_all, *moms),
        [VMEM] * 4,
    )
    updates = call(
        functools.partial(update_kernel, bins),
        [jax.ShapeDtypeStruct(m.shape, jnp.bfloat16) for m in moms],
        (upd_all,),
        [VMEM],
    )
    return (
        news[0][None],
        news[1].T[None],
        news[2].T,
        updates[0][None],
        updates[1].T[None],
        updates[2].T,
    )


def solution(mesh):
    placed_in = (
        P("rep", None, "shard", None),
        P("rep", None, None, "shard"),
        P("rep", None, "shard"),
        P(None, "shard", None),
        P(None, None, "shard"),
        P(None, "shard"),
    )
    return jax.shard_map(
        per_device,
        mesh=mesh,
        in_specs=placed_in,
        out_specs=placed_in[3:] + placed_in[3:],
        check_vma=False,
    )
```

time: 77.5 us -> 93.1 us (1.20)
  blocking collectives: 0 us -> 41.9 us
  starting transfers between devices: 28.4 us -> 9.22 us
  Pallas kernels: 24.1 us -> 17.6 us
  waiting for transfers between devices: 23.9 us -> 22.3 us
    all_to_all x0 -> x2, blocking collectives: none -> 41.9 us  [exchange(): return lax.all_to_all(value, axis, 0, 0, axis_index_groups=groups)]
    ppermute x26 -> x1, starting transfers between devices: 28.4 us -> 0.01 us  [per_device(): other = lax.ppermute(same, 'shard', [(i, i ^ 1) for i in range(n_shard)])]
    ppermute x26 -> x1, waiting for transfers between devices: 23.9 us -> 0.01 us  [per_device(): other = lax.ppermute(same, 'shard', [(i, i ^ 1) for i in range(n_shard)])]
    all_to_all x0 -> x2, waiting for transfers between devices: none -> 22.3 us  [exchange(): return lax.all_to_all(value, axis, 0, 0, axis_index_groups=groups)]
    all_to_all x0 -> x2, starting transfers between devices: none -> 9.22 us  [exchange(): return lax.all_to_all(value, axis, 0, 0, axis_index_groups=groups)]
    pallas_call x10 -> x5, Pallas kernels: 24.1 us -> 17.6 us  [call(): pl.pallas_call(kernel, out_shape=tuple(outs), in_specs=specs, out_specs=t...]
  transfers between devices with their start and end apart: 26 -> 3, of which waited for: 10 -> 2; matrix products, arithmetic and copies ran while one was open for 0% -> 0% of each run, Pallas kernels for 12% -> 1%
where the time goes in v4:
time: 93.1 us; the launch traced here: 92.7 us
  blocking collectives  41.9 us (45%)
  waiting for transfers between devices  22.3 us (24%)
  Pallas kernels  17.6 us (19%)
  starting transfers between devices  9.22 us (10%)
  local copies, waits for them, and re-layouts  0.94 us (1%)
    all_to_all x2, blocking collectives, exchange(): return lax.all_to_all(value, axis, 0, 0, axis_index_groups=groups)  41.9 us
    all_to_all x2, waiting for transfers between devices, exchange(): return lax.all_to_all(value, axis, 0, 0, axis_index_groups=groups)  22.3 us
    pallas_call x5, Pallas kernels, call(): pl.pallas_call(kernel, out_shape=tuple(outs), in_specs=specs, out_specs=t...  17.6 us
    all_to_all x2, starting transfers between devices, exchange(): return lax.all_to_all(value, axis, 0, 0, axis_index_groups=groups)  9.22 us
  transfers between devices with their start and end apart: 3, of which 2 were waited for; matrix products, arithmetic and copies ran while one was open for 0% of the time, Pallas kernels for 1%

profile of v4, /device:TPU:0, one launch (start us, length us, event | category | flops | bytes accessed | tf_op | source)
XLA Modules:
  0.0 92.7 jit_solution(3781395597341634184)
XLA Ops:
  0.6 2.3 %shard_map.109 = bf16[4,48,2304]{2,1,0:T(8,128)(2,1)} custom-call(f32[48,5376]{1,0:T(8,128)} %bitcast.33, f32[48,1536]{1,0:T(8,128)} %bitcast.34, f32[48,1001]{1,0:T(8,128)} %bitcast.35), custom_call_target="tpu_custom_call" | custom-call | bytes 2404032 | tf_op jit(solution)/shard_map/pallas_call | solution.py:226
  2.9 0.0 copy-start
  2.9 0.0 copy-start.1
  3.0 0.0 copy-start.3
  3.0 5.3 %all-to-all-start = ((bf16[4,48,2304]{2,1,0:T(8,128)(2,1)}), bf16[4,48,2304]{2,1,0:T(8,128)(2,1)S(1)}, u32[]{:S(2)}, u32[]{:S(2)}) async-start(bf16[4,48,2304]{2,1,0:T(8,128)(2,1)} %shard_map.109), calls=%async_computation | async-start | bytes 1769472 | tf_op jit(solution)/shard_map/all_to_all | solution.py:238
  8.3 0.1 pad_add_fusion.index
  8.4 11.8 %all-to-all-done.received = bf16[4,48,2304]{2,1,0:T(8,128)(2,1)S(1)} async-done(((bf16[4,48,2304]{2,1,0:T(8,128)(2,1)}), bf16[4,48,2304]{2,1,0:T(8,128)(2,1)S(1)}, u32[]{:S(2)}, u32[]{:S(2)}) %all-to-all-start) | async-done | bytes 884768 | tf_op jit(solution)/shard_map/all_to_all | solution.py:238
  20.2 0.0 copy-done
  20.2 0.0 copy-done.1
  20.2 0.0 copy-done.3
  20.2 0.8 shard_map.110
  20.9 26.1 %all_to_all.20 = bf16[4,48,2304]{2,1,0:T(8,128)(2,1)S(1)} all-to-all(bf16[4,48,2304]{2,1,0:T(8,128)(2,1)S(1)} %get-tuple-element.18), channel_id=1, replica_groups={{0,2,4,6},{1,3,5,7},{8,10,12,14},{9,11,13,15},{16,18,20,22},{17,19,21,2..., dimensions={0} | all-to-all | bytes 1769472 | tf_op jit(solution)/shard_map/all_to_all | solution.py:238
  47.0 0.0 collective-permute-start
  47.0 15.8 %all_to_all.21.gathered.rest_0_ = bf16[4,48,2304]{2,1,0:T(8,128)(2,1)S(1)} all-to-all(bf16[4,48,2304]{2,1,0:T(8,128)(2,1)S(1)} %get-tuple-element.14), channel_id=1, replica_groups=mesh['rep'=4,'shard'=8] {'rep'}, dimensions={0} | all-to-all | bytes 1769472 | tf_op jit(solution)/shard_map/all_to_all | solution.py:238
  62.9 0.0 collective-permute-done.other
  62.9 12.4 %shard_map.112 = bf16[4,48,2304]{2,1,0:T(8,128)(2,1)S(1)} custom-call(s32[2]{0:T(128)S(1)} %pad_add_fusion.index, bf16[192,2304]{1,0:T(8,128)(2,1)S(1)} %bitcast.30, bf16[192,2304]{1,0:T(8,128)(2,1)S(1)} %collective-permute-done.other, bf16[4,48,2304]{2,1,0:T(8,128)(2,1)S(1)} %all_to_all.21.gathered.rest_0_), custom_call_target="tpu_custom_call" | custom-call | flops 7361003520 | bytes 3538952 | tf_op jit(solution)/shard_map/pallas_call | solution.py:226
  75.3 0.0 copy-start.2
  75.3 0.9 copy-done.2
  76.2 3.9 %all-to-all-start.3 = ((bf16[4,48,2304]{2,1,0:T(8,128)(2,1)}), bf16[4,48,2304]{2,1,0:T(8,128)(2,1)S(1)}, u32[]{:S(2)}, u32[]{:S(2)}) async-start(bf16[4,48,2304]{2,1,0:T(8,128)(2,1)} %copy-done.2), calls=%async_computation.3 | async-start | bytes 1769472 | tf_op jit(solution)/shard_map/all_to_all | solution.py:238
  80.1 1.2 %shard_map.111 = (f32[48,5376]{1,0:T(8,128)}, f32[48,1536]{1,0:T(8,128)}, f32[48,1001]{1,0:T(8,128)}) custom-call(bf16[4,48,2304]{2,1,0:T(8,128)(2,1)S(1)} %all_to_all.21.gathered.rest_0_, f32[48,5376]{1,0:T(8,128)S(1)} %bitcast.26, f32[48,1536]{1,0:T(8,128)S(1)} %bitcast.28, f32[48,1001]{1,0:T(8,128)S(1)} %bitcast.32), custom_call_target="tpu_custom_call" | custom-call | bytes 3923328 | tf_op jit(solution)/shard_map/pallas_call | solution.py:226
  81.3 10.5 %all-to-all-done.3.gathered = bf16[4,48,2304]{2,1,0:T(8,128)(2,1)S(1)} async-done(((bf16[4,48,2304]{2,1,0:T(8,128)(2,1)}), bf16[4,48,2304]{2,1,0:T(8,128)(2,1)S(1)}, u32[]{:S(2)}, u32[]{:S(2)}) %all-to-all-start.3) | async-done | bytes 884768 | tf_op jit(solution)/shard_map/all_to_all | solution.py:238
  91.8 0.9 shard_map.113
Async XLA Ops:
  2.9 17.2 %copy-start = (f32[1,48,5376]{2,1,0:T(8,128)S(1)}, f32[1,48,5376]{2,1,0:T(8,128)}, u32[]{:S(2)}) copy-start(f32[1,48,5376]{2,1,0:T(8,128)} %param.9) | copy-start | bytes 3096580
  2.9 17.2 %copy-start.1 = (f32[1,1536,48]{1,2,0:T(8,128)S(1)}, f32[1,1536,48]{1,2,0:T(8,128)}, u32[]{:S(2)}) copy-start(f32[1,1536,48]{1,2,0:T(8,128)} %param.10) | copy-start | bytes 884740
  3.0 17.2 %copy-start.3 = (f32[1001,48]{0,1:T(8,128)S(1)}, f32[1001,48]{0,1:T(8,128)}, u32[]{:S(2)}) copy-start(f32[1001,48]{0,1:T(8,128)} %param.11) | copy-start | bytes 576580
  3.0 17.2 %all-to-all-start = ((bf16[4,48,2304]{2,1,0:T(8,128)(2,1)}), bf16[4,48,2304]{2,1,0:T(8,128)(2,1)S(1)}, u32[]{:S(2)}, u32[]{:S(2)}) async-start(bf16[4,48,2304]{2,1,0:T(8,128)(2,1)} %shard_map.109), calls=%async_computation | async-start | bytes 1769472 | tf_op jit(solution)/shard_map/all_to_all | solution.py:238
  47.0 15.8 %collective-permute-start = (bf16[192,2304]{1,0:T(8,128)(2,1)S(1)}, bf16[192,2304]{1,0:T(8,128)(2,1)S(1)}, u32[]{:S(2)}, u32[]{:S(2)}) collective-permute-start(bf16[192,2304]{1,0:T(8,128)(2,1)S(1)} %bitcast.29), channel_id=1, source_target_pairs={{0,1},{1,0},{2,3},{3,2},{4,5},{5,4},{6,7},{7,6},{8,9},{9,8},{10,11... | collective-permute-start | bytes 2654216 | tf_op jit(solution)/shard_map/ppermute | solution.py:273
  75.3 0.9 %copy-start.2 = (bf16[4,48,2304]{2,1,0:T(8,128)(2,1)}, bf16[4,48,2304]{2,1,0:T(8,128)(2,1)S(1)}, u32[]{:S(2)}) copy-start(bf16[4,48,2304]{2,1,0:T(8,128)(2,1)S(1)} %shard_map.112) | copy-start | bytes 2654212
  76.2 15.6 %all-to-all-start.3 = ((bf16[4,48,2304]{2,1,0:T(8,128)(2,1)}), bf16[4,48,2304]{2,1,0:T(8,128)(2,1)S(1)}, u32[]{:S(2)}, u32[]{:S(2)}) async-start(bf16[4,48,2304]{2,1,0:T(8,128)(2,1)} %copy-done.2), calls=%async_computation.3 | async-start | bytes 1769472 | tf_op jit(solution)/shard_map/all_to_all | solution.py:238

commit v5 on v3

v5 whole, which is shorter than its diff:
```python
import functools
import math

import jax
import jax.numpy as jnp
from jax import lax
from jax.experimental import pallas as pl
from jax.experimental.pallas import tpu as pltpu
from jax.sharding import PartitionSpec as P

D = 384
MLP = 1536
ADA = 2304
CLASSES = 1001
NS_ITERS = 5
QKV = 1152

COEF_A = 3.4445
COEF_B = -4.775
COEF_C = 2.0315
MOMENTUM = 0.95
EPSILON = 1e-07

VMEM_LIMIT = 48 * 1024 * 1024
VMEM_ALL = 63 * 1024 * 1024

WIDTHS = [QKV, D, MLP, ADA, MLP, CLASSES]
OFFSETS = [0, QKV, QKV + D, QKV + D + MLP]
PADDED = [-(-width // 128) * 128 for width in WIDTHS]
DOWN, EMBED = 4, 5
TILE = 256


def plan(n_rep):
    bins = [[] for _ in range(n_rep)]
    loads = [0] * n_rep
    for matrix in sorted(range(6), key=lambda m: -PADDED[m]):
        owner = loads.index(min(loads))
        bins[owner].append(matrix)
        loads[owner] += PADDED[matrix]
    return bins, max(loads)


def window(group, low, high):
    found = []
    offset = 0
    for matrix in group:
        first, last = max(low - offset, 0), min(high - offset, PADDED[matrix])
        if first < last:
            found.append((matrix, first, offset + first - low, last - first))
        offset += PADDED[matrix]
    return found


def columns(matrix, first, width, wide, down, embed):
    if matrix == DOWN:
        return down[:, first : first + width]
    if matrix == EMBED:
        last = min(first + width, CLASSES)
        value = embed[:, first:last]
        if last < first + width:
            tail = jnp.zeros((value.shape[0], first + width - last), value.dtype)
            value = jnp.concatenate([value, tail], axis=1)
        return value
    return wide[:, OFFSETS[matrix] + first : OFFSETS[matrix] + first + width]


def split_kernel(bins, windows, index, wide, down, embed, *rest):
    n = len(bins)
    outs, held, sems = rest[: len(windows) * n], rest[-4:-1], rest[-1]
    copies = [pltpu.make_async_copy(src, dst, sems.at[i]) for i, (src, dst) in enumerate(zip((wide, down, embed), held))]
    for copy in copies:
        copy.start()
    for copy in copies:
        copy.wait()
    for half, (low, high) in enumerate(windows):
        for k in range(n):
            dst = outs[half * n + k]
            for target, group in enumerate(bins):

                @pl.when((index[0] ^ k) == target)
                def _():
                    end = 0
                    for matrix, first, place, width in window(group, low, high):
                        dst[:, place : place + width] = columns(matrix, first, width, *held).astype(dst.dtype)
                        end = place + width
                    if end < high - low:
                        dst[:, end:] = jnp.zeros((dst.shape[0], high - low - end), dst.dtype)


def own_kernel(bins, index, wide, down, embed, out):
    for target, group in enumerate(bins):

        @pl.when(index[0] == target)
        def _():
            end = 0
            for matrix, first, place, width in window(group, 0, out.shape[1]):
                out[:, place : place + width] = columns(matrix, first, width, wide, down, embed)
                end = place + width
            if end < out.shape[1]:
                out[:, end:] = jnp.zeros((out.shape[0], out.shape[1] - end), out.dtype)


def sum_kernel(count, mom, *rest):
    received, g_out, y_out = rest[:count], rest[count], rest[count + 1]
    g = received[0][...].astype(jnp.float32)
    for piece in received[1:]:
        g = g + piece[...].astype(jnp.float32)
    g_out[...] = g.astype(jnp.bfloat16)
    y_out[...] = (g + MOMENTUM * (MOMENTUM * mom[...] + g)).astype(jnp.bfloat16)


def stack_kernel(count, *rest):
    out, rows = rest[-1], rest[0].shape[0]
    for number in range(count):
        out[number * rows : (number + 1) * rows, :] = rest[number][...]


def newton_kernel(bins, count, rows, index, *rest):
    pieces, out, x_ref = rest[:count], rest[-2], rest[-1]
    start = 0
    for piece in pieces:
        x_ref[start : start + piece.shape[0], :] = piece[...]
        start += piece.shape[0]

    def branch(group):
        spans = []
        offset = 0
        for matrix in group:
            end = offset + PADDED[matrix]
            tiles = [slice(low, min(low + TILE, end)) for low in range(offset, end, TILE)]
            spans.append((slice(offset, end), tiles, math.sqrt(max(D, WIDTHS[matrix]))))
            offset = end

        def outer(span):
            x = x_ref[:, span]
            return lax.dot_general(x, x, (((1,), (1,)), ((), ())), preferred_element_type=jnp.float32)

        def polynomial(gram):
            gram = gram.astype(jnp.bfloat16)
            square = jnp.dot(gram, gram, preferred_element_type=jnp.float32)
            return COEF_B * gram.astype(jnp.float32) + COEF_C * square

        def advance(tiles, poly, factor):
            for tile in tiles:
                x = x_ref[:, tile]
                x_ref[:, tile] = (
                    factor * x.astype(jnp.float32) + jnp.dot(poly, x, preferred_element_type=jnp.float32)
                ).astype(jnp.bfloat16)

        diagonal = lax.broadcasted_iota(jnp.int32, (D, D), 0) == lax.broadcasted_iota(jnp.int32, (D, D), 1)
        for span, tiles, _ in spans:
            gram = outer(span)
            scale = 1.0 / (jnp.sqrt(jnp.sum(jnp.where(diagonal, gram, 0.0))) + EPSILON)
            poly = (scale * polynomial(gram * scale * scale)).astype(jnp.bfloat16)
            advance(tiles, poly, COEF_A * scale)

        def step(_, carry):
            polys = [polynomial(outer(span)).astype(jnp.bfloat16) for span, _, _ in spans]
            for poly, (_, tiles, _) in zip(polys, spans):
                advance(tiles, poly, COEF_A)
            return carry

        lax.fori_loop(0, NS_ITERS - 2, step, 0)
        for span, tiles, factor in spans:
            poly = polynomial(outer(span))[:rows].astype(jnp.bfloat16)
            for tile in tiles:
                x = x_ref[:, tile]
                out[:, tile] = (
                    factor
                    * (COEF_A * x[:rows].astype(jnp.float32) + jnp.dot(poly, x, preferred_element_type=jnp.float32))
                ).astype(jnp.bfloat16)

    for target, group in enumerate(bins):
        if group:

            @pl.when(index[0] == target)
            def _():
                branch(group)


def placed(bins):
    where = {}
    for owner, group in enumerate(bins):
        offset = 0
        for matrix in group:
            where[matrix] = (owner, offset)
            offset += PADDED[matrix]
    return where


def per_index(bins, index, body):
    for mine in range(len(bins)):

        @pl.when(index[0] == mine)
        def _():
            body(mine)


def momentum_kernel(bins, index, wide, down, embed, *rest):
    n = len(bins)
    pieces, (new_wide, new_down, new_embed) = rest[:n], rest[n:]
    where = placed(bins)

    def body(mine):
        for matrix in range(6):
            owner, offset = where[matrix]
            g = pieces[mine ^ owner][:, offset : offset + PADDED[matrix]].astype(jnp.float32)
            if matrix == DOWN:
                new_down[...] = MOMENTUM * down[...] + g
            elif matrix == EMBED:
                new_embed[...] = MOMENTUM * embed[...] + g[:, :CLASSES]
            else:
                span = slice(OFFSETS[matrix], OFFSETS[matrix] + WIDTHS[matrix])
                new_wide[:, span] = MOMENTUM * wide[:, span] + g

    per_index(bins, index, body)


def update_kernel(bins, index, *rest):
    n = len(bins)
    pieces, (upd_wide, upd_down, upd_embed) = rest[:n], rest[n:]
    where = placed(bins)

    def body(mine):
        for matrix in range(6):
            owner, offset = where[matrix]
            value = pieces[mine ^ owner][:, offset : offset + PADDED[matrix]]
            if matrix == DOWN:
                upd_down[...] = value
            elif matrix == EMBED:
                upd_embed[...] = value[:, :CLASSES]
            else:
                upd_wide[:, OFFSETS[matrix] : OFFSETS[matrix] + WIDTHS[matrix]] = value

    per_index(bins, index, body)


VMEM = pl.BlockSpec(memory_space=pltpu.VMEM)
SMEM = pl.BlockSpec(memory_space=pltpu.SMEM)
ANY = pl.BlockSpec(memory_space=pl.ANY)


def call(kernel, outs, args, specs, scratch=(), flops=0, limit=VMEM_LIMIT):
    size = sum(a.size * a.dtype.itemsize for a in args) + sum(
        math.prod(o.shape) * o.dtype.itemsize for o in outs
    )
    return pl.pallas_call(
        kernel,
        out_shape=tuple(outs),
        in_specs=specs,
        out_specs=tuple([VMEM] * len(outs)),
        scratch_shapes=list(scratch),
        compiler_params=pltpu.CompilerParams(vmem_limit_bytes=limit),
        cost_estimate=pl.CostEstimate(flops=flops, bytes_accessed=size, transcendentals=0),
    )(*args)


def swap(value, axis, k, n):
    return lax.ppermute(value, axis, [(i, i ^ k) for i in range(n)])


def spread(value, axis, n):
    return [swap(value, axis, k, n) for k in range(1, n)]


def gather_rows(value, n):
    pieces = [value] + [swap(value, "shard", k, n) for k in range(2, n, 2)]
    rows, width = value.shape
    if rows % 16:
        pieces = [jnp.concatenate(pieces, axis=0)]
        return [jnp.concatenate(pieces + [swap(pieces[0], "shard", 1, n)], axis=0)]
    return pieces + [swap(piece, "shard", 1, n) for piece in pieces]


def per_device(grad_wide, grad_down, grad_embed, mom_wide, mom_down, mom_embed):
    n_rep, n_shard = lax.axis_size("rep"), lax.axis_size("shard")
    bins, width = plan(n_rep)
    index = lax.axis_index("rep").astype(jnp.int32).reshape(1)
    grads = (grad_wide[0, 0], grad_down[0, 0].T, grad_embed[0].T)
    moms = (mom_wide[0], mom_down[0].T, mom_embed.T)
    rows = grads[0].shape[0]
    whole = jax.ShapeDtypeStruct((rows, width), jnp.bfloat16)

    own, *sends = call(
        functools.partial(split_kernel, bins, [(0, width)]),
        [whole] * n_rep,
        (index, *grads),
        [SMEM] + [ANY] * 3,
        [pltpu.VMEM(array.shape, jnp.float32) for array in grads] + [pltpu.SemaphoreType.DMA((3,))],
        limit=VMEM_ALL,
    )
    received = [own] + [swap(piece, "rep", k + 1, n_rep) for k, piece in enumerate(sends)]
    (mom_own,) = call(
        functools.partial(own_kernel, bins),
        [jax.ShapeDtypeStruct((rows, width), jnp.float32)],
        (index, *moms),
        [SMEM] + [VMEM] * 3,
    )
    g, y = call(functools.partial(sum_kernel, n_rep), [whole] * 2, (mom_own, *received), [VMEM] * (n_rep + 1))
    pieces = gather_rows(y, n_shard)
    g_others = spread(g, "rep", n_rep)
    tied = g_others[: n_rep // 2]
    (upd,) = call(
        functools.partial(newton_kernel, bins, len(pieces), rows),
        [whole],
        (index, *pieces, *tied),
        [SMEM] + [VMEM] * len(pieces) + [ANY] * len(tied),
        (pltpu.VMEM((D, width), jnp.bfloat16),),
        flops=NS_ITERS * (4 * D * D * width + 2 * D * D * D),
    )
    upd_others = spread(upd, "rep", n_rep)
    news = call(
        functools.partial(momentum_kernel, bins),
        [jax.ShapeDtypeStruct(m.shape, jnp.float32) for m in moms],
        (index, *moms, g, *g_others),
        [SMEM] + [VMEM] * (3 + n_rep),
    )
    updates = call(
        functools.partial(update_kernel, bins),
        [jax.ShapeDtypeStruct(m.shape, jnp.bfloat16) for m in moms],
        (index, upd, *upd_others),
        [SMEM] + [VMEM] * n_rep,
    )
    return (
        news[0][None],
        news[1].T[None],
        news[2].T,
        updates[0][None],
        updates[1].T[None],
        updates[2].T,
    )


def solution(mesh):
    placed_in = (
        P("rep", None, "shard", None),
        P("rep", None, None, "shard"),
        P("rep", None, "shard"),
        P(None, "shard", None),
        P(None, None, "shard"),
        P(None, "shard"),
    )
    return jax.shard_map(
        per_device,
        mesh=mesh,
        in_specs=placed_in,
        out_specs=placed_in[3:] + placed_in[3:],
        check_vma=False,
    )
```

time: 77.5 us -> 69.2 us (0.89)
  starting transfers between devices: 28.4 us -> 17.6 us
  waiting for transfers between devices: 23.9 us -> 32.7 us
  Pallas kernels: 24.1 us -> 16.7 us
  local copies, waits for them, and re-layouts: 0.04 us -> 1.24 us
    ppermute x26 -> x16, starting transfers between devices: 28.4 us -> 17.6 us  [swap(): return lax.ppermute(value, axis, [(i, i ^ k) for i in range(n)])]
    ppermute x26 -> x16, waiting for transfers between devices: 23.9 us -> 32.7 us  [swap(): return lax.ppermute(value, axis, [(i, i ^ k) for i in range(n)])]
    pallas_call x10 -> x6, Pallas kernels: 24.1 us -> 16.7 us  [call(): pl.pallas_call(kernel, out_shape=tuple(outs), in_specs=specs, out_specs=t...]
    unnamed x14 -> x10, local copies, waits for them, and re-layouts: 0.04 us -> 1.24 us
  transfers between devices with their start and end apart: 26 -> 16, of which waited for: 10 -> 6; matrix products, arithmetic and copies ran while one was open for 0% -> 0% of each run, Pallas kernels for 12% -> 19%
where the time goes in v5:
time: 69.2 us; the launch traced here: 69 us
  waiting for transfers between devices  32.7 us (47%)
  starting transfers between devices  17.6 us (25%)
  Pallas kernels  16.7 us (24%)
  local copies, waits for them, and re-layouts  1.24 us (2%)
  between operations  0.71 us (1%)
    ppermute x16, waiting for transfers between devices, swap(): return lax.ppermute(value, axis, [(i, i ^ k) for i in range(n)])  32.7 us
    ppermute x16, starting transfers between devices, swap(): return lax.ppermute(value, axis, [(i, i ^ k) for i in range(n)])  17.6 us
    pallas_call x6, Pallas kernels, call(): pl.pallas_call(kernel, out_shape=tuple(outs), in_specs=specs, out_specs=t...  16.7 us
  transfers between devices with their start and end apart: 16, of which 6 were waited for; matrix products, arithmetic and copies ran while one was open for 0% of the time, Pallas kernels for 19%

profile of v5, /device:TPU:0, one launch (start us, length us, event | category | flops | bytes accessed | tf_op | source)
XLA Modules:
  0.0 69.0 jit_solution(8418837035337878136)
XLA Ops:
  0.7 2.5 %shard_map.110 = (bf16[48,2304]{1,0:T(8,128)(2,1)}, bf16[48,2304]{1,0:T(8,128)(2,1)}, bf16[48,2304]{1,0:T(8,128)(2,1)}, bf16[48,2304]{1,0:T(8,128)(2,1)}) custom-call(s32[1]{0:T(128)} %bitcast.index, f32[48,5376]{1,0:T(8,128)} %bitcast.29, f32[48,1536]{1,0:T(8,128)} %bitcast.30, f32[48,1001]{1,0:T(8,128)} %bitcast.31), custom_call_target="tpu_custom_call" | custom-call | bytes 2404036 | tf_op jit(solution)/shard_map/pallas_call | solution.py:248
  3.2 3.0 %collective-permute-start = (bf16[48,2304]{1,0:T(8,128)(2,1)}, bf16[48,2304]{1,0:T(8,128)(2,1)S(1)}, u32[]{:S(2)}, u32[]{:S(2)}) collective-permute-start(bf16[48,2304]{1,0:T(8,128)(2,1)} %get-tuple-element.19), channel_id=1, source_target_pairs={{0,8},{8,0},{16,24},{24,16},{1,9},{9,1},{17,25},{25,17},{2,10},{10... | collective-permute-start | bytes 663560 | tf_op jit(solution)/shard_map/ppermute | solution.py:260
  6.2 1.5 %collective-permute-start.1 = (bf16[48,2304]{1,0:T(8,128)(2,1)}, bf16[48,2304]{1,0:T(8,128)(2,1)S(1)}, u32[]{:S(2)}, u32[]{:S(2)}) collective-permute-start(bf16[48,2304]{1,0:T(8,128)(2,1)} %get-tuple-element.20), channel_id=1, source_target_pairs={{0,16},{8,24},{16,0},{24,8},{1,17},{9,25},{17,1},{25,9},{2,18},{10... | collective-permute-start | bytes 663560 | tf_op jit(solution)/shard_map/ppermute | solution.py:260
  7.7 0.0 collective-permute-start.2
  7.7 1.2 %copy-done = f32[1,48,5376]{2,1,0:T(8,128)S(1)} copy-done((f32[1,48,5376]{2,1,0:T(8,128)S(1)}, f32[1,48,5376]{2,1,0:T(8,128)}, u32[]{:S(2)}) %copy-start) | copy-done | bytes 1032216
  9.0 3.6 %collective-permute-done.rest_1_ = bf16[48,2304]{1,0:T(8,128)(2,1)S(1)} collective-permute-done((bf16[48,2304]{1,0:T(8,128)(2,1)}, bf16[48,2304]{1,0:T(8,128)(2,1)S(1)}, u32[]{:S(2)}, u32[]{:S(2)}) %collective-permute-start) | collective-permute-done | bytes 221216 | tf_op jit(solution)/shard_map/ppermute | solution.py:260
  12.6 5.4 %collective-permute-done.1.rest_2_ = bf16[48,2304]{1,0:T(8,128)(2,1)S(1)} collective-permute-done((bf16[48,2304]{1,0:T(8,128)(2,1)}, bf16[48,2304]{1,0:T(8,128)(2,1)S(1)}, u32[]{:S(2)}, u32[]{:S(2)}) %collective-permute-start.1) | collective-permute-done | bytes 221216 | tf_op jit(solution)/shard_map/ppermute | solution.py:260
  18.0 0.0 collective-permute-done.2.rest_3_
  18.0 0.2 shard_map.111
  18.2 1.6 %collective-permute-start.4 = (bf16[48,2304]{1,0:T(8,128)(2,1)S(1)}, bf16[48,2304]{1,0:T(8,128)(2,1)S(1)}, u32[]{:S(2)}, u32[]{:S(2)}) collective-permute-start(bf16[48,2304]{1,0:T(8,128)(2,1)S(1)} %get-tuple-element.22.rest_0_), channel_id=1, source_target_pairs={{0,16},{8,24},{16,0},{24,8},{1,17},{9,25},{17,1},{25,9},{2,18},{10... | collective-permute-start | bytes 663560 | tf_op jit(solution)/shard_map/ppermute | solution.py:260
  19.8 3.6 %collective-permute-start.8 = (bf16[48,2304]{1,0:T(8,128)(2,1)S(1)}, bf16[48,2304]{1,0:T(8,128)(2,1)S(1)}, u32[]{:S(2)}, u32[]{:S(2)}) collective-permute-start(bf16[48,2304]{1,0:T(8,128)(2,1)S(1)} %get-tuple-element.26.rest_0_), channel_id=1, source_target_pairs={{0,6},{1,7},{2,4},{3,5},{4,2},{5,3},{6,0},{7,1},{8,14},{9,15},{10,... | collective-permute-start | bytes 663560 | tf_op jit(solution)/shard_map/ppermute | solution.py:260
  23.4 0.0 collective-permute-start.7
  23.4 0.8 %collective-permute-start.6 = (bf16[48,2304]{1,0:T(8,128)(2,1)S(1)}, bf16[48,2304]{1,0:T(8,128)(2,1)S(1)}, u32[]{:S(2)}, u32[]{:S(2)}) collective-permute-start(bf16[48,2304]{1,0:T(8,128)(2,1)S(1)} %get-tuple-element.26.rest_0_), channel_id=1, source_target_pairs={{0,2},{1,3},{2,0},{3,1},{4,6},{5,7},{6,4},{7,5},{8,10},{9,11},{10,... | collective-permute-start | bytes 663560 | tf_op jit(solution)/shard_map/ppermute | solution.py:260
  24.2 0.5 collective-permute-start.3
  24.7 0.0 collective-permute-start.9
  24.7 5.2 %collective-permute-done.8.rest_3_ = bf16[48,2304]{1,0:T(8,128)(2,1)S(1)} collective-permute-done((bf16[48,2304]{1,0:T(8,128)(2,1)S(1)}, bf16[48,2304]{1,0:T(8,128)(2,1)S(1)}, u32[]{:S(2)}, u32[]{:S(2)}) %collective-permute-start.8) | collective-permute-done | bytes 221216 | tf_op jit(solution)/shard_map/ppermute | solution.py:260
  29.9 0.0 collective-permute-start.12
  29.9 9.9 %collective-permute-done.7.rest_2_ = bf16[48,2304]{1,0:T(8,128)(2,1)S(1)} collective-permute-done((bf16[48,2304]{1,0:T(8,128)(2,1)S(1)}, bf16[48,2304]{1,0:T(8,128)(2,1)S(1)}, u32[]{:S(2)}, u32[]{:S(2)}) %collective-permute-start.7) | collective-permute-done | bytes 221216 | tf_op jit(solution)/shard_map/ppermute | solution.py:260
  39.8 0.5 collective-permute-start.10
  40.3 0.0 collective-permute-done.3.rest_1_.rest_8_
  40.3 2.4 %collective-permute-start.5 = (bf16[48,2304]{1,0:T(8,128)(2,1)S(1)}, bf16[48,2304]{1,0:T(8,128)(2,1)S(1)}, u32[]{:S(2)}, u32[]{:S(2)}) collective-permute-start(bf16[48,2304]{1,0:T(8,128)(2,1)S(1)} %get-tuple-element.22.rest_0_), channel_id=1, source_target_pairs={{0,24},{8,16},{16,8},{24,0},{1,25},{9,17},{17,9},{25,1},{2,26},{10... | collective-permute-start | bytes 663560 | tf_op jit(solution)/shard_map/ppermute | solution.py:260
  42.7 0.0 collective-permute-done.10.rest_5_
  42.7 11.7 %shard_map.113.rest_0_ = bf16[48,2304]{1,0:T(8,128)(2,1)S(1)} custom-call(s32[1]{0:T(128)} %bitcast.index, bf16[48,2304]{1,0:T(8,128)(2,1)S(1)} %get-tuple-element.26.rest_0_, bf16[48,2304]{1,0:T(8,128)(2,1)S(1)} %collective-permute-done.6.rest_1_, bf16[48,2304]{1,0:T(8,128)(2,1)S(1)} %collective-permute-done.7.rest_2_, ...), custom_call_target="tpu_custom_call" | custom-call | flops 7361003520 | bytes 2433028 | tf_op jit(solution)/shard_map/pallas_call | solution.py:248
  54.5 3.0 %collective-permute-start.15 = (bf16[48,2304]{1,0:T(8,128)(2,1)S(1)}, bf16[48,2304]{1,0:T(8,128)(2,1)S(1)}, u32[]{:S(2)}, u32[]{:S(2)}) collective-permute-start(bf16[48,2304]{1,0:T(8,128)(2,1)S(1)} %shard_map.113.rest_0_), channel_id=1, source_target_pairs={{0,24},{8,16},{16,8},{24,0},{1,25},{9,17},{17,9},{25,1},{2,26},{10... | collective-permute-start | bytes 663560 | tf_op jit(solution)/shard_map/ppermute | solution.py:260
  57.5 0.0 collective-permute-start.14
  57.5 0.6 collective-permute-start.13
  58.2 0.0 collective-permute-done.5.rest_3_
  58.2 1.3 %shard_map.112 = (f32[48,5376]{1,0:T(8,128)}, f32[48,1536]{1,0:T(8,128)}, f32[48,1001]{1,0:T(8,128)}) custom-call(s32[1]{0:T(128)} %bitcast.index, f32[48,5376]{1,0:T(8,128)S(1)} %bitcast.24, f32[48,1536]{1,0:T(8,128)S(1)} %bitcast.26, f32[48,1001]{1,0:T(8,128)S(1)} %bitcast.28, bf16[48,2304]{1,0:T(8,128)(2,1)S(1)} %get-tuple-element.22.rest_0_, ...), custom_call_target="tpu_custom_call" | custom-call | bytes 3923332 | tf_op jit(solution)/shard_map/pallas_call | solution.py:248
  59.5 4.3 %collective-permute-done.15.rest_3_ = bf16[48,2304]{1,0:T(8,128)(2,1)S(1)} collective-permute-done((bf16[48,2304]{1,0:T(8,128)(2,1)S(1)}, bf16[48,2304]{1,0:T(8,128)(2,1)S(1)}, u32[]{:S(2)}, u32[]{:S(2)}) %collective-permute-start.15) | collective-permute-done | bytes 221216 | tf_op jit(solution)/shard_map/ppermute | solution.py:260
  63.8 4.3 %collective-permute-done.14.rest_2_ = bf16[48,2304]{1,0:T(8,128)(2,1)S(1)} collective-permute-done((bf16[48,2304]{1,0:T(8,128)(2,1)S(1)}, bf16[48,2304]{1,0:T(8,128)(2,1)S(1)}, u32[]{:S(2)}, u32[]{:S(2)}) %collective-permute-start.14) | collective-permute-done | bytes 221216 | tf_op jit(solution)/shard_map/ppermute | solution.py:260
  68.0 0.0 collective-permute-done.13.rest_1_
  68.0 0.9 %shard_map.114 = (bf16[48,5376]{1,0:T(8,128)(2,1)}, bf16[48,1536]{1,0:T(8,128)(2,1)}, bf16[48,1001]{1,0:T(8,128)(2,1)}) custom-call(s32[1]{0:T(128)} %bitcast.index, bf16[48,2304]{1,0:T(8,128)(2,1)S(1)} %shard_map.113.rest_0_, bf16[48,2304]{1,0:T(8,128)(2,1)S(1)} %collective-permute-done.13.rest_1_, bf16[48,2304]{1,0:T(8,128)(2,1)S(1)} %collective-permute-done.14.rest_2_, ...), custom_call_target="tpu_custom_call" | custom-call | bytes 1644388 | tf_op jit(solution)/shard_map/pallas_call | solution.py:248
  (16 shorter events, 0.1 us)
Async XLA Ops:
  0.6 7.1 %copy-start.2 = (f32[1,1536,48]{1,2,0:T(8,128)S(1)}, f32[1,1536,48]{1,2,0:T(8,128)}, u32[]{:S(2)}) copy-start(f32[1,1536,48]{1,2,0:T(8,128)} %param.10) | copy-start | bytes 884740
  0.6 7.1 %copy-start.3 = (f32[1001,48]{0,1:T(8,128)S(1)}, f32[1001,48]{0,1:T(8,128)}, u32[]{:S(2)}) copy-start(f32[1001,48]{0,1:T(8,128)} %param.11) | copy-start | bytes 576580
  3.2 9.5 %collective-permute-start = (bf16[48,2304]{1,0:T(8,128)(2,1)}, bf16[48,2304]{1,0:T(8,128)(2,1)S(1)}, u32[]{:S(2)}, u32[]{:S(2)}) collective-permute-start(bf16[48,2304]{1,0:T(8,128)(2,1)} %get-tuple-element.19), channel_id=1, source_target_pairs={{0,8},{8,0},{16,24},{24,16},{1,9},{9,1},{17,25},{25,17},{2,10},{10... | collective-permute-start | bytes 663560 | tf_op jit(solution)/shard_map/ppermute | solution.py:260
  6.2 11.8 %collective-permute-start.1 = (bf16[48,2304]{1,0:T(8,128)(2,1)}, bf16[48,2304]{1,0:T(8,128)(2,1)S(1)}, u32[]{:S(2)}, u32[]{:S(2)}) collective-permute-start(bf16[48,2304]{1,0:T(8,128)(2,1)} %get-tuple-element.20), channel_id=1, source_target_pairs={{0,16},{8,24},{16,0},{24,8},{1,17},{9,25},{17,1},{25,9},{2,18},{10... | collective-permute-start | bytes 663560 | tf_op jit(solution)/shard_map/ppermute | solution.py:260
  7.7 10.3 %collective-permute-start.2 = (bf16[48,2304]{1,0:T(8,128)(2,1)}, bf16[48,2304]{1,0:T(8,128)(2,1)S(1)}, u32[]{:S(2)}, u32[]{:S(2)}) collective-permute-start(bf16[48,2304]{1,0:T(8,128)(2,1)} %get-tuple-element.21), channel_id=1, source_target_pairs={{0,24},{8,16},{16,8},{24,0},{1,25},{9,17},{17,9},{25,1},{2,26},{10... | collective-permute-start | bytes 663560 | tf_op jit(solution)/shard_map/ppermute | solution.py:260
  7.7 1.2 %copy-start = (f32[1,48,5376]{2,1,0:T(8,128)S(1)}, f32[1,48,5376]{2,1,0:T(8,128)}, u32[]{:S(2)}) copy-start(f32[1,48,5376]{2,1,0:T(8,128)} %param.9) | copy-start | bytes 3096580
  8.9 9.1 %copy-start.4 = (bf16[48,2304]{1,0:T(8,128)(2,1)S(1)}, bf16[48,2304]{1,0:T(8,128)(2,1)}, u32[]{:S(2)}) copy-start(bf16[48,2304]{1,0:T(8,128)(2,1)} %get-tuple-element.18.rest_0_) | copy-start | bytes 663556
  18.2 6.5 %collective-permute-start.4 = (bf16[48,2304]{1,0:T(8,128)(2,1)S(1)}, bf16[48,2304]{1,0:T(8,128)(2,1)S(1)}, u32[]{:S(2)}, u32[]{:S(2)}) collective-permute-start(bf16[48,2304]{1,0:T(8,128)(2,1)S(1)} %get-tuple-element.22.rest_0_), channel_id=1, source_target_pairs={{0,16},{8,24},{16,0},{24,8},{1,17},{9,25},{17,1},{25,9},{2,18},{10... | collective-permute-start | bytes 663560 | tf_op jit(solution)/shard_map/ppermute | solution.py:260
  19.8 38.4 %copy-start.1 = (f32[1,48,5376]{2,1,0:T(8,128)S(1)}, f32[1,48,5376]{2,1,0:T(8,128)}, u32[]{:S(2)}) copy-start(f32[1,48,5376]{2,1,0:T(8,128)} %param.9) | copy-start | bytes 3096580
  19.8 10.2 %collective-permute-start.8 = (bf16[48,2304]{1,0:T(8,128)(2,1)S(1)}, bf16[48,2304]{1,0:T(8,128)(2,1)S(1)}, u32[]{:S(2)}, u32[]{:S(2)}) collective-permute-start(bf16[48,2304]{1,0:T(8,128)(2,1)S(1)} %get-tuple-element.26.rest_0_), channel_id=1, source_target_pairs={{0,6},{1,7},{2,4},{3,5},{4,2},{5,3},{6,0},{7,1},{8,14},{9,15},{10,... | collective-permute-start | bytes 663560 | tf_op jit(solution)/shard_map/ppermute | solution.py:260
  23.4 16.4 %collective-permute-start.7 = (bf16[48,2304]{1,0:T(8,128)(2,1)S(1)}, bf16[48,2304]{1,0:T(8,128)(2,1)S(1)}, u32[]{:S(2)}, u32[]{:S(2)}) collective-permute-start(bf16[48,2304]{1,0:T(8,128)(2,1)S(1)} %get-tuple-element.26.rest_0_), channel_id=1, source_target_pairs={{0,4},{1,5},{2,6},{3,7},{4,0},{5,1},{6,2},{7,3},{8,12},{9,13},{10,... | collective-permute-start | bytes 663560 | tf_op jit(solution)/shard_map/ppermute | solution.py:260
  23.4 16.4 %collective-permute-start.6 = (bf16[48,2304]{1,0:T(8,128)(2,1)S(1)}, bf16[48,2304]{1,0:T(8,128)(2,1)S(1)}, u32[]{:S(2)}, u32[]{:S(2)}) collective-permute-start(bf16[48,2304]{1,0:T(8,128)(2,1)S(1)} %get-tuple-element.26.rest_0_), channel_id=1, source_target_pairs={{0,2},{1,3},{2,0},{3,1},{4,6},{5,7},{6,4},{7,5},{8,10},{9,11},{10,... | collective-permute-start | bytes 663560 | tf_op jit(solution)/shard_map/ppermute | solution.py:260
  24.2 16.2 %collective-permute-start.3 = (bf16[48,2304]{1,0:T(8,128)(2,1)S(1)}, bf16[48,2304]{1,0:T(8,128)(2,1)S(1)}, u32[]{:S(2)}, u32[]{:S(2)}) collective-permute-start(bf16[48,2304]{1,0:T(8,128)(2,1)S(1)} %get-tuple-element.22.rest_0_), channel_id=1, source_target_pairs={{0,8},{8,0},{16,24},{24,16},{1,9},{9,1},{17,25},{25,17},{2,10},{10... | collective-permute-start | bytes 663560 | tf_op jit(solution)/shard_map/ppermute | solution.py:260
  24.7 18.0 %collective-permute-start.9 = (bf16[48,2304]{1,0:T(8,128)(2,1)S(1)}, bf16[48,2304]{1,0:T(8,128)(2,1)S(1)}, u32[]{:S(2)}, u32[]{:S(2)}) collective-permute-start(bf16[48,2304]{1,0:T(8,128)(2,1)S(1)} %get-tuple-element.26.rest_0_), channel_id=1, source_target_pairs={{0,1},{1,0},{2,3},{3,2},{4,5},{5,4},{6,7},{7,6},{8,9},{9,8},{10,11... | collective-permute-start | bytes 663560 | tf_op jit(solution)/shard_map/ppermute | solution.py:260
  29.9 12.8 %collective-permute-start.12 = (bf16[48,2304]{1,0:T(8,128)(2,1)S(1)}, bf16[48,2304]{1,0:T(8,128)(2,1)S(1)}, u32[]{:S(2)}, u32[]{:S(2)}) collective-permute-start(bf16[48,2304]{1,0:T(8,128)(2,1)S(1)} %collective-permute-done.8.rest_3_), channel_id=1, source_target_pairs={{0,1},{1,0},{2,3},{3,2},{4,5},{5,4},{6,7},{7,6},{8,9},{9,8},{10,11... | collective-permute-start | bytes 663560 | tf_op jit(solution)/shard_map/ppermute | solution.py:260
  39.8 2.9 %collective-permute-start.11 = (bf16[48,2304]{1,0:T(8,128)(2,1)S(1)}, bf16[48,2304]{1,0:T(8,128)(2,1)S(1)}, u32[]{:S(2)}, u32[]{:S(2)}) collective-permute-start(bf16[48,2304]{1,0:T(8,128)(2,1)S(1)} %collective-permute-done.7.rest_2_), channel_id=1, source_target_pairs={{0,1},{1,0},{2,3},{3,2},{4,5},{5,4},{6,7},{7,6},{8,9},{9,8},{10,11... | collective-permute-start | bytes 663560 | tf_op jit(solution)/shard_map/ppermute | solution.py:260
  39.8 2.9 %collective-permute-start.10 = (bf16[48,2304]{1,0:T(8,128)(2,1)S(1)}, bf16[48,2304]{1,0:T(8,128)(2,1)S(1)}, u32[]{:S(2)}, u32[]{:S(2)}) collective-permute-start(bf16[48,2304]{1,0:T(8,128)(2,1)S(1)} %collective-permute-done.6.rest_1_), channel_id=1, source_target_pairs={{0,1},{1,0},{2,3},{3,2},{4,5},{5,4},{6,7},{7,6},{8,9},{9,8},{10,11... | collective-permute-start | bytes 663560 | tf_op jit(solution)/shard_map/ppermute | solution.py:260
  40.3 17.8 %collective-permute-start.5 = (bf16[48,2304]{1,0:T(8,128)(2,1)S(1)}, bf16[48,2304]{1,0:T(8,128)(2,1)S(1)}, u32[]{:S(2)}, u32[]{:S(2)}) collective-permute-start(bf16[48,2304]{1,0:T(8,128)(2,1)S(1)} %get-tuple-element.22.rest_0_), channel_id=1, source_target_pairs={{0,24},{8,16},{16,8},{24,0},{1,25},{9,17},{17,9},{25,1},{2,26},{10... | collective-permute-start | bytes 663560 | tf_op jit(solution)/shard_map/ppermute | solution.py:260
  54.5 9.3 %collective-permute-start.15 = (bf16[48,2304]{1,0:T(8,128)(2,1)S(1)}, bf16[48,2304]{1,0:T(8,128)(2,1)S(1)}, u32[]{:S(2)}, u32[]{:S(2)}) collective-permute-start(bf16[48,2304]{1,0:T(8,128)(2,1)S(1)} %shard_map.113.rest_0_), channel_id=1, source_target_pairs={{0,24},{8,16},{16,8},{24,0},{1,25},{9,17},{17,9},{25,1},{2,26},{10... | collective-permute-start | bytes 663560 | tf_op jit(solution)/shard_map/ppermute | solution.py:260
  57.5 10.5 %collective-permute-start.14 = (bf16[48,2304]{1,0:T(8,128)(2,1)S(1)}, bf16[48,2304]{1,0:T(8,128)(2,1)S(1)}, u32[]{:S(2)}, u32[]{:S(2)}) collective-permute-start(bf16[48,2304]{1,0:T(8,128)(2,1)S(1)} %shard_map.113.rest_0_), channel_id=1, source_target_pairs={{0,16},{8,24},{16,0},{24,8},{1,17},{9,25},{17,1},{25,9},{2,18},{10... | collective-permute-start | bytes 663560 | tf_op jit(solution)/shard_map/ppermute | solution.py:260
  57.5 10.5 %collective-permute-start.13 = (bf16[48,2304]{1,0:T(8,128)(2,1)S(1)}, bf16[48,2304]{1,0:T(8,128)(2,1)S(1)}, u32[]{:S(2)}, u32[]{:S(2)}) collective-permute-start(bf16[48,2304]{1,0:T(8,128)(2,1)S(1)} %shard_map.113.rest_0_), channel_id=1, source_target_pairs={{0,8},{8,0},{16,24},{24,16},{1,9},{9,1},{17,25},{25,17},{2,10},{10... | collective-permute-start | bytes 663560 | tf_op jit(solution)/shard_map/ppermute | solution.py:260

commit v6 on v5

--- a/solution.py
+++ b/solution.py
@@ -88,21 +88,22 @@
                         dst[:, end:] = jnp.zeros((dst.shape[0], high - low - end), dst.dtype)
 
 
-def own_kernel(bins, index, wide, down, embed, out):
+def own_kernel(bins, windows, index, wide, down, embed, *outs):
     for target, group in enumerate(bins):
 
         @pl.when(index[0] == target)
         def _():
-            end = 0
-            for matrix, first, place, width in window(group, 0, out.shape[1]):
-                out[:, place : place + width] = columns(matrix, first, width, wide, down, embed)
-                end = place + width
-            if end < out.shape[1]:
-                out[:, end:] = jnp.zeros((out.shape[0], out.shape[1] - end), out.dtype)
+            for out, (low, high) in zip(outs, windows):
+                end = 0
+                for matrix, first, place, width in window(group, low, high):
+                    out[:, place : place + width] = columns(matrix, first, width, wide, down, embed)
+                    end = place + width
+                if end < high - low:
+                    out[:, end:] = jnp.zeros((out.shape[0], high - low - end), out.dtype)
 
 
 def sum_kernel(count, mom, *rest):
-    received, g_out, y_out = rest[:count], rest[count], rest[count + 1]
+    received, g_out, y_out = rest[:count], rest[-2], rest[-1]
     g = received[0][...].astype(jnp.float32)
     for piece in received[1:]:
         g = g + piece[...].astype(jnp.float32)
@@ -110,18 +111,29 @@
     y_out[...] = (g + MOMENTUM * (MOMENTUM * mom[...] + g)).astype(jnp.bfloat16)
 
 
+def join_kernel(left, right, *rest):
+    out, half = rest[-1], left.shape[1]
+    out[:, :half] = left[...]
+    out[:, half:] = right[...]
+
+
 def stack_kernel(count, *rest):
     out, rows = rest[-1], rest[0].shape[0]
     for number in range(count):
         out[number * rows : (number + 1) * rows, :] = rest[number][...]
 
 
-def newton_kernel(bins, count, rows, index, *rest):
-    pieces, out, x_ref = rest[:count], rest[-2], rest[-1]
-    start = 0
-    for piece in pieces:
-        x_ref[start : start + piece.shape[0], :] = piece[...]
-        start += piece.shape[0]
+def newton_kernel(bins, halves, count, index, *rest):
+    out, x_ref = rest[-2], rest[-1]
+    left = 0
+    for half in range(halves):
+        pieces = rest[half * count : (half + 1) * count]
+        top = 0
+        for piece in pieces:
+            x_ref[top : top + piece.shape[0], left : left + piece.shape[1]] = piece[...]
+            top += piece.shape[0]
+        left += pieces[0].shape[1]
+    rows = out.shape[0]
 
     def branch(group):
         spans = []
@@ -264,13 +276,16 @@
     return [swap(value, axis, k, n) for k in range(1, n)]
 
 
-def gather_rows(value, n):
-    pieces = [value] + [swap(value, "shard", k, n) for k in range(2, n, 2)]
-    rows, width = value.shape
+def stack(pieces, tied=()):
+    rows, width = pieces[0].shape
     if rows % 16:
-        pieces = [jnp.concatenate(pieces, axis=0)]
-        return [jnp.concatenate(pieces + [swap(pieces[0], "shard", 1, n)], axis=0)]
-    return pieces + [swap(piece, "shard", 1, n) for piece in pieces]
+        return jnp.concatenate(pieces, axis=0)
+    return call(
+        functools.partial(stack_kernel, len(pieces)),
+        [jax.ShapeDtypeStruct((rows * len(pieces), width), pieces[0].dtype)],
+        (*pieces, *tied),
+        [VMEM] * len(pieces) + [ANY] * len(tied),
+    )[0]
 
 
 def per_device(grad_wide, grad_down, grad_embed, mom_wide, mom_down, mom_embed):
@@ -280,32 +295,47 @@
     grads = (grad_wide[0, 0], grad_down[0, 0].T, grad_embed[0].T)
     moms = (mom_wide[0], mom_down[0].T, mom_embed.T)
     rows = grads[0].shape[0]
-    whole = jax.ShapeDtypeStruct((rows, width), jnp.bfloat16)
-
-    own, *sends = call(
-        functools.partial(split_kernel, bins, [(0, width)]),
-        [whole] * n_rep,
+    windows = [(0, width // 2), (width // 2, width)]
+
+    def block(columns, dtype=jnp.bfloat16):
+        return jax.ShapeDtypeStruct((rows, columns), dtype)
+
+    sends = call(
+        functools.partial(split_kernel, bins, windows),
+        [block(high - low) for low, high in windows for _ in range(n_rep)],
         (index, *grads),
         [SMEM] + [ANY] * 3,
         [pltpu.VMEM(array.shape, jnp.float32) for array in grads] + [pltpu.SemaphoreType.DMA((3,))],
         limit=VMEM_ALL,
     )
-    received = [own] + [swap(piece, "rep", k + 1, n_rep) for k, piece in enumerate(sends)]
-    (mom_own,) = call(
-        functools.partial(own_kernel, bins),
-        [jax.ShapeDtypeStruct((rows, width), jnp.float32)],
+    mom_own = call(
+        functools.partial(own_kernel, bins, windows),
+        [block(high - low, jnp.float32) for low, high in windows],
         (index, *moms),
         [SMEM] + [VMEM] * 3,
     )
-    g, y = call(functools.partial(sum_kernel, n_rep), [whole] * 2, (mom_own, *received), [VMEM] * (n_rep + 1))
-    pieces = gather_rows(y, n_shard)
+    gs, arrived = [], []
+    for half, (low, high) in enumerate(windows):
+        own, *others = sends[half * n_rep : (half + 1) * n_rep]
+        received = [own] + [swap(piece, "rep", k + 1, n_rep) for k, piece in enumerate(others)]
+        g, y = call(
+            functools.partial(sum_kernel, n_rep),
+            [block(high - low)] * 2,
+            (mom_own[half], *received),
+            [VMEM] * (n_rep + 1),
+        )
+        gs.append(g)
+        arrived.append([y] + [swap(y, "shard", k, n_shard) for k in range(2, n_shard, 2)])
+    stacks = [None, stack(arrived[1], (arrived[0][0],))]
+    (g,) = call(join_kernel, [block(width)], (*gs, arrived[1][1]), [VMEM] * 2 + [ANY])
     g_others = spread(g, "rep", n_rep)
-    tied = g_others[: n_rep // 2]
+    stacks[0] = stack(arrived[0], g_others[:2])
+    pieces = [piece for whole in stacks for piece in (whole, swap(whole, "shard", 1, n_shard))]
     (upd,) = call(
-        functools.partial(newton_kernel, bins, len(pieces), rows),
-        [whole],
-        (index, *pieces, *tied),
-        [SMEM] + [VMEM] * len(pieces) + [ANY] * len(tied),
+        functools.partial(newton_kernel, bins, 2, 2),
+        [block(width)],
+        (index, *pieces),
+        [SMEM] + [VMEM] * len(pieces),
         (pltpu.VMEM((D, width), jnp.bfloat16),),
         flops=NS_ITERS * (4 * D * D * width + 2 * D * D * D),
     )

time: 69.2 us -> 66.9 us (0.967)
  waiting for transfers between devices: 32.7 us -> 18.4 us
  starting transfers between devices: 17.6 us -> 28.2 us
  local copies, waits for them, and re-layouts: 1.24 us -> 2.07 us
    ppermute x16 -> x20, waiting for transfers between devices: 32.7 us -> 18.4 us  [swap(): return lax.ppermute(value, axis, [(i, i ^ k) for i in range(n)])]
    ppermute x16 -> x20, starting transfers between devices: 17.6 us -> 28.2 us  [swap(): return lax.ppermute(value, axis, [(i, i ^ k) for i in range(n)])]
    unnamed x10 -> x14, local copies, waits for them, and re-layouts: 1.24 us -> 2.07 us
    pallas_call x6 -> x10, Pallas kernels: 16.7 us -> 17.1 us  [call(): pl.pallas_call(kernel, out_shape=tuple(outs), in_specs=specs, out_specs=t...]
  transfers between devices with their start and end apart: 16 -> 20, of which waited for: 6 -> 8; matrix products, arithmetic and copies ran while one was open for 0% -> 0% of each run, Pallas kernels for 19% -> 20%
where the time goes in v6:
time: 66.9 us; the launch traced here: 66.6 us
  starting transfers between devices  28.2 us (42%)
  waiting for transfers between devices  18.4 us (28%)
  Pallas kernels  17.1 us (26%)
  local copies, waits for them, and re-layouts  2.07 us (3%)
  between operations  0.76 us (1%)
    ppermute x20, starting transfers between devices, swap(): return lax.ppermute(value, axis, [(i, i ^ k) for i in range(n)])  28.2 us
    ppermute x20, waiting for transfers between devices, swap(): return lax.ppermute(value, axis, [(i, i ^ k) for i in range(n)])  18.4 us
    pallas_call x10, Pallas kernels, call(): pl.pallas_call(kernel, out_shape=tuple(outs), in_specs=specs, out_specs=t...  17.1 us
    unnamed x14, local copies, waits for them, and re-layouts  2.07 us
  transfers between devices with their start and end apart: 20, of which 8 were waited for; matrix products, arithmetic and copies ran while one was open for 0% of the time, Pallas kernels for 20%

profile of v6, /device:TPU:0, one launch (start us, length us, event | category | flops | bytes accessed | tf_op | source)
XLA Modules:
  0.0 66.6 jit_solution(8479695513470060949)
XLA Ops:
  0.7 2.6 %shard_map.110 = (bf16[48,1152]{1,0:T(8,128)(2,1)}, bf16[48,1152]{1,0:T(8,128)(2,1)}, bf16[48,1152]{1,0:T(8,128)(2,1)}, bf16[48,1152]{1,0:T(8,128)(2,1)}, bf16[4...) custom-call(s32[1]{0:T(128)} %bitcast.index, ...), custom_call_target="tpu_custom_call" | custom-call | bytes 2404036 | tf_op jit(solution)/shard_map/pallas_call | solution.py:260
  3.3 3.0 %collective-permute-start.3 = (bf16[48,1152]{1,0:T(8,128)(2,1)}, bf16[48,1152]{1,0:T(8,128)(2,1)S(1)}, u32[]{:S(2)}, u32[]{:S(2)}) collective-permute-start(bf16[48,1152]{1,0:T(8,128)(2,1)} %get-tuple-element.34), channel_id=1, source_target_pairs={{0,8},{8,0},{16,24},{24,16},{1,9},{9,1},{17,25},{25,17},{2,10},{10... | collective-permute-start | bytes 331784 | tf_op jit(solution)/shard_map/ppermute | solution.py:272
  6.3 1.5 %collective-permute-start.4 = (bf16[48,1152]{1,0:T(8,128)(2,1)}, bf16[48,1152]{1,0:T(8,128)(2,1)S(1)}, u32[]{:S(2)}, u32[]{:S(2)}) collective-permute-start(bf16[48,1152]{1,0:T(8,128)(2,1)} %get-tuple-element.35), channel_id=1, source_target_pairs={{0,16},{8,24},{16,0},{24,8},{1,17},{9,25},{17,1},{25,9},{2,18},{10... | collective-permute-start | bytes 331784 | tf_op jit(solution)/shard_map/ppermute | solution.py:272
  7.8 1.9 %collective-permute-start = (bf16[48,1152]{1,0:T(8,128)(2,1)}, bf16[48,1152]{1,0:T(8,128)(2,1)S(1)}, u32[]{:S(2)}, u32[]{:S(2)}) collective-permute-start(bf16[48,1152]{1,0:T(8,128)(2,1)} %get-tuple-element.28), channel_id=1, source_target_pairs={{0,8},{8,0},{16,24},{24,16},{1,9},{9,1},{17,25},{25,17},{2,10},{10... | collective-permute-start | bytes 331784 | tf_op jit(solution)/shard_map/ppermute | solution.py:272
  9.8 1.5 %collective-permute-start.1 = (bf16[48,1152]{1,0:T(8,128)(2,1)}, bf16[48,1152]{1,0:T(8,128)(2,1)S(1)}, u32[]{:S(2)}, u32[]{:S(2)}) collective-permute-start(bf16[48,1152]{1,0:T(8,128)(2,1)} %get-tuple-element.29), channel_id=1, source_target_pairs={{0,16},{8,24},{16,0},{24,8},{1,17},{9,25},{17,1},{25,9},{2,18},{10... | collective-permute-start | bytes 331784 | tf_op jit(solution)/shard_map/ppermute | solution.py:272
  11.3 1.2 %copy-done = f32[1,48,5376]{2,1,0:T(8,128)S(1)} copy-done((f32[1,48,5376]{2,1,0:T(8,128)S(1)}, f32[1,48,5376]{2,1,0:T(8,128)}, u32[]{:S(2)}) %copy-start) | copy-done | bytes 1032216
  12.6 0.8 %copy-done.6 = bf16[48,1152]{1,0:T(8,128)(2,1)S(1)} copy-done((bf16[48,1152]{1,0:T(8,128)(2,1)S(1)}, bf16[48,1152]{1,0:T(8,128)(2,1)}, u32[]{:S(2)}) %copy-start.6) | copy-done | bytes 110616
  13.4 1.0 %collective-permute-done.5.rest_3_ = bf16[48,1152]{1,0:T(8,128)(2,1)S(1)} collective-permute-done((bf16[48,1152]{1,0:T(8,128)(2,1)}, bf16[48,1152]{1,0:T(8,128)(2,1)S(1)}, u32[]{:S(2)}, u32[]{:S(2)}) %collective-permute-start.5) | collective-permute-done | bytes 110624 | tf_op jit(solution)/shard_map/ppermute | solution.py:272
  14.5 0.1 shard_map.112
  14.6 1.6 %collective-permute-start.6 = (bf16[48,1152]{1,0:T(8,128)(2,1)S(1)}, bf16[48,1152]{1,0:T(8,128)(2,1)S(1)}, u32[]{:S(2)}, u32[]{:S(2)}) collective-permute-start(bf16[48,1152]{1,0:T(8,128)(2,1)S(1)} %get-tuple-element.38.rest_0_), channel_id=1, source_target_pairs={{0,2},{1,3},{2,0},{3,1},{4,6},{5,7},{6,4},{7,5},{8,10},{9,11},{10,... | collective-permute-start | bytes 331784 | tf_op jit(solution)/shard_map/ppermute | solution.py:272
  16.2 2.5 %collective-permute-start.15 = (bf16[48,1152]{1,0:T(8,128)(2,1)S(1)}, bf16[48,1152]{1,0:T(8,128)(2,1)S(1)}, u32[]{:S(2)}, u32[]{:S(2)}) collective-permute-start(bf16[48,1152]{1,0:T(8,128)(2,1)S(1)} %get-tuple-element.38.rest_0_), channel_id=1, source_target_pairs={{0,6},{1,7},{2,4},{3,5},{4,2},{5,3},{6,0},{7,1},{8,14},{9,15},{10,... | collective-permute-start | bytes 331784 | tf_op jit(solution)/shard_map/ppermute | solution.py:272
  18.7 0.1 collective-permute-start.14
  18.8 0.2 collective-permute-done.2.rest_3_
  19.1 0.1 shard_map.111
  19.1 1.6 %collective-permute-done.6.rest_0_.rest_1_ = bf16[48,1152]{1,0:T(8,128)(2,1)S(1)} collective-permute-done((bf16[48,1152]{1,0:T(8,128)(2,1)S(1)}, bf16[48,1152]{1,0:T(8,128)(2,1)S(1)}, u32[]{:S(2)}, u32[]{:S(2)}) %collective-permute-start.6) | collective-permute-done | bytes 110624 | tf_op jit(solution)/shard_map/ppermute | solution.py:272
  20.7 1.5 %collective-permute-start.8 = (bf16[48,2304]{1,0:T(8,128)(2,1)S(1)}, bf16[48,2304]{1,0:T(8,128)(2,1)S(1)}, u32[]{:S(2)}, u32[]{:S(2)}) collective-permute-start(bf16[48,2304]{1,0:T(8,128)(2,1)S(1)} %shard_map.113.rest_0_), channel_id=1, source_target_pairs={{0,16},{8,24},{16,0},{24,8},{1,17},{9,25},{17,1},{25,9},{2,18},{10... | collective-permute-start | bytes 663560 | tf_op jit(solution)/shard_map/ppermute | solution.py:272
  22.2 1.1 %collective-permute-start.7 = (bf16[48,2304]{1,0:T(8,128)(2,1)S(1)}, bf16[48,2304]{1,0:T(8,128)(2,1)S(1)}, u32[]{:S(2)}, u32[]{:S(2)}) collective-permute-start(bf16[48,2304]{1,0:T(8,128)(2,1)S(1)} %shard_map.113.rest_0_), channel_id=1, source_target_pairs={{0,8},{8,0},{16,24},{24,16},{1,9},{9,1},{17,25},{25,17},{2,10},{10... | collective-permute-start | bytes 663560 | tf_op jit(solution)/shard_map/ppermute | solution.py:272
  23.3 3.4 %collective-permute-start.12 = (bf16[48,1152]{1,0:T(8,128)(2,1)S(1)}, bf16[48,1152]{1,0:T(8,128)(2,1)S(1)}, u32[]{:S(2)}, u32[]{:S(2)}) collective-permute-start(bf16[48,1152]{1,0:T(8,128)(2,1)S(1)} %get-tuple-element.42.rest_0_.rest_4_), channel_id=1, source_target_pairs={{0,6},{1,7},{2,4},{3,5},{4,2},{5,3},{6,0},{7,1},{8,14},{9,15},{10,... | collective-permute-start | bytes 331784 | tf_op jit(solution)/shard_map/ppermute | solution.py:272
  26.7 3.3 %collective-permute-start.11 = (bf16[48,1152]{1,0:T(8,128)(2,1)S(1)}, bf16[48,1152]{1,0:T(8,128)(2,1)S(1)}, u32[]{:S(2)}, u32[]{:S(2)}) collective-permute-start(bf16[48,1152]{1,0:T(8,128)(2,1)S(1)} %get-tuple-element.42.rest_0_.rest_4_), channel_id=1, source_target_pairs={{0,4},{1,5},{2,6},{3,7},{4,0},{5,1},{6,2},{7,3},{8,12},{9,13},{10,... | collective-permute-start | bytes 331784 | tf_op jit(solution)/shard_map/ppermute | solution.py:272
  29.9 1.4 %collective-permute-done.14.rest_2_ = bf16[48,1152]{1,0:T(8,128)(2,1)S(1)} collective-permute-done((bf16[48,1152]{1,0:T(8,128)(2,1)S(1)}, bf16[48,1152]{1,0:T(8,128)(2,1)S(1)}, u32[]{:S(2)}, u32[]{:S(2)}) %collective-permute-start.14) | collective-permute-done | bytes 110624 | tf_op jit(solution)/shard_map/ppermute | solution.py:272
  31.4 0.1 collective-permute-start.16
  31.5 4.6 %collective-permute-done.11.rest_2_ = bf16[48,1152]{1,0:T(8,128)(2,1)S(1)} collective-permute-done((bf16[48,1152]{1,0:T(8,128)(2,1)S(1)}, bf16[48,1152]{1,0:T(8,128)(2,1)S(1)}, u32[]{:S(2)}, u32[]{:S(2)}) %collective-permute-start.11) | collective-permute-done | bytes 110624 | tf_op jit(solution)/shard_map/ppermute | solution.py:272
  36.0 1.1 %collective-permute-done.10.rest_1_ = bf16[48,1152]{1,0:T(8,128)(2,1)S(1)} collective-permute-done((bf16[48,1152]{1,0:T(8,128)(2,1)S(1)}, bf16[48,1152]{1,0:T(8,128)(2,1)S(1)}, u32[]{:S(2)}, u32[]{:S(2)}) %collective-permute-start.10) | collective-permute-done | bytes 110624 | tf_op jit(solution)/shard_map/ppermute | solution.py:272
  37.2 0.1 collective-permute-start.13
  37.3 2.5 %collective-permute-start.9 = (bf16[48,2304]{1,0:T(8,128)(2,1)S(1)}, bf16[48,2304]{1,0:T(8,128)(2,1)S(1)}, u32[]{:S(2)}, u32[]{:S(2)}) collective-permute-start(bf16[48,2304]{1,0:T(8,128)(2,1)S(1)} %shard_map.113.rest_0_), channel_id=1, source_target_pairs={{0,24},{8,16},{16,8},{24,0},{1,25},{9,17},{17,9},{25,1},{2,26},{10... | collective-permute-start | bytes 663560 | tf_op jit(solution)/shard_map/ppermute | solution.py:272
  39.8 12.0 %shard_map.117.rest_0_ = bf16[48,2304]{1,0:T(8,128)(2,1)S(1)} custom-call(s32[1]{0:T(128)} %bitcast.index, bf16[192,1152]{1,0:T(8,128)(2,1)S(1)} %shard_map.115.rest_0_, bf16[192,1152]{1,0:T(8,128)(2,1)S(1)} %collective-permute-done.13.rest_1_, bf16[192,1152]{1,0:T(8,128)(2,1)S(1)} %shard_map.116.rest_2_, bf16[192,1152]{1,0:T(8,128)(2,1)S(1)} %collective-permute-done.16.rest_3_), custom_call_target="tpu_custom_call" | custom-call | flops 7361003520 | bytes 1990660 | tf_op jit(solution)/shard_map/pallas_call | solution.py:260
  51.7 3.5 %collective-permute-start.19 = (bf16[48,2304]{1,0:T(8,128)(2,1)S(1)}, bf16[48,2304]{1,0:T(8,128)(2,1)S(1)}, u32[]{:S(2)}, u32[]{:S(2)}) collective-permute-start(bf16[48,2304]{1,0:T(8,128)(2,1)S(1)} %shard_map.117.rest_0_), channel_id=1, source_target_pairs={{0,24},{8,16},{16,8},{24,0},{1,25},{9,17},{17,9},{25,1},{2,26},{10... | collective-permute-start | bytes 663560 | tf_op jit(solution)/shard_map/ppermute | solution.py:272
  55.2 0.6 collective-permute-start.17
  55.9 1.3 %shard_map.114 = (f32[48,5376]{1,0:T(8,128)}, f32[48,1536]{1,0:T(8,128)}, f32[48,1001]{1,0:T(8,128)}) custom-call(s32[1]{0:T(128)} %bitcast.index, f32[48,5376]{1,0:T(8,128)S(1)} %bitcast.24, f32[48,1536]{1,0:T(8,128)S(1)} %bitcast.26, f32[48,1001]{1,0:T(8,128)S(1)} %bitcast.28, bf16[48,2304]{1,0:T(8,128)(2,1)S(1)} %shard_map.113.rest_0_, ...), custom_call_target="tpu_custom_call" | custom-call | bytes 3923332 | tf_op jit(solution)/shard_map/pallas_call | solution.py:260
  57.2 4.3 %collective-permute-done.19.rest_3_ = bf16[48,2304]{1,0:T(8,128)(2,1)S(1)} collective-permute-done((bf16[48,2304]{1,0:T(8,128)(2,1)S(1)}, bf16[48,2304]{1,0:T(8,128)(2,1)S(1)}, u32[]{:S(2)}, u32[]{:S(2)}) %collective-permute-start.19) | collective-permute-done | bytes 221216 | tf_op jit(solution)/shard_map/ppermute | solution.py:272
  61.5 4.2 %collective-permute-done.18.rest_2_ = bf16[48,2304]{1,0:T(8,128)(2,1)S(1)} collective-permute-done((bf16[48,2304]{1,0:T(8,128)(2,1)S(1)}, bf16[48,2304]{1,0:T(8,128)(2,1)S(1)}, u32[]{:S(2)}, u32[]{:S(2)}) %collective-permute-start.18) | collective-permute-done | bytes 221216 | tf_op jit(solution)/shard_map/ppermute | solution.py:272
  65.7 0.9 %shard_map.118 = (bf16[48,5376]{1,0:T(8,128)(2,1)}, bf16[48,1536]{1,0:T(8,128)(2,1)}, bf16[48,1001]{1,0:T(8,128)(2,1)}) custom-call(s32[1]{0:T(128)} %bitcast.index, bf16[48,2304]{1,0:T(8,128)(2,1)S(1)} %shard_map.117.rest_0_, bf16[48,2304]{1,0:T(8,128)(2,1)S(1)} %collective-permute-done.17.rest_1_, bf16[48,2304]{1,0:T(8,128)(2,1)S(1)} %collective-permute-done.18.rest_2_, ...), custom_call_target="tpu_custom_call" | custom-call | bytes 1644388 | tf_op jit(solution)/shard_map/pallas_call | solution.py:260
  (32 shorter events, 0.3 us)
Async XLA Ops:
  0.6 10.6 %copy-start.2 = (f32[1,1536,48]{1,2,0:T(8,128)S(1)}, f32[1,1536,48]{1,2,0:T(8,128)}, u32[]{:S(2)}) copy-start(f32[1,1536,48]{1,2,0:T(8,128)} %param.10) | copy-start | bytes 884740
  0.6 10.6 %copy-start.3 = (f32[1001,48]{0,1:T(8,128)S(1)}, f32[1001,48]{0,1:T(8,128)}, u32[]{:S(2)}) copy-start(f32[1001,48]{0,1:T(8,128)} %param.11) | copy-start | bytes 576580
  3.3 9.3 %collective-permute-start.3 = (bf16[48,1152]{1,0:T(8,128)(2,1)}, bf16[48,1152]{1,0:T(8,128)(2,1)S(1)}, u32[]{:S(2)}, u32[]{:S(2)}) collective-permute-start(bf16[48,1152]{1,0:T(8,128)(2,1)} %get-tuple-element.34), channel_id=1, source_target_pairs={{0,8},{8,0},{16,24},{24,16},{1,9},{9,1},{17,25},{25,17},{2,10},{10... | collective-permute-start | bytes 331784 | tf_op jit(solution)/shard_map/ppermute | solution.py:272
  6.3 7.2 %collective-permute-start.4 = (bf16[48,1152]{1,0:T(8,128)(2,1)}, bf16[48,1152]{1,0:T(8,128)(2,1)S(1)}, u32[]{:S(2)}, u32[]{:S(2)}) collective-permute-start(bf16[48,1152]{1,0:T(8,128)(2,1)} %get-tuple-element.35), channel_id=1, source_target_pairs={{0,16},{8,24},{16,0},{24,8},{1,17},{9,25},{17,1},{25,9},{2,18},{10... | collective-permute-start | bytes 331784 | tf_op jit(solution)/shard_map/ppermute | solution.py:272
  7.8 6.7 %collective-permute-start.5 = (bf16[48,1152]{1,0:T(8,128)(2,1)}, bf16[48,1152]{1,0:T(8,128)(2,1)S(1)}, u32[]{:S(2)}, u32[]{:S(2)}) collective-permute-start(bf16[48,1152]{1,0:T(8,128)(2,1)} %get-tuple-element.36), channel_id=1, source_target_pairs={{0,24},{8,16},{16,8},{24,0},{1,25},{9,17},{17,9},{25,1},{2,26},{10... | collective-permute-start | bytes 331784 | tf_op jit(solution)/shard_map/ppermute | solution.py:272
  7.8 10.9 %collective-permute-start = (bf16[48,1152]{1,0:T(8,128)(2,1)}, bf16[48,1152]{1,0:T(8,128)(2,1)S(1)}, u32[]{:S(2)}, u32[]{:S(2)}) collective-permute-start(bf16[48,1152]{1,0:T(8,128)(2,1)} %get-tuple-element.28), channel_id=1, source_target_pairs={{0,8},{8,0},{16,24},{24,16},{1,9},{9,1},{17,25},{25,17},{2,10},{10... | collective-permute-start | bytes 331784 | tf_op jit(solution)/shard_map/ppermute | solution.py:272
  9.8 9.0 %collective-permute-start.1 = (bf16[48,1152]{1,0:T(8,128)(2,1)}, bf16[48,1152]{1,0:T(8,128)(2,1)S(1)}, u32[]{:S(2)}, u32[]{:S(2)}) collective-permute-start(bf16[48,1152]{1,0:T(8,128)(2,1)} %get-tuple-element.29), channel_id=1, source_target_pairs={{0,16},{8,24},{16,0},{24,8},{1,17},{9,25},{17,1},{25,9},{2,18},{10... | collective-permute-start | bytes 331784 | tf_op jit(solution)/shard_map/ppermute | solution.py:272
  11.3 1.2 %copy-start = (f32[1,48,5376]{2,1,0:T(8,128)S(1)}, f32[1,48,5376]{2,1,0:T(8,128)}, u32[]{:S(2)}) copy-start(f32[1,48,5376]{2,1,0:T(8,128)} %param.9) | copy-start | bytes 3096580
  12.5 0.9 %copy-start.6 = (bf16[48,1152]{1,0:T(8,128)(2,1)S(1)}, bf16[48,1152]{1,0:T(8,128)(2,1)}, u32[]{:S(2)}) copy-start(bf16[48,1152]{1,0:T(8,128)(2,1)} %get-tuple-element.30) | copy-start | bytes 331780
  12.5 2.0 %copy-start.5 = (bf16[48,1152]{1,0:T(8,128)(2,1)S(1)}, bf16[48,1152]{1,0:T(8,128)(2,1)}, u32[]{:S(2)}) copy-start(bf16[48,1152]{1,0:T(8,128)(2,1)} %get-tuple-element.33.rest_0_) | copy-start | bytes 331780
  13.4 5.6 %collective-permute-start.2 = (bf16[48,1152]{1,0:T(8,128)(2,1)S(1)}, bf16[48,1152]{1,0:T(8,128)(2,1)S(1)}, u32[]{:S(2)}, u32[]{:S(2)}) collective-permute-start(bf16[48,1152]{1,0:T(8,128)(2,1)S(1)} %copy-done.6), channel_id=1, source_target_pairs={{0,24},{8,16},{16,8},{24,0},{1,25},{9,17},{17,9},{25,1},{2,26},{10... | collective-permute-start | bytes 331784 | tf_op jit(solution)/shard_map/ppermute | solution.py:272
  14.5 4.6 %copy-start.4 = (bf16[48,1152]{1,0:T(8,128)(2,1)S(1)}, bf16[48,1152]{1,0:T(8,128)(2,1)}, u32[]{:S(2)}) copy-start(bf16[48,1152]{1,0:T(8,128)(2,1)} %get-tuple-element.27.rest_0_) | copy-start | bytes 331780
  14.6 6.1 %collective-permute-start.6 = (bf16[48,1152]{1,0:T(8,128)(2,1)S(1)}, bf16[48,1152]{1,0:T(8,128)(2,1)S(1)}, u32[]{:S(2)}, u32[]{:S(2)}) collective-permute-start(bf16[48,1152]{1,0:T(8,128)(2,1)S(1)} %get-tuple-element.38.rest_0_), channel_id=1, source_target_pairs={{0,2},{1,3},{2,0},{3,1},{4,6},{5,7},{6,4},{7,5},{8,10},{9,11},{10,... | collective-permute-start | bytes 331784 | tf_op jit(solution)/shard_map/ppermute | solution.py:272
  16.2 10.5 %collective-permute-start.15 = (bf16[48,1152]{1,0:T(8,128)(2,1)S(1)}, bf16[48,1152]{1,0:T(8,128)(2,1)S(1)}, u32[]{:S(2)}, u32[]{:S(2)}) collective-permute-start(bf16[48,1152]{1,0:T(8,128)(2,1)S(1)} %get-tuple-element.38.rest_0_), channel_id=1, source_target_pairs={{0,6},{1,7},{2,4},{3,5},{4,2},{5,3},{6,0},{7,1},{8,14},{9,15},{10,... | collective-permute-start | bytes 331784 | tf_op jit(solution)/shard_map/ppermute | solution.py:272
  18.7 12.7 %collective-permute-start.14 = (bf16[48,1152]{1,0:T(8,128)(2,1)S(1)}, bf16[48,1152]{1,0:T(8,128)(2,1)S(1)}, u32[]{:S(2)}, u32[]{:S(2)}) collective-permute-start(bf16[48,1152]{1,0:T(8,128)(2,1)S(1)} %get-tuple-element.38.rest_0_), channel_id=1, source_target_pairs={{0,4},{1,5},{2,6},{3,7},{4,0},{5,1},{6,2},{7,3},{8,12},{9,13},{10,... | collective-permute-start | bytes 331784 | tf_op jit(solution)/shard_map/ppermute | solution.py:272
  20.7 16.4 %collective-permute-start.8 = (bf16[48,2304]{1,0:T(8,128)(2,1)S(1)}, bf16[48,2304]{1,0:T(8,128)(2,1)S(1)}, u32[]{:S(2)}, u32[]{:S(2)}) collective-permute-start(bf16[48,2304]{1,0:T(8,128)(2,1)S(1)} %shard_map.113.rest_0_), channel_id=1, source_target_pairs={{0,16},{8,24},{16,0},{24,8},{1,17},{9,25},{17,1},{25,9},{2,18},{10... | collective-permute-start | bytes 663560 | tf_op jit(solution)/shard_map/ppermute | solution.py:272
  22.2 14.9 %collective-permute-start.7 = (bf16[48,2304]{1,0:T(8,128)(2,1)S(1)}, bf16[48,2304]{1,0:T(8,128)(2,1)S(1)}, u32[]{:S(2)}, u32[]{:S(2)}) collective-permute-start(bf16[48,2304]{1,0:T(8,128)(2,1)S(1)} %shard_map.113.rest_0_), channel_id=1, source_target_pairs={{0,8},{8,0},{16,24},{24,16},{1,9},{9,1},{17,25},{25,17},{2,10},{10... | collective-permute-start | bytes 663560 | tf_op jit(solution)/shard_map/ppermute | solution.py:272
  23.3 8.1 %collective-permute-start.12 = (bf16[48,1152]{1,0:T(8,128)(2,1)S(1)}, bf16[48,1152]{1,0:T(8,128)(2,1)S(1)}, u32[]{:S(2)}, u32[]{:S(2)}) collective-permute-start(bf16[48,1152]{1,0:T(8,128)(2,1)S(1)} %get-tuple-element.42.rest_0_.rest_4_), channel_id=1, source_target_pairs={{0,6},{1,7},{2,4},{3,5},{4,2},{5,3},{6,0},{7,1},{8,14},{9,15},{10,... | collective-permute-start | bytes 331784 | tf_op jit(solution)/shard_map/ppermute | solution.py:272
  26.7 9.4 %collective-permute-start.11 = (bf16[48,1152]{1,0:T(8,128)(2,1)S(1)}, bf16[48,1152]{1,0:T(8,128)(2,1)S(1)}, u32[]{:S(2)}, u32[]{:S(2)}) collective-permute-start(bf16[48,1152]{1,0:T(8,128)(2,1)S(1)} %get-tuple-element.42.rest_0_.rest_4_), channel_id=1, source_target_pairs={{0,4},{1,5},{2,6},{3,7},{4,0},{5,1},{6,2},{7,3},{8,12},{9,13},{10,... | collective-permute-start | bytes 331784 | tf_op jit(solution)/shard_map/ppermute | solution.py:272
  31.4 5.8 %collective-permute-start.10 = (bf16[48,1152]{1,0:T(8,128)(2,1)S(1)}, bf16[48,1152]{1,0:T(8,128)(2,1)S(1)}, u32[]{:S(2)}, u32[]{:S(2)}) collective-permute-start(bf16[48,1152]{1,0:T(8,128)(2,1)S(1)} %get-tuple-element.42.rest_0_.rest_4_), channel_id=1, source_target_pairs={{0,2},{1,3},{2,0},{3,1},{4,6},{5,7},{6,4},{7,5},{8,10},{9,11},{10,... | collective-permute-start | bytes 331784 | tf_op jit(solution)/shard_map/ppermute | solution.py:272
  31.4 8.3 %collective-permute-start.16 = (bf16[192,1152]{1,0:T(8,128)(2,1)S(1)}, bf16[192,1152]{1,0:T(8,128)(2,1)S(1)}, u32[]{:S(2)}, u32[]{:S(2)}) collective-permute-start(bf16[192,1152]{1,0:T(8,128)(2,1)S(1)} %shard_map.116.rest_2_), channel_id=1, source_target_pairs={{0,1},{1,0},{2,3},{3,2},{4,5},{5,4},{6,7},{7,6},{8,9},{9,8},{10,11... | collective-permute-start | bytes 1327112 | tf_op jit(solution)/shard_map/ppermute | solution.py:272
  37.2 18.7 %copy-start.1 = (f32[1,48,5376]{2,1,0:T(8,128)S(1)}, f32[1,48,5376]{2,1,0:T(8,128)}, u32[]{:S(2)}) copy-start(f32[1,48,5376]{2,1,0:T(8,128)} %param.9) | copy-start | bytes 3096580
  37.2 2.6 %collective-permute-start.13 = (bf16[192,1152]{1,0:T(8,128)(2,1)S(1)}, bf16[192,1152]{1,0:T(8,128)(2,1)S(1)}, u32[]{:S(2)}, u32[]{:S(2)}) collective-permute-start(bf16[192,1152]{1,0:T(8,128)(2,1)S(1)} %shard_map.115.rest_0_), channel_id=1, source_target_pairs={{0,1},{1,0},{2,3},{3,2},{4,5},{5,4},{6,7},{7,6},{8,9},{9,8},{10,11... | collective-permute-start | bytes 1327112 | tf_op jit(solution)/shard_map/ppermute | solution.py:272
  37.3 18.6 %collective-permute-start.9 = (bf16[48,2304]{1,0:T(8,128)(2,1)S(1)}, bf16[48,2304]{1,0:T(8,128)(2,1)S(1)}, u32[]{:S(2)}, u32[]{:S(2)}) collective-permute-start(bf16[48,2304]{1,0:T(8,128)(2,1)S(1)} %shard_map.113.rest_0_), channel_id=1, source_target_pairs={{0,24},{8,16},{16,8},{24,0},{1,25},{9,17},{17,9},{25,1},{2,26},{10... | collective-permute-start | bytes 663560 | tf_op jit(solution)/shard_map/ppermute | solution.py:272
  51.7 9.8 %collective-permute-start.19 = (bf16[48,2304]{1,0:T(8,128)(2,1)S(1)}, bf16[48,2304]{1,0:T(8,128)(2,1)S(1)}, u32[]{:S(2)}, u32[]{:S(2)}) collective-permute-start(bf16[48,2304]{1,0:T(8,128)(2,1)S(1)} %shard_map.117.rest_0_), channel_id=1, source_target_pairs={{0,24},{8,16},{16,8},{24,0},{1,25},{9,17},{17,9},{25,1},{2,26},{10... | collective-permute-start | bytes 663560 | tf_op jit(solution)/shard_map/ppermute | solution.py:272
  55.2 10.5 %collective-permute-start.18 = (bf16[48,2304]{1,0:T(8,128)(2,1)S(1)}, bf16[48,2304]{1,0:T(8,128)(2,1)S(1)}, u32[]{:S(2)}, u32[]{:S(2)}) collective-permute-start(bf16[48,2304]{1,0:T(8,128)(2,1)S(1)} %shard_map.117.rest_0_), channel_id=1, source_target_pairs={{0,16},{8,24},{16,0},{24,8},{1,17},{9,25},{17,1},{25,9},{2,18},{10... | collective-permute-start | bytes 663560 | tf_op jit(solution)/shard_map/ppermute | solution.py:272
  55.2 10.5 %collective-permute-start.17 = (bf16[48,2304]{1,0:T(8,128)(2,1)S(1)}, bf16[48,2304]{1,0:T(8,128)(2,1)S(1)}, u32[]{:S(2)}, u32[]{:S(2)}) collective-permute-start(bf16[48,2304]{1,0:T(8,128)(2,1)S(1)} %shard_map.117.rest_0_), channel_id=1, source_target_pairs={{0,8},{8,0},{16,24},{24,16},{1,9},{9,1},{17,25},{25,17},{2,10},{10... | collective-permute-start | bytes 663560 | tf_op jit(solution)/shard_map/ppermute | solution.py:272

commit v7 on v6

--- a/solution.py
+++ b/solution.py
@@ -21,8 +21,9 @@
 MOMENTUM = 0.95
 EPSILON = 1e-07
 
+FORWARD = (True, True)
 VMEM_LIMIT = 48 * 1024 * 1024
-VMEM_ALL = 63 * 1024 * 1024
+VMEM_ALL = 62 * 1024 * 1024
 
 WIDTHS = [QKV, D, MLP, ADA, MLP, CLASSES]
 OFFSETS = [0, QKV, QKV + D, QKV + D + MLP]
@@ -117,10 +118,13 @@
     out[:, half:] = right[...]
 
 
-def stack_kernel(count, *rest):
+def stack_kernel(blocks, *rest):
     out, rows = rest[-1], rest[0].shape[0]
-    for number in range(count):
-        out[number * rows : (number + 1) * rows, :] = rest[number][...]
+    for number, (first, *others) in enumerate(blocks):
+        value = rest[first][...]
+        for extra in others:
+            value = value + rest[extra][...]
+        out[number * rows : (number + 1) * rows, :] = value
 
 
 def newton_kernel(bins, halves, count, index, *rest):
@@ -210,14 +214,17 @@
 
 
 def momentum_kernel(bins, index, wide, down, embed, *rest):
-    n = len(bins)
-    pieces, (new_wide, new_down, new_embed) = rest[:n], rest[n:]
+    pieces, (new_wide, new_down, new_embed) = rest[:-3], rest[-3:]
     where = placed(bins)
+    rows = wide.shape[0]
+    each = pieces[0].shape[0] // rows
 
     def body(mine):
         for matrix in range(6):
             owner, offset = where[matrix]
-            g = pieces[mine ^ owner][:, offset : offset + PADDED[matrix]].astype(jnp.float32)
+            number, place = divmod(mine ^ owner, each)
+            block = pieces[number][place * rows : (place + 1) * rows, offset : offset + PADDED[matrix]]
+            g = block.astype(jnp.float32)
             if matrix == DOWN:
                 new_down[...] = MOMENTUM * down[...] + g
             elif matrix == EMBED:
@@ -276,16 +283,32 @@
     return [swap(value, axis, k, n) for k in range(1, n)]
 
 
-def stack(pieces, tied=()):
+def stack(pieces, tied=(), blocks=None):
     rows, width = pieces[0].shape
+    blocks = blocks or [[number] for number in range(len(pieces))]
     if rows % 16:
-        return jnp.concatenate(pieces, axis=0)
+        return jnp.concatenate([sum(pieces[i] for i in block) for block in blocks], axis=0)
     return call(
-        functools.partial(stack_kernel, len(pieces)),
-        [jax.ShapeDtypeStruct((rows * len(pieces), width), pieces[0].dtype)],
+        functools.partial(stack_kernel, blocks),
+        [jax.ShapeDtypeStruct((rows * len(blocks), width), pieces[0].dtype)],
         (*pieces, *tied),
         [VMEM] * len(pieces) + [ANY] * len(tied),
     )[0]
+
+
+def along(value, hops):
+    return lax.ppermute(value, "shard", [(2 * a + c, 2 * b + c) for a, b in hops for c in range(2)])
+
+
+def cross(value, n, forward):
+    if n == 8 and forward:
+        far = along(value, [(0, 2), (2, 0), (1, 3), (3, 1)])
+        near = along(value, [(0, 1), (1, 0), (2, 3), (3, 2)])
+        middle = along(value, [(1, 2), (2, 1)])
+        ends = along(far, [(2, 3), (1, 0)])
+        return [value, near, far, middle, ends], [[0], [1], [2], [3, 4]]
+    pieces = [value] + [swap(value, "shard", k, n) for k in range(2, n, 2)]
+    return pieces, [[number] for number in range(len(pieces))]
 
 
 def per_device(grad_wide, grad_down, grad_embed, mom_wide, mom_down, mom_embed):
@@ -314,7 +337,7 @@
         (index, *moms),
         [SMEM] + [VMEM] * 3,
     )
-    gs, arrived = [], []
+    gs, arrived, blocks = [], [], []
     for half, (low, high) in enumerate(windows):
         own, *others = sends[half * n_rep : (half + 1) * n_rep]
         received = [own] + [swap(piece, "rep", k + 1, n_rep) for k, piece in enumerate(others)]
@@ -325,17 +348,25 @@
             [VMEM] * (n_rep + 1),
         )
         gs.append(g)
-        arrived.append([y] + [swap(y, "shard", k, n_shard) for k in range(2, n_shard, 2)])
-    stacks = [None, stack(arrived[1], (arrived[0][0],))]
+        crossed = cross(y, n_shard, FORWARD[half])
+        arrived.append(crossed[0])
+        blocks.append(crossed[1])
+    stacks = [None, stack(arrived[1], (arrived[0][0],), blocks[1])]
     (g,) = call(join_kernel, [block(width)], (*gs, arrived[1][1]), [VMEM] * 2 + [ANY])
-    g_others = spread(g, "rep", n_rep)
-    stacks[0] = stack(arrived[0], g_others[:2])
+    g_first = swap(g, "rep", 1, n_rep)
+    g_pair = [g, g_first]
+    if n_rep == 4 and rows % 16 == 0:
+        twice = stack(g_pair)
+        g_all = [twice, swap(twice, "rep", 2, n_rep)]
+    else:
+        g_all = g_pair + spread(g, "rep", n_rep)[1:]
+    stacks[0] = stack(arrived[0], (g_first,), blocks[0])
     pieces = [piece for whole in stacks for piece in (whole, swap(whole, "shard", 1, n_shard))]
     (upd,) = call(
         functools.partial(newton_kernel, bins, 2, 2),
         [block(width)],
-        (index, *pieces),
-        [SMEM] + [VMEM] * len(pieces),
+        (index, *pieces, g_all[-1]),
+        [SMEM] + [VMEM] * len(pieces) + [ANY],
         (pltpu.VMEM((D, width), jnp.bfloat16),),
         flops=NS_ITERS * (4 * D * D * width + 2 * D * D * D),
     )
@@ -343,8 +374,8 @@
     news = call(
         functools.partial(momentum_kernel, bins),
         [jax.ShapeDtypeStruct(m.shape, jnp.float32) for m in moms],
-        (index, *moms, g, *g_others),
-        [SMEM] + [VMEM] * (3 + n_rep),
+        (index, *moms, *g_all),
+        [SMEM] + [VMEM] * (3 + len(g_all)),
     )
     updates = call(
         functools.partial(update_kernel, bins),

time: 66.9 us -> 73.9 us (1.10)
  waiting for transfers between devices: 18.4 us -> 23.3 us
  starting transfers between devices: 28.2 us -> 31.4 us
  local copies, waits for them, and re-layouts: 2.07 us -> 0.83 us
    ppermute x0 -> x8, starting transfers between devices: none -> 13.9 us  [along(): lax.ppermute(value, 'shard', [(2 * a + c, 2 * b + c) for a, b in hops for...]
    ppermute x20 -> x13, starting transfers between devices: 28.2 us -> 17.6 us  [swap(): return lax.ppermute(value, axis, [(i, i ^ k) for i in range(n)])]
    ppermute x0 -> x8, waiting for transfers between devices: none -> 5.03 us  [along(): lax.ppermute(value, 'shard', [(2 * a + c, 2 * b + c) for a, b in hops for...]
    unnamed x14 -> x12, local copies, waits for them, and re-layouts: 2.07 us -> 0.83 us
    ppermute x20 -> x13, waiting for transfers between devices: 18.4 us -> 18.3 us  [swap(): return lax.ppermute(value, axis, [(i, i ^ k) for i in range(n)])]
    pallas_call x10 -> x11, Pallas kernels: 17.1 us -> 17.3 us  [call(): pl.pallas_call(kernel, out_shape=tuple(outs), in_specs=specs, out_specs=t...]
  transfers between devices with their start and end apart: 20 -> 21, of which waited for: 8 -> 9; matrix products, arithmetic and copies ran while one was open for 0% -> 0% of each run, Pallas kernels for 20% -> 2%
where the time goes in v7:
time: 73.9 us; the launch traced here: 73.7 us
  starting transfers between devices  31.4 us (42%)
  waiting for transfers between devices  23.3 us (32%)
  Pallas kernels  17.3 us (23%)
  local copies, waits for them, and re-layouts  0.83 us (1%)
  between operations  0.83 us (1%)
    ppermute x13, waiting for transfers between devices, swap(): return lax.ppermute(value, axis, [(i, i ^ k) for i in range(n)])  18.3 us
    ppermute x13, starting transfers between devices, swap(): return lax.ppermute(value, axis, [(i, i ^ k) for i in range(n)])  17.6 us
    pallas_call x11, Pallas kernels, call(): pl.pallas_call(kernel, out_shape=tuple(outs), in_specs=specs, out_specs=t...  17.3 us
    ppermute x8, starting transfers between devices, along(): lax.ppermute(value, 'shard', [(2 * a + c, 2 * b + c) for a, b in hops for...  13.9 us
    ppermute x8, waiting for transfers between devices, along(): lax.ppermute(value, 'shard', [(2 * a + c, 2 * b + c) for a, b in hops for...  5.03 us
  transfers between devices with their start and end apart: 21, of which 9 were waited for; matrix products, arithmetic and copies ran while one was open for 0% of the time, Pallas kernels for 2%

profile of v7, /device:TPU:0, one launch (start us, length us, event | category | flops | bytes accessed | tf_op | source)
XLA Modules:
  0.0 73.7 jit_solution(14076679588382351005)
XLA Ops:
  0.7 2.7 %shard_map.110 = (bf16[48,1152]{1,0:T(8,128)(2,1)}, bf16[48,1152]{1,0:T(8,128)(2,1)}, bf16[48,1152]{1,0:T(8,128)(2,1)}, bf16[48,1152]{1,0:T(8,128)(2,1)}, bf16[4...) custom-call(s32[1]{0:T(128)} %bitcast.index, ...), custom_call_target="tpu_custom_call" | custom-call | bytes 2404036 | tf_op jit(solution)/shard_map/pallas_call | solution.py:267
  3.4 3.0 %collective-permute-start.3 = (bf16[48,1152]{1,0:T(8,128)(2,1)}, bf16[48,1152]{1,0:T(8,128)(2,1)S(1)}, u32[]{:S(2)}, u32[]{:S(2)}) collective-permute-start(bf16[48,1152]{1,0:T(8,128)(2,1)} %get-tuple-element.34), channel_id=1, source_target_pairs={{0,8},{8,0},{16,24},{24,16},{1,9},{9,1},{17,25},{25,17},{2,10},{10... | collective-permute-start | bytes 331784 | tf_op jit(solution)/shard_map/ppermute | solution.py:279
  6.3 1.5 %collective-permute-start.4 = (bf16[48,1152]{1,0:T(8,128)(2,1)}, bf16[48,1152]{1,0:T(8,128)(2,1)S(1)}, u32[]{:S(2)}, u32[]{:S(2)}) collective-permute-start(bf16[48,1152]{1,0:T(8,128)(2,1)} %get-tuple-element.35), channel_id=1, source_target_pairs={{0,16},{8,24},{16,0},{24,8},{1,17},{9,25},{17,1},{25,9},{2,18},{10... | collective-permute-start | bytes 331784 | tf_op jit(solution)/shard_map/ppermute | solution.py:279
  7.9 1.9 %collective-permute-start = (bf16[48,1152]{1,0:T(8,128)(2,1)}, bf16[48,1152]{1,0:T(8,128)(2,1)S(1)}, u32[]{:S(2)}, u32[]{:S(2)}) collective-permute-start(bf16[48,1152]{1,0:T(8,128)(2,1)} %get-tuple-element.28), channel_id=1, source_target_pairs={{0,8},{8,0},{16,24},{24,16},{1,9},{9,1},{17,25},{25,17},{2,10},{10... | collective-permute-start | bytes 331784 | tf_op jit(solution)/shard_map/ppermute | solution.py:279
  9.8 1.5 %collective-permute-start.1 = (bf16[48,1152]{1,0:T(8,128)(2,1)}, bf16[48,1152]{1,0:T(8,128)(2,1)S(1)}, u32[]{:S(2)}, u32[]{:S(2)}) collective-permute-start(bf16[48,1152]{1,0:T(8,128)(2,1)} %get-tuple-element.29), channel_id=1, source_target_pairs={{0,16},{8,24},{16,0},{24,8},{1,17},{9,25},{17,1},{25,9},{2,18},{10... | collective-permute-start | bytes 331784 | tf_op jit(solution)/shard_map/ppermute | solution.py:279
  11.4 0.8 %copy-done.5 = bf16[48,1152]{1,0:T(8,128)(2,1)S(1)} copy-done((bf16[48,1152]{1,0:T(8,128)(2,1)S(1)}, bf16[48,1152]{1,0:T(8,128)(2,1)}, u32[]{:S(2)}) %copy-start.5) | copy-done | bytes 110616
  12.2 1.0 %collective-permute-start.2 = (bf16[48,1152]{1,0:T(8,128)(2,1)S(1)}, bf16[48,1152]{1,0:T(8,128)(2,1)S(1)}, u32[]{:S(2)}, u32[]{:S(2)}) collective-permute-start(bf16[48,1152]{1,0:T(8,128)(2,1)S(1)} %copy-done.5), channel_id=1, source_target_pairs={{0,24},{8,16},{16,8},{24,0},{1,25},{9,17},{17,9},{25,1},{2,26},{10... | collective-permute-start | bytes 331784 | tf_op jit(solution)/shard_map/ppermute | solution.py:279
  13.2 0.8 %collective-permute-done.4.rest_2_ = bf16[48,1152]{1,0:T(8,128)(2,1)S(1)} collective-permute-done((bf16[48,1152]{1,0:T(8,128)(2,1)}, bf16[48,1152]{1,0:T(8,128)(2,1)S(1)}, u32[]{:S(2)}, u32[]{:S(2)}) %collective-permute-start.4) | collective-permute-done | bytes 110624 | tf_op jit(solution)/shard_map/ppermute | solution.py:279
  14.1 0.7 collective-permute-done.5.rest_3_
  14.8 1.6 %collective-permute-start.6 = (bf16[48,1152]{1,0:T(8,128)(2,1)S(1)}, bf16[48,1152]{1,0:T(8,128)(2,1)S(1)}, u32[]{:S(2)}, u32[]{:S(2)}) collective-permute-start(bf16[48,1152]{1,0:T(8,128)(2,1)S(1)} %get-tuple-element.38.rest_0_), channel_id=1, source_target_pairs={{0,2},{1,3},{2,0},{3,1},{4,6},{5,7},{6,4},{7,5},{8,10},{9,11},{10,... | collective-permute-start | bytes 331784 | tf_op jit(solution)/shard_map/ppermute | solution.py:300
  16.5 2.6 %collective-permute-start.14 = (bf16[48,1152]{1,0:T(8,128)(2,1)S(1)}, bf16[48,1152]{1,0:T(8,128)(2,1)S(1)}, u32[]{:S(2)}, u32[]{:S(2)}) collective-permute-start(bf16[48,1152]{1,0:T(8,128)(2,1)S(1)} %get-tuple-element.38.rest_0_), channel_id=1, source_target_pairs={{0,4},{1,5},{4,0},{5,1},{2,6},{3,7},{6,2},{7,3},{8,12},{9,13},{12,... | collective-permute-start | bytes 331784 | tf_op jit(solution)/shard_map/ppermute | solution.py:300
  19.1 0.1 shard_map.111
  19.2 0.5 collective-permute-done.6.rest_0_.rest_1_
  19.7 1.5 %collective-permute-start.7 = (bf16[48,2304]{1,0:T(8,128)(2,1)S(1)}, bf16[48,2304]{1,0:T(8,128)(2,1)S(1)}, u32[]{:S(2)}, u32[]{:S(2)}) collective-permute-start(bf16[48,2304]{1,0:T(8,128)(2,1)S(1)} %shard_map.113.rest_0_), channel_id=1, source_target_pairs={{0,8},{8,0},{16,24},{24,16},{1,9},{9,1},{17,25},{25,17},{2,10},{10... | collective-permute-start | bytes 663560 | tf_op jit(solution)/shard_map/ppermute | solution.py:279
  21.2 2.0 %collective-permute-start.10 = (bf16[48,1152]{1,0:T(8,128)(2,1)S(1)}, bf16[48,1152]{1,0:T(8,128)(2,1)S(1)}, u32[]{:S(2)}, u32[]{:S(2)}) collective-permute-start(bf16[48,1152]{1,0:T(8,128)(2,1)S(1)} %get-tuple-element.42.rest_0_.rest_5_), channel_id=1, source_target_pairs={{0,4},{1,5},{4,0},{5,1},{2,6},{3,7},{6,2},{7,3},{8,12},{9,13},{12,... | collective-permute-start | bytes 331784 | tf_op jit(solution)/shard_map/ppermute | solution.py:300
  23.2 0.7 collective-permute-start.15
  23.8 1.0 %collective-permute-done.14.rest_2_ = bf16[48,1152]{1,0:T(8,128)(2,1)S(1)} collective-permute-done((bf16[48,1152]{1,0:T(8,128)(2,1)S(1)}, bf16[48,1152]{1,0:T(8,128)(2,1)S(1)}, u32[]{:S(2)}, u32[]{:S(2)}) %collective-permute-start.14) | collective-permute-done | bytes 110624 | tf_op jit(solution)/shard_map/ppermute | solution.py:300
  24.8 1.3 %collective-permute-start.16 = (bf16[48,1152]{1,0:T(8,128)(2,1)S(1)}, bf16[48,1152]{1,0:T(8,128)(2,1)S(1)}, u32[]{:S(2)}, u32[]{:S(2)}) collective-permute-start(bf16[48,1152]{1,0:T(8,128)(2,1)S(1)} %collective-permute-done.14.rest_2_), channel_id=1, source_target_pairs={{4,6},{5,7},{2,0},{3,1},{12,14},{13,15},{10,8},{11,9},{20,22},{21,... | collective-permute-start | bytes 331784 | tf_op jit(solution)/shard_map/ppermute | solution.py:300
  26.1 0.7 collective-permute-start.11
  26.8 1.5 %collective-permute-done.10.rest_2_ = bf16[48,1152]{1,0:T(8,128)(2,1)S(1)} collective-permute-done((bf16[48,1152]{1,0:T(8,128)(2,1)S(1)}, bf16[48,1152]{1,0:T(8,128)(2,1)S(1)}, u32[]{:S(2)}, u32[]{:S(2)}) %collective-permute-start.10) | collective-permute-done | bytes 110624 | tf_op jit(solution)/shard_map/ppermute | solution.py:300
  28.3 3.7 %collective-permute-start.9 = (bf16[48,1152]{1,0:T(8,128)(2,1)S(1)}, bf16[48,1152]{1,0:T(8,128)(2,1)S(1)}, u32[]{:S(2)}, u32[]{:S(2)}) collective-permute-start(bf16[48,1152]{1,0:T(8,128)(2,1)S(1)} %get-tuple-element.42.rest_0_.rest_5_), channel_id=1, source_target_pairs={{0,2},{1,3},{2,0},{3,1},{4,6},{5,7},{6,4},{7,5},{8,10},{9,11},{10,... | collective-permute-start | bytes 331784 | tf_op jit(solution)/shard_map/ppermute | solution.py:300
  32.1 1.3 %collective-permute-start.12 = (bf16[48,1152]{1,0:T(8,128)(2,1)S(1)}, bf16[48,1152]{1,0:T(8,128)(2,1)S(1)}, u32[]{:S(2)}, u32[]{:S(2)}) collective-permute-start(bf16[48,1152]{1,0:T(8,128)(2,1)S(1)} %collective-permute-done.10.rest_2_), channel_id=1, source_target_pairs={{4,6},{5,7},{2,0},{3,1},{12,14},{13,15},{10,8},{11,9},{20,22},{21,... | collective-permute-start | bytes 331784 | tf_op jit(solution)/shard_map/ppermute | solution.py:300
  33.5 3.2 %collective-permute-start.8 = (bf16[96,2304]{1,0:T(8,128)(2,1)S(1)}, bf16[96,2304]{1,0:T(8,128)(2,1)S(1)}, u32[]{:S(2)}, u32[]{:S(2)}) collective-permute-start(bf16[96,2304]{1,0:T(8,128)(2,1)S(1)} %shard_map.114.rest_0_), channel_id=1, source_target_pairs={{0,16},{8,24},{16,0},{24,8},{1,17},{9,25},{17,1},{25,9},{2,18},{10... | collective-permute-start | bytes 1327112 | tf_op jit(solution)/shard_map/ppermute | solution.py:279
  36.7 2.0 %collective-permute-done.12.rest_4_ = bf16[48,1152]{1,0:T(8,128)(2,1)S(1)} collective-permute-done((bf16[48,1152]{1,0:T(8,128)(2,1)S(1)}, bf16[48,1152]{1,0:T(8,128)(2,1)S(1)}, u32[]{:S(2)}, u32[]{:S(2)}) %collective-permute-start.12) | collective-permute-done | bytes 110624 | tf_op jit(solution)/shard_map/ppermute | solution.py:300
  38.8 8.7 %collective-permute-done.8.rest_1_.rest_4_ = bf16[96,2304]{1,0:T(8,128)(2,1)S(1)} collective-permute-done((bf16[96,2304]{1,0:T(8,128)(2,1)S(1)}, bf16[96,2304]{1,0:T(8,128)(2,1)S(1)}, u32[]{:S(2)}, u32[]{:S(2)}) %collective-permute-start.8) | collective-permute-done | bytes 442400 | tf_op jit(solution)/shard_map/ppermute | solution.py:279
  47.5 12.0 %shard_map.118.rest_0_ = bf16[48,2304]{1,0:T(8,128)(2,1)S(1)} custom-call(s32[1]{0:T(128)} %bitcast.index, bf16[192,1152]{1,0:T(8,128)(2,1)S(1)} %shard_map.116.rest_0_, bf16[192,1152]{1,0:T(8,128)(2,1)S(1)} %collective-permute-done.13.rest_1_, bf16[192,1152]{1,0:T(8,128)(2,1)S(1)} %shard_map.117.rest_2_, ...), custom_call_target="tpu_custom_call" | custom-call | flops 7361003520 | bytes 2433028 | tf_op jit(solution)/shard_map/pallas_call | solution.py:267
  59.5 3.2 %collective-permute-start.20 = (bf16[48,2304]{1,0:T(8,128)(2,1)S(1)}, bf16[48,2304]{1,0:T(8,128)(2,1)S(1)}, u32[]{:S(2)}, u32[]{:S(2)}) collective-permute-start(bf16[48,2304]{1,0:T(8,128)(2,1)S(1)} %shard_map.118.rest_0_), channel_id=1, source_target_pairs={{0,24},{8,16},{16,8},{24,0},{1,25},{9,17},{17,9},{25,1},{2,26},{10... | collective-permute-start | bytes 663560 | tf_op jit(solution)/shard_map/ppermute | solution.py:279
  62.7 0.6 collective-permute-start.18
  63.3 1.3 %shard_map.115 = (f32[48,5376]{1,0:T(8,128)}, f32[48,1536]{1,0:T(8,128)}, f32[48,1001]{1,0:T(8,128)}) custom-call(s32[1]{0:T(128)} %bitcast.index, f32[48,5376]{1,0:T(8,128)S(1)} %bitcast.24, f32[48,1536]{1,0:T(8,128)S(1)} %bitcast.26, f32[48,1001]{1,0:T(8,128)S(1)} %bitcast.28, bf16[96,2304]{1,0:T(8,128)(2,1)S(1)} %shard_map.114.rest_0_, ...), custom_call_target="tpu_custom_call" | custom-call | bytes 3923332 | tf_op jit(solution)/shard_map/pallas_call | solution.py:267
  64.6 4.4 %collective-permute-done.20.rest_3_ = bf16[48,2304]{1,0:T(8,128)(2,1)S(1)} collective-permute-done((bf16[48,2304]{1,0:T(8,128)(2,1)S(1)}, bf16[48,2304]{1,0:T(8,128)(2,1)S(1)}, u32[]{:S(2)}, u32[]{:S(2)}) %collective-permute-start.20) | collective-permute-done | bytes 221216 | tf_op jit(solution)/shard_map/ppermute | solution.py:279
  69.0 3.7 %collective-permute-done.19.rest_2_ = bf16[48,2304]{1,0:T(8,128)(2,1)S(1)} collective-permute-done((bf16[48,2304]{1,0:T(8,128)(2,1)S(1)}, bf16[48,2304]{1,0:T(8,128)(2,1)S(1)}, u32[]{:S(2)}, u32[]{:S(2)}) %collective-permute-start.19) | collective-permute-done | bytes 221216 | tf_op jit(solution)/shard_map/ppermute | solution.py:279
  72.7 0.9 %shard_map.119 = (bf16[48,5376]{1,0:T(8,128)(2,1)}, bf16[48,1536]{1,0:T(8,128)(2,1)}, bf16[48,1001]{1,0:T(8,128)(2,1)}) custom-call(s32[1]{0:T(128)} %bitcast.index, bf16[48,2304]{1,0:T(8,128)(2,1)S(1)} %shard_map.118.rest_0_, bf16[48,2304]{1,0:T(8,128)(2,1)S(1)} %collective-permute-done.18.rest_1_, bf16[48,2304]{1,0:T(8,128)(2,1)S(1)} %collective-permute-done.19.rest_2_, ...), custom_call_target="tpu_custom_call" | custom-call | bytes 1644388 | tf_op jit(solution)/shard_map/pallas_call | solution.py:267
  (33 shorter events, 0.5 us)
Async XLA Ops:
  0.6 10.7 %copy-start = (f32[1,48,5376]{2,1,0:T(8,128)S(1)}, f32[1,48,5376]{2,1,0:T(8,128)}, u32[]{:S(2)}) copy-start(f32[1,48,5376]{2,1,0:T(8,128)} %param.9) | copy-start | bytes 3096580
  0.6 10.7 %copy-start.1 = (f32[1,1536,48]{1,2,0:T(8,128)S(1)}, f32[1,1536,48]{1,2,0:T(8,128)}, u32[]{:S(2)}) copy-start(f32[1,1536,48]{1,2,0:T(8,128)} %param.10) | copy-start | bytes 884740
  0.7 10.7 %copy-start.2 = (f32[1001,48]{0,1:T(8,128)S(1)}, f32[1001,48]{0,1:T(8,128)}, u32[]{:S(2)}) copy-start(f32[1001,48]{0,1:T(8,128)} %param.11) | copy-start | bytes 576580
  3.4 8.1 %collective-permute-start.3 = (bf16[48,1152]{1,0:T(8,128)(2,1)}, bf16[48,1152]{1,0:T(8,128)(2,1)S(1)}, u32[]{:S(2)}, u32[]{:S(2)}) collective-permute-start(bf16[48,1152]{1,0:T(8,128)(2,1)} %get-tuple-element.34), channel_id=1, source_target_pairs={{0,8},{8,0},{16,24},{24,16},{1,9},{9,1},{17,25},{25,17},{2,10},{10... | collective-permute-start | bytes 331784 | tf_op jit(solution)/shard_map/ppermute | solution.py:279
  6.3 7.7 %collective-permute-start.4 = (bf16[48,1152]{1,0:T(8,128)(2,1)}, bf16[48,1152]{1,0:T(8,128)(2,1)S(1)}, u32[]{:S(2)}, u32[]{:S(2)}) collective-permute-start(bf16[48,1152]{1,0:T(8,128)(2,1)} %get-tuple-element.35), channel_id=1, source_target_pairs={{0,16},{8,24},{16,0},{24,8},{1,17},{9,25},{17,1},{25,9},{2,18},{10... | collective-permute-start | bytes 331784 | tf_op jit(solution)/shard_map/ppermute | solution.py:279
  7.9 6.9 %collective-permute-start.5 = (bf16[48,1152]{1,0:T(8,128)(2,1)}, bf16[48,1152]{1,0:T(8,128)(2,1)S(1)}, u32[]{:S(2)}, u32[]{:S(2)}) collective-permute-start(bf16[48,1152]{1,0:T(8,128)(2,1)} %get-tuple-element.36), channel_id=1, source_target_pairs={{0,24},{8,16},{16,8},{24,0},{1,25},{9,17},{17,9},{25,1},{2,26},{10... | collective-permute-start | bytes 331784 | tf_op jit(solution)/shard_map/ppermute | solution.py:279
  7.9 11.2 %collective-permute-start = (bf16[48,1152]{1,0:T(8,128)(2,1)}, bf16[48,1152]{1,0:T(8,128)(2,1)S(1)}, u32[]{:S(2)}, u32[]{:S(2)}) collective-permute-start(bf16[48,1152]{1,0:T(8,128)(2,1)} %get-tuple-element.28), channel_id=1, source_target_pairs={{0,8},{8,0},{16,24},{24,16},{1,9},{9,1},{17,25},{25,17},{2,10},{10... | collective-permute-start | bytes 331784 | tf_op jit(solution)/shard_map/ppermute | solution.py:279
  9.8 9.2 %collective-permute-start.1 = (bf16[48,1152]{1,0:T(8,128)(2,1)}, bf16[48,1152]{1,0:T(8,128)(2,1)S(1)}, u32[]{:S(2)}, u32[]{:S(2)}) collective-permute-start(bf16[48,1152]{1,0:T(8,128)(2,1)} %get-tuple-element.29), channel_id=1, source_target_pairs={{0,16},{8,24},{16,0},{24,8},{1,17},{9,25},{17,1},{25,9},{2,18},{10... | collective-permute-start | bytes 331784 | tf_op jit(solution)/shard_map/ppermute | solution.py:279
  11.4 0.9 %copy-start.5 = (bf16[48,1152]{1,0:T(8,128)(2,1)S(1)}, bf16[48,1152]{1,0:T(8,128)(2,1)}, u32[]{:S(2)}) copy-start(bf16[48,1152]{1,0:T(8,128)(2,1)} %get-tuple-element.30) | copy-start | bytes 331780
  11.4 3.4 %copy-start.4 = (bf16[48,1152]{1,0:T(8,128)(2,1)S(1)}, bf16[48,1152]{1,0:T(8,128)(2,1)}, u32[]{:S(2)}) copy-start(bf16[48,1152]{1,0:T(8,128)(2,1)} %get-tuple-element.33.rest_0_) | copy-start | bytes 331780
  12.2 6.8 %collective-permute-start.2 = (bf16[48,1152]{1,0:T(8,128)(2,1)S(1)}, bf16[48,1152]{1,0:T(8,128)(2,1)S(1)}, u32[]{:S(2)}, u32[]{:S(2)}) collective-permute-start(bf16[48,1152]{1,0:T(8,128)(2,1)S(1)} %copy-done.5), channel_id=1, source_target_pairs={{0,24},{8,16},{16,8},{24,0},{1,25},{9,17},{17,9},{25,1},{2,26},{10... | collective-permute-start | bytes 331784 | tf_op jit(solution)/shard_map/ppermute | solution.py:279
  14.7 4.3 %copy-start.3 = (bf16[48,1152]{1,0:T(8,128)(2,1)S(1)}, bf16[48,1152]{1,0:T(8,128)(2,1)}, u32[]{:S(2)}) copy-start(bf16[48,1152]{1,0:T(8,128)(2,1)} %get-tuple-element.27.rest_0_) | copy-start | bytes 331780
  14.8 4.9 %collective-permute-start.6 = (bf16[48,1152]{1,0:T(8,128)(2,1)S(1)}, bf16[48,1152]{1,0:T(8,128)(2,1)S(1)}, u32[]{:S(2)}, u32[]{:S(2)}) collective-permute-start(bf16[48,1152]{1,0:T(8,128)(2,1)S(1)} %get-tuple-element.38.rest_0_), channel_id=1, source_target_pairs={{0,2},{1,3},{2,0},{3,1},{4,6},{5,7},{6,4},{7,5},{8,10},{9,11},{10,... | collective-permute-start | bytes 331784 | tf_op jit(solution)/shard_map/ppermute | solution.py:300
  16.5 8.4 %collective-permute-start.14 = (bf16[48,1152]{1,0:T(8,128)(2,1)S(1)}, bf16[48,1152]{1,0:T(8,128)(2,1)S(1)}, u32[]{:S(2)}, u32[]{:S(2)}) collective-permute-start(bf16[48,1152]{1,0:T(8,128)(2,1)S(1)} %get-tuple-element.38.rest_0_), channel_id=1, source_target_pairs={{0,4},{1,5},{4,0},{5,1},{2,6},{3,7},{6,2},{7,3},{8,12},{9,13},{12,... | collective-permute-start | bytes 331784 | tf_op jit(solution)/shard_map/ppermute | solution.py:300
  19.7 13.8 %collective-permute-start.7 = (bf16[48,2304]{1,0:T(8,128)(2,1)S(1)}, bf16[48,2304]{1,0:T(8,128)(2,1)S(1)}, u32[]{:S(2)}, u32[]{:S(2)}) collective-permute-start(bf16[48,2304]{1,0:T(8,128)(2,1)S(1)} %shard_map.113.rest_0_), channel_id=1, source_target_pairs={{0,8},{8,0},{16,24},{24,16},{1,9},{9,1},{17,25},{25,17},{2,10},{10... | collective-permute-start | bytes 663560 | tf_op jit(solution)/shard_map/ppermute | solution.py:279
  21.2 7.1 %collective-permute-start.10 = (bf16[48,1152]{1,0:T(8,128)(2,1)S(1)}, bf16[48,1152]{1,0:T(8,128)(2,1)S(1)}, u32[]{:S(2)}, u32[]{:S(2)}) collective-permute-start(bf16[48,1152]{1,0:T(8,128)(2,1)S(1)} %get-tuple-element.42.rest_0_.rest_5_), channel_id=1, source_target_pairs={{0,4},{1,5},{4,0},{5,1},{2,6},{3,7},{6,2},{7,3},{8,12},{9,13},{12,... | collective-permute-start | bytes 331784 | tf_op jit(solution)/shard_map/ppermute | solution.py:300
  23.2 8.9 %collective-permute-start.15 = (bf16[48,1152]{1,0:T(8,128)(2,1)S(1)}, bf16[48,1152]{1,0:T(8,128)(2,1)S(1)}, u32[]{:S(2)}, u32[]{:S(2)}) collective-permute-start(bf16[48,1152]{1,0:T(8,128)(2,1)S(1)} %get-tuple-element.38.rest_0_), channel_id=1, source_target_pairs={{2,4},{3,5},{4,2},{5,3},{10,12},{11,13},{12,10},{13,11},{18,20},{1... | collective-permute-start | bytes 331784 | tf_op jit(solution)/shard_map/ppermute | solution.py:300
  24.8 8.5 %collective-permute-start.16 = (bf16[48,1152]{1,0:T(8,128)(2,1)S(1)}, bf16[48,1152]{1,0:T(8,128)(2,1)S(1)}, u32[]{:S(2)}, u32[]{:S(2)}) collective-permute-start(bf16[48,1152]{1,0:T(8,128)(2,1)S(1)} %collective-permute-done.14.rest_2_), channel_id=1, source_target_pairs={{4,6},{5,7},{2,0},{3,1},{12,14},{13,15},{10,8},{11,9},{20,22},{21,... | collective-permute-start | bytes 331784 | tf_op jit(solution)/shard_map/ppermute | solution.py:300
  26.1 10.6 %collective-permute-start.11 = (bf16[48,1152]{1,0:T(8,128)(2,1)S(1)}, bf16[48,1152]{1,0:T(8,128)(2,1)S(1)}, u32[]{:S(2)}, u32[]{:S(2)}) collective-permute-start(bf16[48,1152]{1,0:T(8,128)(2,1)S(1)} %get-tuple-element.42.rest_0_.rest_5_), channel_id=1, source_target_pairs={{2,4},{3,5},{4,2},{5,3},{10,12},{11,13},{12,10},{13,11},{18,20},{1... | collective-permute-start | bytes 331784 | tf_op jit(solution)/shard_map/ppermute | solution.py:300
  28.3 8.4 %collective-permute-start.9 = (bf16[48,1152]{1,0:T(8,128)(2,1)S(1)}, bf16[48,1152]{1,0:T(8,128)(2,1)S(1)}, u32[]{:S(2)}, u32[]{:S(2)}) collective-permute-start(bf16[48,1152]{1,0:T(8,128)(2,1)S(1)} %get-tuple-element.42.rest_0_.rest_5_), channel_id=1, source_target_pairs={{0,2},{1,3},{2,0},{3,1},{4,6},{5,7},{6,4},{7,5},{8,10},{9,11},{10,... | collective-permute-start | bytes 331784 | tf_op jit(solution)/shard_map/ppermute | solution.py:300
  32.1 6.6 %collective-permute-start.12 = (bf16[48,1152]{1,0:T(8,128)(2,1)S(1)}, bf16[48,1152]{1,0:T(8,128)(2,1)S(1)}, u32[]{:S(2)}, u32[]{:S(2)}) collective-permute-start(bf16[48,1152]{1,0:T(8,128)(2,1)S(1)} %collective-permute-done.10.rest_2_), channel_id=1, source_target_pairs={{4,6},{5,7},{2,0},{3,1},{12,14},{13,15},{10,8},{11,9},{20,22},{21,... | collective-permute-start | bytes 331784 | tf_op jit(solution)/shard_map/ppermute | solution.py:300
  33.4 5.4 %collective-permute-start.17 = (bf16[192,1152]{1,0:T(8,128)(2,1)S(1)}, bf16[192,1152]{1,0:T(8,128)(2,1)S(1)}, u32[]{:S(2)}, u32[]{:S(2)}) collective-permute-start(bf16[192,1152]{1,0:T(8,128)(2,1)S(1)} %shard_map.117.rest_2_), channel_id=1, source_target_pairs={{0,1},{1,0},{2,3},{3,2},{4,5},{5,4},{6,7},{7,6},{8,9},{9,8},{10,11... | collective-permute-start | bytes 1327112 | tf_op jit(solution)/shard_map/ppermute | solution.py:279
  33.5 14.0 %collective-permute-start.8 = (bf16[96,2304]{1,0:T(8,128)(2,1)S(1)}, bf16[96,2304]{1,0:T(8,128)(2,1)S(1)}, u32[]{:S(2)}, u32[]{:S(2)}) collective-permute-start(bf16[96,2304]{1,0:T(8,128)(2,1)S(1)} %shard_map.114.rest_0_), channel_id=1, source_target_pairs={{0,16},{8,24},{16,0},{24,8},{1,17},{9,25},{17,1},{25,9},{2,18},{10... | collective-permute-start | bytes 1327112 | tf_op jit(solution)/shard_map/ppermute | solution.py:279
  38.7 8.8 %collective-permute-start.13 = (bf16[192,1152]{1,0:T(8,128)(2,1)S(1)}, bf16[192,1152]{1,0:T(8,128)(2,1)S(1)}, u32[]{:S(2)}, u32[]{:S(2)}) collective-permute-start(bf16[192,1152]{1,0:T(8,128)(2,1)S(1)} %shard_map.116.rest_0_), channel_id=1, source_target_pairs={{0,1},{1,0},{2,3},{3,2},{4,5},{5,4},{6,7},{7,6},{8,9},{9,8},{10,11... | collective-permute-start | bytes 1327112 | tf_op jit(solution)/shard_map/ppermute | solution.py:279
  59.5 9.5 %collective-permute-start.20 = (bf16[48,2304]{1,0:T(8,128)(2,1)S(1)}, bf16[48,2304]{1,0:T(8,128)(2,1)S(1)}, u32[]{:S(2)}, u32[]{:S(2)}) collective-permute-start(bf16[48,2304]{1,0:T(8,128)(2,1)S(1)} %shard_map.118.rest_0_), channel_id=1, source_target_pairs={{0,24},{8,16},{16,8},{24,0},{1,25},{9,17},{17,9},{25,1},{2,26},{10... | collective-permute-start | bytes 663560 | tf_op jit(solution)/shard_map/ppermute | solution.py:279
  62.7 10.0 %collective-permute-start.19 = (bf16[48,2304]{1,0:T(8,128)(2,1)S(1)}, bf16[48,2304]{1,0:T(8,128)(2,1)S(1)}, u32[]{:S(2)}, u32[]{:S(2)}) collective-permute-start(bf16[48,2304]{1,0:T(8,128)(2,1)S(1)} %shard_map.118.rest_0_), channel_id=1, source_target_pairs={{0,16},{8,24},{16,0},{24,8},{1,17},{9,25},{17,1},{25,9},{2,18},{10... | collective-permute-start | bytes 663560 | tf_op jit(solution)/shard_map/ppermute | solution.py:279
  62.7 10.0 %collective-permute-start.18 = (bf16[48,2304]{1,0:T(8,128)(2,1)S(1)}, bf16[48,2304]{1,0:T(8,128)(2,1)S(1)}, u32[]{:S(2)}, u32[]{:S(2)}) collective-permute-start(bf16[48,2304]{1,0:T(8,128)(2,1)S(1)} %shard_map.118.rest_0_), channel_id=1, source_target_pairs={{0,8},{8,0},{16,24},{24,16},{1,9},{9,1},{17,25},{25,17},{2,10},{10... | collective-permute-start | bytes 663560 | tf_op jit(solution)/shard_map/ppermute | solution.py:279

commit v8 on v6

--- a/solution.py
+++ b/solution.py
@@ -22,13 +22,14 @@
 EPSILON = 1e-07
 
 VMEM_LIMIT = 48 * 1024 * 1024
-VMEM_ALL = 63 * 1024 * 1024
+VMEM_ALL = 62 * 1024 * 1024
 
 WIDTHS = [QKV, D, MLP, ADA, MLP, CLASSES]
 OFFSETS = [0, QKV, QKV + D, QKV + D + MLP]
 PADDED = [-(-width // 128) * 128 for width in WIDTHS]
 DOWN, EMBED = 4, 5
 TILE = 256
+SPLIT = 256
 
 
 def plan(n_rep):
@@ -144,44 +145,55 @@
             spans.append((slice(offset, end), tiles, math.sqrt(max(D, WIDTHS[matrix]))))
             offset = end
 
+        def product(left, right, sides):
+            return lax.dot_general(left, right, ((sides[0], sides[1]), ((), ())), preferred_element_type=jnp.float32)
+
+        def symmetric(left, corner):
+            right = jnp.concatenate([left[SPLIT:, :].T, corner], axis=0)
+            return jnp.concatenate([left, right], axis=1)
+
         def outer(span):
-            x = x_ref[:, span]
-            return lax.dot_general(x, x, (((1,), (1,)), ((), ())), preferred_element_type=jnp.float32)
-
-        def polynomial(gram):
+            sides = ((1,), (1,))
+            left = product(x_ref[:, span], x_ref[:SPLIT, span], sides)
+            low = x_ref[SPLIT:, span]
+            return symmetric(left, product(low, low, sides))
+
+        def polynomial(gram, scale=1.0):
             gram = gram.astype(jnp.bfloat16)
-            square = jnp.dot(gram, gram, preferred_element_type=jnp.float32)
-            return COEF_B * gram.astype(jnp.float32) + COEF_C * square
-
-        def advance(tiles, poly, factor):
+            sides = ((1,), (0,))
+
+            def entries(value, square, diagonal):
+                value = COEF_B * value.astype(jnp.float32) + COEF_C * square
+                return scale * (value + jnp.where(diagonal, COEF_A, 0.0))
+
+            left = entries(gram[:, :SPLIT], product(gram, gram[:, :SPLIT], sides), diagonal[:, :SPLIT])
+            corner = product(gram[SPLIT:, :], gram[:, SPLIT:], sides)
+            corner = entries(gram[SPLIT:, SPLIT:], corner, diagonal[SPLIT:, SPLIT:])
+            return symmetric(left, corner).astype(jnp.bfloat16)
+
+        def advance(tiles, poly):
             for tile in tiles:
-                x = x_ref[:, tile]
-                x_ref[:, tile] = (
-                    factor * x.astype(jnp.float32) + jnp.dot(poly, x, preferred_element_type=jnp.float32)
-                ).astype(jnp.bfloat16)
-
-        diagonal = lax.broadcasted_iota(jnp.int32, (D, D), 0) == lax.broadcasted_iota(jnp.int32, (D, D), 1)
+                x_ref[:, tile] = product(poly, x_ref[:, tile], ((1,), (0,))).astype(jnp.bfloat16)
+
+        row = lax.broadcasted_iota(jnp.int32, (D, D), 0)
+        diagonal = row == lax.broadcasted_iota(jnp.int32, (D, D), 1)
         for span, tiles, _ in spans:
             gram = outer(span)
             scale = 1.0 / (jnp.sqrt(jnp.sum(jnp.where(diagonal, gram, 0.0))) + EPSILON)
-            poly = (scale * polynomial(gram * scale * scale)).astype(jnp.bfloat16)
-            advance(tiles, poly, COEF_A * scale)
+            advance(tiles, polynomial(gram * scale * scale, scale))
 
         def step(_, carry):
-            polys = [polynomial(outer(span)).astype(jnp.bfloat16) for span, _, _ in spans]
+            polys = [polynomial(outer(span)) for span, _, _ in spans]
             for poly, (_, tiles, _) in zip(polys, spans):
-                advance(tiles, poly, COEF_A)
+                advance(tiles, poly)
             return carry
 
         lax.fori_loop(0, NS_ITERS - 2, step, 0)
         for span, tiles, factor in spans:
-            poly = polynomial(outer(span))[:rows].astype(jnp.bfloat16)
+            poly = polynomial(outer(span))[:rows]
             for tile in tiles:
-                x = x_ref[:, tile]
-                out[:, tile] = (
-                    factor
-                    * (COEF_A * x[:rows].astype(jnp.float32) + jnp.dot(poly, x, preferred_element_type=jnp.float32))
-                ).astype(jnp.bfloat16)
+                value = product(poly, x_ref[:, tile], ((1,), (0,)))
+                out[:, tile] = (factor * value).astype(jnp.bfloat16)
 
     for target, group in enumerate(bins):
         if group:

time: 66.9 us -> 66.8 us (level)
  local copies, waits for them, and re-layouts: 2.07 us -> 0.83 us
  Pallas kernels: 17.1 us -> 18.3 us
    unnamed x14 -> x12, local copies, waits for them, and re-layouts: 2.07 us -> 0.83 us
    pallas_call x10, Pallas kernels: 17.1 us -> 18.3 us  [call(): pl.pallas_call(kernel, out_shape=tuple(outs), in_specs=specs, out_specs=t...]
  transfers between devices with their start and end apart: 20 -> 20, of which waited for: 8 -> 8; matrix products, arithmetic and copies ran while one was open for 0% -> 0% of each run, Pallas kernels for 20% -> 22%
where the time goes in v8:
time: 66.8 us; the launch traced here: 66.6 us
  starting transfers between devices  28.4 us (43%)
  Pallas kernels  18.3 us (27%)
  waiting for transfers between devices  18.2 us (27%)
  local copies, waits for them, and re-layouts  0.83 us (1%)
  between operations  0.78 us (1%)
    ppermute x20, starting transfers between devices, swap(): return lax.ppermute(value, axis, [(i, i ^ k) for i in range(n)])  28.4 us
    pallas_call x10, Pallas kernels, call(): pl.pallas_call(kernel, out_shape=tuple(outs), in_specs=specs, out_specs=t...  18.3 us
    ppermute x20, waiting for transfers between devices, swap(): return lax.ppermute(value, axis, [(i, i ^ k) for i in range(n)])  18.2 us
  transfers between devices with their start and end apart: 20, of which 8 were waited for; matrix products, arithmetic and copies ran while one was open for 0% of the time, Pallas kernels for 22%

profile of v8, /device:TPU:0, one launch (start us, length us, event | category | flops | bytes accessed | tf_op | source)
XLA Modules:
  0.0 66.6 jit_solution(5748998103449787395)
XLA Ops:
  0.7 2.7 %shard_map.110 = (bf16[48,1152]{1,0:T(8,128)(2,1)}, bf16[48,1152]{1,0:T(8,128)(2,1)}, bf16[48,1152]{1,0:T(8,128)(2,1)}, bf16[48,1152]{1,0:T(8,128)(2,1)}, bf16[4...) custom-call(s32[1]{0:T(128)} %bitcast.index, ...), custom_call_target="tpu_custom_call" | custom-call | bytes 2404036 | tf_op jit(solution)/shard_map/pallas_call | solution.py:272
  3.4 3.0 %collective-permute-start.3 = (bf16[48,1152]{1,0:T(8,128)(2,1)}, bf16[48,1152]{1,0:T(8,128)(2,1)S(1)}, u32[]{:S(2)}, u32[]{:S(2)}) collective-permute-start(bf16[48,1152]{1,0:T(8,128)(2,1)} %get-tuple-element.34), channel_id=1, source_target_pairs={{0,8},{8,0},{16,24},{24,16},{1,9},{9,1},{17,25},{25,17},{2,10},{10... | collective-permute-start | bytes 331784 | tf_op jit(solution)/shard_map/ppermute | solution.py:284
  6.4 1.5 %collective-permute-start.4 = (bf16[48,1152]{1,0:T(8,128)(2,1)}, bf16[48,1152]{1,0:T(8,128)(2,1)S(1)}, u32[]{:S(2)}, u32[]{:S(2)}) collective-permute-start(bf16[48,1152]{1,0:T(8,128)(2,1)} %get-tuple-element.35), channel_id=1, source_target_pairs={{0,16},{8,24},{16,0},{24,8},{1,17},{9,25},{17,1},{25,9},{2,18},{10... | collective-permute-start | bytes 331784 | tf_op jit(solution)/shard_map/ppermute | solution.py:284
  7.9 1.9 %collective-permute-start = (bf16[48,1152]{1,0:T(8,128)(2,1)}, bf16[48,1152]{1,0:T(8,128)(2,1)S(1)}, u32[]{:S(2)}, u32[]{:S(2)}) collective-permute-start(bf16[48,1152]{1,0:T(8,128)(2,1)} %get-tuple-element.28), channel_id=1, source_target_pairs={{0,8},{8,0},{16,24},{24,16},{1,9},{9,1},{17,25},{25,17},{2,10},{10... | collective-permute-start | bytes 331784 | tf_op jit(solution)/shard_map/ppermute | solution.py:284
  9.8 1.5 %collective-permute-start.1 = (bf16[48,1152]{1,0:T(8,128)(2,1)}, bf16[48,1152]{1,0:T(8,128)(2,1)S(1)}, u32[]{:S(2)}, u32[]{:S(2)}) collective-permute-start(bf16[48,1152]{1,0:T(8,128)(2,1)} %get-tuple-element.29), channel_id=1, source_target_pairs={{0,16},{8,24},{16,0},{24,8},{1,17},{9,25},{17,1},{25,9},{2,18},{10... | collective-permute-start | bytes 331784 | tf_op jit(solution)/shard_map/ppermute | solution.py:284
  11.4 0.1 shard_map.109
  11.5 0.8 %copy-done.5 = bf16[48,1152]{1,0:T(8,128)(2,1)S(1)} copy-done((bf16[48,1152]{1,0:T(8,128)(2,1)S(1)}, bf16[48,1152]{1,0:T(8,128)(2,1)}, u32[]{:S(2)}) %copy-start.5) | copy-done | bytes 110616
  12.3 1.0 %collective-permute-start.2 = (bf16[48,1152]{1,0:T(8,128)(2,1)S(1)}, bf16[48,1152]{1,0:T(8,128)(2,1)S(1)}, u32[]{:S(2)}, u32[]{:S(2)}) collective-permute-start(bf16[48,1152]{1,0:T(8,128)(2,1)S(1)} %copy-done.5), channel_id=1, source_target_pairs={{0,24},{8,16},{16,8},{24,0},{1,25},{9,17},{17,9},{25,1},{2,26},{10... | collective-permute-start | bytes 331784 | tf_op jit(solution)/shard_map/ppermute | solution.py:284
  13.2 0.8 %collective-permute-done.4.rest_2_ = bf16[48,1152]{1,0:T(8,128)(2,1)S(1)} collective-permute-done((bf16[48,1152]{1,0:T(8,128)(2,1)}, bf16[48,1152]{1,0:T(8,128)(2,1)S(1)}, u32[]{:S(2)}, u32[]{:S(2)}) %collective-permute-start.4) | collective-permute-done | bytes 110624 | tf_op jit(solution)/shard_map/ppermute | solution.py:284
  14.1 0.7 collective-permute-done.5.rest_3_
  14.7 0.1 shard_map.112
  14.8 1.6 %collective-permute-start.6 = (bf16[48,1152]{1,0:T(8,128)(2,1)S(1)}, bf16[48,1152]{1,0:T(8,128)(2,1)S(1)}, u32[]{:S(2)}, u32[]{:S(2)}) collective-permute-start(bf16[48,1152]{1,0:T(8,128)(2,1)S(1)} %get-tuple-element.38.rest_0_), channel_id=1, source_target_pairs={{0,2},{1,3},{2,0},{3,1},{4,6},{5,7},{6,4},{7,5},{8,10},{9,11},{10,... | collective-permute-start | bytes 331784 | tf_op jit(solution)/shard_map/ppermute | solution.py:284
  16.5 2.5 %collective-permute-start.15 = (bf16[48,1152]{1,0:T(8,128)(2,1)S(1)}, bf16[48,1152]{1,0:T(8,128)(2,1)S(1)}, u32[]{:S(2)}, u32[]{:S(2)}) collective-permute-start(bf16[48,1152]{1,0:T(8,128)(2,1)S(1)} %get-tuple-element.38.rest_0_), channel_id=1, source_target_pairs={{0,6},{1,7},{2,4},{3,5},{4,2},{5,3},{6,0},{7,1},{8,14},{9,15},{10,... | collective-permute-start | bytes 331784 | tf_op jit(solution)/shard_map/ppermute | solution.py:284
  18.9 0.1 collective-permute-start.14
  19.1 0.1 shard_map.111
  19.2 1.2 %collective-permute-done.6.rest_0_.rest_1_ = bf16[48,1152]{1,0:T(8,128)(2,1)S(1)} collective-permute-done((bf16[48,1152]{1,0:T(8,128)(2,1)S(1)}, bf16[48,1152]{1,0:T(8,128)(2,1)S(1)}, u32[]{:S(2)}, u32[]{:S(2)}) %collective-permute-start.6) | collective-permute-done | bytes 110624 | tf_op jit(solution)/shard_map/ppermute | solution.py:284
  20.4 2.7 %collective-permute-start.8 = (bf16[48,2304]{1,0:T(8,128)(2,1)S(1)}, bf16[48,2304]{1,0:T(8,128)(2,1)S(1)}, u32[]{:S(2)}, u32[]{:S(2)}) collective-permute-start(bf16[48,2304]{1,0:T(8,128)(2,1)S(1)} %shard_map.113.rest_0_), channel_id=1, source_target_pairs={{0,16},{8,24},{16,0},{24,8},{1,17},{9,25},{17,1},{25,9},{2,18},{10... | collective-permute-start | bytes 663560 | tf_op jit(solution)/shard_map/ppermute | solution.py:284
  23.1 3.0 %collective-permute-start.12 = (bf16[48,1152]{1,0:T(8,128)(2,1)S(1)}, bf16[48,1152]{1,0:T(8,128)(2,1)S(1)}, u32[]{:S(2)}, u32[]{:S(2)}) collective-permute-start(bf16[48,1152]{1,0:T(8,128)(2,1)S(1)} %get-tuple-element.42.rest_0_.rest_4_), channel_id=1, source_target_pairs={{0,6},{1,7},{2,4},{3,5},{4,2},{5,3},{6,0},{7,1},{8,14},{9,15},{10,... | collective-permute-start | bytes 331784 | tf_op jit(solution)/shard_map/ppermute | solution.py:284
  26.1 3.7 %collective-permute-start.11 = (bf16[48,1152]{1,0:T(8,128)(2,1)S(1)}, bf16[48,1152]{1,0:T(8,128)(2,1)S(1)}, u32[]{:S(2)}, u32[]{:S(2)}) collective-permute-start(bf16[48,1152]{1,0:T(8,128)(2,1)S(1)} %get-tuple-element.42.rest_0_.rest_4_), channel_id=1, source_target_pairs={{0,4},{1,5},{2,6},{3,7},{4,0},{5,1},{6,2},{7,3},{8,12},{9,13},{10,... | collective-permute-start | bytes 331784 | tf_op jit(solution)/shard_map/ppermute | solution.py:284
  29.8 1.6 %collective-permute-done.14.rest_2_ = bf16[48,1152]{1,0:T(8,128)(2,1)S(1)} collective-permute-done((bf16[48,1152]{1,0:T(8,128)(2,1)S(1)}, bf16[48,1152]{1,0:T(8,128)(2,1)S(1)}, u32[]{:S(2)}, u32[]{:S(2)}) %collective-permute-start.14) | collective-permute-done | bytes 110624 | tf_op jit(solution)/shard_map/ppermute | solution.py:284
  31.4 0.1 collective-permute-start.16
  31.5 4.4 %collective-permute-done.11.rest_2_ = bf16[48,1152]{1,0:T(8,128)(2,1)S(1)} collective-permute-done((bf16[48,1152]{1,0:T(8,128)(2,1)S(1)}, bf16[48,1152]{1,0:T(8,128)(2,1)S(1)}, u32[]{:S(2)}, u32[]{:S(2)}) %collective-permute-start.11) | collective-permute-done | bytes 110624 | tf_op jit(solution)/shard_map/ppermute | solution.py:284
  35.9 1.1 %collective-permute-done.10.rest_1_ = bf16[48,1152]{1,0:T(8,128)(2,1)S(1)} collective-permute-done((bf16[48,1152]{1,0:T(8,128)(2,1)S(1)}, bf16[48,1152]{1,0:T(8,128)(2,1)S(1)}, u32[]{:S(2)}, u32[]{:S(2)}) %collective-permute-start.10) | collective-permute-done | bytes 110624 | tf_op jit(solution)/shard_map/ppermute | solution.py:284
  37.0 0.1 collective-permute-start.13
  37.1 1.9 %collective-permute-start.9 = (bf16[48,2304]{1,0:T(8,128)(2,1)S(1)}, bf16[48,2304]{1,0:T(8,128)(2,1)S(1)}, u32[]{:S(2)}, u32[]{:S(2)}) collective-permute-start(bf16[48,2304]{1,0:T(8,128)(2,1)S(1)} %shard_map.113.rest_0_), channel_id=1, source_target_pairs={{0,24},{8,16},{16,8},{24,0},{1,25},{9,17},{17,9},{25,1},{2,26},{10... | collective-permute-start | bytes 663560 | tf_op jit(solution)/shard_map/ppermute | solution.py:284
  39.1 13.0 %shard_map.117.rest_0_ = bf16[48,2304]{1,0:T(8,128)(2,1)S(1)} custom-call(s32[1]{0:T(128)} %bitcast.index, bf16[192,1152]{1,0:T(8,128)(2,1)S(1)} %shard_map.115.rest_0_, bf16[192,1152]{1,0:T(8,128)(2,1)S(1)} %collective-permute-done.13.rest_1_, bf16[192,1152]{1,0:T(8,128)(2,1)S(1)} %shard_map.116.rest_2_, bf16[192,1152]{1,0:T(8,128)(2,1)S(1)} %collective-permute-done.16.rest_3_), custom_call_target="tpu_custom_call" | custom-call | flops 7361003520 | bytes 1990660 | tf_op jit(solution)/shard_map/pallas_call | solution.py:272
  52.1 3.1 %collective-permute-start.19 = (bf16[48,2304]{1,0:T(8,128)(2,1)S(1)}, bf16[48,2304]{1,0:T(8,128)(2,1)S(1)}, u32[]{:S(2)}, u32[]{:S(2)}) collective-permute-start(bf16[48,2304]{1,0:T(8,128)(2,1)S(1)} %shard_map.117.rest_0_), channel_id=1, source_target_pairs={{0,24},{8,16},{16,8},{24,0},{1,25},{9,17},{17,9},{25,1},{2,26},{10... | collective-permute-start | bytes 663560 | tf_op jit(solution)/shard_map/ppermute | solution.py:284
  55.2 0.7 %collective-permute-start.18 = (bf16[48,2304]{1,0:T(8,128)(2,1)S(1)}, bf16[48,2304]{1,0:T(8,128)(2,1)S(1)}, u32[]{:S(2)}, u32[]{:S(2)}) collective-permute-start(bf16[48,2304]{1,0:T(8,128)(2,1)S(1)} %shard_map.117.rest_0_), channel_id=1, source_target_pairs={{0,16},{8,24},{16,0},{24,8},{1,17},{9,25},{17,1},{25,9},{2,18},{10... | collective-permute-start | bytes 663560 | tf_op jit(solution)/shard_map/ppermute | solution.py:284
  55.9 1.3 %shard_map.114 = (f32[48,5376]{1,0:T(8,128)}, f32[48,1536]{1,0:T(8,128)}, f32[48,1001]{1,0:T(8,128)}) custom-call(s32[1]{0:T(128)} %bitcast.index, f32[48,5376]{1,0:T(8,128)S(1)} %bitcast.24, f32[48,1536]{1,0:T(8,128)S(1)} %bitcast.26, f32[48,1001]{1,0:T(8,128)S(1)} %bitcast.28, bf16[48,2304]{1,0:T(8,128)(2,1)S(1)} %shard_map.113.rest_0_, ...), custom_call_target="tpu_custom_call" | custom-call | bytes 3923332 | tf_op jit(solution)/shard_map/pallas_call | solution.py:272
  57.2 4.2 %collective-permute-done.19.rest_3_ = bf16[48,2304]{1,0:T(8,128)(2,1)S(1)} collective-permute-done((bf16[48,2304]{1,0:T(8,128)(2,1)S(1)}, bf16[48,2304]{1,0:T(8,128)(2,1)S(1)}, u32[]{:S(2)}, u32[]{:S(2)}) %collective-permute-start.19) | collective-permute-done | bytes 221216 | tf_op jit(solution)/shard_map/ppermute | solution.py:284
  61.4 4.2 %collective-permute-done.18.rest_2_ = bf16[48,2304]{1,0:T(8,128)(2,1)S(1)} collective-permute-done((bf16[48,2304]{1,0:T(8,128)(2,1)S(1)}, bf16[48,2304]{1,0:T(8,128)(2,1)S(1)}, u32[]{:S(2)}, u32[]{:S(2)}) %collective-permute-start.18) | collective-permute-done | bytes 221216 | tf_op jit(solution)/shard_map/ppermute | solution.py:284
  65.7 0.9 %shard_map.118 = (bf16[48,5376]{1,0:T(8,128)(2,1)}, bf16[48,1536]{1,0:T(8,128)(2,1)}, bf16[48,1001]{1,0:T(8,128)(2,1)}) custom-call(s32[1]{0:T(128)} %bitcast.index, bf16[48,2304]{1,0:T(8,128)(2,1)S(1)} %shard_map.117.rest_0_, bf16[48,2304]{1,0:T(8,128)(2,1)S(1)} %collective-permute-done.17.rest_1_, bf16[48,2304]{1,0:T(8,128)(2,1)S(1)} %collective-permute-done.18.rest_2_, ...), custom_call_target="tpu_custom_call" | custom-call | bytes 1644388 | tf_op jit(solution)/shard_map/pallas_call | solution.py:272
  (30 shorter events, 0.2 us)
Async XLA Ops:
  0.6 10.7 %copy-start = (f32[1,48,5376]{2,1,0:T(8,128)S(1)}, f32[1,48,5376]{2,1,0:T(8,128)}, u32[]{:S(2)}) copy-start(f32[1,48,5376]{2,1,0:T(8,128)} %param.9) | copy-start | bytes 3096580
  0.6 10.7 %copy-start.1 = (f32[1,1536,48]{1,2,0:T(8,128)S(1)}, f32[1,1536,48]{1,2,0:T(8,128)}, u32[]{:S(2)}) copy-start(f32[1,1536,48]{1,2,0:T(8,128)} %param.10) | copy-start | bytes 884740
  0.7 10.7 %copy-start.2 = (f32[1001,48]{0,1:T(8,128)S(1)}, f32[1001,48]{0,1:T(8,128)}, u32[]{:S(2)}) copy-start(f32[1001,48]{0,1:T(8,128)} %param.11) | copy-start | bytes 576580
  3.4 8.1 %collective-permute-start.3 = (bf16[48,1152]{1,0:T(8,128)(2,1)}, bf16[48,1152]{1,0:T(8,128)(2,1)S(1)}, u32[]{:S(2)}, u32[]{:S(2)}) collective-permute-start(bf16[48,1152]{1,0:T(8,128)(2,1)} %get-tuple-element.34), channel_id=1, source_target_pairs={{0,8},{8,0},{16,24},{24,16},{1,9},{9,1},{17,25},{25,17},{2,10},{10... | collective-permute-start | bytes 331784 | tf_op jit(solution)/shard_map/ppermute | solution.py:284
  6.4 7.7 %collective-permute-start.4 = (bf16[48,1152]{1,0:T(8,128)(2,1)}, bf16[48,1152]{1,0:T(8,128)(2,1)S(1)}, u32[]{:S(2)}, u32[]{:S(2)}) collective-permute-start(bf16[48,1152]{1,0:T(8,128)(2,1)} %get-tuple-element.35), channel_id=1, source_target_pairs={{0,16},{8,24},{16,0},{24,8},{1,17},{9,25},{17,1},{25,9},{2,18},{10... | collective-permute-start | bytes 331784 | tf_op jit(solution)/shard_map/ppermute | solution.py:284
  7.9 6.9 %collective-permute-start.5 = (bf16[48,1152]{1,0:T(8,128)(2,1)}, bf16[48,1152]{1,0:T(8,128)(2,1)S(1)}, u32[]{:S(2)}, u32[]{:S(2)}) collective-permute-start(bf16[48,1152]{1,0:T(8,128)(2,1)} %get-tuple-element.36), channel_id=1, source_target_pairs={{0,24},{8,16},{16,8},{24,0},{1,25},{9,17},{17,9},{25,1},{2,26},{10... | collective-permute-start | bytes 331784 | tf_op jit(solution)/shard_map/ppermute | solution.py:284
  7.9 11.1 %collective-permute-start = (bf16[48,1152]{1,0:T(8,128)(2,1)}, bf16[48,1152]{1,0:T(8,128)(2,1)S(1)}, u32[]{:S(2)}, u32[]{:S(2)}) collective-permute-start(bf16[48,1152]{1,0:T(8,128)(2,1)} %get-tuple-element.28), channel_id=1, source_target_pairs={{0,8},{8,0},{16,24},{24,16},{1,9},{9,1},{17,25},{25,17},{2,10},{10... | collective-permute-start | bytes 331784 | tf_op jit(solution)/shard_map/ppermute | solution.py:284
  9.8 9.2 %collective-permute-start.1 = (bf16[48,1152]{1,0:T(8,128)(2,1)}, bf16[48,1152]{1,0:T(8,128)(2,1)S(1)}, u32[]{:S(2)}, u32[]{:S(2)}) collective-permute-start(bf16[48,1152]{1,0:T(8,128)(2,1)} %get-tuple-element.29), channel_id=1, source_target_pairs={{0,16},{8,24},{16,0},{24,8},{1,17},{9,25},{17,1},{25,9},{2,18},{10... | collective-permute-start | bytes 331784 | tf_op jit(solution)/shard_map/ppermute | solution.py:284
  11.4 0.9 %copy-start.5 = (bf16[48,1152]{1,0:T(8,128)(2,1)S(1)}, bf16[48,1152]{1,0:T(8,128)(2,1)}, u32[]{:S(2)}) copy-start(bf16[48,1152]{1,0:T(8,128)(2,1)} %get-tuple-element.30) | copy-start | bytes 331780
  11.4 3.4 %copy-start.4 = (bf16[48,1152]{1,0:T(8,128)(2,1)S(1)}, bf16[48,1152]{1,0:T(8,128)(2,1)}, u32[]{:S(2)}) copy-start(bf16[48,1152]{1,0:T(8,128)(2,1)} %get-tuple-element.33.rest_0_) | copy-start | bytes 331780
  12.3 6.8 %collective-permute-start.2 = (bf16[48,1152]{1,0:T(8,128)(2,1)S(1)}, bf16[48,1152]{1,0:T(8,128)(2,1)S(1)}, u32[]{:S(2)}, u32[]{:S(2)}) collective-permute-start(bf16[48,1152]{1,0:T(8,128)(2,1)S(1)} %copy-done.5), channel_id=1, source_target_pairs={{0,24},{8,16},{16,8},{24,0},{1,25},{9,17},{17,9},{25,1},{2,26},{10... | collective-permute-start | bytes 331784 | tf_op jit(solution)/shard_map/ppermute | solution.py:284
  14.7 4.3 %copy-start.3 = (bf16[48,1152]{1,0:T(8,128)(2,1)S(1)}, bf16[48,1152]{1,0:T(8,128)(2,1)}, u32[]{:S(2)}) copy-start(bf16[48,1152]{1,0:T(8,128)(2,1)} %get-tuple-element.27.rest_0_) | copy-start | bytes 331780
  14.8 5.6 %collective-permute-start.6 = (bf16[48,1152]{1,0:T(8,128)(2,1)S(1)}, bf16[48,1152]{1,0:T(8,128)(2,1)S(1)}, u32[]{:S(2)}, u32[]{:S(2)}) collective-permute-start(bf16[48,1152]{1,0:T(8,128)(2,1)S(1)} %get-tuple-element.38.rest_0_), channel_id=1, source_target_pairs={{0,2},{1,3},{2,0},{3,1},{4,6},{5,7},{6,4},{7,5},{8,10},{9,11},{10,... | collective-permute-start | bytes 331784 | tf_op jit(solution)/shard_map/ppermute | solution.py:284
  16.5 9.6 %collective-permute-start.15 = (bf16[48,1152]{1,0:T(8,128)(2,1)S(1)}, bf16[48,1152]{1,0:T(8,128)(2,1)S(1)}, u32[]{:S(2)}, u32[]{:S(2)}) collective-permute-start(bf16[48,1152]{1,0:T(8,128)(2,1)S(1)} %get-tuple-element.38.rest_0_), channel_id=1, source_target_pairs={{0,6},{1,7},{2,4},{3,5},{4,2},{5,3},{6,0},{7,1},{8,14},{9,15},{10,... | collective-permute-start | bytes 331784 | tf_op jit(solution)/shard_map/ppermute | solution.py:284
  18.9 12.4 %collective-permute-start.14 = (bf16[48,1152]{1,0:T(8,128)(2,1)S(1)}, bf16[48,1152]{1,0:T(8,128)(2,1)S(1)}, u32[]{:S(2)}, u32[]{:S(2)}) collective-permute-start(bf16[48,1152]{1,0:T(8,128)(2,1)S(1)} %get-tuple-element.38.rest_0_), channel_id=1, source_target_pairs={{0,4},{1,5},{2,6},{3,7},{4,0},{5,1},{6,2},{7,3},{8,12},{9,13},{10,... | collective-permute-start | bytes 331784 | tf_op jit(solution)/shard_map/ppermute | solution.py:284
  20.4 16.6 %collective-permute-start.8 = (bf16[48,2304]{1,0:T(8,128)(2,1)S(1)}, bf16[48,2304]{1,0:T(8,128)(2,1)S(1)}, u32[]{:S(2)}, u32[]{:S(2)}) collective-permute-start(bf16[48,2304]{1,0:T(8,128)(2,1)S(1)} %shard_map.113.rest_0_), channel_id=1, source_target_pairs={{0,16},{8,24},{16,0},{24,8},{1,17},{9,25},{17,1},{25,9},{2,18},{10... | collective-permute-start | bytes 663560 | tf_op jit(solution)/shard_map/ppermute | solution.py:284
  23.1 13.9 %collective-permute-start.7 = (bf16[48,2304]{1,0:T(8,128)(2,1)S(1)}, bf16[48,2304]{1,0:T(8,128)(2,1)S(1)}, u32[]{:S(2)}, u32[]{:S(2)}) collective-permute-start(bf16[48,2304]{1,0:T(8,128)(2,1)S(1)} %shard_map.113.rest_0_), channel_id=1, source_target_pairs={{0,8},{8,0},{16,24},{24,16},{1,9},{9,1},{17,25},{25,17},{2,10},{10... | collective-permute-start | bytes 663560 | tf_op jit(solution)/shard_map/ppermute | solution.py:284
  23.1 8.3 %collective-permute-start.12 = (bf16[48,1152]{1,0:T(8,128)(2,1)S(1)}, bf16[48,1152]{1,0:T(8,128)(2,1)S(1)}, u32[]{:S(2)}, u32[]{:S(2)}) collective-permute-start(bf16[48,1152]{1,0:T(8,128)(2,1)S(1)} %get-tuple-element.42.rest_0_.rest_4_), channel_id=1, source_target_pairs={{0,6},{1,7},{2,4},{3,5},{4,2},{5,3},{6,0},{7,1},{8,14},{9,15},{10,... | collective-permute-start | bytes 331784 | tf_op jit(solution)/shard_map/ppermute | solution.py:284
  26.1 9.8 %collective-permute-start.11 = (bf16[48,1152]{1,0:T(8,128)(2,1)S(1)}, bf16[48,1152]{1,0:T(8,128)(2,1)S(1)}, u32[]{:S(2)}, u32[]{:S(2)}) collective-permute-start(bf16[48,1152]{1,0:T(8,128)(2,1)S(1)} %get-tuple-element.42.rest_0_.rest_4_), channel_id=1, source_target_pairs={{0,4},{1,5},{2,6},{3,7},{4,0},{5,1},{6,2},{7,3},{8,12},{9,13},{10,... | collective-permute-start | bytes 331784 | tf_op jit(solution)/shard_map/ppermute | solution.py:284
  31.4 5.6 %collective-permute-start.10 = (bf16[48,1152]{1,0:T(8,128)(2,1)S(1)}, bf16[48,1152]{1,0:T(8,128)(2,1)S(1)}, u32[]{:S(2)}, u32[]{:S(2)}) collective-permute-start(bf16[48,1152]{1,0:T(8,128)(2,1)S(1)} %get-tuple-element.42.rest_0_.rest_4_), channel_id=1, source_target_pairs={{0,2},{1,3},{2,0},{3,1},{4,6},{5,7},{6,4},{7,5},{8,10},{9,11},{10,... | collective-permute-start | bytes 331784 | tf_op jit(solution)/shard_map/ppermute | solution.py:284
  31.4 7.6 %collective-permute-start.16 = (bf16[192,1152]{1,0:T(8,128)(2,1)S(1)}, bf16[192,1152]{1,0:T(8,128)(2,1)S(1)}, u32[]{:S(2)}, u32[]{:S(2)}) collective-permute-start(bf16[192,1152]{1,0:T(8,128)(2,1)S(1)} %shard_map.116.rest_2_), channel_id=1, source_target_pairs={{0,1},{1,0},{2,3},{3,2},{4,5},{5,4},{6,7},{7,6},{8,9},{9,8},{10,11... | collective-permute-start | bytes 1327112 | tf_op jit(solution)/shard_map/ppermute | solution.py:284
  37.0 2.0 %collective-permute-start.13 = (bf16[192,1152]{1,0:T(8,128)(2,1)S(1)}, bf16[192,1152]{1,0:T(8,128)(2,1)S(1)}, u32[]{:S(2)}, u32[]{:S(2)}) collective-permute-start(bf16[192,1152]{1,0:T(8,128)(2,1)S(1)} %shard_map.115.rest_0_), channel_id=1, source_target_pairs={{0,1},{1,0},{2,3},{3,2},{4,5},{5,4},{6,7},{7,6},{8,9},{9,8},{10,11... | collective-permute-start | bytes 1327112 | tf_op jit(solution)/shard_map/ppermute | solution.py:284
  37.1 18.8 %collective-permute-start.9 = (bf16[48,2304]{1,0:T(8,128)(2,1)S(1)}, bf16[48,2304]{1,0:T(8,128)(2,1)S(1)}, u32[]{:S(2)}, u32[]{:S(2)}) collective-permute-start(bf16[48,2304]{1,0:T(8,128)(2,1)S(1)} %shard_map.113.rest_0_), channel_id=1, source_target_pairs={{0,24},{8,16},{16,8},{24,0},{1,25},{9,17},{17,9},{25,1},{2,26},{10... | collective-permute-start | bytes 663560 | tf_op jit(solution)/shard_map/ppermute | solution.py:284
  52.1 9.3 %collective-permute-start.19 = (bf16[48,2304]{1,0:T(8,128)(2,1)S(1)}, bf16[48,2304]{1,0:T(8,128)(2,1)S(1)}, u32[]{:S(2)}, u32[]{:S(2)}) collective-permute-start(bf16[48,2304]{1,0:T(8,128)(2,1)S(1)} %shard_map.117.rest_0_), channel_id=1, source_target_pairs={{0,24},{8,16},{16,8},{24,0},{1,25},{9,17},{17,9},{25,1},{2,26},{10... | collective-permute-start | bytes 663560 | tf_op jit(solution)/shard_map/ppermute | solution.py:284
  55.2 10.5 %collective-permute-start.18 = (bf16[48,2304]{1,0:T(8,128)(2,1)S(1)}, bf16[48,2304]{1,0:T(8,128)(2,1)S(1)}, u32[]{:S(2)}, u32[]{:S(2)}) collective-permute-start(bf16[48,2304]{1,0:T(8,128)(2,1)S(1)} %shard_map.117.rest_0_), channel_id=1, source_target_pairs={{0,16},{8,24},{16,0},{24,8},{1,17},{9,25},{17,1},{25,9},{2,18},{10... | collective-permute-start | bytes 663560 | tf_op jit(solution)/shard_map/ppermute | solution.py:284
  55.9 9.8 %collective-permute-start.17 = (bf16[48,2304]{1,0:T(8,128)(2,1)S(1)}, bf16[48,2304]{1,0:T(8,128)(2,1)S(1)}, u32[]{:S(2)}, u32[]{:S(2)}) collective-permute-start(bf16[48,2304]{1,0:T(8,128)(2,1)S(1)} %shard_map.117.rest_0_), channel_id=1, source_target_pairs={{0,8},{8,0},{16,24},{24,16},{1,9},{9,1},{17,25},{25,17},{2,10},{10... | collective-permute-start | bytes 663560 | tf_op jit(solution)/shard_map/ppermute | solution.py:284

commit v9 on v8

--- a/solution.py
+++ b/solution.py
@@ -29,7 +29,6 @@
 PADDED = [-(-width // 128) * 128 for width in WIDTHS]
 DOWN, EMBED = 4, 5
 TILE = 256
-SPLIT = 256
 
 
 def plan(n_rep):
@@ -148,49 +147,46 @@
         def product(left, right, sides):
             return lax.dot_general(left, right, ((sides[0], sides[1]), ((), ())), preferred_element_type=jnp.float32)
 
-        def symmetric(left, corner):
-            right = jnp.concatenate([left[SPLIT:, :].T, corner], axis=0)
-            return jnp.concatenate([left, right], axis=1)
-
-        def outer(span):
-            sides = ((1,), (1,))
-            left = product(x_ref[:, span], x_ref[:SPLIT, span], sides)
-            low = x_ref[SPLIT:, span]
-            return symmetric(left, product(low, low, sides))
-
-        def polynomial(gram, scale=1.0):
-            gram = gram.astype(jnp.bfloat16)
-            sides = ((1,), (0,))
-
-            def entries(value, square, diagonal):
-                value = COEF_B * value.astype(jnp.float32) + COEF_C * square
-                return scale * (value + jnp.where(diagonal, COEF_A, 0.0))
-
-            left = entries(gram[:, :SPLIT], product(gram, gram[:, :SPLIT], sides), diagonal[:, :SPLIT])
-            corner = product(gram[SPLIT:, :], gram[:, SPLIT:], sides)
-            corner = entries(gram[SPLIT:, SPLIT:], corner, diagonal[SPLIT:, SPLIT:])
-            return symmetric(left, corner).astype(jnp.bfloat16)
-
-        def advance(tiles, poly):
-            for tile in tiles:
-                x_ref[:, tile] = product(poly, x_ref[:, tile], ((1,), (0,))).astype(jnp.bfloat16)
+        def grams():
+            found = []
+            for span, _, _ in spans:
+                x = x_ref[:, span]
+                found.append(product(x, x, ((1,), (1,))))
+            return found
+
+        def polynomials(grams, scales, count=D):
+            halves = [gram.astype(jnp.bfloat16) for gram in grams]
+            squares = [product(gram[:count], gram, ((1,), (0,))) for gram in halves]
+            return [
+                (
+                    scale
+                    * (
+                        COEF_B * gram[:count].astype(jnp.float32)
+                        + COEF_C * square
+                        + jnp.where(diagonal[:count], COEF_A, 0.0)
+                    )
+                ).astype(jnp.bfloat16)
+                for gram, square, scale in zip(halves, squares, scales)
+            ]
+
+        def advance(polys):
+            for poly, (_, tiles, _) in zip(polys, spans):
+                for tile in tiles:
+                    x_ref[:, tile] = product(poly, x_ref[:, tile], ((1,), (0,))).astype(jnp.bfloat16)
 
         row = lax.broadcasted_iota(jnp.int32, (D, D), 0)
         diagonal = row == lax.broadcasted_iota(jnp.int32, (D, D), 1)
-        for span, tiles, _ in spans:
-            gram = outer(span)
-            scale = 1.0 / (jnp.sqrt(jnp.sum(jnp.where(diagonal, gram, 0.0))) + EPSILON)
-            advance(tiles, polynomial(gram * scale * scale, scale))
+        ones = [1.0] * len(spans)
+        first = grams()
+        scales = [1.0 / (jnp.sqrt(jnp.sum(jnp.where(diagonal, gram, 0.0))) + EPSILON) for gram in first]
+        advance(polynomials([gram * scale * scale for gram, scale in zip(first, scales)], scales))
 
         def step(_, carry):
-            polys = [polynomial(outer(span)) for span, _, _ in spans]
-            for poly, (_, tiles, _) in zip(polys, spans):
-                advance(tiles, poly)
+            advance(polynomials(grams(), ones))
             return carry
 
         lax.fori_loop(0, NS_ITERS - 2, step, 0)
-        for span, tiles, factor in spans:
-            poly = polynomial(outer(span))[:rows]
+        for poly, (_, tiles, factor) in zip(polynomials(grams(), ones, rows), spans):
             for tile in tiles:
                 value = product(poly, x_ref[:, tile], ((1,), (0,)))
                 out[:, tile] = (factor * value).astype(jnp.bfloat16)

time: 66.8 us -> 65.1 us (0.975)
  Pallas kernels: 18.3 us -> 17 us
    pallas_call x10, Pallas kernels: 18.3 us -> 17 us  [call(): pl.pallas_call(kernel, out_shape=tuple(outs), in_specs=specs, out_specs=t...]
  transfers between devices with their start and end apart: 20 -> 20, of which waited for: 8 -> 8; matrix products, arithmetic and copies ran while one was open for 0% -> 0% of each run, Pallas kernels for 22% -> 21%
where the time goes in v9:
time: 65.1 us; the launch traced here: 65 us
  starting transfers between devices  28.2 us (43%)
  waiting for transfers between devices  18.1 us (28%)
  Pallas kernels  17 us (26%)
  local copies, waits for them, and re-layouts  0.83 us (1%)
  between operations  0.78 us (1%)
    ppermute x20, starting transfers between devices, swap(): return lax.ppermute(value, axis, [(i, i ^ k) for i in range(n)])  28.2 us
    ppermute x20, waiting for transfers between devices, swap(): return lax.ppermute(value, axis, [(i, i ^ k) for i in range(n)])  18.1 us
    pallas_call x10, Pallas kernels, call(): pl.pallas_call(kernel, out_shape=tuple(outs), in_specs=specs, out_specs=t...  17 us
  transfers between devices with their start and end apart: 20, of which 8 were waited for; matrix products, arithmetic and copies ran while one was open for 0% of the time, Pallas kernels for 21%

profile of v9, /device:TPU:0, one launch (start us, length us, event | category | flops | bytes accessed | tf_op | source)
XLA Modules:
  0.0 65.0 jit_solution(10689400051616904399)
XLA Ops:
  0.7 2.7 %shard_map.110 = (bf16[48,1152]{1,0:T(8,128)(2,1)}, bf16[48,1152]{1,0:T(8,128)(2,1)}, bf16[48,1152]{1,0:T(8,128)(2,1)}, bf16[48,1152]{1,0:T(8,128)(2,1)}, bf16[4...) custom-call(s32[1]{0:T(128)} %bitcast.index, ...), custom_call_target="tpu_custom_call" | custom-call | bytes 2404036 | tf_op jit(solution)/shard_map/pallas_call | solution.py:268
  3.4 3.0 %collective-permute-start.3 = (bf16[48,1152]{1,0:T(8,128)(2,1)}, bf16[48,1152]{1,0:T(8,128)(2,1)S(1)}, u32[]{:S(2)}, u32[]{:S(2)}) collective-permute-start(bf16[48,1152]{1,0:T(8,128)(2,1)} %get-tuple-element.34), channel_id=1, source_target_pairs={{0,8},{8,0},{16,24},{24,16},{1,9},{9,1},{17,25},{25,17},{2,10},{10... | collective-permute-start | bytes 331784 | tf_op jit(solution)/shard_map/ppermute | solution.py:280
  6.4 1.5 %collective-permute-start.4 = (bf16[48,1152]{1,0:T(8,128)(2,1)}, bf16[48,1152]{1,0:T(8,128)(2,1)S(1)}, u32[]{:S(2)}, u32[]{:S(2)}) collective-permute-start(bf16[48,1152]{1,0:T(8,128)(2,1)} %get-tuple-element.35), channel_id=1, source_target_pairs={{0,16},{8,24},{16,0},{24,8},{1,17},{9,25},{17,1},{25,9},{2,18},{10... | collective-permute-start | bytes 331784 | tf_op jit(solution)/shard_map/ppermute | solution.py:280
  7.9 1.9 %collective-permute-start = (bf16[48,1152]{1,0:T(8,128)(2,1)}, bf16[48,1152]{1,0:T(8,128)(2,1)S(1)}, u32[]{:S(2)}, u32[]{:S(2)}) collective-permute-start(bf16[48,1152]{1,0:T(8,128)(2,1)} %get-tuple-element.28), channel_id=1, source_target_pairs={{0,8},{8,0},{16,24},{24,16},{1,9},{9,1},{17,25},{25,17},{2,10},{10... | collective-permute-start | bytes 331784 | tf_op jit(solution)/shard_map/ppermute | solution.py:280
  9.8 1.5 %collective-permute-start.1 = (bf16[48,1152]{1,0:T(8,128)(2,1)}, bf16[48,1152]{1,0:T(8,128)(2,1)S(1)}, u32[]{:S(2)}, u32[]{:S(2)}) collective-permute-start(bf16[48,1152]{1,0:T(8,128)(2,1)} %get-tuple-element.29), channel_id=1, source_target_pairs={{0,16},{8,24},{16,0},{24,8},{1,17},{9,25},{17,1},{25,9},{2,18},{10... | collective-permute-start | bytes 331784 | tf_op jit(solution)/shard_map/ppermute | solution.py:280
  11.5 0.8 %copy-done.5 = bf16[48,1152]{1,0:T(8,128)(2,1)S(1)} copy-done((bf16[48,1152]{1,0:T(8,128)(2,1)S(1)}, bf16[48,1152]{1,0:T(8,128)(2,1)}, u32[]{:S(2)}) %copy-start.5) | copy-done | bytes 110616
  12.3 1.0 %collective-permute-start.2 = (bf16[48,1152]{1,0:T(8,128)(2,1)S(1)}, bf16[48,1152]{1,0:T(8,128)(2,1)S(1)}, u32[]{:S(2)}, u32[]{:S(2)}) collective-permute-start(bf16[48,1152]{1,0:T(8,128)(2,1)S(1)} %copy-done.5), channel_id=1, source_target_pairs={{0,24},{8,16},{16,8},{24,0},{1,25},{9,17},{17,9},{25,1},{2,26},{10... | collective-permute-start | bytes 331784 | tf_op jit(solution)/shard_map/ppermute | solution.py:280
  13.2 0.8 %collective-permute-done.4.rest_2_ = bf16[48,1152]{1,0:T(8,128)(2,1)S(1)} collective-permute-done((bf16[48,1152]{1,0:T(8,128)(2,1)}, bf16[48,1152]{1,0:T(8,128)(2,1)S(1)}, u32[]{:S(2)}, u32[]{:S(2)}) %collective-permute-start.4) | collective-permute-done | bytes 110624 | tf_op jit(solution)/shard_map/ppermute | solution.py:280
  14.1 0.7 %collective-permute-done.5.rest_3_ = bf16[48,1152]{1,0:T(8,128)(2,1)S(1)} collective-permute-done((bf16[48,1152]{1,0:T(8,128)(2,1)}, bf16[48,1152]{1,0:T(8,128)(2,1)S(1)}, u32[]{:S(2)}, u32[]{:S(2)}) %collective-permute-start.5) | collective-permute-done | bytes 110624 | tf_op jit(solution)/shard_map/ppermute | solution.py:280
  14.7 0.1 shard_map.112
  14.8 1.6 %collective-permute-start.6 = (bf16[48,1152]{1,0:T(8,128)(2,1)S(1)}, bf16[48,1152]{1,0:T(8,128)(2,1)S(1)}, u32[]{:S(2)}, u32[]{:S(2)}) collective-permute-start(bf16[48,1152]{1,0:T(8,128)(2,1)S(1)} %get-tuple-element.38.rest_0_), channel_id=1, source_target_pairs={{0,2},{1,3},{2,0},{3,1},{4,6},{5,7},{6,4},{7,5},{8,10},{9,11},{10,... | collective-permute-start | bytes 331784 | tf_op jit(solution)/shard_map/ppermute | solution.py:280
  16.5 2.5 %collective-permute-start.15 = (bf16[48,1152]{1,0:T(8,128)(2,1)S(1)}, bf16[48,1152]{1,0:T(8,128)(2,1)S(1)}, u32[]{:S(2)}, u32[]{:S(2)}) collective-permute-start(bf16[48,1152]{1,0:T(8,128)(2,1)S(1)} %get-tuple-element.38.rest_0_), channel_id=1, source_target_pairs={{0,6},{1,7},{2,4},{3,5},{4,2},{5,3},{6,0},{7,1},{8,14},{9,15},{10,... | collective-permute-start | bytes 331784 | tf_op jit(solution)/shard_map/ppermute | solution.py:280
  18.9 0.1 collective-permute-start.14
  19.1 0.1 shard_map.111
  19.2 1.2 %collective-permute-done.6.rest_0_.rest_1_ = bf16[48,1152]{1,0:T(8,128)(2,1)S(1)} collective-permute-done((bf16[48,1152]{1,0:T(8,128)(2,1)S(1)}, bf16[48,1152]{1,0:T(8,128)(2,1)S(1)}, u32[]{:S(2)}, u32[]{:S(2)}) %collective-permute-start.6) | collective-permute-done | bytes 110624 | tf_op jit(solution)/shard_map/ppermute | solution.py:280
  20.4 2.7 %collective-permute-start.8 = (bf16[48,2304]{1,0:T(8,128)(2,1)S(1)}, bf16[48,2304]{1,0:T(8,128)(2,1)S(1)}, u32[]{:S(2)}, u32[]{:S(2)}) collective-permute-start(bf16[48,2304]{1,0:T(8,128)(2,1)S(1)} %shard_map.113.rest_0_), channel_id=1, source_target_pairs={{0,16},{8,24},{16,0},{24,8},{1,17},{9,25},{17,1},{25,9},{2,18},{10... | collective-permute-start | bytes 663560 | tf_op jit(solution)/shard_map/ppermute | solution.py:280
  23.1 3.0 %collective-permute-start.12 = (bf16[48,1152]{1,0:T(8,128)(2,1)S(1)}, bf16[48,1152]{1,0:T(8,128)(2,1)S(1)}, u32[]{:S(2)}, u32[]{:S(2)}) collective-permute-start(bf16[48,1152]{1,0:T(8,128)(2,1)S(1)} %get-tuple-element.42.rest_0_.rest_4_), channel_id=1, source_target_pairs={{0,6},{1,7},{2,4},{3,5},{4,2},{5,3},{6,0},{7,1},{8,14},{9,15},{10,... | collective-permute-start | bytes 331784 | tf_op jit(solution)/shard_map/ppermute | solution.py:280
  26.1 3.7 %collective-permute-start.11 = (bf16[48,1152]{1,0:T(8,128)(2,1)S(1)}, bf16[48,1152]{1,0:T(8,128)(2,1)S(1)}, u32[]{:S(2)}, u32[]{:S(2)}) collective-permute-start(bf16[48,1152]{1,0:T(8,128)(2,1)S(1)} %get-tuple-element.42.rest_0_.rest_4_), channel_id=1, source_target_pairs={{0,4},{1,5},{2,6},{3,7},{4,0},{5,1},{6,2},{7,3},{8,12},{9,13},{10,... | collective-permute-start | bytes 331784 | tf_op jit(solution)/shard_map/ppermute | solution.py:280
  29.8 1.6 %collective-permute-done.14.rest_2_ = bf16[48,1152]{1,0:T(8,128)(2,1)S(1)} collective-permute-done((bf16[48,1152]{1,0:T(8,128)(2,1)S(1)}, bf16[48,1152]{1,0:T(8,128)(2,1)S(1)}, u32[]{:S(2)}, u32[]{:S(2)}) %collective-permute-start.14) | collective-permute-done | bytes 110624 | tf_op jit(solution)/shard_map/ppermute | solution.py:280
  31.4 0.1 collective-permute-start.16
  31.5 4.4 %collective-permute-done.11.rest_2_ = bf16[48,1152]{1,0:T(8,128)(2,1)S(1)} collective-permute-done((bf16[48,1152]{1,0:T(8,128)(2,1)S(1)}, bf16[48,1152]{1,0:T(8,128)(2,1)S(1)}, u32[]{:S(2)}, u32[]{:S(2)}) %collective-permute-start.11) | collective-permute-done | bytes 110624 | tf_op jit(solution)/shard_map/ppermute | solution.py:280
  35.9 1.1 %collective-permute-done.10.rest_1_ = bf16[48,1152]{1,0:T(8,128)(2,1)S(1)} collective-permute-done((bf16[48,1152]{1,0:T(8,128)(2,1)S(1)}, bf16[48,1152]{1,0:T(8,128)(2,1)S(1)}, u32[]{:S(2)}, u32[]{:S(2)}) %collective-permute-start.10) | collective-permute-done | bytes 110624 | tf_op jit(solution)/shard_map/ppermute | solution.py:280
  37.0 0.1 collective-permute-start.13
  37.1 1.9 %collective-permute-start.9 = (bf16[48,2304]{1,0:T(8,128)(2,1)S(1)}, bf16[48,2304]{1,0:T(8,128)(2,1)S(1)}, u32[]{:S(2)}, u32[]{:S(2)}) collective-permute-start(bf16[48,2304]{1,0:T(8,128)(2,1)S(1)} %shard_map.113.rest_0_), channel_id=1, source_target_pairs={{0,24},{8,16},{16,8},{24,0},{1,25},{9,17},{17,9},{25,1},{2,26},{10... | collective-permute-start | bytes 663560 | tf_op jit(solution)/shard_map/ppermute | solution.py:280
  39.1 11.8 %shard_map.117.rest_0_ = bf16[48,2304]{1,0:T(8,128)(2,1)S(1)} custom-call(s32[1]{0:T(128)} %bitcast.index, bf16[192,1152]{1,0:T(8,128)(2,1)S(1)} %shard_map.115.rest_0_, bf16[192,1152]{1,0:T(8,128)(2,1)S(1)} %collective-permute-done.13.rest_1_, bf16[192,1152]{1,0:T(8,128)(2,1)S(1)} %shard_map.116.rest_2_, bf16[192,1152]{1,0:T(8,128)(2,1)S(1)} %collective-permute-done.16.rest_3_), custom_call_target="tpu_custom_call" | custom-call | flops 7361003520 | bytes 1990660 | tf_op jit(solution)/shard_map/pallas_call | solution.py:268
  50.8 1.5 %collective-permute-start.19 = (bf16[48,2304]{1,0:T(8,128)(2,1)S(1)}, bf16[48,2304]{1,0:T(8,128)(2,1)S(1)}, u32[]{:S(2)}, u32[]{:S(2)}) collective-permute-start(bf16[48,2304]{1,0:T(8,128)(2,1)S(1)} %shard_map.117.rest_0_), channel_id=1, source_target_pairs={{0,24},{8,16},{16,8},{24,0},{1,25},{9,17},{17,9},{25,1},{2,26},{10... | collective-permute-start | bytes 663560 | tf_op jit(solution)/shard_map/ppermute | solution.py:280
  52.3 0.5 collective-permute-start.18
  52.8 1.6 %collective-permute-start.17 = (bf16[48,2304]{1,0:T(8,128)(2,1)S(1)}, bf16[48,2304]{1,0:T(8,128)(2,1)S(1)}, u32[]{:S(2)}, u32[]{:S(2)}) collective-permute-start(bf16[48,2304]{1,0:T(8,128)(2,1)S(1)} %shard_map.117.rest_0_), channel_id=1, source_target_pairs={{0,8},{8,0},{16,24},{24,16},{1,9},{9,1},{17,25},{25,17},{2,10},{10... | collective-permute-start | bytes 663560 | tf_op jit(solution)/shard_map/ppermute | solution.py:280
  54.4 1.3 %shard_map.114 = (f32[48,5376]{1,0:T(8,128)}, f32[48,1536]{1,0:T(8,128)}, f32[48,1001]{1,0:T(8,128)}) custom-call(s32[1]{0:T(128)} %bitcast.index, f32[48,5376]{1,0:T(8,128)S(1)} %bitcast.24, f32[48,1536]{1,0:T(8,128)S(1)} %bitcast.26, f32[48,1001]{1,0:T(8,128)S(1)} %bitcast.28, bf16[48,2304]{1,0:T(8,128)(2,1)S(1)} %shard_map.113.rest_0_, ...), custom_call_target="tpu_custom_call" | custom-call | bytes 3923332 | tf_op jit(solution)/shard_map/pallas_call | solution.py:268
  55.7 4.4 %collective-permute-done.19.rest_3_ = bf16[48,2304]{1,0:T(8,128)(2,1)S(1)} collective-permute-done((bf16[48,2304]{1,0:T(8,128)(2,1)S(1)}, bf16[48,2304]{1,0:T(8,128)(2,1)S(1)}, u32[]{:S(2)}, u32[]{:S(2)}) %collective-permute-start.19) | collective-permute-done | bytes 221216 | tf_op jit(solution)/shard_map/ppermute | solution.py:280
  60.1 3.9 %collective-permute-done.18.rest_2_ = bf16[48,2304]{1,0:T(8,128)(2,1)S(1)} collective-permute-done((bf16[48,2304]{1,0:T(8,128)(2,1)S(1)}, bf16[48,2304]{1,0:T(8,128)(2,1)S(1)}, u32[]{:S(2)}, u32[]{:S(2)}) %collective-permute-start.18) | collective-permute-done | bytes 221216 | tf_op jit(solution)/shard_map/ppermute | solution.py:280
  64.0 0.9 %shard_map.118 = (bf16[48,5376]{1,0:T(8,128)(2,1)}, bf16[48,1536]{1,0:T(8,128)(2,1)}, bf16[48,1001]{1,0:T(8,128)(2,1)}) custom-call(s32[1]{0:T(128)} %bitcast.index, bf16[48,2304]{1,0:T(8,128)(2,1)S(1)} %shard_map.117.rest_0_, bf16[48,2304]{1,0:T(8,128)(2,1)S(1)} %collective-permute-done.17.rest_1_, bf16[48,2304]{1,0:T(8,128)(2,1)S(1)} %collective-permute-done.18.rest_2_, ...), custom_call_target="tpu_custom_call" | custom-call | bytes 1644388 | tf_op jit(solution)/shard_map/pallas_call | solution.py:268
  (30 shorter events, 0.2 us)
Async XLA Ops:
  0.6 10.7 %copy-start = (f32[1,48,5376]{2,1,0:T(8,128)S(1)}, f32[1,48,5376]{2,1,0:T(8,128)}, u32[]{:S(2)}) copy-start(f32[1,48,5376]{2,1,0:T(8,128)} %param.9) | copy-start | bytes 3096580
  0.6 10.7 %copy-start.1 = (f32[1,1536,48]{1,2,0:T(8,128)S(1)}, f32[1,1536,48]{1,2,0:T(8,128)}, u32[]{:S(2)}) copy-start(f32[1,1536,48]{1,2,0:T(8,128)} %param.10) | copy-start | bytes 884740
  0.7 10.7 %copy-start.2 = (f32[1001,48]{0,1:T(8,128)S(1)}, f32[1001,48]{0,1:T(8,128)}, u32[]{:S(2)}) copy-start(f32[1001,48]{0,1:T(8,128)} %param.11) | copy-start | bytes 576580
  3.4 8.1 %collective-permute-start.3 = (bf16[48,1152]{1,0:T(8,128)(2,1)}, bf16[48,1152]{1,0:T(8,128)(2,1)S(1)}, u32[]{:S(2)}, u32[]{:S(2)}) collective-permute-start(bf16[48,1152]{1,0:T(8,128)(2,1)} %get-tuple-element.34), channel_id=1, source_target_pairs={{0,8},{8,0},{16,24},{24,16},{1,9},{9,1},{17,25},{25,17},{2,10},{10... | collective-permute-start | bytes 331784 | tf_op jit(solution)/shard_map/ppermute | solution.py:280
  6.4 7.7 %collective-permute-start.4 = (bf16[48,1152]{1,0:T(8,128)(2,1)}, bf16[48,1152]{1,0:T(8,128)(2,1)S(1)}, u32[]{:S(2)}, u32[]{:S(2)}) collective-permute-start(bf16[48,1152]{1,0:T(8,128)(2,1)} %get-tuple-element.35), channel_id=1, source_target_pairs={{0,16},{8,24},{16,0},{24,8},{1,17},{9,25},{17,1},{25,9},{2,18},{10... | collective-permute-start | bytes 331784 | tf_op jit(solution)/shard_map/ppermute | solution.py:280
  7.9 6.9 %collective-permute-start.5 = (bf16[48,1152]{1,0:T(8,128)(2,1)}, bf16[48,1152]{1,0:T(8,128)(2,1)S(1)}, u32[]{:S(2)}, u32[]{:S(2)}) collective-permute-start(bf16[48,1152]{1,0:T(8,128)(2,1)} %get-tuple-element.36), channel_id=1, source_target_pairs={{0,24},{8,16},{16,8},{24,0},{1,25},{9,17},{17,9},{25,1},{2,26},{10... | collective-permute-start | bytes 331784 | tf_op jit(solution)/shard_map/ppermute | solution.py:280
  7.9 11.1 %collective-permute-start = (bf16[48,1152]{1,0:T(8,128)(2,1)}, bf16[48,1152]{1,0:T(8,128)(2,1)S(1)}, u32[]{:S(2)}, u32[]{:S(2)}) collective-permute-start(bf16[48,1152]{1,0:T(8,128)(2,1)} %get-tuple-element.28), channel_id=1, source_target_pairs={{0,8},{8,0},{16,24},{24,16},{1,9},{9,1},{17,25},{25,17},{2,10},{10... | collective-permute-start | bytes 331784 | tf_op jit(solution)/shard_map/ppermute | solution.py:280
  9.8 9.2 %collective-permute-start.1 = (bf16[48,1152]{1,0:T(8,128)(2,1)}, bf16[48,1152]{1,0:T(8,128)(2,1)S(1)}, u32[]{:S(2)}, u32[]{:S(2)}) collective-permute-start(bf16[48,1152]{1,0:T(8,128)(2,1)} %get-tuple-element.29), channel_id=1, source_target_pairs={{0,16},{8,24},{16,0},{24,8},{1,17},{9,25},{17,1},{25,9},{2,18},{10... | collective-permute-start | bytes 331784 | tf_op jit(solution)/shard_map/ppermute | solution.py:280
  11.4 0.9 %copy-start.5 = (bf16[48,1152]{1,0:T(8,128)(2,1)S(1)}, bf16[48,1152]{1,0:T(8,128)(2,1)}, u32[]{:S(2)}) copy-start(bf16[48,1152]{1,0:T(8,128)(2,1)} %get-tuple-element.30) | copy-start | bytes 331780
  11.4 3.4 %copy-start.4 = (bf16[48,1152]{1,0:T(8,128)(2,1)S(1)}, bf16[48,1152]{1,0:T(8,128)(2,1)}, u32[]{:S(2)}) copy-start(bf16[48,1152]{1,0:T(8,128)(2,1)} %get-tuple-element.33.rest_0_) | copy-start | bytes 331780
  12.3 6.8 %collective-permute-start.2 = (bf16[48,1152]{1,0:T(8,128)(2,1)S(1)}, bf16[48,1152]{1,0:T(8,128)(2,1)S(1)}, u32[]{:S(2)}, u32[]{:S(2)}) collective-permute-start(bf16[48,1152]{1,0:T(8,128)(2,1)S(1)} %copy-done.5), channel_id=1, source_target_pairs={{0,24},{8,16},{16,8},{24,0},{1,25},{9,17},{17,9},{25,1},{2,26},{10... | collective-permute-start | bytes 331784 | tf_op jit(solution)/shard_map/ppermute | solution.py:280
  14.7 4.3 %copy-start.3 = (bf16[48,1152]{1,0:T(8,128)(2,1)S(1)}, bf16[48,1152]{1,0:T(8,128)(2,1)}, u32[]{:S(2)}) copy-start(bf16[48,1152]{1,0:T(8,128)(2,1)} %get-tuple-element.27.rest_0_) | copy-start | bytes 331780
  14.8 5.6 %collective-permute-start.6 = (bf16[48,1152]{1,0:T(8,128)(2,1)S(1)}, bf16[48,1152]{1,0:T(8,128)(2,1)S(1)}, u32[]{:S(2)}, u32[]{:S(2)}) collective-permute-start(bf16[48,1152]{1,0:T(8,128)(2,1)S(1)} %get-tuple-element.38.rest_0_), channel_id=1, source_target_pairs={{0,2},{1,3},{2,0},{3,1},{4,6},{5,7},{6,4},{7,5},{8,10},{9,11},{10,... | collective-permute-start | bytes 331784 | tf_op jit(solution)/shard_map/ppermute | solution.py:280
  16.5 9.6 %collective-permute-start.15 = (bf16[48,1152]{1,0:T(8,128)(2,1)S(1)}, bf16[48,1152]{1,0:T(8,128)(2,1)S(1)}, u32[]{:S(2)}, u32[]{:S(2)}) collective-permute-start(bf16[48,1152]{1,0:T(8,128)(2,1)S(1)} %get-tuple-element.38.rest_0_), channel_id=1, source_target_pairs={{0,6},{1,7},{2,4},{3,5},{4,2},{5,3},{6,0},{7,1},{8,14},{9,15},{10,... | collective-permute-start | bytes 331784 | tf_op jit(solution)/shard_map/ppermute | solution.py:280
  18.9 12.4 %collective-permute-start.14 = (bf16[48,1152]{1,0:T(8,128)(2,1)S(1)}, bf16[48,1152]{1,0:T(8,128)(2,1)S(1)}, u32[]{:S(2)}, u32[]{:S(2)}) collective-permute-start(bf16[48,1152]{1,0:T(8,128)(2,1)S(1)} %get-tuple-element.38.rest_0_), channel_id=1, source_target_pairs={{0,4},{1,5},{2,6},{3,7},{4,0},{5,1},{6,2},{7,3},{8,12},{9,13},{10,... | collective-permute-start | bytes 331784 | tf_op jit(solution)/shard_map/ppermute | solution.py:280
  20.4 16.6 %collective-permute-start.8 = (bf16[48,2304]{1,0:T(8,128)(2,1)S(1)}, bf16[48,2304]{1,0:T(8,128)(2,1)S(1)}, u32[]{:S(2)}, u32[]{:S(2)}) collective-permute-start(bf16[48,2304]{1,0:T(8,128)(2,1)S(1)} %shard_map.113.rest_0_), channel_id=1, source_target_pairs={{0,16},{8,24},{16,0},{24,8},{1,17},{9,25},{17,1},{25,9},{2,18},{10... | collective-permute-start | bytes 663560 | tf_op jit(solution)/shard_map/ppermute | solution.py:280
  23.1 13.9 %collective-permute-start.7 = (bf16[48,2304]{1,0:T(8,128)(2,1)S(1)}, bf16[48,2304]{1,0:T(8,128)(2,1)S(1)}, u32[]{:S(2)}, u32[]{:S(2)}) collective-permute-start(bf16[48,2304]{1,0:T(8,128)(2,1)S(1)} %shard_map.113.rest_0_), channel_id=1, source_target_pairs={{0,8},{8,0},{16,24},{24,16},{1,9},{9,1},{17,25},{25,17},{2,10},{10... | collective-permute-start | bytes 663560 | tf_op jit(solution)/shard_map/ppermute | solution.py:280
  23.1 8.3 %collective-permute-start.12 = (bf16[48,1152]{1,0:T(8,128)(2,1)S(1)}, bf16[48,1152]{1,0:T(8,128)(2,1)S(1)}, u32[]{:S(2)}, u32[]{:S(2)}) collective-permute-start(bf16[48,1152]{1,0:T(8,128)(2,1)S(1)} %get-tuple-element.42.rest_0_.rest_4_), channel_id=1, source_target_pairs={{0,6},{1,7},{2,4},{3,5},{4,2},{5,3},{6,0},{7,1},{8,14},{9,15},{10,... | collective-permute-start | bytes 331784 | tf_op jit(solution)/shard_map/ppermute | solution.py:280
  26.1 9.8 %collective-permute-start.11 = (bf16[48,1152]{1,0:T(8,128)(2,1)S(1)}, bf16[48,1152]{1,0:T(8,128)(2,1)S(1)}, u32[]{:S(2)}, u32[]{:S(2)}) collective-permute-start(bf16[48,1152]{1,0:T(8,128)(2,1)S(1)} %get-tuple-element.42.rest_0_.rest_4_), channel_id=1, source_target_pairs={{0,4},{1,5},{2,6},{3,7},{4,0},{5,1},{6,2},{7,3},{8,12},{9,13},{10,... | collective-permute-start | bytes 331784 | tf_op jit(solution)/shard_map/ppermute | solution.py:280
  31.4 5.6 %collective-permute-start.10 = (bf16[48,1152]{1,0:T(8,128)(2,1)S(1)}, bf16[48,1152]{1,0:T(8,128)(2,1)S(1)}, u32[]{:S(2)}, u32[]{:S(2)}) collective-permute-start(bf16[48,1152]{1,0:T(8,128)(2,1)S(1)} %get-tuple-element.42.rest_0_.rest_4_), channel_id=1, source_target_pairs={{0,2},{1,3},{2,0},{3,1},{4,6},{5,7},{6,4},{7,5},{8,10},{9,11},{10,... | collective-permute-start | bytes 331784 | tf_op jit(solution)/shard_map/ppermute | solution.py:280
  31.4 7.6 %collective-permute-start.16 = (bf16[192,1152]{1,0:T(8,128)(2,1)S(1)}, bf16[192,1152]{1,0:T(8,128)(2,1)S(1)}, u32[]{:S(2)}, u32[]{:S(2)}) collective-permute-start(bf16[192,1152]{1,0:T(8,128)(2,1)S(1)} %shard_map.116.rest_2_), channel_id=1, source_target_pairs={{0,1},{1,0},{2,3},{3,2},{4,5},{5,4},{6,7},{7,6},{8,9},{9,8},{10,11... | collective-permute-start | bytes 1327112 | tf_op jit(solution)/shard_map/ppermute | solution.py:280
  37.0 2.0 %collective-permute-start.13 = (bf16[192,1152]{1,0:T(8,128)(2,1)S(1)}, bf16[192,1152]{1,0:T(8,128)(2,1)S(1)}, u32[]{:S(2)}, u32[]{:S(2)}) collective-permute-start(bf16[192,1152]{1,0:T(8,128)(2,1)S(1)} %shard_map.115.rest_0_), channel_id=1, source_target_pairs={{0,1},{1,0},{2,3},{3,2},{4,5},{5,4},{6,7},{7,6},{8,9},{9,8},{10,11... | collective-permute-start | bytes 1327112 | tf_op jit(solution)/shard_map/ppermute | solution.py:280
  37.1 17.3 %collective-permute-start.9 = (bf16[48,2304]{1,0:T(8,128)(2,1)S(1)}, bf16[48,2304]{1,0:T(8,128)(2,1)S(1)}, u32[]{:S(2)}, u32[]{:S(2)}) collective-permute-start(bf16[48,2304]{1,0:T(8,128)(2,1)S(1)} %shard_map.113.rest_0_), channel_id=1, source_target_pairs={{0,24},{8,16},{16,8},{24,0},{1,25},{9,17},{17,9},{25,1},{2,26},{10... | collective-permute-start | bytes 663560 | tf_op jit(solution)/shard_map/ppermute | solution.py:280
  50.8 9.3 %collective-permute-start.19 = (bf16[48,2304]{1,0:T(8,128)(2,1)S(1)}, bf16[48,2304]{1,0:T(8,128)(2,1)S(1)}, u32[]{:S(2)}, u32[]{:S(2)}) collective-permute-start(bf16[48,2304]{1,0:T(8,128)(2,1)S(1)} %shard_map.117.rest_0_), channel_id=1, source_target_pairs={{0,24},{8,16},{16,8},{24,0},{1,25},{9,17},{17,9},{25,1},{2,26},{10... | collective-permute-start | bytes 663560 | tf_op jit(solution)/shard_map/ppermute | solution.py:280
  52.3 11.7 %collective-permute-start.18 = (bf16[48,2304]{1,0:T(8,128)(2,1)S(1)}, bf16[48,2304]{1,0:T(8,128)(2,1)S(1)}, u32[]{:S(2)}, u32[]{:S(2)}) collective-permute-start(bf16[48,2304]{1,0:T(8,128)(2,1)S(1)} %shard_map.117.rest_0_), channel_id=1, source_target_pairs={{0,16},{8,24},{16,0},{24,8},{1,17},{9,25},{17,1},{25,9},{2,18},{10... | collective-permute-start | bytes 663560 | tf_op jit(solution)/shard_map/ppermute | solution.py:280
  52.8 11.3 %collective-permute-start.17 = (bf16[48,2304]{1,0:T(8,128)(2,1)S(1)}, bf16[48,2304]{1,0:T(8,128)(2,1)S(1)}, u32[]{:S(2)}, u32[]{:S(2)}) collective-permute-start(bf16[48,2304]{1,0:T(8,128)(2,1)S(1)} %shard_map.117.rest_0_), channel_id=1, source_target_pairs={{0,8},{8,0},{16,24},{24,16},{1,9},{9,1},{17,25},{25,17},{2,10},{10... | collective-permute-start | bytes 663560 | tf_op jit(solution)/shard_map/ppermute | solution.py:280

commit v10 on v9

--- a/solution.py
+++ b/solution.py
@@ -28,7 +28,7 @@
 OFFSETS = [0, QKV, QKV + D, QKV + D + MLP]
 PADDED = [-(-width // 128) * 128 for width in WIDTHS]
 DOWN, EMBED = 4, 5
-TILE = 256
+TILE = 768
 
 
 def plan(n_rep):
@@ -68,9 +68,14 @@
 def split_kernel(bins, windows, index, wide, down, embed, *rest):
     n = len(bins)
     outs, held, sems = rest[: len(windows) * n], rest[-4:-1], rest[-1]
-    copies = [pltpu.make_async_copy(src, dst, sems.at[i]) for i, (src, dst) in enumerate(zip((wide, down, embed), held))]
-    for copy in copies:
-        copy.start()
+    copies = []
+    for matrix, width in enumerate(WIDTHS):
+        src, dst = (down, held[1]) if matrix == DOWN else (embed, held[2]) if matrix == EMBED else (wide, held[0])
+        if matrix not in (DOWN, EMBED):
+            span = slice(OFFSETS[matrix], OFFSETS[matrix] + width)
+            src, dst = src.at[:, span], dst.at[:, span]
+        copies.append(pltpu.make_async_copy(src, dst, sems.at[matrix]))
+        copies[-1].start()
     for copy in copies:
         copy.wait()
     for half, (low, high) in enumerate(windows):
@@ -313,7 +318,7 @@
         [block(high - low) for low, high in windows for _ in range(n_rep)],
         (index, *grads),
         [SMEM] + [ANY] * 3,
-        [pltpu.VMEM(array.shape, jnp.float32) for array in grads] + [pltpu.SemaphoreType.DMA((3,))],
+        [pltpu.VMEM(array.shape, jnp.float32) for array in grads] + [pltpu.SemaphoreType.DMA((6,))],
         limit=VMEM_ALL,
     )
     mom_own = call(

time: 65.1 us -> 65.2 us (level)
  no operation moved by 1% of the time
where the time goes in v10:
time: 65.2 us; the launch traced here: 65 us
  starting transfers between devices  28.2 us (43%)
  waiting for transfers between devices  18.1 us (28%)
  Pallas kernels  17.1 us (26%)
  local copies, waits for them, and re-layouts  0.83 us (1%)
  between operations  0.78 us (1%)
    ppermute x20, starting transfers between devices, swap(): return lax.ppermute(value, axis, [(i, i ^ k) for i in range(n)])  28.2 us
    ppermute x20, waiting for transfers between devices, swap(): return lax.ppermute(value, axis, [(i, i ^ k) for i in range(n)])  18.1 us
    pallas_call x10, Pallas kernels, call(): pl.pallas_call(kernel, out_shape=tuple(outs), in_specs=specs, out_specs=t...  17.1 us
  transfers between devices with their start and end apart: 20, of which 8 were waited for; matrix products, arithmetic and copies ran while one was open for 0% of the time, Pallas kernels for 21%

profile of v10, /device:TPU:0, one launch (start us, length us, event | category | flops | bytes accessed | tf_op | source)
XLA Modules:
  0.0 65.0 jit_solution(4540310140144127849)
XLA Ops:
  0.7 2.8 %shard_map.110 = (bf16[48,1152]{1,0:T(8,128)(2,1)}, bf16[48,1152]{1,0:T(8,128)(2,1)}, bf16[48,1152]{1,0:T(8,128)(2,1)}, bf16[48,1152]{1,0:T(8,128)(2,1)}, bf16[4...) custom-call(s32[1]{0:T(128)} %bitcast.index, ...), custom_call_target="tpu_custom_call" | custom-call | bytes 2404036 | tf_op jit(solution)/shard_map/pallas_call | solution.py:273
  3.4 3.0 %collective-permute-start.3 = (bf16[48,1152]{1,0:T(8,128)(2,1)}, bf16[48,1152]{1,0:T(8,128)(2,1)S(1)}, u32[]{:S(2)}, u32[]{:S(2)}) collective-permute-start(bf16[48,1152]{1,0:T(8,128)(2,1)} %get-tuple-element.34), channel_id=1, source_target_pairs={{0,8},{8,0},{16,24},{24,16},{1,9},{9,1},{17,25},{25,17},{2,10},{10... | collective-permute-start | bytes 331784 | tf_op jit(solution)/shard_map/ppermute | solution.py:285
  6.4 1.5 %collective-permute-start.4 = (bf16[48,1152]{1,0:T(8,128)(2,1)}, bf16[48,1152]{1,0:T(8,128)(2,1)S(1)}, u32[]{:S(2)}, u32[]{:S(2)}) collective-permute-start(bf16[48,1152]{1,0:T(8,128)(2,1)} %get-tuple-element.35), channel_id=1, source_target_pairs={{0,16},{8,24},{16,0},{24,8},{1,17},{9,25},{17,1},{25,9},{2,18},{10... | collective-permute-start | bytes 331784 | tf_op jit(solution)/shard_map/ppermute | solution.py:285
  8.0 1.9 %collective-permute-start = (bf16[48,1152]{1,0:T(8,128)(2,1)}, bf16[48,1152]{1,0:T(8,128)(2,1)S(1)}, u32[]{:S(2)}, u32[]{:S(2)}) collective-permute-start(bf16[48,1152]{1,0:T(8,128)(2,1)} %get-tuple-element.28), channel_id=1, source_target_pairs={{0,8},{8,0},{16,24},{24,16},{1,9},{9,1},{17,25},{25,17},{2,10},{10... | collective-permute-start | bytes 331784 | tf_op jit(solution)/shard_map/ppermute | solution.py:285
  9.9 1.5 %collective-permute-start.1 = (bf16[48,1152]{1,0:T(8,128)(2,1)}, bf16[48,1152]{1,0:T(8,128)(2,1)S(1)}, u32[]{:S(2)}, u32[]{:S(2)}) collective-permute-start(bf16[48,1152]{1,0:T(8,128)(2,1)} %get-tuple-element.29), channel_id=1, source_target_pairs={{0,16},{8,24},{16,0},{24,8},{1,17},{9,25},{17,1},{25,9},{2,18},{10... | collective-permute-start | bytes 331784 | tf_op jit(solution)/shard_map/ppermute | solution.py:285
  11.5 0.8 %copy-done.5 = bf16[48,1152]{1,0:T(8,128)(2,1)S(1)} copy-done((bf16[48,1152]{1,0:T(8,128)(2,1)S(1)}, bf16[48,1152]{1,0:T(8,128)(2,1)}, u32[]{:S(2)}) %copy-start.5) | copy-done | bytes 110616
  12.3 1.0 %collective-permute-start.2 = (bf16[48,1152]{1,0:T(8,128)(2,1)S(1)}, bf16[48,1152]{1,0:T(8,128)(2,1)S(1)}, u32[]{:S(2)}, u32[]{:S(2)}) collective-permute-start(bf16[48,1152]{1,0:T(8,128)(2,1)S(1)} %copy-done.5), channel_id=1, source_target_pairs={{0,24},{8,16},{16,8},{24,0},{1,25},{9,17},{17,9},{25,1},{2,26},{10... | collective-permute-start | bytes 331784 | tf_op jit(solution)/shard_map/ppermute | solution.py:285
  13.3 0.8 %collective-permute-done.4.rest_2_ = bf16[48,1152]{1,0:T(8,128)(2,1)S(1)} collective-permute-done((bf16[48,1152]{1,0:T(8,128)(2,1)}, bf16[48,1152]{1,0:T(8,128)(2,1)S(1)}, u32[]{:S(2)}, u32[]{:S(2)}) %collective-permute-start.4) | collective-permute-done | bytes 110624 | tf_op jit(solution)/shard_map/ppermute | solution.py:285
  14.1 0.7 %collective-permute-done.5.rest_3_ = bf16[48,1152]{1,0:T(8,128)(2,1)S(1)} collective-permute-done((bf16[48,1152]{1,0:T(8,128)(2,1)}, bf16[48,1152]{1,0:T(8,128)(2,1)S(1)}, u32[]{:S(2)}, u32[]{:S(2)}) %collective-permute-start.5) | collective-permute-done | bytes 110624 | tf_op jit(solution)/shard_map/ppermute | solution.py:285
  14.8 0.1 shard_map.112
  14.9 1.6 %collective-permute-start.6 = (bf16[48,1152]{1,0:T(8,128)(2,1)S(1)}, bf16[48,1152]{1,0:T(8,128)(2,1)S(1)}, u32[]{:S(2)}, u32[]{:S(2)}) collective-permute-start(bf16[48,1152]{1,0:T(8,128)(2,1)S(1)} %get-tuple-element.38.rest_0_), channel_id=1, source_target_pairs={{0,2},{1,3},{2,0},{3,1},{4,6},{5,7},{6,4},{7,5},{8,10},{9,11},{10,... | collective-permute-start | bytes 331784 | tf_op jit(solution)/shard_map/ppermute | solution.py:285
  16.6 2.5 %collective-permute-start.15 = (bf16[48,1152]{1,0:T(8,128)(2,1)S(1)}, bf16[48,1152]{1,0:T(8,128)(2,1)S(1)}, u32[]{:S(2)}, u32[]{:S(2)}) collective-permute-start(bf16[48,1152]{1,0:T(8,128)(2,1)S(1)} %get-tuple-element.38.rest_0_), channel_id=1, source_target_pairs={{0,6},{1,7},{2,4},{3,5},{4,2},{5,3},{6,0},{7,1},{8,14},{9,15},{10,... | collective-permute-start | bytes 331784 | tf_op jit(solution)/shard_map/ppermute | solution.py:285
  19.0 0.1 collective-permute-start.14
  19.2 0.1 shard_map.111
  19.3 1.2 %collective-permute-done.6.rest_0_.rest_1_ = bf16[48,1152]{1,0:T(8,128)(2,1)S(1)} collective-permute-done((bf16[48,1152]{1,0:T(8,128)(2,1)S(1)}, bf16[48,1152]{1,0:T(8,128)(2,1)S(1)}, u32[]{:S(2)}, u32[]{:S(2)}) %collective-permute-start.6) | collective-permute-done | bytes 110624 | tf_op jit(solution)/shard_map/ppermute | solution.py:285
  20.5 2.7 %collective-permute-start.8 = (bf16[48,2304]{1,0:T(8,128)(2,1)S(1)}, bf16[48,2304]{1,0:T(8,128)(2,1)S(1)}, u32[]{:S(2)}, u32[]{:S(2)}) collective-permute-start(bf16[48,2304]{1,0:T(8,128)(2,1)S(1)} %shard_map.113.rest_0_), channel_id=1, source_target_pairs={{0,16},{8,24},{16,0},{24,8},{1,17},{9,25},{17,1},{25,9},{2,18},{10... | collective-permute-start | bytes 663560 | tf_op jit(solution)/shard_map/ppermute | solution.py:285
  23.2 3.0 %collective-permute-start.12 = (bf16[48,1152]{1,0:T(8,128)(2,1)S(1)}, bf16[48,1152]{1,0:T(8,128)(2,1)S(1)}, u32[]{:S(2)}, u32[]{:S(2)}) collective-permute-start(bf16[48,1152]{1,0:T(8,128)(2,1)S(1)} %get-tuple-element.42.rest_0_.rest_4_), channel_id=1, source_target_pairs={{0,6},{1,7},{2,4},{3,5},{4,2},{5,3},{6,0},{7,1},{8,14},{9,15},{10,... | collective-permute-start | bytes 331784 | tf_op jit(solution)/shard_map/ppermute | solution.py:285
  26.2 3.7 %collective-permute-start.11 = (bf16[48,1152]{1,0:T(8,128)(2,1)S(1)}, bf16[48,1152]{1,0:T(8,128)(2,1)S(1)}, u32[]{:S(2)}, u32[]{:S(2)}) collective-permute-start(bf16[48,1152]{1,0:T(8,128)(2,1)S(1)} %get-tuple-element.42.rest_0_.rest_4_), channel_id=1, source_target_pairs={{0,4},{1,5},{2,6},{3,7},{4,0},{5,1},{6,2},{7,3},{8,12},{9,13},{10,... | collective-permute-start | bytes 331784 | tf_op jit(solution)/shard_map/ppermute | solution.py:285
  29.9 1.6 %collective-permute-done.14.rest_2_ = bf16[48,1152]{1,0:T(8,128)(2,1)S(1)} collective-permute-done((bf16[48,1152]{1,0:T(8,128)(2,1)S(1)}, bf16[48,1152]{1,0:T(8,128)(2,1)S(1)}, u32[]{:S(2)}, u32[]{:S(2)}) %collective-permute-start.14) | collective-permute-done | bytes 110624 | tf_op jit(solution)/shard_map/ppermute | solution.py:285
  31.5 0.1 collective-permute-start.16
  31.6 4.4 %collective-permute-done.11.rest_2_ = bf16[48,1152]{1,0:T(8,128)(2,1)S(1)} collective-permute-done((bf16[48,1152]{1,0:T(8,128)(2,1)S(1)}, bf16[48,1152]{1,0:T(8,128)(2,1)S(1)}, u32[]{:S(2)}, u32[]{:S(2)}) %collective-permute-start.11) | collective-permute-done | bytes 110624 | tf_op jit(solution)/shard_map/ppermute | solution.py:285
  36.0 1.1 %collective-permute-done.10.rest_1_ = bf16[48,1152]{1,0:T(8,128)(2,1)S(1)} collective-permute-done((bf16[48,1152]{1,0:T(8,128)(2,1)S(1)}, bf16[48,1152]{1,0:T(8,128)(2,1)S(1)}, u32[]{:S(2)}, u32[]{:S(2)}) %collective-permute-start.10) | collective-permute-done | bytes 110624 | tf_op jit(solution)/shard_map/ppermute | solution.py:285
  37.1 0.1 collective-permute-start.13
  37.2 1.9 %collective-permute-start.9 = (bf16[48,2304]{1,0:T(8,128)(2,1)S(1)}, bf16[48,2304]{1,0:T(8,128)(2,1)S(1)}, u32[]{:S(2)}, u32[]{:S(2)}) collective-permute-start(bf16[48,2304]{1,0:T(8,128)(2,1)S(1)} %shard_map.113.rest_0_), channel_id=1, source_target_pairs={{0,24},{8,16},{16,8},{24,0},{1,25},{9,17},{17,9},{25,1},{2,26},{10... | collective-permute-start | bytes 663560 | tf_op jit(solution)/shard_map/ppermute | solution.py:285
  39.1 11.8 %shard_map.117.rest_0_ = bf16[48,2304]{1,0:T(8,128)(2,1)S(1)} custom-call(s32[1]{0:T(128)} %bitcast.index, bf16[192,1152]{1,0:T(8,128)(2,1)S(1)} %shard_map.115.rest_0_, bf16[192,1152]{1,0:T(8,128)(2,1)S(1)} %collective-permute-done.13.rest_1_, bf16[192,1152]{1,0:T(8,128)(2,1)S(1)} %shard_map.116.rest_2_, bf16[192,1152]{1,0:T(8,128)(2,1)S(1)} %collective-permute-done.16.rest_3_), custom_call_target="tpu_custom_call" | custom-call | flops 7361003520 | bytes 1990660 | tf_op jit(solution)/shard_map/pallas_call | solution.py:273
  50.9 1.5 %collective-permute-start.19 = (bf16[48,2304]{1,0:T(8,128)(2,1)S(1)}, bf16[48,2304]{1,0:T(8,128)(2,1)S(1)}, u32[]{:S(2)}, u32[]{:S(2)}) collective-permute-start(bf16[48,2304]{1,0:T(8,128)(2,1)S(1)} %shard_map.117.rest_0_), channel_id=1, source_target_pairs={{0,24},{8,16},{16,8},{24,0},{1,25},{9,17},{17,9},{25,1},{2,26},{10... | collective-permute-start | bytes 663560 | tf_op jit(solution)/shard_map/ppermute | solution.py:285
  52.4 0.5 collective-permute-start.18
  52.9 1.6 %collective-permute-start.17 = (bf16[48,2304]{1,0:T(8,128)(2,1)S(1)}, bf16[48,2304]{1,0:T(8,128)(2,1)S(1)}, u32[]{:S(2)}, u32[]{:S(2)}) collective-permute-start(bf16[48,2304]{1,0:T(8,128)(2,1)S(1)} %shard_map.117.rest_0_), channel_id=1, source_target_pairs={{0,8},{8,0},{16,24},{24,16},{1,9},{9,1},{17,25},{25,17},{2,10},{10... | collective-permute-start | bytes 663560 | tf_op jit(solution)/shard_map/ppermute | solution.py:285
  54.5 1.3 %shard_map.114 = (f32[48,5376]{1,0:T(8,128)}, f32[48,1536]{1,0:T(8,128)}, f32[48,1001]{1,0:T(8,128)}) custom-call(s32[1]{0:T(128)} %bitcast.index, f32[48,5376]{1,0:T(8,128)S(1)} %bitcast.24, f32[48,1536]{1,0:T(8,128)S(1)} %bitcast.26, f32[48,1001]{1,0:T(8,128)S(1)} %bitcast.28, bf16[48,2304]{1,0:T(8,128)(2,1)S(1)} %shard_map.113.rest_0_, ...), custom_call_target="tpu_custom_call" | custom-call | bytes 3923332 | tf_op jit(solution)/shard_map/pallas_call | solution.py:273
  55.8 4.4 %collective-permute-done.19.rest_3_ = bf16[48,2304]{1,0:T(8,128)(2,1)S(1)} collective-permute-done((bf16[48,2304]{1,0:T(8,128)(2,1)S(1)}, bf16[48,2304]{1,0:T(8,128)(2,1)S(1)}, u32[]{:S(2)}, u32[]{:S(2)}) %collective-permute-start.19) | collective-permute-done | bytes 221216 | tf_op jit(solution)/shard_map/ppermute | solution.py:285
  60.2 3.9 %collective-permute-done.18.rest_2_ = bf16[48,2304]{1,0:T(8,128)(2,1)S(1)} collective-permute-done((bf16[48,2304]{1,0:T(8,128)(2,1)S(1)}, bf16[48,2304]{1,0:T(8,128)(2,1)S(1)}, u32[]{:S(2)}, u32[]{:S(2)}) %collective-permute-start.18) | collective-permute-done | bytes 221216 | tf_op jit(solution)/shard_map/ppermute | solution.py:285
  64.1 0.9 %shard_map.118 = (bf16[48,5376]{1,0:T(8,128)(2,1)}, bf16[48,1536]{1,0:T(8,128)(2,1)}, bf16[48,1001]{1,0:T(8,128)(2,1)}) custom-call(s32[1]{0:T(128)} %bitcast.index, bf16[48,2304]{1,0:T(8,128)(2,1)S(1)} %shard_map.117.rest_0_, bf16[48,2304]{1,0:T(8,128)(2,1)S(1)} %collective-permute-done.17.rest_1_, bf16[48,2304]{1,0:T(8,128)(2,1)S(1)} %collective-permute-done.18.rest_2_, ...), custom_call_target="tpu_custom_call" | custom-call | bytes 1644388 | tf_op jit(solution)/shard_map/pallas_call | solution.py:273
  (30 shorter events, 0.2 us)
Async XLA Ops:
  0.6 10.8 %copy-start = (f32[1,48,5376]{2,1,0:T(8,128)S(1)}, f32[1,48,5376]{2,1,0:T(8,128)}, u32[]{:S(2)}) copy-start(f32[1,48,5376]{2,1,0:T(8,128)} %param.9) | copy-start | bytes 3096580
  0.6 10.8 %copy-start.1 = (f32[1,1536,48]{1,2,0:T(8,128)S(1)}, f32[1,1536,48]{1,2,0:T(8,128)}, u32[]{:S(2)}) copy-start(f32[1,1536,48]{1,2,0:T(8,128)} %param.10) | copy-start | bytes 884740
  0.7 10.8 %copy-start.2 = (f32[1001,48]{0,1:T(8,128)S(1)}, f32[1001,48]{0,1:T(8,128)}, u32[]{:S(2)}) copy-start(f32[1001,48]{0,1:T(8,128)} %param.11) | copy-start | bytes 576580
  3.4 8.1 %collective-permute-start.3 = (bf16[48,1152]{1,0:T(8,128)(2,1)}, bf16[48,1152]{1,0:T(8,128)(2,1)S(1)}, u32[]{:S(2)}, u32[]{:S(2)}) collective-permute-start(bf16[48,1152]{1,0:T(8,128)(2,1)} %get-tuple-element.34), channel_id=1, source_target_pairs={{0,8},{8,0},{16,24},{24,16},{1,9},{9,1},{17,25},{25,17},{2,10},{10... | collective-permute-start | bytes 331784 | tf_op jit(solution)/shard_map/ppermute | solution.py:285
  6.4 7.7 %collective-permute-start.4 = (bf16[48,1152]{1,0:T(8,128)(2,1)}, bf16[48,1152]{1,0:T(8,128)(2,1)S(1)}, u32[]{:S(2)}, u32[]{:S(2)}) collective-permute-start(bf16[48,1152]{1,0:T(8,128)(2,1)} %get-tuple-element.35), channel_id=1, source_target_pairs={{0,16},{8,24},{16,0},{24,8},{1,17},{9,25},{17,1},{25,9},{2,18},{10... | collective-permute-start | bytes 331784 | tf_op jit(solution)/shard_map/ppermute | solution.py:285
  7.9 6.9 %collective-permute-start.5 = (bf16[48,1152]{1,0:T(8,128)(2,1)}, bf16[48,1152]{1,0:T(8,128)(2,1)S(1)}, u32[]{:S(2)}, u32[]{:S(2)}) collective-permute-start(bf16[48,1152]{1,0:T(8,128)(2,1)} %get-tuple-element.36), channel_id=1, source_target_pairs={{0,24},{8,16},{16,8},{24,0},{1,25},{9,17},{17,9},{25,1},{2,26},{10... | collective-permute-start | bytes 331784 | tf_op jit(solution)/shard_map/ppermute | solution.py:285
  8.0 11.1 %collective-permute-start = (bf16[48,1152]{1,0:T(8,128)(2,1)}, bf16[48,1152]{1,0:T(8,128)(2,1)S(1)}, u32[]{:S(2)}, u32[]{:S(2)}) collective-permute-start(bf16[48,1152]{1,0:T(8,128)(2,1)} %get-tuple-element.28), channel_id=1, source_target_pairs={{0,8},{8,0},{16,24},{24,16},{1,9},{9,1},{17,25},{25,17},{2,10},{10... | collective-permute-start | bytes 331784 | tf_op jit(solution)/shard_map/ppermute | solution.py:285
  9.9 9.2 %collective-permute-start.1 = (bf16[48,1152]{1,0:T(8,128)(2,1)}, bf16[48,1152]{1,0:T(8,128)(2,1)S(1)}, u32[]{:S(2)}, u32[]{:S(2)}) collective-permute-start(bf16[48,1152]{1,0:T(8,128)(2,1)} %get-tuple-element.29), channel_id=1, source_target_pairs={{0,16},{8,24},{16,0},{24,8},{1,17},{9,25},{17,1},{25,9},{2,18},{10... | collective-permute-start | bytes 331784 | tf_op jit(solution)/shard_map/ppermute | solution.py:285
  11.4 0.9 %copy-start.5 = (bf16[48,1152]{1,0:T(8,128)(2,1)S(1)}, bf16[48,1152]{1,0:T(8,128)(2,1)}, u32[]{:S(2)}) copy-start(bf16[48,1152]{1,0:T(8,128)(2,1)} %get-tuple-element.30) | copy-start | bytes 331780
  11.4 3.4 %copy-start.4 = (bf16[48,1152]{1,0:T(8,128)(2,1)S(1)}, bf16[48,1152]{1,0:T(8,128)(2,1)}, u32[]{:S(2)}) copy-start(bf16[48,1152]{1,0:T(8,128)(2,1)} %get-tuple-element.33.rest_0_) | copy-start | bytes 331780
  12.3 6.8 %collective-permute-start.2 = (bf16[48,1152]{1,0:T(8,128)(2,1)S(1)}, bf16[48,1152]{1,0:T(8,128)(2,1)S(1)}, u32[]{:S(2)}, u32[]{:S(2)}) collective-permute-start(bf16[48,1152]{1,0:T(8,128)(2,1)S(1)} %copy-done.5), channel_id=1, source_target_pairs={{0,24},{8,16},{16,8},{24,0},{1,25},{9,17},{17,9},{25,1},{2,26},{10... | collective-permute-start | bytes 331784 | tf_op jit(solution)/shard_map/ppermute | solution.py:285
  14.8 4.3 %copy-start.3 = (bf16[48,1152]{1,0:T(8,128)(2,1)S(1)}, bf16[48,1152]{1,0:T(8,128)(2,1)}, u32[]{:S(2)}) copy-start(bf16[48,1152]{1,0:T(8,128)(2,1)} %get-tuple-element.27.rest_0_) | copy-start | bytes 331780
  14.9 5.6 %collective-permute-start.6 = (bf16[48,1152]{1,0:T(8,128)(2,1)S(1)}, bf16[48,1152]{1,0:T(8,128)(2,1)S(1)}, u32[]{:S(2)}, u32[]{:S(2)}) collective-permute-start(bf16[48,1152]{1,0:T(8,128)(2,1)S(1)} %get-tuple-element.38.rest_0_), channel_id=1, source_target_pairs={{0,2},{1,3},{2,0},{3,1},{4,6},{5,7},{6,4},{7,5},{8,10},{9,11},{10,... | collective-permute-start | bytes 331784 | tf_op jit(solution)/shard_map/ppermute | solution.py:285
  16.6 9.6 %collective-permute-start.15 = (bf16[48,1152]{1,0:T(8,128)(2,1)S(1)}, bf16[48,1152]{1,0:T(8,128)(2,1)S(1)}, u32[]{:S(2)}, u32[]{:S(2)}) collective-permute-start(bf16[48,1152]{1,0:T(8,128)(2,1)S(1)} %get-tuple-element.38.rest_0_), channel_id=1, source_target_pairs={{0,6},{1,7},{2,4},{3,5},{4,2},{5,3},{6,0},{7,1},{8,14},{9,15},{10,... | collective-permute-start | bytes 331784 | tf_op jit(solution)/shard_map/ppermute | solution.py:285
  19.0 12.4 %collective-permute-start.14 = (bf16[48,1152]{1,0:T(8,128)(2,1)S(1)}, bf16[48,1152]{1,0:T(8,128)(2,1)S(1)}, u32[]{:S(2)}, u32[]{:S(2)}) collective-permute-start(bf16[48,1152]{1,0:T(8,128)(2,1)S(1)} %get-tuple-element.38.rest_0_), channel_id=1, source_target_pairs={{0,4},{1,5},{2,6},{3,7},{4,0},{5,1},{6,2},{7,3},{8,12},{9,13},{10,... | collective-permute-start | bytes 331784 | tf_op jit(solution)/shard_map/ppermute | solution.py:285
  20.5 16.6 %collective-permute-start.8 = (bf16[48,2304]{1,0:T(8,128)(2,1)S(1)}, bf16[48,2304]{1,0:T(8,128)(2,1)S(1)}, u32[]{:S(2)}, u32[]{:S(2)}) collective-permute-start(bf16[48,2304]{1,0:T(8,128)(2,1)S(1)} %shard_map.113.rest_0_), channel_id=1, source_target_pairs={{0,16},{8,24},{16,0},{24,8},{1,17},{9,25},{17,1},{25,9},{2,18},{10... | collective-permute-start | bytes 663560 | tf_op jit(solution)/shard_map/ppermute | solution.py:285
  23.2 13.9 %collective-permute-start.7 = (bf16[48,2304]{1,0:T(8,128)(2,1)S(1)}, bf16[48,2304]{1,0:T(8,128)(2,1)S(1)}, u32[]{:S(2)}, u32[]{:S(2)}) collective-permute-start(bf16[48,2304]{1,0:T(8,128)(2,1)S(1)} %shard_map.113.rest_0_), channel_id=1, source_target_pairs={{0,8},{8,0},{16,24},{24,16},{1,9},{9,1},{17,25},{25,17},{2,10},{10... | collective-permute-start | bytes 663560 | tf_op jit(solution)/shard_map/ppermute | solution.py:285
  23.2 8.3 %collective-permute-start.12 = (bf16[48,1152]{1,0:T(8,128)(2,1)S(1)}, bf16[48,1152]{1,0:T(8,128)(2,1)S(1)}, u32[]{:S(2)}, u32[]{:S(2)}) collective-permute-start(bf16[48,1152]{1,0:T(8,128)(2,1)S(1)} %get-tuple-element.42.rest_0_.rest_4_), channel_id=1, source_target_pairs={{0,6},{1,7},{2,4},{3,5},{4,2},{5,3},{6,0},{7,1},{8,14},{9,15},{10,... | collective-permute-start | bytes 331784 | tf_op jit(solution)/shard_map/ppermute | solution.py:285
  26.2 9.8 %collective-permute-start.11 = (bf16[48,1152]{1,0:T(8,128)(2,1)S(1)}, bf16[48,1152]{1,0:T(8,128)(2,1)S(1)}, u32[]{:S(2)}, u32[]{:S(2)}) collective-permute-start(bf16[48,1152]{1,0:T(8,128)(2,1)S(1)} %get-tuple-element.42.rest_0_.rest_4_), channel_id=1, source_target_pairs={{0,4},{1,5},{2,6},{3,7},{4,0},{5,1},{6,2},{7,3},{8,12},{9,13},{10,... | collective-permute-start | bytes 331784 | tf_op jit(solution)/shard_map/ppermute | solution.py:285
  31.5 5.6 %collective-permute-start.10 = (bf16[48,1152]{1,0:T(8,128)(2,1)S(1)}, bf16[48,1152]{1,0:T(8,128)(2,1)S(1)}, u32[]{:S(2)}, u32[]{:S(2)}) collective-permute-start(bf16[48,1152]{1,0:T(8,128)(2,1)S(1)} %get-tuple-element.42.rest_0_.rest_4_), channel_id=1, source_target_pairs={{0,2},{1,3},{2,0},{3,1},{4,6},{5,7},{6,4},{7,5},{8,10},{9,11},{10,... | collective-permute-start | bytes 331784 | tf_op jit(solution)/shard_map/ppermute | solution.py:285
  31.5 7.6 %collective-permute-start.16 = (bf16[192,1152]{1,0:T(8,128)(2,1)S(1)}, bf16[192,1152]{1,0:T(8,128)(2,1)S(1)}, u32[]{:S(2)}, u32[]{:S(2)}) collective-permute-start(bf16[192,1152]{1,0:T(8,128)(2,1)S(1)} %shard_map.116.rest_2_), channel_id=1, source_target_pairs={{0,1},{1,0},{2,3},{3,2},{4,5},{5,4},{6,7},{7,6},{8,9},{9,8},{10,11... | collective-permute-start | bytes 1327112 | tf_op jit(solution)/shard_map/ppermute | solution.py:285
  37.1 2.0 %collective-permute-start.13 = (bf16[192,1152]{1,0:T(8,128)(2,1)S(1)}, bf16[192,1152]{1,0:T(8,128)(2,1)S(1)}, u32[]{:S(2)}, u32[]{:S(2)}) collective-permute-start(bf16[192,1152]{1,0:T(8,128)(2,1)S(1)} %shard_map.115.rest_0_), channel_id=1, source_target_pairs={{0,1},{1,0},{2,3},{3,2},{4,5},{5,4},{6,7},{7,6},{8,9},{9,8},{10,11... | collective-permute-start | bytes 1327112 | tf_op jit(solution)/shard_map/ppermute | solution.py:285
  37.2 17.3 %collective-permute-start.9 = (bf16[48,2304]{1,0:T(8,128)(2,1)S(1)}, bf16[48,2304]{1,0:T(8,128)(2,1)S(1)}, u32[]{:S(2)}, u32[]{:S(2)}) collective-permute-start(bf16[48,2304]{1,0:T(8,128)(2,1)S(1)} %shard_map.113.rest_0_), channel_id=1, source_target_pairs={{0,24},{8,16},{16,8},{24,0},{1,25},{9,17},{17,9},{25,1},{2,26},{10... | collective-permute-start | bytes 663560 | tf_op jit(solution)/shard_map/ppermute | solution.py:285
  50.9 9.3 %collective-permute-start.19 = (bf16[48,2304]{1,0:T(8,128)(2,1)S(1)}, bf16[48,2304]{1,0:T(8,128)(2,1)S(1)}, u32[]{:S(2)}, u32[]{:S(2)}) collective-permute-start(bf16[48,2304]{1,0:T(8,128)(2,1)S(1)} %shard_map.117.rest_0_), channel_id=1, source_target_pairs={{0,24},{8,16},{16,8},{24,0},{1,25},{9,17},{17,9},{25,1},{2,26},{10... | collective-permute-start | bytes 663560 | tf_op jit(solution)/shard_map/ppermute | solution.py:285
  52.4 11.7 %collective-permute-start.18 = (bf16[48,2304]{1,0:T(8,128)(2,1)S(1)}, bf16[48,2304]{1,0:T(8,128)(2,1)S(1)}, u32[]{:S(2)}, u32[]{:S(2)}) collective-permute-start(bf16[48,2304]{1,0:T(8,128)(2,1)S(1)} %shard_map.117.rest_0_), channel_id=1, source_target_pairs={{0,16},{8,24},{16,0},{24,8},{1,17},{9,25},{17,1},{25,9},{2,18},{10... | collective-permute-start | bytes 663560 | tf_op jit(solution)/shard_map/ppermute | solution.py:285
  52.9 11.3 %collective-permute-start.17 = (bf16[48,2304]{1,0:T(8,128)(2,1)S(1)}, bf16[48,2304]{1,0:T(8,128)(2,1)S(1)}, u32[]{:S(2)}, u32[]{:S(2)}) collective-permute-start(bf16[48,2304]{1,0:T(8,128)(2,1)S(1)} %shard_map.117.rest_0_), channel_id=1, source_target_pairs={{0,8},{8,0},{16,24},{24,16},{1,9},{9,1},{17,25},{25,17},{2,10},{10... | collective-permute-start | bytes 663560 | tf_op jit(solution)/shard_map/ppermute | solution.py:285

commit v11 on v9

--- a/solution.py
+++ b/solution.py
@@ -38,7 +38,8 @@
         owner = loads.index(min(loads))
         bins[owner].append(matrix)
         loads[owner] += PADDED[matrix]
-    return bins, max(loads)
+    order = sorted(range(n_rep), key=lambda owner: loads[owner])
+    return [bins[owner] for owner in order], max(loads)
 
 
 def window(group, low, high):

time: 65.1 us -> 64.9 us (level)
  Pallas kernels: 17 us -> 14.2 us
  starting transfers between devices: 28.2 us -> 30.2 us
    pallas_call x10, Pallas kernels: 17 us -> 14.2 us  [call(): pl.pallas_call(kernel, out_shape=tuple(outs), in_specs=specs, out_specs=t...]
    ppermute x20, starting transfers between devices: 28.2 us -> 30.2 us  [swap(): return lax.ppermute(value, axis, [(i, i ^ k) for i in range(n)])]
  transfers between devices with their start and end apart: 20 -> 20, of which waited for: 8 -> 9; matrix products, arithmetic and copies ran while one was open for 0% -> 0% of each run, Pallas kernels for 21% -> 16%
where the time goes in v11:
time: 64.9 us; the launch traced here: 64.8 us
  starting transfers between devices  30.2 us (47%)
  waiting for transfers between devices  18.7 us (29%)
  Pallas kernels  14.2 us (22%)
  local copies, waits for them, and re-layouts  0.83 us (1%)
  between operations  0.78 us (1%)
    ppermute x20, starting transfers between devices, swap(): return lax.ppermute(value, axis, [(i, i ^ k) for i in range(n)])  30.2 us
    ppermute x20, waiting for transfers between devices, swap(): return lax.ppermute(value, axis, [(i, i ^ k) for i in range(n)])  18.7 us
    pallas_call x10, Pallas kernels, call(): pl.pallas_call(kernel, out_shape=tuple(outs), in_specs=specs, out_specs=t...  14.2 us
  transfers between devices with their start and end apart: 20, of which 9 were waited for; matrix products, arithmetic and copies ran while one was open for 0% of the time, Pallas kernels for 16%

profile of v11, /device:TPU:0, one launch (start us, length us, event | category | flops | bytes accessed | tf_op | source)
XLA Modules:
  0.0 64.8 jit_solution(4655917460564667252)
XLA Ops:
  0.7 2.7 %shard_map.110 = (bf16[48,1152]{1,0:T(8,128)(2,1)}, bf16[48,1152]{1,0:T(8,128)(2,1)}, bf16[48,1152]{1,0:T(8,128)(2,1)}, bf16[48,1152]{1,0:T(8,128)(2,1)}, bf16[4...) custom-call(s32[1]{0:T(128)} %bitcast.index, ...), custom_call_target="tpu_custom_call" | custom-call | bytes 2404036 | tf_op jit(solution)/shard_map/pallas_call | solution.py:269
  3.4 3.0 %collective-permute-start.3 = (bf16[48,1152]{1,0:T(8,128)(2,1)}, bf16[48,1152]{1,0:T(8,128)(2,1)S(1)}, u32[]{:S(2)}, u32[]{:S(2)}) collective-permute-start(bf16[48,1152]{1,0:T(8,128)(2,1)} %get-tuple-element.34), channel_id=1, source_target_pairs={{0,8},{8,0},{16,24},{24,16},{1,9},{9,1},{17,25},{25,17},{2,10},{10... | collective-permute-start | bytes 331784 | tf_op jit(solution)/shard_map/ppermute | solution.py:281
  6.4 1.5 %collective-permute-start.4 = (bf16[48,1152]{1,0:T(8,128)(2,1)}, bf16[48,1152]{1,0:T(8,128)(2,1)S(1)}, u32[]{:S(2)}, u32[]{:S(2)}) collective-permute-start(bf16[48,1152]{1,0:T(8,128)(2,1)} %get-tuple-element.35), channel_id=1, source_target_pairs={{0,16},{8,24},{16,0},{24,8},{1,17},{9,25},{17,1},{25,9},{2,18},{10... | collective-permute-start | bytes 331784 | tf_op jit(solution)/shard_map/ppermute | solution.py:281
  7.9 1.9 %collective-permute-start = (bf16[48,1152]{1,0:T(8,128)(2,1)}, bf16[48,1152]{1,0:T(8,128)(2,1)S(1)}, u32[]{:S(2)}, u32[]{:S(2)}) collective-permute-start(bf16[48,1152]{1,0:T(8,128)(2,1)} %get-tuple-element.28), channel_id=1, source_target_pairs={{0,8},{8,0},{16,24},{24,16},{1,9},{9,1},{17,25},{25,17},{2,10},{10... | collective-permute-start | bytes 331784 | tf_op jit(solution)/shard_map/ppermute | solution.py:281
  9.8 1.5 %collective-permute-start.1 = (bf16[48,1152]{1,0:T(8,128)(2,1)}, bf16[48,1152]{1,0:T(8,128)(2,1)S(1)}, u32[]{:S(2)}, u32[]{:S(2)}) collective-permute-start(bf16[48,1152]{1,0:T(8,128)(2,1)} %get-tuple-element.29), channel_id=1, source_target_pairs={{0,16},{8,24},{16,0},{24,8},{1,17},{9,25},{17,1},{25,9},{2,18},{10... | collective-permute-start | bytes 331784 | tf_op jit(solution)/shard_map/ppermute | solution.py:281
  11.5 0.8 %copy-done.5 = bf16[48,1152]{1,0:T(8,128)(2,1)S(1)} copy-done((bf16[48,1152]{1,0:T(8,128)(2,1)S(1)}, bf16[48,1152]{1,0:T(8,128)(2,1)}, u32[]{:S(2)}) %copy-start.5) | copy-done | bytes 110616
  12.3 1.0 %collective-permute-start.2 = (bf16[48,1152]{1,0:T(8,128)(2,1)S(1)}, bf16[48,1152]{1,0:T(8,128)(2,1)S(1)}, u32[]{:S(2)}, u32[]{:S(2)}) collective-permute-start(bf16[48,1152]{1,0:T(8,128)(2,1)S(1)} %copy-done.5), channel_id=1, source_target_pairs={{0,24},{8,16},{16,8},{24,0},{1,25},{9,17},{17,9},{25,1},{2,26},{10... | collective-permute-start | bytes 331784 | tf_op jit(solution)/shard_map/ppermute | solution.py:281
  13.2 0.8 %collective-permute-done.4.rest_2_ = bf16[48,1152]{1,0:T(8,128)(2,1)S(1)} collective-permute-done((bf16[48,1152]{1,0:T(8,128)(2,1)}, bf16[48,1152]{1,0:T(8,128)(2,1)S(1)}, u32[]{:S(2)}, u32[]{:S(2)}) %collective-permute-start.4) | collective-permute-done | bytes 110624 | tf_op jit(solution)/shard_map/ppermute | solution.py:281
  14.1 0.7 %collective-permute-done.5.rest_3_ = bf16[48,1152]{1,0:T(8,128)(2,1)S(1)} collective-permute-done((bf16[48,1152]{1,0:T(8,128)(2,1)}, bf16[48,1152]{1,0:T(8,128)(2,1)S(1)}, u32[]{:S(2)}, u32[]{:S(2)}) %collective-permute-start.5) | collective-permute-done | bytes 110624 | tf_op jit(solution)/shard_map/ppermute | solution.py:281
  14.7 0.1 shard_map.112
  14.8 1.6 %collective-permute-start.6 = (bf16[48,1152]{1,0:T(8,128)(2,1)S(1)}, bf16[48,1152]{1,0:T(8,128)(2,1)S(1)}, u32[]{:S(2)}, u32[]{:S(2)}) collective-permute-start(bf16[48,1152]{1,0:T(8,128)(2,1)S(1)} %get-tuple-element.38.rest_0_), channel_id=1, source_target_pairs={{0,2},{1,3},{2,0},{3,1},{4,6},{5,7},{6,4},{7,5},{8,10},{9,11},{10,... | collective-permute-start | bytes 331784 | tf_op jit(solution)/shard_map/ppermute | solution.py:281
  16.5 2.5 %collective-permute-start.15 = (bf16[48,1152]{1,0:T(8,128)(2,1)S(1)}, bf16[48,1152]{1,0:T(8,128)(2,1)S(1)}, u32[]{:S(2)}, u32[]{:S(2)}) collective-permute-start(bf16[48,1152]{1,0:T(8,128)(2,1)S(1)} %get-tuple-element.38.rest_0_), channel_id=1, source_target_pairs={{0,6},{1,7},{2,4},{3,5},{4,2},{5,3},{6,0},{7,1},{8,14},{9,15},{10,... | collective-permute-start | bytes 331784 | tf_op jit(solution)/shard_map/ppermute | solution.py:281
  18.9 0.1 collective-permute-start.14
  19.1 0.1 shard_map.111
  19.2 1.2 %collective-permute-done.6.rest_0_.rest_1_ = bf16[48,1152]{1,0:T(8,128)(2,1)S(1)} collective-permute-done((bf16[48,1152]{1,0:T(8,128)(2,1)S(1)}, bf16[48,1152]{1,0:T(8,128)(2,1)S(1)}, u32[]{:S(2)}, u32[]{:S(2)}) %collective-permute-start.6) | collective-permute-done | bytes 110624 | tf_op jit(solution)/shard_map/ppermute | solution.py:281
  20.4 2.7 %collective-permute-start.8 = (bf16[48,2304]{1,0:T(8,128)(2,1)S(1)}, bf16[48,2304]{1,0:T(8,128)(2,1)S(1)}, u32[]{:S(2)}, u32[]{:S(2)}) collective-permute-start(bf16[48,2304]{1,0:T(8,128)(2,1)S(1)} %shard_map.113.rest_0_), channel_id=1, source_target_pairs={{0,16},{8,24},{16,0},{24,8},{1,17},{9,25},{17,1},{25,9},{2,18},{10... | collective-permute-start | bytes 663560 | tf_op jit(solution)/shard_map/ppermute | solution.py:281
  23.1 3.0 %collective-permute-start.12 = (bf16[48,1152]{1,0:T(8,128)(2,1)S(1)}, bf16[48,1152]{1,0:T(8,128)(2,1)S(1)}, u32[]{:S(2)}, u32[]{:S(2)}) collective-permute-start(bf16[48,1152]{1,0:T(8,128)(2,1)S(1)} %get-tuple-element.42.rest_0_.rest_4_), channel_id=1, source_target_pairs={{0,6},{1,7},{2,4},{3,5},{4,2},{5,3},{6,0},{7,1},{8,14},{9,15},{10,... | collective-permute-start | bytes 331784 | tf_op jit(solution)/shard_map/ppermute | solution.py:281
  26.1 3.7 %collective-permute-start.11 = (bf16[48,1152]{1,0:T(8,128)(2,1)S(1)}, bf16[48,1152]{1,0:T(8,128)(2,1)S(1)}, u32[]{:S(2)}, u32[]{:S(2)}) collective-permute-start(bf16[48,1152]{1,0:T(8,128)(2,1)S(1)} %get-tuple-element.42.rest_0_.rest_4_), channel_id=1, source_target_pairs={{0,4},{1,5},{2,6},{3,7},{4,0},{5,1},{6,2},{7,3},{8,12},{9,13},{10,... | collective-permute-start | bytes 331784 | tf_op jit(solution)/shard_map/ppermute | solution.py:281
  29.8 1.6 %collective-permute-done.14.rest_2_ = bf16[48,1152]{1,0:T(8,128)(2,1)S(1)} collective-permute-done((bf16[48,1152]{1,0:T(8,128)(2,1)S(1)}, bf16[48,1152]{1,0:T(8,128)(2,1)S(1)}, u32[]{:S(2)}, u32[]{:S(2)}) %collective-permute-start.14) | collective-permute-done | bytes 110624 | tf_op jit(solution)/shard_map/ppermute | solution.py:281
  31.4 0.1 collective-permute-start.16
  31.5 4.4 %collective-permute-done.11.rest_2_ = bf16[48,1152]{1,0:T(8,128)(2,1)S(1)} collective-permute-done((bf16[48,1152]{1,0:T(8,128)(2,1)S(1)}, bf16[48,1152]{1,0:T(8,128)(2,1)S(1)}, u32[]{:S(2)}, u32[]{:S(2)}) %collective-permute-start.11) | collective-permute-done | bytes 110624 | tf_op jit(solution)/shard_map/ppermute | solution.py:281
  35.9 1.1 %collective-permute-done.10.rest_1_ = bf16[48,1152]{1,0:T(8,128)(2,1)S(1)} collective-permute-done((bf16[48,1152]{1,0:T(8,128)(2,1)S(1)}, bf16[48,1152]{1,0:T(8,128)(2,1)S(1)}, u32[]{:S(2)}, u32[]{:S(2)}) %collective-permute-start.10) | collective-permute-done | bytes 110624 | tf_op jit(solution)/shard_map/ppermute | solution.py:281
  37.1 1.9 %collective-permute-start.9 = (bf16[48,2304]{1,0:T(8,128)(2,1)S(1)}, bf16[48,2304]{1,0:T(8,128)(2,1)S(1)}, u32[]{:S(2)}, u32[]{:S(2)}) collective-permute-start(bf16[48,2304]{1,0:T(8,128)(2,1)S(1)} %shard_map.113.rest_0_), channel_id=1, source_target_pairs={{0,24},{8,16},{16,8},{24,0},{1,25},{9,17},{17,9},{25,1},{2,26},{10... | collective-permute-start | bytes 663560 | tf_op jit(solution)/shard_map/ppermute | solution.py:281
  39.1 8.9 %shard_map.117.rest_0_ = bf16[48,2304]{1,0:T(8,128)(2,1)S(1)} custom-call(s32[1]{0:T(128)} %bitcast.index, bf16[192,1152]{1,0:T(8,128)(2,1)S(1)} %shard_map.115.rest_0_, bf16[192,1152]{1,0:T(8,128)(2,1)S(1)} %collective-permute-done.13.rest_1_, bf16[192,1152]{1,0:T(8,128)(2,1)S(1)} %shard_map.116.rest_2_, bf16[192,1152]{1,0:T(8,128)(2,1)S(1)} %collective-permute-done.16.rest_3_), custom_call_target="tpu_custom_call" | custom-call | flops 7361003520 | bytes 1990660 | tf_op jit(solution)/shard_map/pallas_call | solution.py:269
  48.0 4.6 %collective-permute-start.19 = (bf16[48,2304]{1,0:T(8,128)(2,1)S(1)}, bf16[48,2304]{1,0:T(8,128)(2,1)S(1)}, u32[]{:S(2)}, u32[]{:S(2)}) collective-permute-start(bf16[48,2304]{1,0:T(8,128)(2,1)S(1)} %shard_map.117.rest_0_), channel_id=1, source_target_pairs={{0,24},{8,16},{16,8},{24,0},{1,25},{9,17},{17,9},{25,1},{2,26},{10... | collective-permute-start | bytes 663560 | tf_op jit(solution)/shard_map/ppermute | solution.py:281
  52.6 0.2 collective-permute-start.18
  52.8 0.8 %collective-permute-start.17 = (bf16[48,2304]{1,0:T(8,128)(2,1)S(1)}, bf16[48,2304]{1,0:T(8,128)(2,1)S(1)}, u32[]{:S(2)}, u32[]{:S(2)}) collective-permute-start(bf16[48,2304]{1,0:T(8,128)(2,1)S(1)} %shard_map.117.rest_0_), channel_id=1, source_target_pairs={{0,8},{8,0},{16,24},{24,16},{1,9},{9,1},{17,25},{25,17},{2,10},{10... | collective-permute-start | bytes 663560 | tf_op jit(solution)/shard_map/ppermute | solution.py:281
  53.6 1.3 %shard_map.114 = (f32[48,5376]{1,0:T(8,128)}, f32[48,1536]{1,0:T(8,128)}, f32[48,1001]{1,0:T(8,128)}) custom-call(s32[1]{0:T(128)} %bitcast.index, f32[48,5376]{1,0:T(8,128)S(1)} %bitcast.24, f32[48,1536]{1,0:T(8,128)S(1)} %bitcast.26, f32[48,1001]{1,0:T(8,128)S(1)} %bitcast.28, bf16[48,2304]{1,0:T(8,128)(2,1)S(1)} %shard_map.113.rest_0_, ...), custom_call_target="tpu_custom_call" | custom-call | bytes 3923332 | tf_op jit(solution)/shard_map/pallas_call | solution.py:269
  54.9 4.0 %collective-permute-done.19.rest_3_ = bf16[48,2304]{1,0:T(8,128)(2,1)S(1)} collective-permute-done((bf16[48,2304]{1,0:T(8,128)(2,1)S(1)}, bf16[48,2304]{1,0:T(8,128)(2,1)S(1)}, u32[]{:S(2)}, u32[]{:S(2)}) %collective-permute-start.19) | collective-permute-done | bytes 221216 | tf_op jit(solution)/shard_map/ppermute | solution.py:281
  58.9 4.2 %collective-permute-done.18.rest_2_ = bf16[48,2304]{1,0:T(8,128)(2,1)S(1)} collective-permute-done((bf16[48,2304]{1,0:T(8,128)(2,1)S(1)}, bf16[48,2304]{1,0:T(8,128)(2,1)S(1)}, u32[]{:S(2)}, u32[]{:S(2)}) %collective-permute-start.18) | collective-permute-done | bytes 221216 | tf_op jit(solution)/shard_map/ppermute | solution.py:281
  63.1 0.7 %collective-permute-done.17.rest_1_ = bf16[48,2304]{1,0:T(8,128)(2,1)S(1)} collective-permute-done((bf16[48,2304]{1,0:T(8,128)(2,1)S(1)}, bf16[48,2304]{1,0:T(8,128)(2,1)S(1)}, u32[]{:S(2)}, u32[]{:S(2)}) %collective-permute-start.17) | collective-permute-done | bytes 221216 | tf_op jit(solution)/shard_map/ppermute | solution.py:281
  63.8 0.9 %shard_map.118 = (bf16[48,5376]{1,0:T(8,128)(2,1)}, bf16[48,1536]{1,0:T(8,128)(2,1)}, bf16[48,1001]{1,0:T(8,128)(2,1)}) custom-call(s32[1]{0:T(128)} %bitcast.index, bf16[48,2304]{1,0:T(8,128)(2,1)S(1)} %shard_map.117.rest_0_, bf16[48,2304]{1,0:T(8,128)(2,1)S(1)} %collective-permute-done.17.rest_1_, bf16[48,2304]{1,0:T(8,128)(2,1)S(1)} %collective-permute-done.18.rest_2_, ...), custom_call_target="tpu_custom_call" | custom-call | bytes 1644388 | tf_op jit(solution)/shard_map/pallas_call | solution.py:269
  (30 shorter events, 0.3 us)
Async XLA Ops:
  0.6 10.7 %copy-start = (f32[1,48,5376]{2,1,0:T(8,128)S(1)}, f32[1,48,5376]{2,1,0:T(8,128)}, u32[]{:S(2)}) copy-start(f32[1,48,5376]{2,1,0:T(8,128)} %param.9) | copy-start | bytes 3096580
  0.6 10.7 %copy-start.1 = (f32[1,1536,48]{1,2,0:T(8,128)S(1)}, f32[1,1536,48]{1,2,0:T(8,128)}, u32[]{:S(2)}) copy-start(f32[1,1536,48]{1,2,0:T(8,128)} %param.10) | copy-start | bytes 884740
  0.7 10.7 %copy-start.2 = (f32[1001,48]{0,1:T(8,128)S(1)}, f32[1001,48]{0,1:T(8,128)}, u32[]{:S(2)}) copy-start(f32[1001,48]{0,1:T(8,128)} %param.11) | copy-start | bytes 576580
  3.4 8.1 %collective-permute-start.3 = (bf16[48,1152]{1,0:T(8,128)(2,1)}, bf16[48,1152]{1,0:T(8,128)(2,1)S(1)}, u32[]{:S(2)}, u32[]{:S(2)}) collective-permute-start(bf16[48,1152]{1,0:T(8,128)(2,1)} %get-tuple-element.34), channel_id=1, source_target_pairs={{0,8},{8,0},{16,24},{24,16},{1,9},{9,1},{17,25},{25,17},{2,10},{10... | collective-permute-start | bytes 331784 | tf_op jit(solution)/shard_map/ppermute | solution.py:281
  6.4 7.7 %collective-permute-start.4 = (bf16[48,1152]{1,0:T(8,128)(2,1)}, bf16[48,1152]{1,0:T(8,128)(2,1)S(1)}, u32[]{:S(2)}, u32[]{:S(2)}) collective-permute-start(bf16[48,1152]{1,0:T(8,128)(2,1)} %get-tuple-element.35), channel_id=1, source_target_pairs={{0,16},{8,24},{16,0},{24,8},{1,17},{9,25},{17,1},{25,9},{2,18},{10... | collective-permute-start | bytes 331784 | tf_op jit(solution)/shard_map/ppermute | solution.py:281
  7.9 6.9 %collective-permute-start.5 = (bf16[48,1152]{1,0:T(8,128)(2,1)}, bf16[48,1152]{1,0:T(8,128)(2,1)S(1)}, u32[]{:S(2)}, u32[]{:S(2)}) collective-permute-start(bf16[48,1152]{1,0:T(8,128)(2,1)} %get-tuple-element.36), channel_id=1, source_target_pairs={{0,24},{8,16},{16,8},{24,0},{1,25},{9,17},{17,9},{25,1},{2,26},{10... | collective-permute-start | bytes 331784 | tf_op jit(solution)/shard_map/ppermute | solution.py:281
  7.9 11.1 %collective-permute-start = (bf16[48,1152]{1,0:T(8,128)(2,1)}, bf16[48,1152]{1,0:T(8,128)(2,1)S(1)}, u32[]{:S(2)}, u32[]{:S(2)}) collective-permute-start(bf16[48,1152]{1,0:T(8,128)(2,1)} %get-tuple-element.28), channel_id=1, source_target_pairs={{0,8},{8,0},{16,24},{24,16},{1,9},{9,1},{17,25},{25,17},{2,10},{10... | collective-permute-start | bytes 331784 | tf_op jit(solution)/shard_map/ppermute | solution.py:281
  9.8 9.2 %collective-permute-start.1 = (bf16[48,1152]{1,0:T(8,128)(2,1)}, bf16[48,1152]{1,0:T(8,128)(2,1)S(1)}, u32[]{:S(2)}, u32[]{:S(2)}) collective-permute-start(bf16[48,1152]{1,0:T(8,128)(2,1)} %get-tuple-element.29), channel_id=1, source_target_pairs={{0,16},{8,24},{16,0},{24,8},{1,17},{9,25},{17,1},{25,9},{2,18},{10... | collective-permute-start | bytes 331784 | tf_op jit(solution)/shard_map/ppermute | solution.py:281
  11.4 0.9 %copy-start.5 = (bf16[48,1152]{1,0:T(8,128)(2,1)S(1)}, bf16[48,1152]{1,0:T(8,128)(2,1)}, u32[]{:S(2)}) copy-start(bf16[48,1152]{1,0:T(8,128)(2,1)} %get-tuple-element.30) | copy-start | bytes 331780
  11.4 3.4 %copy-start.4 = (bf16[48,1152]{1,0:T(8,128)(2,1)S(1)}, bf16[48,1152]{1,0:T(8,128)(2,1)}, u32[]{:S(2)}) copy-start(bf16[48,1152]{1,0:T(8,128)(2,1)} %get-tuple-element.33.rest_0_) | copy-start | bytes 331780
  12.3 6.8 %collective-permute-start.2 = (bf16[48,1152]{1,0:T(8,128)(2,1)S(1)}, bf16[48,1152]{1,0:T(8,128)(2,1)S(1)}, u32[]{:S(2)}, u32[]{:S(2)}) collective-permute-start(bf16[48,1152]{1,0:T(8,128)(2,1)S(1)} %copy-done.5), channel_id=1, source_target_pairs={{0,24},{8,16},{16,8},{24,0},{1,25},{9,17},{17,9},{25,1},{2,26},{10... | collective-permute-start | bytes 331784 | tf_op jit(solution)/shard_map/ppermute | solution.py:281
  14.7 4.3 %copy-start.3 = (bf16[48,1152]{1,0:T(8,128)(2,1)S(1)}, bf16[48,1152]{1,0:T(8,128)(2,1)}, u32[]{:S(2)}) copy-start(bf16[48,1152]{1,0:T(8,128)(2,1)} %get-tuple-element.27.rest_0_) | copy-start | bytes 331780
  14.8 5.6 %collective-permute-start.6 = (bf16[48,1152]{1,0:T(8,128)(2,1)S(1)}, bf16[48,1152]{1,0:T(8,128)(2,1)S(1)}, u32[]{:S(2)}, u32[]{:S(2)}) collective-permute-start(bf16[48,1152]{1,0:T(8,128)(2,1)S(1)} %get-tuple-element.38.rest_0_), channel_id=1, source_target_pairs={{0,2},{1,3},{2,0},{3,1},{4,6},{5,7},{6,4},{7,5},{8,10},{9,11},{10,... | collective-permute-start | bytes 331784 | tf_op jit(solution)/shard_map/ppermute | solution.py:281
  16.5 9.6 %collective-permute-start.15 = (bf16[48,1152]{1,0:T(8,128)(2,1)S(1)}, bf16[48,1152]{1,0:T(8,128)(2,1)S(1)}, u32[]{:S(2)}, u32[]{:S(2)}) collective-permute-start(bf16[48,1152]{1,0:T(8,128)(2,1)S(1)} %get-tuple-element.38.rest_0_), channel_id=1, source_target_pairs={{0,6},{1,7},{2,4},{3,5},{4,2},{5,3},{6,0},{7,1},{8,14},{9,15},{10,... | collective-permute-start | bytes 331784 | tf_op jit(solution)/shard_map/ppermute | solution.py:281
  18.9 12.4 %collective-permute-start.14 = (bf16[48,1152]{1,0:T(8,128)(2,1)S(1)}, bf16[48,1152]{1,0:T(8,128)(2,1)S(1)}, u32[]{:S(2)}, u32[]{:S(2)}) collective-permute-start(bf16[48,1152]{1,0:T(8,128)(2,1)S(1)} %get-tuple-element.38.rest_0_), channel_id=1, source_target_pairs={{0,4},{1,5},{2,6},{3,7},{4,0},{5,1},{6,2},{7,3},{8,12},{9,13},{10,... | collective-permute-start | bytes 331784 | tf_op jit(solution)/shard_map/ppermute | solution.py:281
  20.4 16.6 %collective-permute-start.8 = (bf16[48,2304]{1,0:T(8,128)(2,1)S(1)}, bf16[48,2304]{1,0:T(8,128)(2,1)S(1)}, u32[]{:S(2)}, u32[]{:S(2)}) collective-permute-start(bf16[48,2304]{1,0:T(8,128)(2,1)S(1)} %shard_map.113.rest_0_), channel_id=1, source_target_pairs={{0,16},{8,24},{16,0},{24,8},{1,17},{9,25},{17,1},{25,9},{2,18},{10... | collective-permute-start | bytes 663560 | tf_op jit(solution)/shard_map/ppermute | solution.py:281
  23.1 13.9 %collective-permute-start.7 = (bf16[48,2304]{1,0:T(8,128)(2,1)S(1)}, bf16[48,2304]{1,0:T(8,128)(2,1)S(1)}, u32[]{:S(2)}, u32[]{:S(2)}) collective-permute-start(bf16[48,2304]{1,0:T(8,128)(2,1)S(1)} %shard_map.113.rest_0_), channel_id=1, source_target_pairs={{0,8},{8,0},{16,24},{24,16},{1,9},{9,1},{17,25},{25,17},{2,10},{10... | collective-permute-start | bytes 663560 | tf_op jit(solution)/shard_map/ppermute | solution.py:281
  23.1 8.3 %collective-permute-start.12 = (bf16[48,1152]{1,0:T(8,128)(2,1)S(1)}, bf16[48,1152]{1,0:T(8,128)(2,1)S(1)}, u32[]{:S(2)}, u32[]{:S(2)}) collective-permute-start(bf16[48,1152]{1,0:T(8,128)(2,1)S(1)} %get-tuple-element.42.rest_0_.rest_4_), channel_id=1, source_target_pairs={{0,6},{1,7},{2,4},{3,5},{4,2},{5,3},{6,0},{7,1},{8,14},{9,15},{10,... | collective-permute-start | bytes 331784 | tf_op jit(solution)/shard_map/ppermute | solution.py:281
  26.1 9.8 %collective-permute-start.11 = (bf16[48,1152]{1,0:T(8,128)(2,1)S(1)}, bf16[48,1152]{1,0:T(8,128)(2,1)S(1)}, u32[]{:S(2)}, u32[]{:S(2)}) collective-permute-start(bf16[48,1152]{1,0:T(8,128)(2,1)S(1)} %get-tuple-element.42.rest_0_.rest_4_), channel_id=1, source_target_pairs={{0,4},{1,5},{2,6},{3,7},{4,0},{5,1},{6,2},{7,3},{8,12},{9,13},{10,... | collective-permute-start | bytes 331784 | tf_op jit(solution)/shard_map/ppermute | solution.py:281
  31.4 5.6 %collective-permute-start.10 = (bf16[48,1152]{1,0:T(8,128)(2,1)S(1)}, bf16[48,1152]{1,0:T(8,128)(2,1)S(1)}, u32[]{:S(2)}, u32[]{:S(2)}) collective-permute-start(bf16[48,1152]{1,0:T(8,128)(2,1)S(1)} %get-tuple-element.42.rest_0_.rest_4_), channel_id=1, source_target_pairs={{0,2},{1,3},{2,0},{3,1},{4,6},{5,7},{6,4},{7,5},{8,10},{9,11},{10,... | collective-permute-start | bytes 331784 | tf_op jit(solution)/shard_map/ppermute | solution.py:281
  31.4 7.6 %collective-permute-start.16 = (bf16[192,1152]{1,0:T(8,128)(2,1)S(1)}, bf16[192,1152]{1,0:T(8,128)(2,1)S(1)}, u32[]{:S(2)}, u32[]{:S(2)}) collective-permute-start(bf16[192,1152]{1,0:T(8,128)(2,1)S(1)} %shard_map.116.rest_2_), channel_id=1, source_target_pairs={{0,1},{1,0},{2,3},{3,2},{4,5},{5,4},{6,7},{7,6},{8,9},{9,8},{10,11... | collective-permute-start | bytes 1327112 | tf_op jit(solution)/shard_map/ppermute | solution.py:281
  37.0 2.0 %collective-permute-start.13 = (bf16[192,1152]{1,0:T(8,128)(2,1)S(1)}, bf16[192,1152]{1,0:T(8,128)(2,1)S(1)}, u32[]{:S(2)}, u32[]{:S(2)}) collective-permute-start(bf16[192,1152]{1,0:T(8,128)(2,1)S(1)} %shard_map.115.rest_0_), channel_id=1, source_target_pairs={{0,1},{1,0},{2,3},{3,2},{4,5},{5,4},{6,7},{7,6},{8,9},{9,8},{10,11... | collective-permute-start | bytes 1327112 | tf_op jit(solution)/shard_map/ppermute | solution.py:281
  37.1 16.5 %collective-permute-start.9 = (bf16[48,2304]{1,0:T(8,128)(2,1)S(1)}, bf16[48,2304]{1,0:T(8,128)(2,1)S(1)}, u32[]{:S(2)}, u32[]{:S(2)}) collective-permute-start(bf16[48,2304]{1,0:T(8,128)(2,1)S(1)} %shard_map.113.rest_0_), channel_id=1, source_target_pairs={{0,24},{8,16},{16,8},{24,0},{1,25},{9,17},{17,9},{25,1},{2,26},{10... | collective-permute-start | bytes 663560 | tf_op jit(solution)/shard_map/ppermute | solution.py:281
  48.0 10.9 %collective-permute-start.19 = (bf16[48,2304]{1,0:T(8,128)(2,1)S(1)}, bf16[48,2304]{1,0:T(8,128)(2,1)S(1)}, u32[]{:S(2)}, u32[]{:S(2)}) collective-permute-start(bf16[48,2304]{1,0:T(8,128)(2,1)S(1)} %shard_map.117.rest_0_), channel_id=1, source_target_pairs={{0,24},{8,16},{16,8},{24,0},{1,25},{9,17},{17,9},{25,1},{2,26},{10... | collective-permute-start | bytes 663560 | tf_op jit(solution)/shard_map/ppermute | solution.py:281
  52.6 10.5 %collective-permute-start.18 = (bf16[48,2304]{1,0:T(8,128)(2,1)S(1)}, bf16[48,2304]{1,0:T(8,128)(2,1)S(1)}, u32[]{:S(2)}, u32[]{:S(2)}) collective-permute-start(bf16[48,2304]{1,0:T(8,128)(2,1)S(1)} %shard_map.117.rest_0_), channel_id=1, source_target_pairs={{0,16},{8,24},{16,0},{24,8},{1,17},{9,25},{17,1},{25,9},{2,18},{10... | collective-permute-start | bytes 663560 | tf_op jit(solution)/shard_map/ppermute | solution.py:281
  52.8 11.1 %collective-permute-start.17 = (bf16[48,2304]{1,0:T(8,128)(2,1)S(1)}, bf16[48,2304]{1,0:T(8,128)(2,1)S(1)}, u32[]{:S(2)}, u32[]{:S(2)}) collective-permute-start(bf16[48,2304]{1,0:T(8,128)(2,1)S(1)} %shard_map.117.rest_0_), channel_id=1, source_target_pairs={{0,8},{8,0},{16,24},{24,16},{1,9},{9,1},{17,25},{25,17},{2,10},{10... | collective-permute-start | bytes 663560 | tf_op jit(solution)/shard_map/ppermute | solution.py:281
